TPU v7x, 32 devices: a whole 2x2x4 slice. The times are simulated.
32 devices in a mesh: src: 2 (over x), tgt: 4 (over z), feat: 4 (over y, core).
Axes of the slice: x: 2, y: 2, z: 4, core: 2. Of those that a mesh axis runs over, the one named last changes fastest.
Arguments:
- errors: bfloat16 [8, 1024, 2048], P('tgt', 'feat', 'src'), may hold values from -0.796875 to 0.796875
- saved_codes: bfloat16 [8, 1024, 2048], P('src', None, 'feat'), may hold values from 0 to 2
- active_mask: int32 [8, 1024, 2048], P('src', 'tgt', 'feat'), may hold values 0 or 1
- decoder: bfloat16 [8, 8, 2048, 2048], P('src', 'tgt', 'feat'), may hold values from -0.125 to 0.125
Outputs:
- code_grads: bfloat16 [8, 1024, 2048], P('src', 'tgt', 'feat')
- decoder_grads: bfloat16 [8, 8, 2048, 2048], P('src', 'tgt', 'feat')
All inputs are finite; a program needn't handle non-finite values. No bound on the sum of `active_mask` on one device may be relied on, other than what follows from the above.
Results may differ from a plain program's by a relative error of at most 0.001.
Values may be sent and summed in bfloat16 or wider, within the bound.
No kernel may reach another device: no remote copies, remote signals or barrier semaphores. Data moves between devices by JAX's collectives and lax.ppermute only.
A program may use at most 128 MiB of HBM per device.

v0:
```python
import jax
import jax.numpy as jnp
from jax import lax
from jax.sharding import PartitionSpec as P


def body(errors, saved_codes, active_mask, decoder):
    src_count = decoder.shape[0]
    tgt_count = decoder.shape[1]
    feat_count = decoder.shape[2]
    tokens_all = saved_codes.shape[1]
    src_ids = lax.axis_index("src") * src_count + jnp.arange(src_count, dtype=jnp.int32)
    tgt_ids = lax.axis_index("tgt") * tgt_count + jnp.arange(tgt_count, dtype=jnp.int32)
    upper_mask = (tgt_ids[None, :] >= src_ids[:, None]).astype(jnp.float32)
    dec_kept = decoder * upper_mask[:, :, None, None].astype(jnp.bfloat16)
    all_columns = lax.all_gather(errors, "src", axis=2, tiled=True)
    portion = lax.all_gather(all_columns, "feat", axis=1, tiled=True)
    grad_block = jnp.einsum(
        "itf,jtd->ijfd", saved_codes, portion, preferred_element_type=jnp.float32
    )
    tile_grads = grad_block
    state_out = (tile_grads, portion)
    tile_grads, gathered = state_out
    term = jnp.einsum("jtd,ijfd->tif", gathered, dec_kept, preferred_element_type=jnp.float32)
    shares = lax.psum_scatter(
        term.reshape(
            tokens_all // lax.axis_size("tgt") * lax.axis_size("tgt"), src_count * feat_count
        ),
        "tgt",
        scatter_dimension=0,
        tiled=True,
    )
    summed = shares.reshape(-1, src_count, feat_count).transpose(1, 0, 2)
    code_grads = (summed * active_mask.astype(jnp.float32)).astype(jnp.bfloat16)
    decoder_grads = (tile_grads * upper_mask[:, :, None, None]).astype(jnp.bfloat16)
    return (code_grads, decoder_grads)


def solution(mesh):
    in_specs = (
        P("tgt", "feat", "src"),
        P("src", None, "feat"),
        P("src", "tgt", "feat"),
        P("src", "tgt", "feat", None),
    )
    out_specs = (P("src", "tgt", "feat"), P("src", "tgt", "feat", None))
    return jax.shard_map(body, mesh=mesh, in_specs=in_specs, out_specs=out_specs, check_vma=False)
```

profile of v0, /device:TPU:0, one launch (start us, length us, event | category | flops | bytes accessed | tf_op | source)
XLA Modules:
  0.0 283.8 jit_solution(2194667225887718104)
XLA Ops:
  7.2 0.0 all-gather.3.cloned.1.call-start
  7.2 0.7 all-gather.3.cloned.1.call-update
  7.9 0.0 all-gather.5.cloned.1.call-start
  7.9 37.4 %all-gather.3.cloned.1.call-done = bf16[2,256,2048]{2,1,0:T(8,128)(2,1)} async-done(((bf16[2,256,1024]{2,1,0:T(8,128)(2,1)}), bf16[2,256,2048]{2,1,0:T(8,128)(2,1)}) %all-gather.3.cloned.1.call-update) | async-done | bytes 2097168 | tf_op jit(solution)/shard_map/all_gather | solution.py:16
  45.4 0.0 all-gather.5.cloned.1.call-update
  45.4 0.0 reduce-scatter.2.cloned.1.call-start
  45.5 0.1 compare_convert_fusion
  45.6 0.1 copy.9
  45.7 59.6 %all-gather.5.cloned.1.call-done = bf16[2,1024,2048]{2,1,0:T(8,128)(2,1)} async-done(((bf16[2,256,2048]{2,1,0:T(8,128)(2,1)}), bf16[2,1024,2048]{2,1,0:T(8,128)(2,1)}) %all-gather.5.cloned.1.call-update) | async-done | bytes 8388624 | tf_op jit(solution)/shard_map/all_gather | solution.py:17
  105.3 24.1 %fusion.1 = f32[4,512,1024,1]{2,1,3,0:T(8,128)} fusion(bf16[4,2,512,2048]{3,2,1,0:T(8,128)(2,1)} %param.7, bf16[2,1024,2048]{2,1,0:T(8,128)(2,1)} %all-gather.5.cloned.1.call-done, bf16[4,2]{1,0:T(4,128)(2,1)S(1)} %copy.9), kind=kOutput, calls=%fused_computation.2 | convolution fusion | flops 17188257792 | bytes 33554448 | tf_op jit(solution)/shard_map/jtd,ijfd->tif/dot_general | solution.py:24
  129.4 0.0 reduce-scatter.2.cloned.1.call-update
  129.4 1.9 copy.10
  131.4 24.8 %fusion = bf16[4,2,512,2048]{2,3,0,1:T(8,128)(2,1)} fusion(f32[4,2]{0,1:T(2,128)S(1)} %get-tuple-element.6, bf16[2,1024,2048]{2,1,0:T(8,128)(2,1)} %all-gather.5.cloned.1.call-done, bf16[4,1024,512]{2,1,0:T(8,128)(2,1)} %param.5), kind=kOutput, calls=%fused_computation.1 | convolution fusion | flops 17196646400 | bytes 29360160 | tf_op jit(solution)/shard_map/itf,jtd->ijfd/dot_general | solution.py:18
  156.1 21.6 %copy.13 = bf16[4,2,512,2048]{3,2,1,0:T(8,128)(2,1)} copy(bf16[4,2,512,2048]{2,3,0,1:T(8,128)(2,1)} %fusion) | data formatting | bytes 33554432
  177.7 96.3 %reduce-scatter.2.cloned.1.call-done = f32[256,2048]{0,1:T(8,128)} async-done(((f32[1024,2048]{0,1:T(8,128)}), f32[256,2048]{0,1:T(8,128)}) %reduce-scatter.2.cloned.1.call-update) | async-done | bytes 2097168 | tf_op jit(solution)/shard_map/reduce_scatter | solution.py:25
  274.1 1.9 multiply_convert_fusion
  276.0 1.3 copy.12
  (2 shorter events, 0.0 us)
Async XLA Ops:
  7.2 38.2 %all-gather.3.cloned.1.call-start = ((), (), s32[]{:S(2)}) async-start(), calls=%async_computation.1 | async-start | bytes 3145728 | tf_op jit(solution)/shard_map/all_gather | solution.py:16
  7.9 97.4 %all-gather.5.cloned.1.call-start = ((), (), s32[]{:S(2)}) async-start(), calls=%async_computation.2 | async-start | bytes 10485760 | tf_op jit(solution)/shard_map/all_gather | solution.py:17
  45.4 228.6 %reduce-scatter.2.cloned.1.call-start = ((), (), s32[]{:S(2)}) async-start(), calls=%async_computation.3 | async-start | bytes 10485760 | tf_op jit(solution)/shard_map/reduce_scatter | solution.py:25
Sparse Core Ops, SparseCore 0:
  9.5 35.7 all-gather.2
  46.9 58.2 all-gather.4
  129.6 144.4 reduce-scatter.1
where the time goes:
time: 285 us; the launch traced here: 284 us
  waiting for transfers between devices  194 us (68%)
  matrix products  48.9 us (17%)
  local copies, waits for them, and re-layouts  24.9 us (9%)
  between operations  13.8 us (5%)
    reduce_scatter x1, waiting for transfers between devices, body(): lax.psum_scatter(term.reshape(tokens_all // lax.axis_size('tgt') * lax.ax...  96.3 us
    all_gather x1, waiting for transfers between devices, body(): portion = lax.all_gather(all_columns, 'feat', axis=1, tiled=True)  59.6 us
    all_gather x1, waiting for transfers between devices, body(): all_columns = lax.all_gather(errors, 'src', axis=2, tiled=True)  37.4 us
    unnamed x3, local copies, waits for them, and re-layouts  24.8 us
    dot_general x1, matrix products, body(): jnp.einsum('itf,jtd->ijfd', saved_codes, portion, preferred_element_type=...  24.8 us
    dot_general x1, matrix products, body(): jnp.einsum('jtd,ijfd->tif', gathered, dec_kept, preferred_element_type=jn...  24.1 us
  transfers between devices with their start and end apart: 3, of which 3 were waited for; matrix products, arithmetic and copies ran while one was open for 17% of the time, Pallas kernels for 0%

commit v1 on v0

v1 whole, which is shorter than its diff:
```python
import functools

import jax
import jax.numpy as jnp
from jax import lax
from jax.experimental import pallas as pl
from jax.experimental.pallas import tpu as pltpu
from jax.sharding import PartitionSpec as P

LANES = 128
SUBLANES = 8
STEPS_PER_OCTAVE = 64
TOP = 32760.0
FLOOR = 1e-30
EIGHTHS = (2, 2, 2, 2)
MIB = 1 << 20


def quantize(v, out_ref, lead, layer):
    rows, width = v.shape
    half, tiles = rows // 2, width // LANES
    peak = jnp.maximum(jnp.max(jnp.abs(v), axis=1, keepdims=True), FLOOR)
    scale = jnp.ceil(jnp.log2(peak) * STEPS_PER_OCTAVE)
    gain = jnp.exp2(scale * (-1.0 / STEPS_PER_OCTAVE)) * TOP
    q = jnp.floor(v * gain + 0.5).astype(jnp.int32)
    scale = scale.astype(jnp.int32)
    words = (q[half:] << 16) | (q[:half] & 0xFFFF)
    scale_words = (scale[half:] << 16) | (scale[:half] & 0xFFFF)
    for tile in range(tiles):
        start = (layer * tiles + tile) * half
        if not isinstance(start, int):
            start = pl.multiple_of(start, SUBLANES)
        out_ref[lead, pl.ds(start, half), :] = words[:, tile * LANES : (tile + 1) * LANES]
    end = out_ref.shape[1] - SUBLANES
    lane = lax.broadcasted_iota(jnp.int32, (SUBLANES, LANES), 1)
    tail = out_ref[lead, pl.ds(end, SUBLANES), :]
    for group in range(half // SUBLANES):
        piece = scale_words[group * SUBLANES : (group + 1) * SUBLANES]
        tail = jnp.where(lane == layer * (half // SUBLANES) + group, piece, tail)
    out_ref[lead, pl.ds(end, SUBLANES), :] = tail


def dequantize(in_ref, lead, layer, rows, width):
    half, tiles = rows // 2, width // LANES
    groups = half // SUBLANES
    end = in_ref.shape[1] - SUBLANES
    words = jnp.concatenate(
        [in_ref[lead, pl.ds((layer * tiles + tile) * half, half), :] for tile in range(tiles)], axis=1
    )
    tail = in_ref[lead, pl.ds(end, SUBLANES), :]
    scale_words = jnp.concatenate(
        [tail[:, layer * groups + group : layer * groups + group + 1] for group in range(groups)], axis=0
    )

    def step(scale):
        return jnp.exp2(scale.astype(jnp.float32) * (1.0 / STEPS_PER_OCTAVE)) * (1.0 / TOP)

    low = ((words << 16) >> 16).astype(jnp.float32) * step((scale_words << 16) >> 16)
    high = (words >> 16).astype(jnp.float32) * step(scale_words >> 16)
    return jnp.concatenate([low, high], axis=0)


def payload_rows(layers, rows, width):
    return layers * (width // LANES) * (rows // 2) + SUBLANES


def terms_kernel(n_tgt, n_pieces, place, keep, order, *refs):
    pieces = refs[:n_pieces]
    dec_ref, own_ref, send_ref, err_ref, acc = refs[n_pieces:]
    layer = pl.program_id(0)
    tgt_count, total_rows, _ = err_ref.shape
    rows = total_rows // n_tgt
    width = acc.shape[1]

    @pl.when(layer == 0)
    def _():
        for index, piece in enumerate(pieces):
            _, tokens, columns = piece.shape
            row = pl.multiple_of(place[2 * index] * tokens, tokens)
            column = pl.multiple_of(place[2 * index + 1] * columns, columns)
            for tgt in range(tgt_count):
                err_ref[tgt, pl.ds(row, tokens), pl.ds(column, columns)] = piece[tgt]
        for lead in range(n_tgt - 1):
            send_ref[lead, pl.ds(send_ref.shape[1] - SUBLANES, SUBLANES), :] = jnp.zeros((SUBLANES, LANES), jnp.int32)

    acc[...] = jnp.zeros_like(acc)
    for tgt in range(tgt_count):

        @pl.when(keep[layer * tgt_count + tgt] == 1)
        def _():
            acc[...] += lax.dot_general(
                err_ref[tgt], dec_ref[0, tgt], (((1,), (1,)), ((), ())), preferred_element_type=jnp.float32
            )

    own_ref[0] = acc[...]
    for lead in range(n_tgt - 1):
        start = pl.multiple_of(order[lead] * rows, rows)
        quantize(acc[pl.ds(start, rows), :], send_ref, lead, layer)


def terms_call(pieces, place, keep, order, decoder, n_tgt, total_rows):
    src_count, tgt_count, width, columns = decoder.shape
    rows = total_rows // n_tgt
    payload = (n_tgt - 1, payload_rows(src_count, rows, width), LANES)
    whole = lambda shape: pl.BlockSpec(shape, lambda i, *_: (0,) * len(shape))
    return pl.pallas_call(
        functools.partial(terms_kernel, n_tgt, len(pieces)),
        grid_spec=pltpu.PrefetchScalarGridSpec(
            num_scalar_prefetch=3,
            grid=(src_count,),
            in_specs=[whole(piece.shape) for piece in pieces]
            + [pl.BlockSpec((1, tgt_count, width, columns), lambda i, *_: (i, 0, 0, 0))],
            out_specs=[
                pl.BlockSpec((1, total_rows, width), lambda i, *_: (i, 0, 0)),
                whole(payload),
                whole((tgt_count, total_rows, columns)),
            ],
            scratch_shapes=[pltpu.VMEM((total_rows, width), jnp.float32)],
        ),
        out_shape=[
            jax.ShapeDtypeStruct((src_count, total_rows, width), jnp.float32),
            jax.ShapeDtypeStruct(payload, jnp.int32),
            jax.ShapeDtypeStruct((tgt_count, total_rows, columns), jnp.bfloat16),
        ],
        compiler_params=pltpu.CompilerParams(vmem_limit_bytes=48 * MIB),
        cost_estimate=pl.CostEstimate(
            flops=2 * total_rows * width * columns * src_count * tgt_count,
            bytes_accessed=decoder.size * 2 + src_count * total_rows * width * 4 + 4 * total_rows * columns * tgt_count,
            transcendentals=0,
        ),
        name="terms",
    )(place, keep, order, *pieces, decoder)


def relay_kernel(order, own_ref, got_ref, send_ref):
    src_count, rows, width = own_ref.shape
    send_ref[0, pl.ds(send_ref.shape[1] - SUBLANES, SUBLANES), :] = jnp.zeros((SUBLANES, LANES), jnp.int32)
    for layer in range(src_count):
        quantize(own_ref[layer] + dequantize(got_ref, 0, layer, rows, width), send_ref, 0, layer)


def relay_call(order, own, got, n_tgt):
    src_count, total_rows, width = own.shape
    rows = total_rows // n_tgt
    blocks, length, _ = got.shape
    return pl.pallas_call(
        relay_kernel,
        grid_spec=pltpu.PrefetchScalarGridSpec(
            num_scalar_prefetch=1,
            grid=(blocks - 1,),
            in_specs=[
                pl.BlockSpec((src_count, rows, width), lambda i, order: (0, order[i], 0)),
                pl.BlockSpec((1, length, LANES), lambda i, order: (i, 0, 0)),
            ],
            out_specs=pl.BlockSpec((1, length, LANES), lambda i, order: (i, 0, 0)),
        ),
        out_shape=jax.ShapeDtypeStruct((blocks - 1, length, LANES), jnp.int32),
        compiler_params=pltpu.CompilerParams(vmem_limit_bytes=24 * MIB),
        cost_estimate=pl.CostEstimate(
            flops=20 * src_count * rows * width * (blocks - 1),
            bytes_accessed=(blocks - 1) * (8 * length * LANES + 4 * src_count * rows * width),
            transcendentals=0,
        ),
        name="relay",
    )(order, own, got)


def finish_kernel(n_got, offset, stride, here, own_ref, *refs):
    gots = refs[:n_got]
    mask_ref, out_ref, mask_tile, out_tile, in_sem, out_sem = refs[n_got : n_got + 1] + refs[-5:]
    src_count, rows, width = own_ref.shape
    parts = mask_ref.shape[1] // stride
    tokens = rows // parts

    def mask_copy(part):
        return pltpu.make_async_copy(
            mask_ref.at[:, pl.ds(part * stride + offset, tokens), :],
            mask_tile.at[:, pl.ds(part * tokens, tokens), :],
            in_sem.at[part],
        )

    def out_copy(part):
        return pltpu.make_async_copy(
            out_tile.at[:, pl.ds(part * tokens, tokens), :],
            out_ref.at[:, pl.ds(part * stride + offset, tokens), :],
            out_sem.at[part],
        )

    for part in range(parts):
        mask_copy(part).start()
    for part in range(parts):
        mask_copy(part).wait()
    for layer in range(src_count):
        total = own_ref[layer]
        for got in gots:
            total += dequantize(got, 0, layer, rows, width)
        out_tile[layer] = (total * mask_tile[layer].astype(jnp.float32)).astype(jnp.bfloat16)
    for part in range(parts):
        out_copy(part).start()
    for part in range(parts):
        out_copy(part).wait()


def finish_call(here, own, gots, mask, out, offset, stride, n_tgt):
    src_count, total_rows, width = own.shape
    rows = total_rows // n_tgt
    parts = mask.shape[1] // stride
    length = gots[0].shape[1]
    anywhere = pl.BlockSpec(memory_space=pl.ANY)
    in_specs = [pl.BlockSpec((src_count, rows, width), lambda i, here: (0, here[0], 0))]
    for got in gots:
        last = got.shape[0] - 1
        in_specs.append(pl.BlockSpec((1, length, LANES), lambda i, here, last=last: (last, 0, 0)))
    in_specs.append(anywhere)
    operands = [here, own, *gots, mask]
    aliases = {}
    if out is not None:
        in_specs.append(anywhere)
        aliases = {len(operands): 0}
        operands.append(out)
    return pl.pallas_call(
        functools.partial(finish_kernel, len(gots), offset, stride),
        grid_spec=pltpu.PrefetchScalarGridSpec(
            num_scalar_prefetch=1,
            grid=(1,),
            in_specs=in_specs,
            out_specs=anywhere,
            scratch_shapes=[
                pltpu.VMEM((src_count, rows, width), jnp.int32),
                pltpu.VMEM((src_count, rows, width), jnp.bfloat16),
                pltpu.SemaphoreType.DMA((parts,)),
                pltpu.SemaphoreType.DMA((parts,)),
            ],
        ),
        out_shape=jax.ShapeDtypeStruct(mask.shape, jnp.bfloat16),
        input_output_aliases=aliases,
        compiler_params=pltpu.CompilerParams(vmem_limit_bytes=24 * MIB),
        cost_estimate=pl.CostEstimate(
            flops=20 * src_count * rows * width,
            bytes_accessed=src_count * rows * width * 10 + 4 * length * LANES * len(gots),
            transcendentals=0,
        ),
        name="finish",
    )(*operands)


def turn_kernel(spans, codes_ref, out_ref):
    tokens = codes_ref.shape[1]
    stride = sum(spans)
    blocks = tokens // stride
    offset = column = 0
    for span in spans:
        rows = jnp.concatenate(
            [codes_ref[0, pl.ds(block * stride + offset, span), :] for block in range(blocks)], axis=0
        )
        out_ref[0, :, pl.ds(column, blocks * span)] = rows.T
        offset += span
        column += blocks * span


def turn_call(codes, spans):
    src_count, tokens, width = codes.shape
    return pl.pallas_call(
        functools.partial(turn_kernel, spans),
        grid=(src_count,),
        in_specs=[pl.BlockSpec((1, tokens, width), lambda i: (i, 0, 0))],
        out_specs=pl.BlockSpec((1, width, tokens), lambda i: (i, 0, 0)),
        out_shape=jax.ShapeDtypeStruct((src_count, width, tokens), jnp.bfloat16),
        compiler_params=pltpu.CompilerParams(vmem_limit_bytes=24 * MIB),
        cost_estimate=pl.CostEstimate(flops=codes.size, bytes_accessed=codes.size * 4, transcendentals=0),
        name="turn",
    )(codes)


def grads_kernel(layer, n_chunks, keep, codes_ref, *refs):
    chunks = refs[:n_chunks]
    out_ref = refs[-2]
    acc = refs[-1]
    tgt = pl.program_id(0)
    kept = keep[layer * pl.num_programs(0) + tgt] == 1

    @pl.when(kept)
    def _():
        column = 0
        for index, chunk in enumerate(chunks):
            depth = chunk.shape[1]
            term = jnp.dot(
                codes_ref[0, :, pl.ds(column, depth)], chunk[0], preferred_element_type=jnp.float32
            )
            if index == 0:
                acc[...] = term
            elif index < n_chunks - 1:
                acc[...] += term
            else:
                out_ref[0, 0] = (acc[...] + term).astype(jnp.bfloat16)
            column += depth

    @pl.when(jnp.logical_not(kept))
    def _():
        out_ref[...] = jnp.zeros_like(out_ref)


def grads_call(layer, keep, codes_t, chunks, out, shape):
    src_count, tgt_count, width, columns = shape
    tokens = codes_t.shape[2]
    in_specs = [pl.BlockSpec((1, width, tokens), lambda i, *_: (layer, 0, 0))]
    for chunk in chunks:
        in_specs.append(pl.BlockSpec((1, chunk.shape[1], columns), lambda i, *_: (i, 0, 0)))
    operands = [keep, codes_t, *chunks]
    aliases = {}
    if out is not None:
        in_specs.append(pl.BlockSpec(memory_space=pl.ANY))
        aliases = {len(operands): 0}
        operands.append(out)
    return pl.pallas_call(
        functools.partial(grads_kernel, layer, len(chunks)),
        grid_spec=pltpu.PrefetchScalarGridSpec(
            num_scalar_prefetch=1,
            grid=(tgt_count,),
            in_specs=in_specs,
            out_specs=pl.BlockSpec((1, 1, width, columns), lambda i, *_: (layer, i, 0, 0)),
            scratch_shapes=[pltpu.VMEM((width, columns), jnp.float32)],
        ),
        out_shape=jax.ShapeDtypeStruct(shape, jnp.bfloat16),
        input_output_aliases=aliases,
        compiler_params=pltpu.CompilerParams(vmem_limit_bytes=48 * MIB),
        cost_estimate=pl.CostEstimate(
            flops=2 * tgt_count * width * columns * tokens,
            bytes_accessed=2 * tgt_count * (width * columns + tokens * columns) + 2 * width * tokens,
            transcendentals=0,
        ),
        name="grads",
    )(*operands)


def swap(x, axes, flips, sizes):
    pairs = []
    total = 1
    for size in sizes:
        total *= size
    for index in range(total):
        rest, other, weight = index, 0, 1
        for size, flip in reversed(list(zip(sizes, flips))):
            other += ((rest % size) ^ flip) * weight
            rest //= size
            weight *= size
        pairs.append((index, other))
    return lax.ppermute(x, axes, pairs)


def gather_pieces(part, chunk, n_src, n_feat):
    src, feat = lax.axis_index("src"), lax.axis_index("feat")
    if (n_src, n_feat) != (2, 4):
        columns = lax.all_gather(part, "src", axis=2, tiled=True)
        return [lax.all_gather(columns, "feat", axis=1, tiled=True)], [0, 0]
    over_x = lambda x: swap(x, "src", (1,), (n_src,))
    over_y = lambda x: swap(x, "feat", (2,), (n_feat,))
    over_core = lambda x: swap(x, "feat", (1,), (n_feat,))
    from_x, from_y = over_x(part), over_y(part)
    from_far = over_y(from_x) if chunk % 2 == 0 else over_x(from_y)
    pieces, place = [], []
    for piece, dx, dy in ((part, 0, 0), (from_x, 1, 0), (from_y, 0, 2), (from_far, 1, 2)):
        pieces += [piece, over_core(piece)]
        place += [feat ^ dy, src ^ dx, feat ^ dy ^ 1, src ^ dx]
    return pieces, place


def body(n_src, n_tgt, n_feat, errors, saved_codes, active_mask, decoder):
    src_count, tgt_count, width, _ = decoder.shape
    stride = errors.shape[1]
    src, tgt = lax.axis_index("src"), lax.axis_index("tgt")
    src_ids = src * src_count + jnp.arange(src_count, dtype=jnp.int32)
    tgt_ids = tgt * tgt_count + jnp.arange(tgt_count, dtype=jnp.int32)
    keep = (tgt_ids[None, :] >= src_ids[:, None]).astype(jnp.int32).reshape(-1)
    here = jnp.reshape(tgt, (1,)).astype(jnp.int32)
    lead = jnp.arange(n_tgt, dtype=jnp.int32)
    orders = [jnp.where(tgt == n_tgt - 1 - hop, lead, n_tgt - 1 - lead) for hop in range(n_tgt - 1)]

    spans = [stride * part // 8 for part in EIGHTHS]
    codes_t = turn_call(saved_codes, spans)
    code_grads = None
    chunks = []
    offset = 0
    for index, span in enumerate(spans):
        part = lax.slice_in_dim(errors, offset, offset + span, axis=1)
        pieces, place = gather_pieces(part, index, n_src, n_feat)
        place = jnp.stack([jnp.asarray(p, jnp.int32) for p in place])
        own, send, chunk = terms_call(pieces, place, keep, orders[0], decoder, n_tgt, n_feat * span)
        chunks.append(chunk)
        gots = []
        for hop in range(n_tgt - 1):
            if hop:
                send = relay_call(orders[hop], own, gots[-1], n_tgt)
            pairs = [(n_tgt - 1 - hop, n_tgt - 2 - hop), (hop, hop + 1)]
            gots.append(lax.ppermute(send, "tgt", pairs))
        code_grads = finish_call(here, own, gots, active_mask, code_grads, offset, stride, n_tgt)
        offset += span
    decoder_grads = None
    for layer in range(src_count):
        decoder_grads = grads_call(layer, keep, codes_t, chunks, decoder_grads, decoder.shape)
    return code_grads, decoder_grads


def solution(mesh):
    sizes = [mesh.shape[axis] for axis in ("src", "tgt", "feat")]
    in_specs = (
        P("tgt", "feat", "src"),
        P("src", None, "feat"),
        P("src", "tgt", "feat"),
        P("src", "tgt", "feat", None),
    )
    out_specs = (P("src", "tgt", "feat"), P("src", "tgt", "feat", None))
    return jax.shard_map(
        functools.partial(body, *sizes), mesh=mesh, in_specs=in_specs, out_specs=out_specs, check_vma=False
    )
```

time: 285 us -> 215 us (0.75)
  waiting for transfers between devices: 194 us -> 54.7 us
  Pallas kernels: 0 us -> 92.6 us
  matrix products: 48.9 us -> 0 us
  starting transfers between devices: 0.11 us -> 42.6 us
  between operations: 13.8 us -> 1.19 us
    all_gather x2 -> x0, waiting for transfers between devices: 97.1 us -> none  [the longest x1 59.6 us: body(): portion = lax.all_gather(all_columns, 'feat', axis=1, tiled=True)]
    reduce_scatter x1 -> x0, waiting for transfers between devices: 96.3 us -> none  [body(): lax.psum_scatter(term.reshape(tokens_all // lax.axis_size('tgt') * lax.ax...]
    pallas_call x0 -> x21, Pallas kernels: none -> 92.6 us  [the longest x4 40.7 us: terms_call(): pl.pallas_call(functools.partial(terms_kernel, n_tgt, len(pieces)), grid_...]
    ppermute x0 -> x40, waiting for transfers between devices: none -> 54.7 us  [the longest x12 35.8 us: body(): gots.append(lax.ppermute(send, 'tgt', pairs))]
    dot_general x2 -> x0, matrix products: 48.9 us -> none  [the longest x1 24.8 us: body(): jnp.einsum('itf,jtd->ijfd', saved_codes, portion, preferred_element_type=...]
    ppermute x0 -> x40, starting transfers between devices: none -> 42.6 us  [the longest x28 21.6 us: swap(): return lax.ppermute(x, axes, pairs)]
    unnamed x3 -> x66, local copies, waits for them, and re-layouts: 24.8 us -> 21.7 us
  transfers between devices with their start and end apart: 3 -> 40, of which waited for: 3 -> 10; matrix products, arithmetic and copies ran while one was open for 17% -> 0% of each run, Pallas kernels for 0% -> 42%
where the time goes in v1:
time: 215 us; the launch traced here: 214 us
  Pallas kernels  92.6 us (43%)
  waiting for transfers between devices  54.7 us (25%)
  starting transfers between devices  42.6 us (20%)
  local copies, waits for them, and re-layouts  23.1 us (11%)
    pallas_call x4, Pallas kernels, terms_call(): pl.pallas_call(functools.partial(terms_kernel, n_tgt, len(pieces)), grid_...  40.7 us
    ppermute x12, waiting for transfers between devices, body(): gots.append(lax.ppermute(send, 'tgt', pairs))  35.8 us
    pallas_call x4, Pallas kernels, grads_call(): pl.pallas_call(functools.partial(grads_kernel, layer, len(chunks)), grid_...  24.4 us
    unnamed x66, local copies, waits for them, and re-layouts  21.7 us
    ppermute x28, starting transfers between devices, swap(): return lax.ppermute(x, axes, pairs)  21.6 us
    ppermute x12, starting transfers between devices, body(): gots.append(lax.ppermute(send, 'tgt', pairs))  21.1 us
    ppermute x28, waiting for transfers between devices, swap(): return lax.ppermute(x, axes, pairs)  18.9 us
    pallas_call x8, Pallas kernels, relay_call(): pl.pallas_call(relay_kernel, grid_spec=pltpu.PrefetchScalarGridSpec(num_s...  17 us
  transfers between devices with their start and end apart: 40, of which 10 were waited for; matrix products, arithmetic and copies ran while one was open for 0% of the time, Pallas kernels for 42%

profile of v1, /device:TPU:0, one launch (start us, length us, event | category | flops | bytes accessed | tf_op | source)
XLA Modules:
  0.0 214.3 jit_solution(16287437996903243459)
XLA Ops:
  0.6 1.3 fusion
  1.9 3.0 %collective-permute-start.33 = (bf16[2,64,1024]{2,1,0:T(8,128)(2,1)S(1)}, bf16[2,64,1024]{2,1,0:T(8,128)(2,1)S(1)}, u32[]{:S(2)}, u32[]{:S(2)}) collective-permute-start(bf16[2,64,1024]{2,1,0:T(8,128)(2,1)S(1)} %get-tuple-element.26.refs_0_), channel_id=1, source_target_pairs={{0,2},{1,3},{2,0},{3,1},{4,6},{5,7},{6,4},{7,5},{8,10},{9,11},{10,... | collective-permute-start | bytes 786440 | tf_op jit(solution)/shard_map/ppermute | solution.py:348
  5.0 1.5 collective-permute-start.31
  7.0 1.5 collective-permute-start.23
  9.0 3.1 %collective-permute-done.33.refs_4_ = bf16[2,64,1024]{2,1,0:T(8,128)(2,1)S(1)} collective-permute-done((bf16[2,64,1024]{2,1,0:T(8,128)(2,1)S(1)}, bf16[2,64,1024]{2,1,0:T(8,128)(2,1)S(1)}, u32[]{:S(2)}, u32[]{:S(2)}) %collective-permute-start.33) | collective-permute-done | bytes 262176 | tf_op jit(solution)/shard_map/ppermute | solution.py:348
  12.1 2.1 collective-permute-start.3
  14.2 1.5 collective-permute-start.1
  15.7 2.0 collective-permute-done.13.refs_4_
  17.7 2.0 collective-permute-start.21
  19.7 3.6 %collective-permute-done.23.refs_4_ = bf16[2,64,1024]{2,1,0:T(8,128)(2,1)S(1)} collective-permute-done((bf16[2,64,1024]{2,1,0:T(8,128)(2,1)S(1)}, bf16[2,64,1024]{2,1,0:T(8,128)(2,1)S(1)}, u32[]{:S(2)}, u32[]{:S(2)}) %collective-permute-start.23) | collective-permute-done | bytes 262176 | tf_op jit(solution)/shard_map/ppermute | solution.py:348
  23.3 2.0 collective-permute-start.25
  25.5 2.8 %collective-permute-done.3.refs_4_ = bf16[2,64,1024]{2,1,0:T(8,128)(2,1)} collective-permute-done((bf16[2,64,1024]{2,1,0:T(8,128)(2,1)S(1)}, bf16[2,64,1024]{2,1,0:T(8,128)(2,1)}, u32[]{:S(2)}, u32[]{:S(2)}) %collective-permute-start.3) | collective-permute-done | bytes 262176 | tf_op jit(solution)/shard_map/ppermute | solution.py:348
  28.9 1.7 collective-permute-start.5
  31.7 4.9 %collective-permute-done.25.refs_6_ = bf16[2,64,1024]{2,1,0:T(8,128)(2,1)S(1)} collective-permute-done((bf16[2,64,1024]{2,1,0:T(8,128)(2,1)S(1)}, bf16[2,64,1024]{2,1,0:T(8,128)(2,1)S(1)}, u32[]{:S(2)}, u32[]{:S(2)}) %collective-permute-start.25) | collective-permute-done | bytes 262176 | tf_op jit(solution)/shard_map/ppermute | solution.py:348
  38.9 2.0 collective-permute-done.5.refs_6_
  43.9 0.9 copy-done.20
  44.9 0.9 copy-done.22
  45.8 0.9 copy-done.24
  46.8 0.9 copy-done.26
  47.7 0.9 copy-done.28
  48.7 0.9 copy-done.30
  49.6 0.9 copy-done.32
  50.6 10.1 %terms.6 = (f32[4,256,512]{2,1,0:T(8,128)S(1)}, s32[3,520,128]{2,1,0:T(8,128)}, bf16[2,256,2048]{2,1,0:T(8,128)(2,1)}) custom-call(s32[16]{0:T(128)S(1)} %stack.20.place, s32[8]{0:T(128)S(1)} %reshape.22.keep, s32[4]{0:T(128)S(1)} %broadcast_select_fusion.2.order, bf16[2,64,1024]{2,1,0:T(8,128)(2,1)S(1)} %get-tuple-element.29.refs_0_, ...), custom_call_target="tpu_custom_call" | custom-call | flops 4294967296 | bytes 23068672 | tf_op jit(solution)/shard_map/terms/pallas_call | solution.py:106
  61.2 1.7 collective-permute-start.35
  63.4 10.3 %terms.4 = (f32[4,256,512]{2,1,0:T(8,128)S(1)}, s32[3,520,128]{2,1,0:T(8,128)}, bf16[2,256,2048]{2,1,0:T(8,128)(2,1)}) custom-call(s32[16]{0:T(128)S(1)} %stack.20.place, s32[8]{0:T(128)S(1)} %reshape.22.keep, s32[4]{0:T(128)S(1)} %broadcast_select_fusion.2.order, bf16[2,64,1024]{2,1,0:T(8,128)(2,1)S(1)} %get-tuple-element.28.refs_0_, ...), custom_call_target="tpu_custom_call" | custom-call | flops 4294967296 | bytes 23068672 | tf_op jit(solution)/shard_map/terms/pallas_call | solution.py:106
  73.7 1.3 copy-done.4
  76.0 6.6 %collective-permute-start.27 = (s32[3,520,128]{2,1,0:T(8,128)}, s32[3,520,128]{2,1,0:T(8,128)}, u32[]{:S(2)}, u32[]{:S(2)}) collective-permute-start(s32[3,520,128]{2,1,0:T(8,128)} %get-tuple-element.19), channel_id=1, source_target_pairs={{12,8},{0,4},{13,9},{1,5},{14,10},{2,6},{15,11},{3,7},{28,24},{16,... | collective-permute-start | bytes 2396168 | tf_op jit(solution)/shard_map/ppermute | solution.py:395
  82.6 10.2 %terms.5 = (f32[4,256,512]{2,1,0:T(8,128)S(1)}, s32[3,520,128]{2,1,0:T(8,128)}, bf16[2,256,2048]{2,1,0:T(8,128)(2,1)}) custom-call(s32[16]{0:T(128)S(1)} %stack.20.place, s32[8]{0:T(128)S(1)} %reshape.22.keep, s32[4]{0:T(128)S(1)} %broadcast_select_fusion.2.order, bf16[2,64,1024]{2,1,0:T(8,128)(2,1)S(1)} %get-tuple-element.27.refs_0_, ...), custom_call_target="tpu_custom_call" | custom-call | flops 4294967296 | bytes 23068672 | tf_op jit(solution)/shard_map/terms/pallas_call | solution.py:106
  92.9 1.4 copy-done.6
  94.3 1.5 collective-permute-start.7
  95.8 2.2 %collective-permute-start.17 = (s32[3,520,128]{2,1,0:T(8,128)}, s32[3,520,128]{2,1,0:T(8,128)}, u32[]{:S(2)}, u32[]{:S(2)}) collective-permute-start(s32[3,520,128]{2,1,0:T(8,128)} %get-tuple-element.17), channel_id=1, source_target_pairs={{12,8},{0,4},{13,9},{1,5},{14,10},{2,6},{15,11},{3,7},{28,24},{16,... | collective-permute-start | bytes 2396168 | tf_op jit(solution)/shard_map/ppermute | solution.py:395
  98.0 10.1 %terms.7 = (f32[4,256,512]{2,1,0:T(8,128)S(1)}, s32[3,520,128]{2,1,0:T(8,128)}, bf16[2,256,2048]{2,1,0:T(8,128)(2,1)}) custom-call(s32[16]{0:T(128)S(1)} %stack.20.place, s32[8]{0:T(128)S(1)} %reshape.22.keep, s32[4]{0:T(128)S(1)} %broadcast_select_fusion.2.order, bf16[2,64,1024]{2,1,0:T(8,128)(2,1)S(1)} %get-tuple-element.26.refs_0_, ...), custom_call_target="tpu_custom_call" | custom-call | flops 4294967296 | bytes 23068672 | tf_op jit(solution)/shard_map/terms/pallas_call | solution.py:106
  108.1 1.3 copy-done.8
  109.4 2.3 %collective-permute-start.37 = (s32[3,520,128]{2,1,0:T(8,128)}, s32[3,520,128]{2,1,0:T(8,128)}, u32[]{:S(2)}, u32[]{:S(2)}) collective-permute-start(s32[3,520,128]{2,1,0:T(8,128)} %get-tuple-element.21), channel_id=1, source_target_pairs={{12,8},{0,4},{13,9},{1,5},{14,10},{2,6},{15,11},{3,7},{28,24},{16,... | collective-permute-start | bytes 2396168 | tf_op jit(solution)/shard_map/ppermute | solution.py:395
  111.8 2.2 %copy-done.10 = bf16[4,1024,512]{2,1,0:T(8,128)(2,1)S(1)} copy-done((bf16[4,1024,512]{2,1,0:T(8,128)(2,1)S(1)}, bf16[4,1024,512]{2,1,0:T(8,128)(2,1)}, u32[]{:S(2)}) %copy-start.10) | copy-done | bytes 4194328
  113.9 1.4 turn.1.codes_ref
  115.4 2.0 copy-done
  117.4 8.5 %grads.4.refs_4_ = bf16[4,2,512,2048]{3,2,1,0:T(8,128)(2,1)} custom-call(s32[8]{0:T(128)S(1)} %reshape.22.keep, bf16[4,512,1024]{2,1,0:T(8,128)(2,1)} %copy-done, bf16[2,256,2048]{2,1,0:T(8,128)(2,1)S(1)} %copy-done.3, bf16[2,256,2048]{2,1,0:T(8,128)(2,1)S(1)} %copy-done.2, bf16[2,256,2048]{2,1,0:T(8,128)(2,1)} %get-tuple-element.24.refs_2_, ...), custom_call_target="tpu_custom_call" | custom-call | flops 4294967296 | bytes 13631488 | tf_op jit(solution)/shard_map/grads/pallas_call | solution.py:315
  125.9 2.4 %relay.12 = s32[2,520,128]{2,1,0:T(8,128)S(1)} custom-call(s32[4]{0:T(128)S(1)} %broadcast_select_fusion.1.order, f32[4,256,512]{2,1,0:T(8,128)S(1)} %get-tuple-element.18.own_ref, s32[3,520,128]{2,1,0:T(8,128)} %collective-permute-done.27.got_ref.refs_0_), custom_call_target="tpu_custom_call" | custom-call | flops 5242880 | bytes 2113536 | tf_op jit(solution)/shard_map/relay/pallas_call | solution.py:146
  128.3 1.0 collective-permute-start.28
  129.3 2.1 relay.8
  131.4 0.8 collective-permute-start.8
  132.2 2.2 %collective-permute-done.17.got_ref.refs_0_ = s32[3,520,128]{2,1,0:T(8,128)} collective-permute-done((s32[3,520,128]{2,1,0:T(8,128)}, s32[3,520,128]{2,1,0:T(8,128)}, u32[]{:S(2)}, u32[]{:S(2)}) %collective-permute-start.17) | collective-permute-done | bytes 798752 | tf_op jit(solution)/shard_map/ppermute | solution.py:395
  134.4 3.0 %relay.10 = s32[2,520,128]{2,1,0:T(8,128)} custom-call(s32[4]{0:T(128)S(1)} %broadcast_select_fusion.1.order, f32[4,256,512]{2,1,0:T(8,128)S(1)} %copy-done.7, s32[3,520,128]{2,1,0:T(8,128)} %collective-permute-done.17.got_ref.refs_0_), custom_call_target="tpu_custom_call" | custom-call | flops 5242880 | bytes 2113536 | tf_op jit(solution)/shard_map/relay/pallas_call | solution.py:146
  138.1 12.5 %collective-permute-done.37.got_ref.refs_0_ = s32[3,520,128]{2,1,0:T(8,128)} collective-permute-done((s32[3,520,128]{2,1,0:T(8,128)}, s32[3,520,128]{2,1,0:T(8,128)}, u32[]{:S(2)}, u32[]{:S(2)}) %collective-permute-start.37) | collective-permute-done | bytes 798752 | tf_op jit(solution)/shard_map/ppermute | solution.py:395
  150.6 3.0 %relay.14 = s32[2,520,128]{2,1,0:T(8,128)} custom-call(s32[4]{0:T(128)S(1)} %broadcast_select_fusion.1.order, f32[4,256,512]{2,1,0:T(8,128)S(1)} %copy-done.9, s32[3,520,128]{2,1,0:T(8,128)} %collective-permute-done.37.got_ref.refs_0_), custom_call_target="tpu_custom_call" | custom-call | flops 5242880 | bytes 2113536 | tf_op jit(solution)/shard_map/relay/pallas_call | solution.py:146
  154.4 6.7 %grads.5.refs_4_ = bf16[4,2,512,2048]{3,2,1,0:T(8,128)(2,1)} custom-call(s32[8]{0:T(128)S(1)} %reshape.22.keep, bf16[4,512,1024]{2,1,0:T(8,128)(2,1)} %copy-done, bf16[2,256,2048]{2,1,0:T(8,128)(2,1)S(1)} %copy-done.3, bf16[2,256,2048]{2,1,0:T(8,128)(2,1)S(1)} %copy-done.2, ...), custom_call_target="tpu_custom_call", output_to_operand_aliasing={{}: (6, {})} | custom-call | flops 4294967296 | bytes 13631488 | tf_op jit(solution)/shard_map/grads/pallas_call | solution.py:315
  161.1 4.6 %grads.6.refs_4_ = bf16[4,2,512,2048]{3,2,1,0:T(8,128)(2,1)} custom-call(s32[8]{0:T(128)S(1)} %reshape.22.keep, bf16[4,512,1024]{2,1,0:T(8,128)(2,1)} %copy-done, bf16[2,256,2048]{2,1,0:T(8,128)(2,1)S(1)} %copy-done.3, bf16[2,256,2048]{2,1,0:T(8,128)(2,1)S(1)} %copy-done.2, ...), custom_call_target="tpu_custom_call", output_to_operand_aliasing={{}: (6, {})} | custom-call | flops 4294967296 | bytes 13631488 | tf_op jit(solution)/shard_map/grads/pallas_call | solution.py:315
  165.7 1.6 relay.13
  167.3 1.3 collective-permute-start.29
  168.6 1.6 relay.9
  170.2 1.3 collective-permute-start.9
  171.5 1.6 relay.11
  173.1 1.3 collective-permute-start.19
  174.4 1.6 relay.15
  176.0 0.8 copy-done.13
  176.8 1.4 collective-permute-start.39
  178.3 4.6 %grads.7 = bf16[4,2,512,2048]{3,2,1,0:T(8,128)(2,1)} custom-call(s32[8]{0:T(128)S(1)} %reshape.22.keep, bf16[4,512,1024]{2,1,0:T(8,128)(2,1)} %copy-done, bf16[2,256,2048]{2,1,0:T(8,128)(2,1)S(1)} %copy-done.3, bf16[2,256,2048]{2,1,0:T(8,128)(2,1)S(1)} %copy-done.2, bf16[2,256,2048]{2,1,0:T(8,128)(2,1)} %get-tuple-element.24.refs_2_, ...), custom_call_target="tpu_custom_call", output_to_operand_aliasing={{}: (6, {})} | custom-call | flops 4294967296 | bytes 13631488 | tf_op jit(solution)/shard_map/grads/pallas_call | solution.py:315
  182.8 21.1 %collective-permute-done.39.refs_2_ = s32[1,520,128]{2,1,0:T(8,128)} collective-permute-done((s32[1,520,128]{2,1,0:T(8,128)}, s32[1,520,128]{2,1,0:T(8,128)}, u32[]{:S(2)}, u32[]{:S(2)}) %collective-permute-start.39) | collective-permute-done | bytes 266272 | tf_op jit(solution)/shard_map/ppermute | solution.py:395
  203.9 1.0 copy-done.14
  204.9 2.3 %finish.4.refs_4_ = bf16[4,256,512]{2,1,0:T(8,128)(2,1)} custom-call(s32[1]{0:T(128)} %bitcast.here, f32[4,256,512]{2,1,0:T(8,128)S(1)} %copy-done.9, s32[3,520,128]{2,1,0:T(8,128)} %collective-permute-done.37.got_ref.refs_0_, s32[2,520,128]{2,1,0:T(8,128)S(1)} %copy-done.14, s32[1,520,128]{2,1,0:T(8,128)} %collective-permute-done.39.refs_2_, ...), custom_call_target="tpu_custom_call" | custom-call | flops 2621440 | bytes 2109440 | tf_op jit(solution)/shard_map/finish/pallas_call | solution.py:221
  207.2 2.3 %finish.5.refs_4_ = bf16[4,256,512]{2,1,0:T(8,128)(2,1)} custom-call(s32[1]{0:T(128)} %bitcast.here, f32[4,256,512]{2,1,0:T(8,128)S(1)} %get-tuple-element.18.own_ref, s32[3,520,128]{2,1,0:T(8,128)} %collective-permute-done.27.got_ref.refs_0_, s32[2,520,128]{2,1,0:T(8,128)S(1)} %collective-permute-done.28.got_ref.refs_1_, ...), custom_call_target="tpu_custom_call", output_to_operand_aliasing={{}: (6, {})} | custom-call | flops 2621440 | bytes 2109440 | tf_op jit(solution)/shard_map/finish/pallas_call | solution.py:221
  209.6 2.3 %finish.6.refs_4_ = bf16[4,256,512]{2,1,0:T(8,128)(2,1)} custom-call(s32[1]{0:T(128)} %bitcast.here, f32[4,256,512]{2,1,0:T(8,128)S(1)} %copy-done.7, s32[3,520,128]{2,1,0:T(8,128)} %collective-permute-done.17.got_ref.refs_0_, s32[2,520,128]{2,1,0:T(8,128)S(1)} %copy-done.12, ...), custom_call_target="tpu_custom_call", output_to_operand_aliasing={{}: (6, {})} | custom-call | flops 2621440 | bytes 2109440 | tf_op jit(solution)/shard_map/finish/pallas_call | solution.py:221
  211.9 2.2 %finish.7 = bf16[4,256,512]{2,1,0:T(8,128)(2,1)} custom-call(s32[1]{0:T(128)} %bitcast.here, f32[4,256,512]{2,1,0:T(8,128)S(1)} %copy-done.5, s32[3,520,128]{2,1,0:T(8,128)S(1)} %collective-permute-done.7.got_ref.refs_0_, s32[2,520,128]{2,1,0:T(8,128)S(1)} %collective-permute-done.8.got_ref.refs_1_, ...), custom_call_target="tpu_custom_call", output_to_operand_aliasing={{}: (6, {})} | custom-call | flops 2621440 | bytes 2109440 | tf_op jit(solution)/shard_map/finish/pallas_call | solution.py:221
  (112 shorter events, 11.7 us)
Async XLA Ops:
  1.9 10.2 %collective-permute-start.33 = (bf16[2,64,1024]{2,1,0:T(8,128)(2,1)S(1)}, bf16[2,64,1024]{2,1,0:T(8,128)(2,1)S(1)}, u32[]{:S(2)}, u32[]{:S(2)}) collective-permute-start(bf16[2,64,1024]{2,1,0:T(8,128)(2,1)S(1)} %get-tuple-element.26.refs_0_), channel_id=1, source_target_pairs={{0,2},{1,3},{2,0},{3,1},{4,6},{5,7},{6,4},{7,5},{8,10},{9,11},{10,... | collective-permute-start | bytes 786440 | tf_op jit(solution)/shard_map/ppermute | solution.py:348
  5.0 9.2 %collective-permute-start.31 = (bf16[2,64,1024]{2,1,0:T(8,128)(2,1)S(1)}, bf16[2,64,1024]{2,1,0:T(8,128)(2,1)S(1)}, u32[]{:S(2)}, u32[]{:S(2)}) collective-permute-start(bf16[2,64,1024]{2,1,0:T(8,128)(2,1)S(1)} %get-tuple-element.26.refs_0_), channel_id=1, source_target_pairs={{0,16},{16,0},{1,17},{17,1},{2,18},{18,2},{3,19},{19,3},{4,20},{20... | collective-permute-start | bytes 786440 | tf_op jit(solution)/shard_map/ppermute | solution.py:348
  6.5 11.3 %collective-permute-start.13 = (bf16[2,64,1024]{2,1,0:T(8,128)(2,1)S(1)}, bf16[2,64,1024]{2,1,0:T(8,128)(2,1)S(1)}, u32[]{:S(2)}, u32[]{:S(2)}) collective-permute-start(bf16[2,64,1024]{2,1,0:T(8,128)(2,1)S(1)} %get-tuple-element.27.refs_0_), channel_id=1, source_target_pairs={{0,2},{1,3},{2,0},{3,1},{4,6},{5,7},{6,4},{7,5},{8,10},{9,11},{10,... | collective-permute-start | bytes 786440 | tf_op jit(solution)/shard_map/ppermute | solution.py:348
  7.0 16.4 %collective-permute-start.23 = (bf16[2,64,1024]{2,1,0:T(8,128)(2,1)S(1)}, bf16[2,64,1024]{2,1,0:T(8,128)(2,1)S(1)}, u32[]{:S(2)}, u32[]{:S(2)}) collective-permute-start(bf16[2,64,1024]{2,1,0:T(8,128)(2,1)S(1)} %get-tuple-element.29.refs_0_), channel_id=1, source_target_pairs={{0,2},{1,3},{2,0},{3,1},{4,6},{5,7},{6,4},{7,5},{8,10},{9,11},{10,... | collective-permute-start | bytes 786440 | tf_op jit(solution)/shard_map/ppermute | solution.py:348
  8.5 16.9 %collective-permute-start.11 = (bf16[2,64,1024]{2,1,0:T(8,128)(2,1)S(1)}, bf16[2,64,1024]{2,1,0:T(8,128)(2,1)}, u32[]{:S(2)}, u32[]{:S(2)}) collective-permute-start(bf16[2,64,1024]{2,1,0:T(8,128)(2,1)S(1)} %get-tuple-element.27.refs_0_), channel_id=1, source_target_pairs={{0,16},{16,0},{1,17},{17,1},{2,18},{18,2},{3,19},{19,3},{4,20},{20... | collective-permute-start | bytes 786440 | tf_op jit(solution)/shard_map/ppermute | solution.py:348
  12.1 16.1 %collective-permute-start.3 = (bf16[2,64,1024]{2,1,0:T(8,128)(2,1)S(1)}, bf16[2,64,1024]{2,1,0:T(8,128)(2,1)}, u32[]{:S(2)}, u32[]{:S(2)}) collective-permute-start(bf16[2,64,1024]{2,1,0:T(8,128)(2,1)S(1)} %get-tuple-element.28.refs_0_), channel_id=1, source_target_pairs={{0,2},{1,3},{2,0},{3,1},{4,6},{5,7},{6,4},{7,5},{8,10},{9,11},{10,... | collective-permute-start | bytes 786440 | tf_op jit(solution)/shard_map/ppermute | solution.py:348
  14.2 9.1 %copy-start.15 = (bf16[2,64,1024]{2,1,0:T(8,128)(2,1)}, bf16[2,64,1024]{2,1,0:T(8,128)(2,1)S(1)}, u32[]{:S(2)}) copy-start(bf16[2,64,1024]{2,1,0:T(8,128)(2,1)S(1)} %collective-permute-done.31.refs_2_) | copy-start | bytes 786436
  14.2 14.8 %collective-permute-start.1 = (bf16[2,64,1024]{2,1,0:T(8,128)(2,1)S(1)}, bf16[2,64,1024]{2,1,0:T(8,128)(2,1)}, u32[]{:S(2)}, u32[]{:S(2)}) collective-permute-start(bf16[2,64,1024]{2,1,0:T(8,128)(2,1)S(1)} %get-tuple-element.28.refs_0_), channel_id=1, source_target_pairs={{0,16},{16,0},{1,17},{17,1},{2,18},{18,2},{3,19},{19,3},{4,20},{20... | collective-permute-start | bytes 786440 | tf_op jit(solution)/shard_map/ppermute | solution.py:348
  17.7 7.7 %copy-start.17 = (bf16[2,64,1024]{2,1,0:T(8,128)(2,1)}, bf16[2,64,1024]{2,1,0:T(8,128)(2,1)S(1)}, u32[]{:S(2)}) copy-start(bf16[2,64,1024]{2,1,0:T(8,128)(2,1)S(1)} %collective-permute-done.13.refs_4_) | copy-start | bytes 786436
  17.7 13.3 %collective-permute-start.21 = (bf16[2,64,1024]{2,1,0:T(8,128)(2,1)S(1)}, bf16[2,64,1024]{2,1,0:T(8,128)(2,1)S(1)}, u32[]{:S(2)}, u32[]{:S(2)}) collective-permute-start(bf16[2,64,1024]{2,1,0:T(8,128)(2,1)S(1)} %get-tuple-element.29.refs_0_), channel_id=1, source_target_pairs={{0,16},{16,0},{1,17},{17,1},{2,18},{18,2},{3,19},{19,3},{4,20},{20... | collective-permute-start | bytes 786440 | tf_op jit(solution)/shard_map/ppermute | solution.py:348
  23.3 13.3 %collective-permute-start.25 = (bf16[2,64,1024]{2,1,0:T(8,128)(2,1)S(1)}, bf16[2,64,1024]{2,1,0:T(8,128)(2,1)S(1)}, u32[]{:S(2)}, u32[]{:S(2)}) collective-permute-start(bf16[2,64,1024]{2,1,0:T(8,128)(2,1)S(1)} %collective-permute-done.23.refs_4_), channel_id=1, source_target_pairs={{0,16},{16,0},{1,17},{17,1},{2,18},{18,2},{3,19},{19,3},{4,20},{20... | collective-permute-start | bytes 786440 | tf_op jit(solution)/shard_map/ppermute | solution.py:348
  25.4 12.3 %collective-permute-start.20 = (bf16[2,64,1024]{2,1,0:T(8,128)(2,1)S(1)}, bf16[2,64,1024]{2,1,0:T(8,128)(2,1)S(1)}, u32[]{:S(2)}, u32[]{:S(2)}) collective-permute-start(bf16[2,64,1024]{2,1,0:T(8,128)(2,1)S(1)} %get-tuple-element.29.refs_0_), channel_id=1, source_target_pairs={{0,1},{1,0},{2,3},{3,2},{4,5},{5,4},{6,7},{7,6},{8,9},{9,8},{10,11... | collective-permute-start | bytes 786440 | tf_op jit(solution)/shard_map/ppermute | solution.py:348
  28.2 12.7 %collective-permute-start.24 = (bf16[2,64,1024]{2,1,0:T(8,128)(2,1)S(1)}, bf16[2,64,1024]{2,1,0:T(8,128)(2,1)S(1)}, u32[]{:S(2)}, u32[]{:S(2)}) collective-permute-start(bf16[2,64,1024]{2,1,0:T(8,128)(2,1)S(1)} %collective-permute-done.23.refs_4_), channel_id=1, source_target_pairs={{0,1},{1,0},{2,3},{3,2},{4,5},{5,4},{6,7},{7,6},{8,9},{9,8},{10,11... | collective-permute-start | bytes 786440 | tf_op jit(solution)/shard_map/ppermute | solution.py:348
  28.9 12.0 %collective-permute-start.5 = (bf16[2,64,1024]{2,1,0:T(8,128)(2,1)}, bf16[2,64,1024]{2,1,0:T(8,128)(2,1)}, u32[]{:S(2)}, u32[]{:S(2)}) collective-permute-start(bf16[2,64,1024]{2,1,0:T(8,128)(2,1)} %collective-permute-done.3.refs_4_), channel_id=1, source_target_pairs={{0,16},{16,0},{1,17},{17,1},{2,18},{18,2},{3,19},{19,3},{4,20},{20... | collective-permute-start | bytes 786440 | tf_op jit(solution)/shard_map/ppermute | solution.py:348
  31.0 10.9 %collective-permute-start.22 = (bf16[2,64,1024]{2,1,0:T(8,128)(2,1)S(1)}, bf16[2,64,1024]{2,1,0:T(8,128)(2,1)S(1)}, u32[]{:S(2)}, u32[]{:S(2)}) collective-permute-start(bf16[2,64,1024]{2,1,0:T(8,128)(2,1)S(1)} %collective-permute-done.21.refs_2_), channel_id=1, source_target_pairs={{0,1},{1,0},{2,3},{3,2},{4,5},{5,4},{6,7},{7,6},{8,9},{9,8},{10,11... | collective-permute-start | bytes 786440 | tf_op jit(solution)/shard_map/ppermute | solution.py:348
  36.7 6.3 %collective-permute-start.26 = (bf16[2,64,1024]{2,1,0:T(8,128)(2,1)S(1)}, bf16[2,64,1024]{2,1,0:T(8,128)(2,1)S(1)}, u32[]{:S(2)}, u32[]{:S(2)}) collective-permute-start(bf16[2,64,1024]{2,1,0:T(8,128)(2,1)S(1)} %collective-permute-done.25.refs_6_), channel_id=1, source_target_pairs={{0,1},{1,0},{2,3},{3,2},{4,5},{5,4},{6,7},{7,6},{8,9},{9,8},{10,11... | collective-permute-start | bytes 786440 | tf_op jit(solution)/shard_map/ppermute | solution.py:348
  37.6 23.6 %copy-start.16 = (bf16[2,64,1024]{2,1,0:T(8,128)(2,1)S(1)}, bf16[2,64,1024]{2,1,0:T(8,128)(2,1)}, u32[]{:S(2)}) copy-start(bf16[2,64,1024]{2,1,0:T(8,128)(2,1)} %copy-done.15) | copy-start | bytes 786436
  37.6 25.2 %copy-start.18 = (bf16[2,64,1024]{2,1,0:T(8,128)(2,1)S(1)}, bf16[2,64,1024]{2,1,0:T(8,128)(2,1)}, u32[]{:S(2)}) copy-start(bf16[2,64,1024]{2,1,0:T(8,128)(2,1)} %copy-done.17) | copy-start | bytes 786436
  38.4 22.3 %collective-permute-start = (bf16[2,64,1024]{2,1,0:T(8,128)(2,1)S(1)}, bf16[2,64,1024]{2,1,0:T(8,128)(2,1)S(1)}, u32[]{:S(2)}, u32[]{:S(2)}) collective-permute-start(bf16[2,64,1024]{2,1,0:T(8,128)(2,1)S(1)} %get-tuple-element.28.refs_0_), channel_id=1, source_target_pairs={{0,1},{1,0},{2,3},{3,2},{4,5},{5,4},{6,7},{7,6},{8,9},{9,8},{10,11... | collective-permute-start | bytes 786440 | tf_op jit(solution)/shard_map/ppermute | solution.py:348
  40.9 20.3 %collective-permute-start.4 = (bf16[2,64,1024]{2,1,0:T(8,128)(2,1)}, bf16[2,64,1024]{2,1,0:T(8,128)(2,1)S(1)}, u32[]{:S(2)}, u32[]{:S(2)}) collective-permute-start(bf16[2,64,1024]{2,1,0:T(8,128)(2,1)} %collective-permute-done.3.refs_4_), channel_id=1, source_target_pairs={{0,1},{1,0},{2,3},{3,2},{4,5},{5,4},{6,7},{7,6},{8,9},{9,8},{10,11... | collective-permute-start | bytes 786440 | tf_op jit(solution)/shard_map/ppermute | solution.py:348
  41.6 19.3 %collective-permute-start.15 = (bf16[2,64,1024]{2,1,0:T(8,128)(2,1)}, bf16[2,64,1024]{2,1,0:T(8,128)(2,1)S(1)}, u32[]{:S(2)}, u32[]{:S(2)}) collective-permute-start(bf16[2,64,1024]{2,1,0:T(8,128)(2,1)} %collective-permute-done.11.refs_2_), channel_id=1, source_target_pairs={{0,2},{1,3},{2,0},{3,1},{4,6},{5,7},{6,4},{7,5},{8,10},{9,11},{10,... | collective-permute-start | bytes 786440 | tf_op jit(solution)/shard_map/ppermute | solution.py:348
  42.7 20.2 %collective-permute-start.2 = (bf16[2,64,1024]{2,1,0:T(8,128)(2,1)}, bf16[2,64,1024]{2,1,0:T(8,128)(2,1)S(1)}, u32[]{:S(2)}, u32[]{:S(2)}) collective-permute-start(bf16[2,64,1024]{2,1,0:T(8,128)(2,1)} %collective-permute-done.1.refs_2_), channel_id=1, source_target_pairs={{0,1},{1,0},{2,3},{3,2},{4,5},{5,4},{6,7},{7,6},{8,9},{9,8},{10,11... | collective-permute-start | bytes 786440 | tf_op jit(solution)/shard_map/ppermute | solution.py:348
  43.6 19.2 %collective-permute-start.6 = (bf16[2,64,1024]{2,1,0:T(8,128)(2,1)}, bf16[2,64,1024]{2,1,0:T(8,128)(2,1)S(1)}, u32[]{:S(2)}, u32[]{:S(2)}) collective-permute-start(bf16[2,64,1024]{2,1,0:T(8,128)(2,1)} %collective-permute-done.5.refs_6_), channel_id=1, source_target_pairs={{0,1},{1,0},{2,3},{3,2},{4,5},{5,4},{6,7},{7,6},{8,9},{9,8},{10,11... | collective-permute-start | bytes 786440 | tf_op jit(solution)/shard_map/ppermute | solution.py:348
  43.9 0.9 copy-start.20
  44.9 0.9 copy-start.22
  45.8 0.9 copy-start.24
  46.8 0.9 copy-start.26
  47.7 0.9 copy-start.28
  48.7 0.9 copy-start.30
  60.7 14.3 %collective-permute-start.10 = (bf16[2,64,1024]{2,1,0:T(8,128)(2,1)S(1)}, bf16[2,64,1024]{2,1,0:T(8,128)(2,1)S(1)}, u32[]{:S(2)}, u32[]{:S(2)}) collective-permute-start(bf16[2,64,1024]{2,1,0:T(8,128)(2,1)S(1)} %get-tuple-element.27.refs_0_), channel_id=1, source_target_pairs={{0,1},{1,0},{2,3},{3,2},{4,5},{5,4},{6,7},{7,6},{8,9},{9,8},{10,11... | collective-permute-start | bytes 786440 | tf_op jit(solution)/shard_map/ppermute | solution.py:348
  60.9 14.7 %collective-permute-start.12 = (bf16[2,64,1024]{2,1,0:T(8,128)(2,1)}, bf16[2,64,1024]{2,1,0:T(8,128)(2,1)S(1)}, u32[]{:S(2)}, u32[]{:S(2)}) collective-permute-start(bf16[2,64,1024]{2,1,0:T(8,128)(2,1)} %collective-permute-done.11.refs_2_), channel_id=1, source_target_pairs={{0,1},{1,0},{2,3},{3,2},{4,5},{5,4},{6,7},{7,6},{8,9},{9,8},{10,11... | collective-permute-start | bytes 786440 | tf_op jit(solution)/shard_map/ppermute | solution.py:348
  61.2 13.9 %collective-permute-start.35 = (bf16[2,64,1024]{2,1,0:T(8,128)(2,1)S(1)}, bf16[2,64,1024]{2,1,0:T(8,128)(2,1)S(1)}, u32[]{:S(2)}, u32[]{:S(2)}) collective-permute-start(bf16[2,64,1024]{2,1,0:T(8,128)(2,1)S(1)} %copy-done.16), channel_id=1, source_target_pairs={{0,2},{1,3},{2,0},{3,1},{4,6},{5,7},{6,4},{7,5},{8,10},{9,11},{10,... | collective-permute-start | bytes 786440 | tf_op jit(solution)/shard_map/ppermute | solution.py:348
  62.9 12.6 %collective-permute-start.14 = (bf16[2,64,1024]{2,1,0:T(8,128)(2,1)S(1)}, bf16[2,64,1024]{2,1,0:T(8,128)(2,1)S(1)}, u32[]{:S(2)}, u32[]{:S(2)}) collective-permute-start(bf16[2,64,1024]{2,1,0:T(8,128)(2,1)S(1)} %copy-done.18), channel_id=1, source_target_pairs={{0,1},{1,0},{2,3},{3,2},{4,5},{5,4},{6,7},{7,6},{8,9},{9,8},{10,11... | collective-permute-start | bytes 786440 | tf_op jit(solution)/shard_map/ppermute | solution.py:348
  62.9 13.1 %collective-permute-start.16 = (bf16[2,64,1024]{2,1,0:T(8,128)(2,1)S(1)}, bf16[2,64,1024]{2,1,0:T(8,128)(2,1)S(1)}, u32[]{:S(2)}, u32[]{:S(2)}) collective-permute-start(bf16[2,64,1024]{2,1,0:T(8,128)(2,1)S(1)} %collective-permute-done.15.refs_6_), channel_id=1, source_target_pairs={{0,1},{1,0},{2,3},{3,2},{4,5},{5,4},{6,7},{7,6},{8,9},{9,8},{10,11... | collective-permute-start | bytes 786440 | tf_op jit(solution)/shard_map/ppermute | solution.py:348
  73.7 1.3 copy-start.4
  75.0 19.3 %collective-permute-start.30 = (bf16[2,64,1024]{2,1,0:T(8,128)(2,1)S(1)}, bf16[2,64,1024]{2,1,0:T(8,128)(2,1)S(1)}, u32[]{:S(2)}, u32[]{:S(2)}) collective-permute-start(bf16[2,64,1024]{2,1,0:T(8,128)(2,1)S(1)} %get-tuple-element.26.refs_0_), channel_id=1, source_target_pairs={{0,1},{1,0},{2,3},{3,2},{4,5},{5,4},{6,7},{7,6},{8,9},{9,8},{10,11... | collective-permute-start | bytes 786440 | tf_op jit(solution)/shard_map/ppermute | solution.py:348
  75.1 23.0 %collective-permute-start.32 = (bf16[2,64,1024]{2,1,0:T(8,128)(2,1)S(1)}, bf16[2,64,1024]{2,1,0:T(8,128)(2,1)S(1)}, u32[]{:S(2)}, u32[]{:S(2)}) collective-permute-start(bf16[2,64,1024]{2,1,0:T(8,128)(2,1)S(1)} %copy-done.16), channel_id=1, source_target_pairs={{0,1},{1,0},{2,3},{3,2},{4,5},{5,4},{6,7},{7,6},{8,9},{9,8},{10,11... | collective-permute-start | bytes 786440 | tf_op jit(solution)/shard_map/ppermute | solution.py:348
  75.5 20.3 %collective-permute-start.34 = (bf16[2,64,1024]{2,1,0:T(8,128)(2,1)S(1)}, bf16[2,64,1024]{2,1,0:T(8,128)(2,1)S(1)}, u32[]{:S(2)}, u32[]{:S(2)}) collective-permute-start(bf16[2,64,1024]{2,1,0:T(8,128)(2,1)S(1)} %collective-permute-done.33.refs_4_), channel_id=1, source_target_pairs={{0,1},{1,0},{2,3},{3,2},{4,5},{5,4},{6,7},{7,6},{8,9},{9,8},{10,11... | collective-permute-start | bytes 786440 | tf_op jit(solution)/shard_map/ppermute | solution.py:348
  75.6 22.4 %collective-permute-start.36 = (bf16[2,64,1024]{2,1,0:T(8,128)(2,1)S(1)}, bf16[2,64,1024]{2,1,0:T(8,128)(2,1)S(1)}, u32[]{:S(2)}, u32[]{:S(2)}) collective-permute-start(bf16[2,64,1024]{2,1,0:T(8,128)(2,1)S(1)} %collective-permute-done.35.refs_6_), channel_id=1, source_target_pairs={{0,1},{1,0},{2,3},{3,2},{4,5},{5,4},{6,7},{7,6},{8,9},{9,8},{10,11... | collective-permute-start | bytes 786440 | tf_op jit(solution)/shard_map/ppermute | solution.py:348
  76.0 49.9 %collective-permute-start.27 = (s32[3,520,128]{2,1,0:T(8,128)}, s32[3,520,128]{2,1,0:T(8,128)}, u32[]{:S(2)}, u32[]{:S(2)}) collective-permute-start(s32[3,520,128]{2,1,0:T(8,128)} %get-tuple-element.19), channel_id=1, source_target_pairs={{12,8},{0,4},{13,9},{1,5},{14,10},{2,6},{15,11},{3,7},{28,24},{16,... | collective-permute-start | bytes 2396168 | tf_op jit(solution)/shard_map/ppermute | solution.py:395
  92.9 1.4 copy-start.6
  94.3 35.0 %collective-permute-start.7 = (s32[3,520,128]{2,1,0:T(8,128)}, s32[3,520,128]{2,1,0:T(8,128)S(1)}, u32[]{:S(2)}, u32[]{:S(2)}) collective-permute-start(s32[3,520,128]{2,1,0:T(8,128)} %get-tuple-element.15), channel_id=1, source_target_pairs={{12,8},{0,4},{13,9},{1,5},{14,10},{2,6},{15,11},{3,7},{28,24},{16,... | collective-permute-start | bytes 2396168 | tf_op jit(solution)/shard_map/ppermute | solution.py:395
  95.8 38.6 %collective-permute-start.17 = (s32[3,520,128]{2,1,0:T(8,128)}, s32[3,520,128]{2,1,0:T(8,128)}, u32[]{:S(2)}, u32[]{:S(2)}) collective-permute-start(s32[3,520,128]{2,1,0:T(8,128)} %get-tuple-element.17), channel_id=1, source_target_pairs={{12,8},{0,4},{13,9},{1,5},{14,10},{2,6},{15,11},{3,7},{28,24},{16,... | collective-permute-start | bytes 2396168 | tf_op jit(solution)/shard_map/ppermute | solution.py:395
  108.1 1.3 copy-start.8
  109.4 41.2 %collective-permute-start.37 = (s32[3,520,128]{2,1,0:T(8,128)}, s32[3,520,128]{2,1,0:T(8,128)}, u32[]{:S(2)}, u32[]{:S(2)}) collective-permute-start(s32[3,520,128]{2,1,0:T(8,128)} %get-tuple-element.21), channel_id=1, source_target_pairs={{12,8},{0,4},{13,9},{1,5},{14,10},{2,6},{15,11},{3,7},{28,24},{16,... | collective-permute-start | bytes 2396168 | tf_op jit(solution)/shard_map/ppermute | solution.py:395
  111.7 2.2 %copy-start.10 = (bf16[4,1024,512]{2,1,0:T(8,128)(2,1)S(1)}, bf16[4,1024,512]{2,1,0:T(8,128)(2,1)}, u32[]{:S(2)}) copy-start(bf16[4,1024,512]{2,1,0:T(8,128)(2,1)} %codes_ref.1) | copy-start | bytes 12582916
  113.9 3.4 %copy-start.2 = (bf16[2,256,2048]{2,1,0:T(8,128)(2,1)S(1)}, bf16[2,256,2048]{2,1,0:T(8,128)(2,1)}, u32[]{:S(2)}) copy-start(bf16[2,256,2048]{2,1,0:T(8,128)(2,1)} %get-tuple-element.23.refs_1_) | copy-start | bytes 6291460
  113.9 3.4 %copy-start.3 = (bf16[2,256,2048]{2,1,0:T(8,128)(2,1)S(1)}, bf16[2,256,2048]{2,1,0:T(8,128)(2,1)}, u32[]{:S(2)}) copy-start(bf16[2,256,2048]{2,1,0:T(8,128)(2,1)} %get-tuple-element.22.refs_0_) | copy-start | bytes 6291460
  115.4 2.0 copy-start
  125.9 3.4 %copy-start.5 = (f32[4,256,512]{2,1,0:T(8,128)S(1)}, f32[4,256,512]{2,1,0:T(8,128)}, u32[]{:S(2)}) copy-start(f32[4,256,512]{2,1,0:T(8,128)} %copy-done.4) | copy-start | bytes 6291460
  128.3 6.1 %copy-start.7 = (f32[4,256,512]{2,1,0:T(8,128)S(1)}, f32[4,256,512]{2,1,0:T(8,128)}, u32[]{:S(2)}) copy-start(f32[4,256,512]{2,1,0:T(8,128)} %copy-done.6) | copy-start | bytes 6291460
  128.3 37.4 %collective-permute-start.28 = (s32[2,520,128]{2,1,0:T(8,128)S(1)}, s32[2,520,128]{2,1,0:T(8,128)S(1)}, u32[]{:S(2)}, u32[]{:S(2)}) collective-permute-start(s32[2,520,128]{2,1,0:T(8,128)S(1)} %relay.12), channel_id=1, source_target_pairs={{8,4},{4,8},{9,5},{5,9},{10,6},{6,10},{11,7},{7,11},{24,20},{20,24... | collective-permute-start | bytes 1597448 | tf_op jit(solution)/shard_map/ppermute | solution.py:395
  131.4 19.2 %copy-start.9 = (f32[4,256,512]{2,1,0:T(8,128)S(1)}, f32[4,256,512]{2,1,0:T(8,128)}, u32[]{:S(2)}) copy-start(f32[4,256,512]{2,1,0:T(8,128)} %copy-done.8) | copy-start | bytes 6291460
  131.4 37.1 %collective-permute-start.8 = (s32[2,520,128]{2,1,0:T(8,128)}, s32[2,520,128]{2,1,0:T(8,128)S(1)}, u32[]{:S(2)}, u32[]{:S(2)}) collective-permute-start(s32[2,520,128]{2,1,0:T(8,128)} %relay.8), channel_id=1, source_target_pairs={{8,4},{4,8},{9,5},{5,9},{10,6},{6,10},{11,7},{7,11},{24,20},{20,24... | collective-permute-start | bytes 1597448 | tf_op jit(solution)/shard_map/ppermute | solution.py:395
  137.4 34.1 %collective-permute-start.18 = (s32[2,520,128]{2,1,0:T(8,128)}, s32[2,520,128]{2,1,0:T(8,128)S(1)}, u32[]{:S(2)}, u32[]{:S(2)}) collective-permute-start(s32[2,520,128]{2,1,0:T(8,128)} %relay.10), channel_id=1, source_target_pairs={{8,4},{4,8},{9,5},{5,9},{10,6},{6,10},{11,7},{7,11},{24,20},{20,24... | collective-permute-start | bytes 1597448 | tf_op jit(solution)/shard_map/ppermute | solution.py:395
  153.7 20.7 %collective-permute-start.38 = (s32[2,520,128]{2,1,0:T(8,128)}, s32[2,520,128]{2,1,0:T(8,128)S(1)}, u32[]{:S(2)}, u32[]{:S(2)}) collective-permute-start(s32[2,520,128]{2,1,0:T(8,128)} %relay.14), channel_id=1, source_target_pairs={{8,4},{4,8},{9,5},{5,9},{10,6},{6,10},{11,7},{7,11},{24,20},{20,24... | collective-permute-start | bytes 1597448 | tf_op jit(solution)/shard_map/ppermute | solution.py:395
  167.3 40.0 %collective-permute-start.29 = (s32[1,520,128]{2,1,0:T(8,128)}, s32[1,520,128]{2,1,0:T(8,128)}, u32[]{:S(2)}, u32[]{:S(2)}) collective-permute-start(s32[1,520,128]{2,1,0:T(8,128)} %relay.13), channel_id=1, source_target_pairs={{4,0},{8,12},{5,1},{9,13},{6,2},{10,14},{7,3},{11,15},{20,16},{24,... | collective-permute-start | bytes 798728 | tf_op jit(solution)/shard_map/ppermute | solution.py:395
  170.2 41.7 %collective-permute-start.9 = (s32[1,520,128]{2,1,0:T(8,128)}, s32[1,520,128]{2,1,0:T(8,128)}, u32[]{:S(2)}, u32[]{:S(2)}) collective-permute-start(s32[1,520,128]{2,1,0:T(8,128)} %relay.9), channel_id=1, source_target_pairs={{4,0},{8,12},{5,1},{9,13},{6,2},{10,14},{7,3},{11,15},{20,16},{24,... | collective-permute-start | bytes 798728 | tf_op jit(solution)/shard_map/ppermute | solution.py:395
  171.5 2.9 %copy-start.11 = (s32[2,520,128]{2,1,0:T(8,128)}, s32[2,520,128]{2,1,0:T(8,128)S(1)}, u32[]{:S(2)}) copy-start(s32[2,520,128]{2,1,0:T(8,128)S(1)} %collective-permute-done.18.got_ref.refs_1_) | copy-start | bytes 1597444
  173.1 36.5 %collective-permute-start.19 = (s32[1,520,128]{2,1,0:T(8,128)}, s32[1,520,128]{2,1,0:T(8,128)}, u32[]{:S(2)}, u32[]{:S(2)}) collective-permute-start(s32[1,520,128]{2,1,0:T(8,128)} %relay.11), channel_id=1, source_target_pairs={{4,0},{8,12},{5,1},{9,13},{6,2},{10,14},{7,3},{11,15},{20,16},{24,... | collective-permute-start | bytes 798728 | tf_op jit(solution)/shard_map/ppermute | solution.py:395
  176.8 27.1 %copy-start.1 = (s32[4,256,512]{2,1,0:T(8,128)S(1)}, s32[4,256,512]{2,1,0:T(8,128)}, u32[]{:S(2)}) copy-start(s32[4,256,512]{2,1,0:T(8,128)} %refs_3_.7) | copy-start | bytes 6291460
  176.8 27.1 %collective-permute-start.39 = (s32[1,520,128]{2,1,0:T(8,128)}, s32[1,520,128]{2,1,0:T(8,128)}, u32[]{:S(2)}, u32[]{:S(2)}) collective-permute-start(s32[1,520,128]{2,1,0:T(8,128)} %relay.15), channel_id=1, source_target_pairs={{4,0},{8,12},{5,1},{9,13},{6,2},{10,14},{7,3},{11,15},{20,16},{24,... | collective-permute-start | bytes 798728 | tf_op jit(solution)/shard_map/ppermute | solution.py:395
  203.9 1.0 copy-start.14
  207.2 2.4 %copy-start.12 = (s32[2,520,128]{2,1,0:T(8,128)S(1)}, s32[2,520,128]{2,1,0:T(8,128)}, u32[]{:S(2)}) copy-start(s32[2,520,128]{2,1,0:T(8,128)} %copy-done.11) | copy-start | bytes 1597444
  (9 other events, 6.7 us)

commit v2 on v0

v2 whole, which is shorter than its diff:
```python
import functools

import jax
import jax.numpy as jnp
from jax import lax
from jax.experimental import pallas as pl
from jax.experimental.pallas import tpu as pltpu
from jax.sharding import PartitionSpec as P

LANES = 128
SUBLANES = 8
STEPS_PER_OCTAVE = 64
TOP = 32760.0
FLOOR = 1e-30
EIGHTHS = (2, 3, 3)
VMEM = 127 << 19
ANYWHERE = pl.BlockSpec(memory_space=pl.ANY)


def pair(x):
    half = x.shape[0] // 2
    return (x[half:] << 16) | (x[:half] & 0xFFFF)


def unpair(words):
    return (words << 16) >> 16, words >> 16


def scale_and_gain(peaks):
    scale = jnp.ceil(jnp.log2(jnp.maximum(peaks, FLOOR)) * STEPS_PER_OCTAVE)
    return scale.astype(jnp.int32), jnp.exp2(scale * (-1.0 / STEPS_PER_OCTAVE)) * TOP


def row_peak(v):
    return jnp.max(jnp.abs(v), axis=1, keepdims=True)


def store_words(out_ref, layer, v, gain, base=0):
    rows, width = v.shape
    half, tiles = rows // 2, width // LANES
    words = pair(jnp.floor(v * gain + 0.5).astype(jnp.int32))
    for tile in range(tiles):
        start = base + (layer * tiles + tile) * half
        out_ref[start : start + half, :] = words[:, tile * LANES : (tile + 1) * LANES]


def lanes_of(shape):
    return lax.broadcasted_iota(jnp.int32, shape, 1)


def load_steps(in_ref):
    end = in_ref.shape[0] - SUBLANES
    low, high = unpair(in_ref[end:, :])
    step = lambda scale: jnp.exp2(scale.astype(jnp.float32) * (1.0 / STEPS_PER_OCTAVE)) * (1.0 / TOP)
    return step(low), step(high)


def load_values(in_ref, steps, layer, layers, rows, width):
    half, tiles = rows // 2, width // LANES
    words = jnp.concatenate(
        [in_ref[(layer * tiles + tile) * half : (layer * tiles + tile + 1) * half, :] for tile in range(tiles)], axis=1
    )
    values = []
    for part, step in zip(unpair(words), steps):
        column = jnp.concatenate(
            [step[:, group * layers + layer][:, None] for group in range(half // SUBLANES)], axis=0
        )
        values.append(part.astype(jnp.float32) * column)
    return jnp.concatenate(values, axis=0)


def payload_rows(layers, rows, width):
    return layers * (width // LANES) * (rows // 2) + SUBLANES


def cost(flops, bytes_accessed):
    return pl.CostEstimate(flops=flops, bytes_accessed=bytes_accessed, transcendentals=0)


def cut_kernel(n_join, offset, errors_ref, *refs):
    sem = refs[-1]
    joined = refs[:n_join]
    outs = refs[-1 - (n_join > 0) - (offset is not None) : -1]
    copies = [(piece, outs[0].at[index]) for index, piece in enumerate(joined)]
    if offset is not None:
        copies.append((errors_ref.at[:, pl.ds(offset, outs[-1].shape[1]), :], outs[-1]))
    copies = [pltpu.make_async_copy(*copy, sem.at[index]) for index, copy in enumerate(copies)]
    for copy in copies:
        copy.start()
    for copy in copies:
        copy.wait()


def cut_call(errors, offset, span, join, after):
    shapes = []
    if join:
        shapes.append(jax.ShapeDtypeStruct((len(join), *join[0].shape), errors.dtype))
    if offset is not None:
        shapes.append(jax.ShapeDtypeStruct((errors.shape[0], span, errors.shape[2]), errors.dtype))
    return pl.pallas_call(
        functools.partial(cut_kernel, len(join), offset),
        in_specs=[ANYWHERE] * (1 + len(join) + len(after)),
        out_specs=[ANYWHERE] * len(shapes),
        out_shape=shapes,
        scratch_shapes=[pltpu.SemaphoreType.DMA((len(join) + 1,))],
        compiler_params=pltpu.CompilerParams(vmem_limit_bytes=VMEM),
        name="cut",
    )(errors, *join, *after)


def terms_kernel(n_tgt, plan, offset, *refs):
    n_pieces = 1 + max(entry[0] for entry in plan)
    pieces = refs[:n_pieces]
    dec_ref = refs[n_pieces]
    own_ref, both_ref, far_ref, all_ref, err, dec, acc, in_sem, dec_sem, own_sem, out_sem = refs[-11:]
    layers, tgt_count, width, columns = dec_ref.shape
    total_rows = err.shape[0]
    rows = total_rows // n_tgt
    half = rows // 2
    src, tgt, feat = (lax.axis_index(axis) for axis in ("src", "tgt", "feat"))

    def piece_copies(index):
        source, lead, skip, tokens, flip_src, flip_feat = plan[index]
        piece = pieces[source] if lead is None else pieces[source].at[lead]
        wide = piece.shape[2]
        row = 0 if flip_feat is None else pl.multiple_of((feat ^ flip_feat) * tokens, tokens)
        column = 0 if flip_src is None else pl.multiple_of((src ^ flip_src) * wide, wide)
        return [
            pltpu.make_async_copy(
                piece.at[t, pl.ds(skip, tokens), :],
                err.at[pl.ds(row, tokens), pl.ds(t * columns + column, wide)],
                in_sem.at[index * tgt_count + t],
            )
            for t in range(tgt_count)
        ]

    def dec_copy(layer, t):
        return pltpu.make_async_copy(
            dec_ref.at[layer, t], dec.at[layer, :, pl.ds(t * columns, columns)], dec_sem.at[layer * tgt_count + t]
        )

    def block(dest):
        return pl.ds(pl.multiple_of(dest * rows, rows), rows)

    def own_copies(layer):
        return [
            pltpu.make_async_copy(
                acc.at[layer, block(tgt ^ flip), :], own_ref.at[index, layer], own_sem.at[layer * 2 + index]
            )
            for index, flip in enumerate((0, 2))
        ]

    out_copy = pltpu.make_async_copy(err, all_ref.at[pl.ds(offset, total_rows), :], out_sem)

    for t in range(tgt_count):
        dec_copy(0, t).start()
    copies = [copy for index in range(len(plan)) for copy in piece_copies(index)]
    for copy in copies:
        copy.start()
    for layer in range(1, layers):
        for t in range(tgt_count):
            dec_copy(layer, t).start()
    for copy in copies:
        copy.wait()
    out_copy.start()

    lane = lanes_of((rows, LANES))
    small = lanes_of((SUBLANES, LANES))
    length = far_ref.shape[0]
    flips = (1, 3)
    tails = [jnp.zeros((SUBLANES, LANES), jnp.int32) for _ in flips]

    def multiply(layer):
        for t in range(tgt_count):
            dec_copy(layer, t).wait()
            kept = tgt * tgt_count + t >= src * layers + layer

            @pl.when(jnp.logical_not(kept))
            def _():
                dec[layer, :, t * columns : (t + 1) * columns] = jnp.zeros((width, columns), jnp.bfloat16)

        acc[layer] = lax.dot_general(
            err[...], dec[layer], (((1,), (1,)), ((), ())), preferred_element_type=jnp.float32
        )
        for copy in own_copies(layer):
            copy.start()

    def encode(layer):
        peaks = jnp.zeros((rows, LANES), jnp.float32)
        for index, flip in enumerate(flips):
            peaks = jnp.where(lane == index, row_peak(acc[layer, block(tgt ^ flip), :]), peaks)
        scale, gain = scale_and_gain(peaks)
        scale_words = pair(scale)
        for index, flip in enumerate(flips):
            v, factor = acc[layer, block(tgt ^ flip), :], gain[:, index : index + 1]
            store_words(both_ref, layer, v, factor, index * length)
            if index:
                store_words(far_ref, layer, v, factor)
            for group in range(half // SUBLANES):
                piece = scale_words[group * SUBLANES : (group + 1) * SUBLANES, index : index + 1]
                tails[index] = jnp.where(small == group * layers + layer, piece, tails[index])

    for layer in range(layers):
        multiply(layer)
        if layer:
            encode(layer - 1)
    encode(layers - 1)
    for index, tail in enumerate(tails):
        both_ref[(index + 1) * length - SUBLANES : (index + 1) * length, :] = tail
    far_ref[length - SUBLANES :, :] = tails[1]
    for layer in range(layers):
        for copy in own_copies(layer):
            copy.wait()
    out_copy.wait()


def terms_call(pieces, plan, decoder, everything, offset, n_tgt, total_rows, tokens, after):
    layers, tgt_count, width, columns = decoder.shape
    rows = total_rows // n_tgt
    payload = (payload_rows(layers, rows, width), LANES)
    whole = pl.BlockSpec(memory_space=pltpu.VMEM)
    operands = [*pieces, decoder]
    aliases = {}
    if everything is not None:
        aliases = {len(operands): 3}
        operands.append(everything)
    operands += after
    return pl.pallas_call(
        functools.partial(terms_kernel, n_tgt, plan, offset),
        in_specs=[ANYWHERE] * len(operands),
        out_specs=[ANYWHERE, whole, whole, ANYWHERE],
        scratch_shapes=[
            pltpu.VMEM((total_rows, tgt_count * columns), jnp.bfloat16),
            pltpu.VMEM((layers, width, tgt_count * columns), jnp.bfloat16),
            pltpu.VMEM((layers, total_rows, width), jnp.float32),
            pltpu.SemaphoreType.DMA((len(plan) * tgt_count,)),
            pltpu.SemaphoreType.DMA((layers * tgt_count,)),
            pltpu.SemaphoreType.DMA((layers * 2,)),
            pltpu.SemaphoreType.DMA,
        ],
        out_shape=[
            jax.ShapeDtypeStruct((2, layers, rows, width), jnp.float32),
            jax.ShapeDtypeStruct((2 * payload[0], LANES), jnp.int32),
            jax.ShapeDtypeStruct(payload, jnp.int32),
            jax.ShapeDtypeStruct((tokens, tgt_count * columns), jnp.bfloat16),
        ],
        input_output_aliases=aliases,
        compiler_params=pltpu.CompilerParams(vmem_limit_bytes=VMEM),
        cost_estimate=cost(2 * total_rows * decoder.size // EASE, decoder.size * 2 // EASE),
        name="terms",
    )(*operands)


def relay_kernel(own_ref, got_ref, *refs):
    send_ref, total = refs[-2:]
    layers, rows, width = total.shape
    half = rows // 2
    tgt = lax.axis_index("tgt")
    inner = jnp.logical_or(tgt == 1, tgt == 2).astype(jnp.float32)
    steps = [step * inner for step in load_steps(got_ref)]
    lane = lanes_of((rows, LANES))
    peaks = jnp.zeros((rows, LANES), jnp.float32)
    for layer in range(layers):
        v = own_ref[0, layer] + load_values(got_ref, steps, layer, layers, rows, width)
        total[layer] = v
        peaks = jnp.where(lane % layers == layer, row_peak(v), peaks)
    scale, gain = scale_and_gain(peaks)
    for layer in range(layers):
        store_words(send_ref, layer, total[layer], gain[:, layer : layer + 1])
    scale_words = pair(scale)
    small = lanes_of((SUBLANES, LANES)) // layers
    tail = jnp.zeros((SUBLANES, LANES), jnp.int32)
    for group in range(half // SUBLANES):
        tail = jnp.where(small == group, scale_words[group * SUBLANES : (group + 1) * SUBLANES], tail)
    send_ref[send_ref.shape[0] - SUBLANES :, :] = tail


def relay_call(own, got, after):
    _, layers, rows, width = own.shape
    shape = (got.shape[0] // 2, LANES)
    return pl.pallas_call(
        relay_kernel,
        grid=(1,),
        in_specs=[
            pl.BlockSpec((1, layers, rows, width), lambda i: (1, 0, 0, 0)),
            pl.BlockSpec(shape, lambda i: (1, 0)),
        ]
        + [ANYWHERE] * len(after),
        out_specs=pl.BlockSpec(shape, lambda i: (0, 0)),
        scratch_shapes=[pltpu.VMEM((layers, rows, width), jnp.float32)],
        out_shape=jax.ShapeDtypeStruct(shape, jnp.int32),
        compiler_params=pltpu.CompilerParams(vmem_limit_bytes=VMEM),
        cost_estimate=cost(20 * layers * rows * width // EASE, 8 * got.size // EASE),
        name="relay",
    )(own, got, *after)


def finish_kernel(n_got, offset, stride, own_ref, *refs):
    gots = refs[:n_got]
    mask_ref = refs[n_got]
    out_ref, mask_tile, out_tile, in_sem, out_sem = refs[-5:]
    layers, rows, width = out_tile.shape
    parts = mask_ref.shape[1] // stride
    tokens = rows // parts

    def mask_copy(part):
        return pltpu.make_async_copy(
            mask_ref.at[:, pl.ds(part * stride + offset, tokens), :],
            mask_tile.at[:, pl.ds(part * tokens, tokens), :],
            in_sem.at[part],
        )

    def out_copy(layer, part):
        return pltpu.make_async_copy(
            out_tile.at[layer, pl.ds(part * tokens, tokens), :],
            out_ref.at[layer, pl.ds(part * stride + offset, tokens), :],
            out_sem.at[layer * parts + part],
        )

    for part in range(parts):
        mask_copy(part).start()
    steps = [load_steps(got) for got in gots]
    for part in range(parts):
        mask_copy(part).wait()
    for layer in range(layers):
        total = own_ref[0, layer]
        for got, step in zip(gots, steps):
            total += load_values(got, step, layer, layers, rows, width)
        out_tile[layer] = (total * mask_tile[layer].astype(jnp.float32)).astype(jnp.bfloat16)
        for part in range(parts):
            out_copy(layer, part).start()
    for layer in range(layers):
        for part in range(parts):
            out_copy(layer, part).wait()


def finish_call(own, gots, mask, out, offset, stride, after):
    _, layers, rows, width = own.shape
    parts = mask.shape[1] // stride
    in_specs = [pl.BlockSpec((1, layers, rows, width), lambda i: (0, 0, 0, 0))]
    in_specs += [pl.BlockSpec(gots[-1].shape, lambda i: (0, 0)) for got in gots]
    in_specs.append(ANYWHERE)
    operands = [own, *gots, mask]
    aliases = {}
    if out is not None:
        in_specs.append(ANYWHERE)
        aliases = {len(operands): 0}
        operands.append(out)
    in_specs += [ANYWHERE] * len(after)
    operands += after
    return pl.pallas_call(
        functools.partial(finish_kernel, len(gots), offset, stride),
        grid=(1,),
        in_specs=in_specs,
        out_specs=ANYWHERE,
        scratch_shapes=[
            pltpu.VMEM((layers, rows, width), jnp.int32),
            pltpu.VMEM((layers, rows, width), jnp.bfloat16),
            pltpu.SemaphoreType.DMA((parts,)),
            pltpu.SemaphoreType.DMA((layers * parts,)),
        ],
        out_shape=jax.ShapeDtypeStruct(mask.shape, jnp.bfloat16),
        input_output_aliases=aliases,
        compiler_params=pltpu.CompilerParams(vmem_limit_bytes=VMEM),
        cost_estimate=cost(20 * layers * rows * width // EASE, layers * rows * width * 16 // EASE),
        name="finish",
    )(*operands)


def turn_kernel(spans, codes_ref, out_ref):
    tokens = codes_ref.shape[1]
    stride = sum(spans)
    blocks = tokens // stride
    offset = column = 0
    for span in spans:
        rows = jnp.concatenate(
            [codes_ref[0, pl.ds(block * stride + offset, span), :] for block in range(blocks)], axis=0
        )
        out_ref[0, :, pl.ds(column, blocks * span)] = rows.T
        offset += span
        column += blocks * span


def turn_call(codes, spans):
    layers, tokens, width = codes.shape
    return pl.pallas_call(
        functools.partial(turn_kernel, spans),
        grid=(layers,),
        in_specs=[pl.BlockSpec((1, tokens, width), lambda i: (i, 0, 0))],
        out_specs=pl.BlockSpec((1, width, tokens), lambda i: (i, 0, 0)),
        out_shape=jax.ShapeDtypeStruct((layers, width, tokens), jnp.bfloat16),
        compiler_params=pltpu.CompilerParams(vmem_limit_bytes=VMEM),
        cost_estimate=cost(codes.size // EASE, codes.size * 4 // EASE),
        name="turn",
    )(codes)


def grads_kernel(t, codes_ref, err_ref, *refs):
    out_ref = refs[-1]
    tgt_count, columns = 1, out_ref.shape[3]
    layer = lax.axis_index("src") * pl.num_programs(0) + pl.program_id(0)
    kept = lax.axis_index("tgt") * t[1] + t[0] >= layer
    step = min(columns, 512)

    @pl.when(kept)
    def _():
        for column in range(0, columns, step):
            out_ref[0, 0, :, column : column + step] = jnp.dot(
                codes_ref[0], err_ref[:, column : column + step], preferred_element_type=jnp.float32
            ).astype(jnp.bfloat16)

    @pl.when(jnp.logical_not(kept))
    def _():
        out_ref[...] = jnp.zeros_like(out_ref)


def grads_call(t, codes_t, everything, out, shape, after):
    layers, tgt_count, width, columns = shape
    tokens = codes_t.shape[2]
    in_specs = [
        pl.BlockSpec((1, width, tokens), lambda i: (i, 0, 0)),
        pl.BlockSpec((tokens, columns), lambda i: (0, t)),
    ]
    operands = [codes_t, everything]
    aliases = {}
    if out is not None:
        aliases = {len(operands): 0}
        operands.append(out)
    operands += after
    in_specs += [ANYWHERE] * (len(operands) - 2)
    return pl.pallas_call(
        functools.partial(grads_kernel, (t, tgt_count)),
        grid=(layers,),
        in_specs=in_specs,
        out_specs=pl.BlockSpec((1, 1, width, columns), lambda i: (i, t, 0, 0)),
        out_shape=jax.ShapeDtypeStruct(shape, jnp.bfloat16),
        input_output_aliases=aliases,
        compiler_params=pltpu.CompilerParams(vmem_limit_bytes=VMEM),
        cost_estimate=cost(
            2 * layers * width * columns * tokens // EASE, 2 * layers * width * (columns + tokens) // EASE
        ),
        name="grads",
    )(*operands)


EASE = 16


def gather_pieces(errors, spans, offsets, n_src, n_feat, codes_t):
    if (n_src, n_feat) != (2, 4):
        for offset, span in zip(offsets, spans):
            part = lax.slice_in_dim(errors, offset, offset + span, axis=1)
            columns = lax.all_gather(part, "src", axis=2, tiled=True)
            piece = lax.all_gather(columns, "feat", axis=1, tiled=True)
            yield [piece], [(0, None, 0, n_feat * span, None, None)]
        return
    axes = ("src", "feat")
    to = lambda x, flip: lax.ppermute(x, axes, [(i, i ^ flip) for i in range(n_src * n_feat)])
    core_own = over_core(errors, n_feat)
    (part,) = cut_call(errors, 0, spans[0], [], [])
    after = [core_own, codes_t]
    for index, (offset, span) in enumerate(zip(offsets, spans)):
        arrived = [to(part, n_feat), to(part, 2), to(part, n_feat + 2)]
        more = index + 1 < len(spans)
        joined, *rest = cut_call(
            errors, offsets[index + 1] if more else None, spans[index + 1] if more else None, arrived, after
        )
        part = rest[0] if more else None
        plan = [(core, None, offset, span, 0, core) for core in (0, 1)]
        for lead, (dx, dy) in enumerate(((1, 0), (0, 2), (1, 2))):
            plan += [(2 + core, lead, 0, span, dx, dy ^ core) for core in (0, 1)]
        after = yield [errors, core_own, joined, over_core(joined, n_feat)], plan


def over_core(x, n_feat):
    return lax.ppermute(x, "feat", [(i, i ^ 1) for i in range(n_feat)])


def body(n_src, n_tgt, n_feat, errors, saved_codes, active_mask, decoder):
    tgt_count = decoder.shape[1]
    stride = errors.shape[1]
    spans = [stride * part // 8 for part in EIGHTHS]
    offsets = [sum(spans[:index]) for index in range(len(spans))]
    near = [(i, i ^ 1) for i in range(n_tgt)]
    middle = [(1, 2), (2, 1)]
    across = [(i, i ^ 2) for i in range(n_tgt)]
    codes_t = turn_call(saved_codes, spans)
    gather = gather_pieces(errors, spans, offsets, n_src, n_feat, codes_t)
    pieces, plan = next(gather)

    last = len(spans) - 1
    owns, gots = [], []
    everything, relayed = None, []
    decoder_grads = None

    def relay(index, after):
        ready = after + gots[index][1:] + [got for group in gots[:index] for got in group]
        sent = relay_call(owns[index], gots[index][0], ready)
        gots[index].append(lax.ppermute(sent, "tgt", across))
        return [sent]

    for index, span in enumerate(spans):
        own, both, far, everything = terms_call(
            pieces,
            plan,
            decoder,
            everything,
            n_feat * offsets[index],
            n_tgt,
            n_feat * span,
            n_feat * stride,
            relayed,
        )
        owns.append(own)
        gots.append([lax.ppermute(both, "tgt", near), lax.ppermute(far, "tgt", middle)])
        if index < last:
            pieces, plan = gather.send([own])
        relayed = relay(index - 1, [own]) if index else gots[0][:2]
    for t in range(tgt_count):
        decoder_grads = grads_call(t, codes_t, everything, decoder_grads, decoder.shape, relayed)
        if t == 0:
            relayed = relay(last, [decoder_grads])
    code_grads = None
    for index in range(len(spans)):
        code_grads = finish_call(
            owns[index], gots[index], active_mask, code_grads, offsets[index], stride, [] if index else [decoder_grads]
        )
    return code_grads, decoder_grads


def plain_body(errors, saved_codes, active_mask, decoder):
    src_count, tgt_count, feat_count, _ = decoder.shape
    src_ids = lax.axis_index("src") * src_count + jnp.arange(src_count, dtype=jnp.int32)
    tgt_ids = lax.axis_index("tgt") * tgt_count + jnp.arange(tgt_count, dtype=jnp.int32)
    kept = (tgt_ids[None, :] >= src_ids[:, None])[:, :, None, None]
    columns = lax.all_gather(errors, "src", axis=2, tiled=True)
    portion = lax.all_gather(columns, "feat", axis=1, tiled=True)
    grads = jnp.einsum("itf,jtd->ijfd", saved_codes, portion, preferred_element_type=jnp.float32)
    decoder = jnp.where(kept, decoder, jnp.zeros_like(decoder))
    term = jnp.einsum("jtd,ijfd->itf", portion, decoder, preferred_element_type=jnp.float32)
    summed = lax.psum_scatter(term, "tgt", scatter_dimension=1, tiled=True)
    code_grads = (summed * active_mask.astype(jnp.float32)).astype(jnp.bfloat16)
    return code_grads, jnp.where(kept, grads, 0.0).astype(jnp.bfloat16)


def solution(mesh):
    sizes = [mesh.shape[axis] for axis in ("src", "tgt", "feat")]
    fits = sizes[1] == 4 and sizes[2] % sizes[1] == 0
    in_specs = (
        P("tgt", "feat", "src"),
        P("src", None, "feat"),
        P("src", "tgt", "feat"),
        P("src", "tgt", "feat", None),
    )
    out_specs = (P("src", "tgt", "feat"), P("src", "tgt", "feat", None))
    return jax.shard_map(
        functools.partial(body, *sizes) if fits else plain_body,
        mesh=mesh,
        in_specs=in_specs,
        out_specs=out_specs,
        check_vma=False,
    )
```

time: 285 us -> 314 us (1.10)
  Pallas kernels: 0 us -> 223 us
  waiting for transfers between devices: 194 us -> 50.9 us
  matrix products: 48.9 us -> 0 us
  starting transfers between devices: 0.11 us -> 34.3 us
  local copies, waits for them, and re-layouts: 24.9 us -> 2.97 us
  between operations: 13.8 us -> 1.01 us
    pallas_call x0 -> x16, Pallas kernels: none -> 223 us  [the longest x4 132 us: cut_call(): pl.pallas_call(functools.partial(cut_kernel, len(join), offset), in_specs...]
    all_gather x2 -> x0, waiting for transfers between devices: 97.1 us -> none  [the longest x1 59.6 us: body(): portion = lax.all_gather(all_columns, 'feat', axis=1, tiled=True)]
    reduce_scatter x1 -> x0, waiting for transfers between devices: 96.3 us -> none  [body(): lax.psum_scatter(term.reshape(tokens_all // lax.axis_size('tgt') * lax.ax...]
    ppermute x0 -> x22, waiting for transfers between devices: none -> 50.9 us  [the longest x3 30.7 us: relay(): gots[index].append(lax.ppermute(sent, 'tgt', across))]
    dot_general x2 -> x0, matrix products: 48.9 us -> none  [the longest x1 24.8 us: body(): jnp.einsum('itf,jtd->ijfd', saved_codes, portion, preferred_element_type=...]
    ppermute x0 -> x22, starting transfers between devices: none -> 34.3 us  [the longest x3 13 us: relay(): gots[index].append(lax.ppermute(sent, 'tgt', across))]
    unnamed x3 -> x14, local copies, waits for them, and re-layouts: 24.8 us -> 2.97 us
  transfers between devices with their start and end apart: 3 -> 22, of which waited for: 3 -> 7; matrix products, arithmetic and copies ran while one was open for 17% -> 0% of each run, Pallas kernels for 0% -> 30%
where the time goes in v2:
time: 314 us; the launch traced here: 312 us
  Pallas kernels  223 us (71%)
  waiting for transfers between devices  50.9 us (16%)
  starting transfers between devices  34.3 us (11%)
    pallas_call x4, Pallas kernels, cut_call(): pl.pallas_call(functools.partial(cut_kernel, len(join), offset), in_specs...  132 us
    pallas_call x3, Pallas kernels, terms_call(): pl.pallas_call(functools.partial(terms_kernel, n_tgt, plan, offset), in_s...  47.9 us
    ppermute x3, waiting for transfers between devices, relay(): gots[index].append(lax.ppermute(sent, 'tgt', across))  30.7 us
    pallas_call x2, Pallas kernels, grads_call(): pl.pallas_call(functools.partial(grads_kernel, (t, tgt_count)), grid=(lay...  20.2 us
    ppermute x3, starting transfers between devices, relay(): gots[index].append(lax.ppermute(sent, 'tgt', across))  13 us
    ppermute x9, starting transfers between devices, gather_pieces(): lax.ppermute(x, axes, [(i, i ^ flip) for i in range(n_src * n_feat)])  11.2 us
    pallas_call x3, Pallas kernels, finish_call(): pl.pallas_call(functools.partial(finish_kernel, len(gots), offset, stride...  10.9 us
    ppermute x9, waiting for transfers between devices, gather_pieces(): lax.ppermute(x, axes, [(i, i ^ flip) for i in range(n_src * n_feat)])  10.8 us
  transfers between devices with their start and end apart: 22, of which 7 were waited for; matrix products, arithmetic and copies ran while one was open for 0% of the time, Pallas kernels for 30%

profile of v2, /device:TPU:0, one launch (start us, length us, event | category | flops | bytes accessed | tf_op | source)
XLA Modules:
  0.0 312.4 jit_solution(190345261901004643)
XLA Ops:
  0.6 0.5 collective-permute-start
  1.1 9.0 %cut.4 = bf16[2,64,1024]{2,1,0:T(8,128)(2,1)} custom-call(bf16[2,256,1024]{2,1,0:T(8,128)(2,1)} %refs_0_.5), custom_call_target="tpu_custom_call" | custom-call | tf_op jit(solution)/shard_map/cut/pallas_call | solution.py:100
  10.2 3.5 %collective-permute-start.3 = (bf16[2,64,1024]{2,1,0:T(8,128)(2,1)}, bf16[2,64,1024]{2,1,0:T(8,128)(2,1)S(1)}, u32[]{:S(2)}, u32[]{:S(2)}) collective-permute-start(bf16[2,64,1024]{2,1,0:T(8,128)(2,1)} %cut.4), channel_id=1, source_target_pairs={{0,18},{1,19},{2,16},{3,17},{16,2},{17,3},{18,0},{19,1},{4,22},{5,... | collective-permute-start | bytes 786440 | tf_op jit(solution)/shard_map/ppermute | solution.py:458
  13.7 0.5 collective-permute-start.2
  14.2 0.1 collective-permute-start.1
  14.4 5.3 %turn.1.refs_4_.codes_ref = bf16[4,512,1024]{2,1,0:T(8,128)(2,1)} custom-call(bf16[4,1024,512]{2,1,0:T(8,128)(2,1)} %codes_ref.1), custom_call_target="tpu_custom_call" | custom-call | flops 131072 | bytes 524288 | tf_op jit(solution)/shard_map/turn/pallas_call | solution.py:386
  19.7 1.5 collective-permute-done.3.refs_2_
  21.1 5.5 %collective-permute-done.2.refs_1_ = bf16[2,64,1024]{2,1,0:T(8,128)(2,1)} collective-permute-done((bf16[2,64,1024]{2,1,0:T(8,128)(2,1)}, bf16[2,64,1024]{2,1,0:T(8,128)(2,1)}, u32[]{:S(2)}, u32[]{:S(2)}) %collective-permute-start.2) | collective-permute-done | bytes 262176 | tf_op jit(solution)/shard_map/ppermute | solution.py:458
  26.6 0.3 collective-permute-done.1.refs_0_
  26.9 0.0 collective-permute-done.refs_3_.refs_1_
  26.9 36.9 %cut.5 = (bf16[3,2,64,1024]{3,2,1,0:T(8,128)(2,1)}, bf16[2,96,1024]{2,1,0:T(8,128)(2,1)}) custom-call(bf16[2,256,1024]{2,1,0:T(8,128)(2,1)} %refs_0_.5, bf16[2,64,1024]{2,1,0:T(8,128)(2,1)} %collective-permute-done.1.refs_0_, bf16[2,64,1024]{2,1,0:T(8,128)(2,1)} %collective-permute-done.2.refs_1_, bf16[2,64,1024]{2,1,0:T(8,128)(2,1)} %copy-done.6, ...), custom_call_target="tpu_custom_call" | custom-call | tf_op jit(solution)/shard_map/cut/pallas_call | solution.py:100
  63.8 0.1 collective-permute-start.7
  63.9 1.6 collective-permute-start.6
  65.5 1.4 collective-permute-start.5
  66.9 0.5 collective-permute-start.4
  67.4 0.0 collective-permute-done.7.refs_3_
  67.4 14.0 %terms.3 = (f32[2,4,64,512]{3,2,1,0:T(8,128)}, s32[1040,128]{1,0:T(8,128)}, s32[520,128]{1,0:T(8,128)}, bf16[1024,4096]{1,0:T(8,128)(2,1)}) custom-call(bf16[2,256,1024]{2,1,0:T(8,128)(2,1)} %refs_0_.5, bf16[2,256,1024]{2,1,0:T(8,128)(2,1)} %collective-permute-done.refs_3_.refs_1_, bf16[3,2,64,1024]{3,2,1,0:T(8,128)(2,1)} %get-tuple-element.19.refs_2_, ...), custom_call_target="tpu_custom_call" | custom-call | flops 268435456 | bytes 1048576 | tf_op jit(solution)/shard_map/terms/pallas_call | solution.py:228
  81.5 0.0 collective-permute-done.6.refs_2_
  81.5 0.0 copy-start.5
  81.5 3.6 %collective-permute-done.5.refs_1_ = bf16[2,96,1024]{2,1,0:T(8,128)(2,1)} collective-permute-done((bf16[2,96,1024]{2,1,0:T(8,128)(2,1)}, bf16[2,96,1024]{2,1,0:T(8,128)(2,1)}, u32[]{:S(2)}, u32[]{:S(2)}) %collective-permute-start.5) | collective-permute-done | bytes 393248 | tf_op jit(solution)/shard_map/ppermute | solution.py:458
  85.1 0.0 collective-permute-done.4.refs_0_
  85.1 48.8 %cut.6 = (bf16[3,2,96,1024]{3,2,1,0:T(8,128)(2,1)}, bf16[2,96,1024]{2,1,0:T(8,128)(2,1)}) custom-call(bf16[2,256,1024]{2,1,0:T(8,128)(2,1)} %refs_0_.5, bf16[2,96,1024]{2,1,0:T(8,128)(2,1)} %collective-permute-done.4.refs_0_, bf16[2,96,1024]{2,1,0:T(8,128)(2,1)} %collective-permute-done.5.refs_1_, bf16[2,96,1024]{2,1,0:T(8,128)(2,1)} %copy-done.5, ...), custom_call_target="tpu_custom_call" | custom-call | tf_op jit(solution)/shard_map/cut/pallas_call | solution.py:100
  133.9 0.1 collective-permute-start.11
  134.0 0.7 collective-permute-start.13
  134.6 4.4 %collective-permute-start.12 = (s32[1040,128]{1,0:T(8,128)}, s32[1040,128]{1,0:T(8,128)}, u32[]{:S(2)}, u32[]{:S(2)}) collective-permute-start(s32[1040,128]{1,0:T(8,128)} %get-tuple-element.24), channel_id=1, source_target_pairs={{0,4},{4,0},{8,12},{12,8},{1,5},{5,1},{9,13},{13,9},{2,6},{6,2},{1... | collective-permute-start | bytes 1597448 | tf_op jit(solution)/shard_map/ppermute | solution.py:515
  139.1 1.7 collective-permute-start.10
  140.7 1.3 collective-permute-start.9
  142.0 0.0 collective-permute-done.13.refs_7_.refs_1_.refs_3_
  142.0 0.5 collective-permute-start.8
  142.6 9.3 %collective-permute-done.12.refs_6_.got_ref.refs_2_.refs_0_ = s32[1040,128]{1,0:T(8,128)} collective-permute-done((s32[1040,128]{1,0:T(8,128)}, s32[1040,128]{1,0:T(8,128)}, u32[]{:S(2)}, u32[]{:S(2)}) %collective-permute-start.12) | collective-permute-done | bytes 532512 | tf_op jit(solution)/shard_map/ppermute | solution.py:515
  151.9 0.0 collective-permute-done.11.refs_3_
  151.9 16.9 %terms.4 = (f32[2,4,96,512]{3,2,1,0:T(8,128)}, s32[1552,128]{1,0:T(8,128)}, s32[776,128]{1,0:T(8,128)}, bf16[1024,4096]{1,0:T(8,128)(2,1)}) custom-call(bf16[2,256,1024]{2,1,0:T(8,128)(2,1)} %refs_0_.5, bf16[2,256,1024]{2,1,0:T(8,128)(2,1)} %collective-permute-done.refs_3_.refs_1_, ...), custom_call_target="tpu_custom_call", output_to_operand_aliasing={{3}: (5, {})} | custom-call | flops 402653184 | bytes 1048576 | tf_op jit(solution)/shard_map/terms/pallas_call | solution.py:228
  168.8 0.0 collective-permute-done.10.refs_2_
  168.8 0.0 collective-permute-done.9.refs_1_
  168.8 0.0 collective-permute-done.8.refs_0_
  168.8 36.9 %cut.7.refs_2_ = bf16[3,2,96,1024]{3,2,1,0:T(8,128)(2,1)} custom-call(bf16[2,256,1024]{2,1,0:T(8,128)(2,1)} %refs_0_.5, bf16[2,96,1024]{2,1,0:T(8,128)(2,1)} %collective-permute-done.8.refs_0_, bf16[2,96,1024]{2,1,0:T(8,128)(2,1)} %collective-permute-done.9.refs_1_, bf16[2,96,1024]{2,1,0:T(8,128)(2,1)} %collective-permute-done.10.refs_2_, ...), custom_call_target="tpu_custom_call" | custom-call | tf_op jit(solution)/shard_map/cut/pallas_call | solution.py:100
  205.7 0.1 collective-permute-start.14
  205.8 1.3 collective-permute-start.17
  207.0 0.7 collective-permute-start.18
  207.7 2.3 relay.3.refs_6_
  210.0 0.0 collective-permute-done.14.refs_3_
  210.0 17.0 %terms.5 = (f32[2,4,96,512]{3,2,1,0:T(8,128)}, s32[1552,128]{1,0:T(8,128)}, s32[776,128]{1,0:T(8,128)}, bf16[1024,4096]{1,0:T(8,128)(2,1)}) custom-call(bf16[2,256,1024]{2,1,0:T(8,128)(2,1)} %refs_0_.5, bf16[2,256,1024]{2,1,0:T(8,128)(2,1)} %collective-permute-done.refs_3_.refs_1_, ...), custom_call_target="tpu_custom_call", output_to_operand_aliasing={{3}: (5, {})} | custom-call | flops 402653184 | bytes 1048576 | tf_op jit(solution)/shard_map/terms/pallas_call | solution.py:228
  227.0 1.6 collective-permute-start.15
  228.6 1.4 collective-permute-start.19
  230.0 21.9 %collective-permute-done.19.refs_4_.refs_2_ = s32[520,128]{1,0:T(8,128)S(1)} collective-permute-done((s32[520,128]{1,0:T(8,128)}, s32[520,128]{1,0:T(8,128)S(1)}, u32[]{:S(2)}, u32[]{:S(2)}) %collective-permute-start.19) | collective-permute-done | bytes 266272 | tf_op jit(solution)/shard_map/ppermute | solution.py:499
  251.9 0.0 collective-permute-done.18.refs_1_.refs_6_
  251.9 0.7 copy-done.2
  252.6 0.0 collective-permute-done.17.got_ref.refs_5_.refs_0_
  252.6 0.8 copy-done.1
  253.4 2.6 relay.4.refs_0_
  256.0 3.3 %collective-permute-start.20 = (s32[776,128]{1,0:T(8,128)}, s32[776,128]{1,0:T(8,128)}, u32[]{:S(2)}, u32[]{:S(2)}) collective-permute-start(s32[776,128]{1,0:T(8,128)} %relay.4.refs_0_), channel_id=1, source_target_pairs={{0,8},{4,12},{8,0},{12,4},{1,9},{5,13},{9,1},{13,5},{2,10},{6,14},... | collective-permute-start | bytes 1191944 | tf_op jit(solution)/shard_map/ppermute | solution.py:499
  259.3 0.7 collective-permute-start.16
  259.9 9.5 %grads.2.refs_0_ = bf16[4,2,512,2048]{3,2,1,0:T(8,128)(2,1)} custom-call(bf16[4,512,1024]{2,1,0:T(8,128)(2,1)} %turn.1.refs_4_.codes_ref, bf16[1024,4096]{1,0:T(8,128)(2,1)} %get-tuple-element.31.err_ref, s32[776,128]{1,0:T(8,128)} %relay.4.refs_0_), custom_call_target="tpu_custom_call" | custom-call | flops 536870912 | bytes 786432 | tf_op jit(solution)/shard_map/grads/pallas_call | solution.py:431
  269.4 8.8 %collective-permute-done.20.refs_7_.refs_2_ = s32[776,128]{1,0:T(8,128)} collective-permute-done((s32[776,128]{1,0:T(8,128)}, s32[776,128]{1,0:T(8,128)}, u32[]{:S(2)}, u32[]{:S(2)}) %collective-permute-start.20) | collective-permute-done | bytes 397344 | tf_op jit(solution)/shard_map/ppermute | solution.py:499
  278.2 0.0 collective-permute-done.15.got_ref.refs_0_
  278.2 0.8 copy-done.3
  278.9 2.6 relay.5.refs_1_
  281.5 8.3 %collective-permute-start.21 = (s32[776,128]{1,0:T(8,128)}, s32[776,128]{1,0:T(8,128)S(1)}, u32[]{:S(2)}, u32[]{:S(2)}) collective-permute-start(s32[776,128]{1,0:T(8,128)} %relay.5.refs_1_), channel_id=1, source_target_pairs={{0,8},{4,12},{8,0},{12,4},{1,9},{5,13},{9,1},{13,5},{2,10},{6,14},... | collective-permute-start | bytes 1191944 | tf_op jit(solution)/shard_map/ppermute | solution.py:499
  289.8 10.7 %grads.3.refs_4_ = bf16[4,2,512,2048]{3,2,1,0:T(8,128)(2,1)} custom-call(bf16[4,512,1024]{2,1,0:T(8,128)(2,1)} %turn.1.refs_4_.codes_ref, bf16[1024,4096]{1,0:T(8,128)(2,1)} %get-tuple-element.31.err_ref, bf16[4,2,512,2048]{3,2,1,0:T(8,128)(2,1)} %grads.2.refs_0_, s32[776,128]{1,0:T(8,128)} %relay.5.refs_1_), custom_call_target="tpu_custom_call", output_to_operand_aliasing={{}: (2, {})} | custom-call | flops 536870912 | bytes 786432 | tf_op jit(solution)/shard_map/grads/pallas_call | solution.py:431
  300.5 3.3 %finish.3.refs_4_ = bf16[4,256,512]{2,1,0:T(8,128)(2,1)} custom-call(f32[2,4,64,512]{3,2,1,0:T(8,128)} %get-tuple-element.20.refs_3_.own_ref, s32[1040,128]{1,0:T(8,128)} %collective-permute-done.12.refs_6_.got_ref.refs_2_.refs_0_, s32[520,128]{1,0:T(8,128)} %copy-done, s32[520,128]{1,0:T(8,128)} %copy-done.2, s32[4,256,512]{2,1,0:T(8,128)} %refs_3_.5, ...), custom_call_target="tpu_custom_call" | custom-call | flops 163840 | bytes 131072 | tf_op jit(solution)/shard_map/finish/pallas_call | solution.py:351
  303.9 3.8 %finish.4.refs_4_ = bf16[4,256,512]{2,1,0:T(8,128)(2,1)} custom-call(f32[2,4,96,512]{3,2,1,0:T(8,128)} %get-tuple-element.26.refs_3_.refs_0_.own_ref, s32[1552,128]{1,0:T(8,128)} %collective-permute-done.17.got_ref.refs_5_.refs_0_, s32[776,128]{1,0:T(8,128)} %copy-done.1, ...), custom_call_target="tpu_custom_call", output_to_operand_aliasing={{}: (5, {})} | custom-call | flops 245760 | bytes 196608 | tf_op jit(solution)/shard_map/finish/pallas_call | solution.py:351
  307.7 0.0 collective-permute-done.21.refs_2_
  307.7 0.7 copy-done.4
  308.4 3.8 %finish.5 = bf16[4,256,512]{2,1,0:T(8,128)(2,1)} custom-call(f32[2,4,96,512]{3,2,1,0:T(8,128)} %get-tuple-element.28.refs_0_.own_ref, s32[1552,128]{1,0:T(8,128)} %collective-permute-done.15.got_ref.refs_0_, s32[776,128]{1,0:T(8,128)} %copy-done.3, s32[776,128]{1,0:T(8,128)} %copy-done.4, s32[4,256,512]{2,1,0:T(8,128)} %refs_3_.5, ...), custom_call_target="tpu_custom_call", output_to_operand_aliasing={{}: (5, {})} | custom-call | flops 245760 | bytes 196608 | tf_op jit(solution)/shard_map/finish/pallas_call | solution.py:351
  (10 shorter events, 0.0 us)
Async XLA Ops:
  0.6 26.3 %collective-permute-start = (bf16[2,256,1024]{2,1,0:T(8,128)(2,1)}, bf16[2,256,1024]{2,1,0:T(8,128)(2,1)}, u32[]{:S(2)}, u32[]{:S(2)}) collective-permute-start(bf16[2,256,1024]{2,1,0:T(8,128)(2,1)} %refs_0_.5), channel_id=1, source_target_pairs={{0,1},{1,0},{2,3},{3,2},{4,5},{5,4},{6,7},{7,6},{8,9},{9,8},{10,11... | collective-permute-start | bytes 3145736 | tf_op jit(solution)/shard_map/ppermute | solution.py:476
  10.2 10.9 %collective-permute-start.3 = (bf16[2,64,1024]{2,1,0:T(8,128)(2,1)}, bf16[2,64,1024]{2,1,0:T(8,128)(2,1)S(1)}, u32[]{:S(2)}, u32[]{:S(2)}) collective-permute-start(bf16[2,64,1024]{2,1,0:T(8,128)(2,1)} %cut.4), channel_id=1, source_target_pairs={{0,18},{1,19},{2,16},{3,17},{16,2},{17,3},{18,0},{19,1},{4,22},{5,... | collective-permute-start | bytes 786440 | tf_op jit(solution)/shard_map/ppermute | solution.py:458
  13.7 12.9 %collective-permute-start.2 = (bf16[2,64,1024]{2,1,0:T(8,128)(2,1)}, bf16[2,64,1024]{2,1,0:T(8,128)(2,1)}, u32[]{:S(2)}, u32[]{:S(2)}) collective-permute-start(bf16[2,64,1024]{2,1,0:T(8,128)(2,1)} %cut.4), channel_id=1, source_target_pairs={{0,2},{1,3},{2,0},{3,1},{16,18},{17,19},{18,16},{19,17},{4,6},{5,7... | collective-permute-start | bytes 786440 | tf_op jit(solution)/shard_map/ppermute | solution.py:458
  14.2 12.7 %collective-permute-start.1 = (bf16[2,64,1024]{2,1,0:T(8,128)(2,1)}, bf16[2,64,1024]{2,1,0:T(8,128)(2,1)}, u32[]{:S(2)}, u32[]{:S(2)}) collective-permute-start(bf16[2,64,1024]{2,1,0:T(8,128)(2,1)} %cut.4), channel_id=1, source_target_pairs={{0,16},{1,17},{2,18},{3,19},{16,0},{17,1},{18,2},{19,3},{4,20},{5,... | collective-permute-start | bytes 786440 | tf_op jit(solution)/shard_map/ppermute | solution.py:458
  21.1 5.8 %copy-start.6 = (bf16[2,64,1024]{2,1,0:T(8,128)(2,1)}, bf16[2,64,1024]{2,1,0:T(8,128)(2,1)S(1)}, u32[]{:S(2)}) copy-start(bf16[2,64,1024]{2,1,0:T(8,128)(2,1)S(1)} %collective-permute-done.3.refs_2_) | copy-start | bytes 786436
  63.8 3.6 %collective-permute-start.7 = (bf16[3,2,64,1024]{3,2,1,0:T(8,128)(2,1)}, bf16[3,2,64,1024]{3,2,1,0:T(8,128)(2,1)}, u32[]{:S(2)}, u32[]{:S(2)}) collective-permute-start(bf16[3,2,64,1024]{3,2,1,0:T(8,128)(2,1)} %get-tuple-element.19.refs_2_), channel_id=1, source_target_pairs={{0,1},{1,0},{2,3},{3,2},{4,5},{5,4},{6,7},{7,6},{8,9},{9,8},{10,11... | collective-permute-start | bytes 2359304 | tf_op jit(solution)/shard_map/ppermute | solution.py:476
  63.9 17.6 %collective-permute-start.6 = (bf16[2,96,1024]{2,1,0:T(8,128)(2,1)}, bf16[2,96,1024]{2,1,0:T(8,128)(2,1)S(1)}, u32[]{:S(2)}, u32[]{:S(2)}) collective-permute-start(bf16[2,96,1024]{2,1,0:T(8,128)(2,1)} %get-tuple-element.18), channel_id=1, source_target_pairs={{0,18},{1,19},{2,16},{3,17},{16,2},{17,3},{18,0},{19,1},{4,22},{5,... | collective-permute-start | bytes 1179656 | tf_op jit(solution)/shard_map/ppermute | solution.py:458
  65.5 19.6 %collective-permute-start.5 = (bf16[2,96,1024]{2,1,0:T(8,128)(2,1)}, bf16[2,96,1024]{2,1,0:T(8,128)(2,1)}, u32[]{:S(2)}, u32[]{:S(2)}) collective-permute-start(bf16[2,96,1024]{2,1,0:T(8,128)(2,1)} %get-tuple-element.18), channel_id=1, source_target_pairs={{0,2},{1,3},{2,0},{3,1},{16,18},{17,19},{18,16},{19,17},{4,6},{5,7... | collective-permute-start | bytes 1179656 | tf_op jit(solution)/shard_map/ppermute | solution.py:458
  66.9 18.2 %collective-permute-start.4 = (bf16[2,96,1024]{2,1,0:T(8,128)(2,1)}, bf16[2,96,1024]{2,1,0:T(8,128)(2,1)}, u32[]{:S(2)}, u32[]{:S(2)}) collective-permute-start(bf16[2,96,1024]{2,1,0:T(8,128)(2,1)} %get-tuple-element.18), channel_id=1, source_target_pairs={{0,16},{1,17},{2,18},{3,19},{16,0},{17,1},{18,2},{19,3},{4,20},{5,... | collective-permute-start | bytes 1179656 | tf_op jit(solution)/shard_map/ppermute | solution.py:458
  81.5 3.6 %copy-start.5 = (bf16[2,96,1024]{2,1,0:T(8,128)(2,1)}, bf16[2,96,1024]{2,1,0:T(8,128)(2,1)S(1)}, u32[]{:S(2)}) copy-start(bf16[2,96,1024]{2,1,0:T(8,128)(2,1)S(1)} %collective-permute-done.6.refs_2_) | copy-start | bytes 1179652
  133.9 18.0 %collective-permute-start.11 = (bf16[3,2,96,1024]{3,2,1,0:T(8,128)(2,1)}, bf16[3,2,96,1024]{3,2,1,0:T(8,128)(2,1)}, u32[]{:S(2)}, u32[]{:S(2)}) collective-permute-start(bf16[3,2,96,1024]{3,2,1,0:T(8,128)(2,1)} %get-tuple-element.22.refs_2_), channel_id=1, source_target_pairs={{0,1},{1,0},{2,3},{3,2},{4,5},{5,4},{6,7},{7,6},{8,9},{9,8},{10,11... | collective-permute-start | bytes 3538952 | tf_op jit(solution)/shard_map/ppermute | solution.py:476
  134.0 8.1 %collective-permute-start.13 = (s32[520,128]{1,0:T(8,128)}, s32[520,128]{1,0:T(8,128)S(1)}, u32[]{:S(2)}, u32[]{:S(2)}) collective-permute-start(s32[520,128]{1,0:T(8,128)} %get-tuple-element.25), channel_id=1, source_target_pairs={{4,8},{8,4},{5,9},{9,5},{6,10},{10,6},{7,11},{11,7},{20,24},{24,20... | collective-permute-start | bytes 798728 | tf_op jit(solution)/shard_map/ppermute | solution.py:515
  134.6 17.2 %collective-permute-start.12 = (s32[1040,128]{1,0:T(8,128)}, s32[1040,128]{1,0:T(8,128)}, u32[]{:S(2)}, u32[]{:S(2)}) collective-permute-start(s32[1040,128]{1,0:T(8,128)} %get-tuple-element.24), channel_id=1, source_target_pairs={{0,4},{4,0},{8,12},{12,8},{1,5},{5,1},{9,13},{13,9},{2,6},{6,2},{1... | collective-permute-start | bytes 1597448 | tf_op jit(solution)/shard_map/ppermute | solution.py:515
  139.1 29.7 %collective-permute-start.10 = (bf16[2,96,1024]{2,1,0:T(8,128)(2,1)}, bf16[2,96,1024]{2,1,0:T(8,128)(2,1)}, u32[]{:S(2)}, u32[]{:S(2)}) collective-permute-start(bf16[2,96,1024]{2,1,0:T(8,128)(2,1)} %get-tuple-element.21), channel_id=1, source_target_pairs={{0,18},{1,19},{2,16},{3,17},{16,2},{17,3},{18,0},{19,1},{4,22},{5,... | collective-permute-start | bytes 1179656 | tf_op jit(solution)/shard_map/ppermute | solution.py:458
  140.7 28.1 %collective-permute-start.9 = (bf16[2,96,1024]{2,1,0:T(8,128)(2,1)}, bf16[2,96,1024]{2,1,0:T(8,128)(2,1)}, u32[]{:S(2)}, u32[]{:S(2)}) collective-permute-start(bf16[2,96,1024]{2,1,0:T(8,128)(2,1)} %get-tuple-element.21), channel_id=1, source_target_pairs={{0,2},{1,3},{2,0},{3,1},{16,18},{17,19},{18,16},{19,17},{4,6},{5,7... | collective-permute-start | bytes 1179656 | tf_op jit(solution)/shard_map/ppermute | solution.py:458
  142.0 9.8 %copy-start = (s32[520,128]{1,0:T(8,128)}, s32[520,128]{1,0:T(8,128)S(1)}, u32[]{:S(2)}) copy-start(s32[520,128]{1,0:T(8,128)S(1)} %collective-permute-done.13.refs_7_.refs_1_.refs_3_) | copy-start | bytes 798724
  142.0 26.8 %collective-permute-start.8 = (bf16[2,96,1024]{2,1,0:T(8,128)(2,1)}, bf16[2,96,1024]{2,1,0:T(8,128)(2,1)}, u32[]{:S(2)}, u32[]{:S(2)}) collective-permute-start(bf16[2,96,1024]{2,1,0:T(8,128)(2,1)} %get-tuple-element.21), channel_id=1, source_target_pairs={{0,16},{1,17},{2,18},{3,19},{16,0},{17,1},{18,2},{19,3},{4,20},{5,... | collective-permute-start | bytes 1179656 | tf_op jit(solution)/shard_map/ppermute | solution.py:458
  205.7 4.3 %collective-permute-start.14 = (bf16[3,2,96,1024]{3,2,1,0:T(8,128)(2,1)}, bf16[3,2,96,1024]{3,2,1,0:T(8,128)(2,1)}, u32[]{:S(2)}, u32[]{:S(2)}) collective-permute-start(bf16[3,2,96,1024]{3,2,1,0:T(8,128)(2,1)} %cut.7.refs_2_), channel_id=1, source_target_pairs={{0,1},{1,0},{2,3},{3,2},{4,5},{5,4},{6,7},{7,6},{8,9},{9,8},{10,11... | collective-permute-start | bytes 3538952 | tf_op jit(solution)/shard_map/ppermute | solution.py:476
  205.8 46.9 %collective-permute-start.17 = (s32[1552,128]{1,0:T(8,128)}, s32[1552,128]{1,0:T(8,128)}, u32[]{:S(2)}, u32[]{:S(2)}) collective-permute-start(s32[1552,128]{1,0:T(8,128)} %get-tuple-element.32), channel_id=1, source_target_pairs={{0,4},{4,0},{8,12},{12,8},{1,5},{5,1},{9,13},{13,9},{2,6},{6,2},{1... | collective-permute-start | bytes 2383880 | tf_op jit(solution)/shard_map/ppermute | solution.py:515
  207.0 44.9 %collective-permute-start.18 = (s32[776,128]{1,0:T(8,128)}, s32[776,128]{1,0:T(8,128)S(1)}, u32[]{:S(2)}, u32[]{:S(2)}) collective-permute-start(s32[776,128]{1,0:T(8,128)} %get-tuple-element.33), channel_id=1, source_target_pairs={{4,8},{8,4},{5,9},{9,5},{6,10},{10,6},{7,11},{11,7},{20,24},{24,20... | collective-permute-start | bytes 1191944 | tf_op jit(solution)/shard_map/ppermute | solution.py:515
  227.0 51.2 %collective-permute-start.15 = (s32[1552,128]{1,0:T(8,128)}, s32[1552,128]{1,0:T(8,128)}, u32[]{:S(2)}, u32[]{:S(2)}) collective-permute-start(s32[1552,128]{1,0:T(8,128)} %get-tuple-element.29), channel_id=1, source_target_pairs={{0,4},{4,0},{8,12},{12,8},{1,5},{5,1},{9,13},{13,9},{2,6},{6,2},{1... | collective-permute-start | bytes 2383880 | tf_op jit(solution)/shard_map/ppermute | solution.py:515
  228.6 23.3 %collective-permute-start.19 = (s32[520,128]{1,0:T(8,128)}, s32[520,128]{1,0:T(8,128)S(1)}, u32[]{:S(2)}, u32[]{:S(2)}) collective-permute-start(s32[520,128]{1,0:T(8,128)} %relay.3.refs_6_), channel_id=1, source_target_pairs={{0,8},{4,12},{8,0},{12,4},{1,9},{5,13},{9,1},{13,5},{2,10},{6,14},... | collective-permute-start | bytes 798728 | tf_op jit(solution)/shard_map/ppermute | solution.py:499
  251.9 0.7 copy-start.2
  252.6 0.8 copy-start.1
  256.0 22.2 %collective-permute-start.20 = (s32[776,128]{1,0:T(8,128)}, s32[776,128]{1,0:T(8,128)}, u32[]{:S(2)}, u32[]{:S(2)}) collective-permute-start(s32[776,128]{1,0:T(8,128)} %relay.4.refs_0_), channel_id=1, source_target_pairs={{0,8},{4,12},{8,0},{12,4},{1,9},{5,13},{9,1},{13,5},{2,10},{6,14},... | collective-permute-start | bytes 1191944 | tf_op jit(solution)/shard_map/ppermute | solution.py:499
  259.3 18.9 %collective-permute-start.16 = (s32[776,128]{1,0:T(8,128)}, s32[776,128]{1,0:T(8,128)S(1)}, u32[]{:S(2)}, u32[]{:S(2)}) collective-permute-start(s32[776,128]{1,0:T(8,128)} %get-tuple-element.30), channel_id=1, source_target_pairs={{4,8},{8,4},{5,9},{9,5},{6,10},{10,6},{7,11},{11,7},{20,24},{24,20... | collective-permute-start | bytes 1191944 | tf_op jit(solution)/shard_map/ppermute | solution.py:515
  278.2 0.8 copy-start.3
  281.5 26.1 %collective-permute-start.21 = (s32[776,128]{1,0:T(8,128)}, s32[776,128]{1,0:T(8,128)S(1)}, u32[]{:S(2)}, u32[]{:S(2)}) collective-permute-start(s32[776,128]{1,0:T(8,128)} %relay.5.refs_1_), channel_id=1, source_target_pairs={{0,8},{4,12},{8,0},{12,4},{1,9},{5,13},{9,1},{13,5},{2,10},{6,14},... | collective-permute-start | bytes 1191944 | tf_op jit(solution)/shard_map/ppermute | solution.py:499
  307.7 0.8 copy-start.4

commit v3 on v2

--- a/solution.py
+++ b/solution.py
@@ -100,7 +100,7 @@
     return pl.pallas_call(
         functools.partial(cut_kernel, len(join), offset),
         in_specs=[ANYWHERE] * (1 + len(join) + len(after)),
-        out_specs=[ANYWHERE] * len(shapes),
+        out_specs=[pl.BlockSpec(memory_space=pltpu.VMEM)] * len(shapes),
         out_shape=shapes,
         scratch_shapes=[pltpu.SemaphoreType.DMA((len(join) + 1,))],
         compiler_params=pltpu.CompilerParams(vmem_limit_bytes=VMEM),

time: 314 us -> 191 us (0.61)
  Pallas kernels: 223 us -> 100 us
    pallas_call x4, Pallas kernels: 132 us -> 8.74 us  [cut_call(): pl.pallas_call(functools.partial(cut_kernel, len(join), offset), in_specs...]
  transfers between devices with their start and end apart: 22 -> 22, of which waited for: 7 -> 7; matrix products, arithmetic and copies ran while one was open for 0% -> 0% of each run, Pallas kernels for 30% -> 46%
where the time goes in v3:
time: 191 us; the launch traced here: 190 us
  Pallas kernels  100 us (52%)
  waiting for transfers between devices  50.9 us (27%)
  starting transfers between devices  34.3 us (18%)
  local copies, waits for them, and re-layouts  2.97 us (2%)
    pallas_call x3, Pallas kernels, terms_call(): pl.pallas_call(functools.partial(terms_kernel, n_tgt, plan, offset), in_s...  47.9 us
    ppermute x3, waiting for transfers between devices, relay(): gots[index].append(lax.ppermute(sent, 'tgt', across))  30.7 us
    pallas_call x2, Pallas kernels, grads_call(): pl.pallas_call(functools.partial(grads_kernel, (t, tgt_count)), grid=(lay...  20.2 us
    ppermute x3, starting transfers between devices, relay(): gots[index].append(lax.ppermute(sent, 'tgt', across))  13 us
    ppermute x9, starting transfers between devices, gather_pieces(): lax.ppermute(x, axes, [(i, i ^ flip) for i in range(n_src * n_feat)])  11.2 us
    pallas_call x3, Pallas kernels, finish_call(): pl.pallas_call(functools.partial(finish_kernel, len(gots), offset, stride...  10.9 us
    ppermute x9, waiting for transfers between devices, gather_pieces(): lax.ppermute(x, axes, [(i, i ^ flip) for i in range(n_src * n_feat)])  10.8 us
    ppermute x3, waiting for transfers between devices, body(): lax.ppermute(both, 'tgt', near)  9.29 us
  transfers between devices with their start and end apart: 22, of which 7 were waited for; matrix products, arithmetic and copies ran while one was open for 0% of the time, Pallas kernels for 46%

profile of v3, /device:TPU:0, one launch (start us, length us, event | category | flops | bytes accessed | tf_op | source)
XLA Modules:
  0.0 189.5 jit_solution(855500602617424651)
XLA Ops:
  0.6 0.5 collective-permute-start
  1.1 1.7 cut.4
  2.8 3.5 %collective-permute-start.3 = (bf16[2,64,1024]{2,1,0:T(8,128)(2,1)}, bf16[2,64,1024]{2,1,0:T(8,128)(2,1)S(1)}, u32[]{:S(2)}, u32[]{:S(2)}) collective-permute-start(bf16[2,64,1024]{2,1,0:T(8,128)(2,1)} %cut.4), channel_id=1, source_target_pairs={{0,18},{1,19},{2,16},{3,17},{16,2},{17,3},{18,0},{19,1},{4,22},{5,... | collective-permute-start | bytes 786440 | tf_op jit(solution)/shard_map/ppermute | solution.py:458
  6.3 0.5 collective-permute-start.2
  6.8 0.1 collective-permute-start.1
  7.0 5.3 %turn.1.refs_4_.codes_ref = bf16[4,512,1024]{2,1,0:T(8,128)(2,1)} custom-call(bf16[4,1024,512]{2,1,0:T(8,128)(2,1)} %codes_ref.1), custom_call_target="tpu_custom_call" | custom-call | flops 131072 | bytes 524288 | tf_op jit(solution)/shard_map/turn/pallas_call | solution.py:386
  12.3 1.5 collective-permute-done.3.refs_2_
  13.8 5.5 %collective-permute-done.2.refs_1_ = bf16[2,64,1024]{2,1,0:T(8,128)(2,1)} collective-permute-done((bf16[2,64,1024]{2,1,0:T(8,128)(2,1)}, bf16[2,64,1024]{2,1,0:T(8,128)(2,1)}, u32[]{:S(2)}, u32[]{:S(2)}) %collective-permute-start.2) | collective-permute-done | bytes 262176 | tf_op jit(solution)/shard_map/ppermute | solution.py:458
  19.2 0.3 collective-permute-done.1.refs_0_
  19.5 0.0 collective-permute-done.refs_3_.refs_1_
  19.5 2.3 %cut.5 = (bf16[3,2,64,1024]{3,2,1,0:T(8,128)(2,1)}, bf16[2,96,1024]{2,1,0:T(8,128)(2,1)}) custom-call(bf16[2,256,1024]{2,1,0:T(8,128)(2,1)} %refs_0_.5, bf16[2,64,1024]{2,1,0:T(8,128)(2,1)} %collective-permute-done.1.refs_0_, bf16[2,64,1024]{2,1,0:T(8,128)(2,1)} %collective-permute-done.2.refs_1_, bf16[2,64,1024]{2,1,0:T(8,128)(2,1)} %copy-done.6, ...), custom_call_target="tpu_custom_call" | custom-call | tf_op jit(solution)/shard_map/cut/pallas_call | solution.py:100
  21.8 0.1 collective-permute-start.7
  21.9 1.6 collective-permute-start.6
  23.5 1.4 collective-permute-start.5
  24.9 0.5 collective-permute-start.4
  25.5 0.0 collective-permute-done.7.refs_3_
  25.5 14.0 %terms.3 = (f32[2,4,64,512]{3,2,1,0:T(8,128)}, s32[1040,128]{1,0:T(8,128)}, s32[520,128]{1,0:T(8,128)}, bf16[1024,4096]{1,0:T(8,128)(2,1)}) custom-call(bf16[2,256,1024]{2,1,0:T(8,128)(2,1)} %refs_0_.5, bf16[2,256,1024]{2,1,0:T(8,128)(2,1)} %collective-permute-done.refs_3_.refs_1_, bf16[3,2,64,1024]{3,2,1,0:T(8,128)(2,1)} %get-tuple-element.19.refs_2_, ...), custom_call_target="tpu_custom_call" | custom-call | flops 268435456 | bytes 1048576 | tf_op jit(solution)/shard_map/terms/pallas_call | solution.py:228
  39.5 0.0 collective-permute-done.6.refs_2_
  39.5 0.0 copy-start.5
  39.5 3.6 %collective-permute-done.5.refs_1_ = bf16[2,96,1024]{2,1,0:T(8,128)(2,1)} collective-permute-done((bf16[2,96,1024]{2,1,0:T(8,128)(2,1)}, bf16[2,96,1024]{2,1,0:T(8,128)(2,1)}, u32[]{:S(2)}, u32[]{:S(2)}) %collective-permute-start.5) | collective-permute-done | bytes 393248 | tf_op jit(solution)/shard_map/ppermute | solution.py:458
  43.1 0.0 collective-permute-done.4.refs_0_
  43.1 2.5 %cut.6 = (bf16[3,2,96,1024]{3,2,1,0:T(8,128)(2,1)}, bf16[2,96,1024]{2,1,0:T(8,128)(2,1)}) custom-call(bf16[2,256,1024]{2,1,0:T(8,128)(2,1)} %refs_0_.5, bf16[2,96,1024]{2,1,0:T(8,128)(2,1)} %collective-permute-done.4.refs_0_, bf16[2,96,1024]{2,1,0:T(8,128)(2,1)} %collective-permute-done.5.refs_1_, bf16[2,96,1024]{2,1,0:T(8,128)(2,1)} %copy-done.5, ...), custom_call_target="tpu_custom_call" | custom-call | tf_op jit(solution)/shard_map/cut/pallas_call | solution.py:100
  45.6 0.1 collective-permute-start.11
  45.7 0.7 collective-permute-start.13
  46.4 4.4 %collective-permute-start.12 = (s32[1040,128]{1,0:T(8,128)}, s32[1040,128]{1,0:T(8,128)}, u32[]{:S(2)}, u32[]{:S(2)}) collective-permute-start(s32[1040,128]{1,0:T(8,128)} %get-tuple-element.24), channel_id=1, source_target_pairs={{0,4},{4,0},{8,12},{12,8},{1,5},{5,1},{9,13},{13,9},{2,6},{6,2},{1... | collective-permute-start | bytes 1597448 | tf_op jit(solution)/shard_map/ppermute | solution.py:515
  50.8 1.7 collective-permute-start.10
  52.5 1.3 collective-permute-start.9
  53.8 0.0 collective-permute-done.13.refs_7_.refs_1_.refs_3_
  53.8 0.5 collective-permute-start.8
  54.3 9.3 %collective-permute-done.12.refs_6_.got_ref.refs_2_.refs_0_ = s32[1040,128]{1,0:T(8,128)} collective-permute-done((s32[1040,128]{1,0:T(8,128)}, s32[1040,128]{1,0:T(8,128)}, u32[]{:S(2)}, u32[]{:S(2)}) %collective-permute-start.12) | collective-permute-done | bytes 532512 | tf_op jit(solution)/shard_map/ppermute | solution.py:515
  63.6 0.0 collective-permute-done.11.refs_3_
  63.6 16.9 %terms.4 = (f32[2,4,96,512]{3,2,1,0:T(8,128)}, s32[1552,128]{1,0:T(8,128)}, s32[776,128]{1,0:T(8,128)}, bf16[1024,4096]{1,0:T(8,128)(2,1)}) custom-call(bf16[2,256,1024]{2,1,0:T(8,128)(2,1)} %refs_0_.5, bf16[2,256,1024]{2,1,0:T(8,128)(2,1)} %collective-permute-done.refs_3_.refs_1_, ...), custom_call_target="tpu_custom_call", output_to_operand_aliasing={{3}: (5, {})} | custom-call | flops 402653184 | bytes 1048576 | tf_op jit(solution)/shard_map/terms/pallas_call | solution.py:228
  80.5 0.0 collective-permute-done.10.refs_2_
  80.5 0.0 collective-permute-done.9.refs_1_
  80.6 0.0 collective-permute-done.8.refs_0_
  80.6 2.3 %cut.7.refs_2_ = bf16[3,2,96,1024]{3,2,1,0:T(8,128)(2,1)} custom-call(bf16[2,256,1024]{2,1,0:T(8,128)(2,1)} %refs_0_.5, bf16[2,96,1024]{2,1,0:T(8,128)(2,1)} %collective-permute-done.8.refs_0_, bf16[2,96,1024]{2,1,0:T(8,128)(2,1)} %collective-permute-done.9.refs_1_, bf16[2,96,1024]{2,1,0:T(8,128)(2,1)} %collective-permute-done.10.refs_2_, ...), custom_call_target="tpu_custom_call" | custom-call | tf_op jit(solution)/shard_map/cut/pallas_call | solution.py:100
  82.9 0.1 collective-permute-start.14
  82.9 1.3 collective-permute-start.17
  84.2 0.7 collective-permute-start.18
  84.9 2.3 %relay.3.refs_6_ = s32[520,128]{1,0:T(8,128)} custom-call(f32[2,4,64,512]{3,2,1,0:T(8,128)} %get-tuple-element.20.refs_3_.own_ref, s32[1040,128]{1,0:T(8,128)} %collective-permute-done.12.refs_6_.got_ref.refs_2_.refs_0_, f32[2,4,96,512]{3,2,1,0:T(8,128)} %get-tuple-element.26.refs_3_.refs_0_.own_ref, s32[520,128]{1,0:T(8,128)} %copy-done), custom_call_target="tpu_custom_call" | custom-call | flops 163840 | bytes 66560 | tf_op jit(solution)/shard_map/relay/pallas_call | solution.py:281
  87.2 0.0 collective-permute-done.14.refs_3_
  87.2 17.0 %terms.5 = (f32[2,4,96,512]{3,2,1,0:T(8,128)}, s32[1552,128]{1,0:T(8,128)}, s32[776,128]{1,0:T(8,128)}, bf16[1024,4096]{1,0:T(8,128)(2,1)}) custom-call(bf16[2,256,1024]{2,1,0:T(8,128)(2,1)} %refs_0_.5, bf16[2,256,1024]{2,1,0:T(8,128)(2,1)} %collective-permute-done.refs_3_.refs_1_, ...), custom_call_target="tpu_custom_call", output_to_operand_aliasing={{3}: (5, {})} | custom-call | flops 402653184 | bytes 1048576 | tf_op jit(solution)/shard_map/terms/pallas_call | solution.py:228
  104.2 1.6 collective-permute-start.15
  105.8 1.4 collective-permute-start.19
  107.2 21.9 %collective-permute-done.19.refs_4_.refs_2_ = s32[520,128]{1,0:T(8,128)S(1)} collective-permute-done((s32[520,128]{1,0:T(8,128)}, s32[520,128]{1,0:T(8,128)S(1)}, u32[]{:S(2)}, u32[]{:S(2)}) %collective-permute-start.19) | collective-permute-done | bytes 266272 | tf_op jit(solution)/shard_map/ppermute | solution.py:499
  129.1 0.0 collective-permute-done.18.refs_1_.refs_6_
  129.1 0.7 copy-done.2
  129.8 0.0 collective-permute-done.17.got_ref.refs_5_.refs_0_
  129.8 0.8 copy-done.1
  130.5 2.6 %relay.4.refs_0_ = s32[776,128]{1,0:T(8,128)} custom-call(f32[2,4,96,512]{3,2,1,0:T(8,128)} %get-tuple-element.26.refs_3_.refs_0_.own_ref, s32[1552,128]{1,0:T(8,128)} %collective-permute-done.17.got_ref.refs_5_.refs_0_, f32[2,4,96,512]{3,2,1,0:T(8,128)} %get-tuple-element.28.refs_0_.own_ref, s32[776,128]{1,0:T(8,128)} %copy-done.1, ...), custom_call_target="tpu_custom_call" | custom-call | flops 245760 | bytes 99328 | tf_op jit(solution)/shard_map/relay/pallas_call | solution.py:281
  133.1 3.3 %collective-permute-start.20 = (s32[776,128]{1,0:T(8,128)}, s32[776,128]{1,0:T(8,128)}, u32[]{:S(2)}, u32[]{:S(2)}) collective-permute-start(s32[776,128]{1,0:T(8,128)} %relay.4.refs_0_), channel_id=1, source_target_pairs={{0,8},{4,12},{8,0},{12,4},{1,9},{5,13},{9,1},{13,5},{2,10},{6,14},... | collective-permute-start | bytes 1191944 | tf_op jit(solution)/shard_map/ppermute | solution.py:499
  136.4 0.7 collective-permute-start.16
  137.1 9.5 %grads.2.refs_0_ = bf16[4,2,512,2048]{3,2,1,0:T(8,128)(2,1)} custom-call(bf16[4,512,1024]{2,1,0:T(8,128)(2,1)} %turn.1.refs_4_.codes_ref, bf16[1024,4096]{1,0:T(8,128)(2,1)} %get-tuple-element.31.err_ref, s32[776,128]{1,0:T(8,128)} %relay.4.refs_0_), custom_call_target="tpu_custom_call" | custom-call | flops 536870912 | bytes 786432 | tf_op jit(solution)/shard_map/grads/pallas_call | solution.py:431
  146.5 8.8 %collective-permute-done.20.refs_7_.refs_2_ = s32[776,128]{1,0:T(8,128)} collective-permute-done((s32[776,128]{1,0:T(8,128)}, s32[776,128]{1,0:T(8,128)}, u32[]{:S(2)}, u32[]{:S(2)}) %collective-permute-start.20) | collective-permute-done | bytes 397344 | tf_op jit(solution)/shard_map/ppermute | solution.py:499
  155.3 0.0 collective-permute-done.16.refs_1_
  155.3 0.0 collective-permute-done.15.got_ref.refs_0_
  155.4 0.8 copy-done.3
  156.1 2.6 %relay.5.refs_1_ = s32[776,128]{1,0:T(8,128)} custom-call(f32[2,4,96,512]{3,2,1,0:T(8,128)} %get-tuple-element.28.refs_0_.own_ref, s32[1552,128]{1,0:T(8,128)} %collective-permute-done.15.got_ref.refs_0_, bf16[4,2,512,2048]{3,2,1,0:T(8,128)(2,1)} %grads.2.refs_0_, s32[776,128]{1,0:T(8,128)} %copy-done.3, ...), custom_call_target="tpu_custom_call" | custom-call | flops 245760 | bytes 99328 | tf_op jit(solution)/shard_map/relay/pallas_call | solution.py:281
  158.7 8.3 %collective-permute-start.21 = (s32[776,128]{1,0:T(8,128)}, s32[776,128]{1,0:T(8,128)S(1)}, u32[]{:S(2)}, u32[]{:S(2)}) collective-permute-start(s32[776,128]{1,0:T(8,128)} %relay.5.refs_1_), channel_id=1, source_target_pairs={{0,8},{4,12},{8,0},{12,4},{1,9},{5,13},{9,1},{13,5},{2,10},{6,14},... | collective-permute-start | bytes 1191944 | tf_op jit(solution)/shard_map/ppermute | solution.py:499
  167.0 10.7 %grads.3.refs_4_ = bf16[4,2,512,2048]{3,2,1,0:T(8,128)(2,1)} custom-call(bf16[4,512,1024]{2,1,0:T(8,128)(2,1)} %turn.1.refs_4_.codes_ref, bf16[1024,4096]{1,0:T(8,128)(2,1)} %get-tuple-element.31.err_ref, bf16[4,2,512,2048]{3,2,1,0:T(8,128)(2,1)} %grads.2.refs_0_, s32[776,128]{1,0:T(8,128)} %relay.5.refs_1_), custom_call_target="tpu_custom_call", output_to_operand_aliasing={{}: (2, {})} | custom-call | flops 536870912 | bytes 786432 | tf_op jit(solution)/shard_map/grads/pallas_call | solution.py:431
  177.7 3.3 %finish.3.refs_4_ = bf16[4,256,512]{2,1,0:T(8,128)(2,1)} custom-call(f32[2,4,64,512]{3,2,1,0:T(8,128)} %get-tuple-element.20.refs_3_.own_ref, s32[1040,128]{1,0:T(8,128)} %collective-permute-done.12.refs_6_.got_ref.refs_2_.refs_0_, s32[520,128]{1,0:T(8,128)} %copy-done, s32[520,128]{1,0:T(8,128)} %copy-done.2, s32[4,256,512]{2,1,0:T(8,128)} %refs_3_.5, ...), custom_call_target="tpu_custom_call" | custom-call | flops 163840 | bytes 131072 | tf_op jit(solution)/shard_map/finish/pallas_call | solution.py:351
  181.0 3.8 %finish.4.refs_4_ = bf16[4,256,512]{2,1,0:T(8,128)(2,1)} custom-call(f32[2,4,96,512]{3,2,1,0:T(8,128)} %get-tuple-element.26.refs_3_.refs_0_.own_ref, s32[1552,128]{1,0:T(8,128)} %collective-permute-done.17.got_ref.refs_5_.refs_0_, s32[776,128]{1,0:T(8,128)} %copy-done.1, ...), custom_call_target="tpu_custom_call", output_to_operand_aliasing={{}: (5, {})} | custom-call | flops 245760 | bytes 196608 | tf_op jit(solution)/shard_map/finish/pallas_call | solution.py:351
  184.8 0.7 copy-done.4
  185.6 3.8 %finish.5 = bf16[4,256,512]{2,1,0:T(8,128)(2,1)} custom-call(f32[2,4,96,512]{3,2,1,0:T(8,128)} %get-tuple-element.28.refs_0_.own_ref, s32[1552,128]{1,0:T(8,128)} %collective-permute-done.15.got_ref.refs_0_, s32[776,128]{1,0:T(8,128)} %copy-done.3, s32[776,128]{1,0:T(8,128)} %copy-done.4, s32[4,256,512]{2,1,0:T(8,128)} %refs_3_.5, ...), custom_call_target="tpu_custom_call", output_to_operand_aliasing={{}: (5, {})} | custom-call | flops 245760 | bytes 196608 | tf_op jit(solution)/shard_map/finish/pallas_call | solution.py:351
  (10 shorter events, 0.0 us)
Async XLA Ops:
  0.6 18.9 %collective-permute-start = (bf16[2,256,1024]{2,1,0:T(8,128)(2,1)}, bf16[2,256,1024]{2,1,0:T(8,128)(2,1)}, u32[]{:S(2)}, u32[]{:S(2)}) collective-permute-start(bf16[2,256,1024]{2,1,0:T(8,128)(2,1)} %refs_0_.5), channel_id=1, source_target_pairs={{0,1},{1,0},{2,3},{3,2},{4,5},{5,4},{6,7},{7,6},{8,9},{9,8},{10,11... | collective-permute-start | bytes 3145736 | tf_op jit(solution)/shard_map/ppermute | solution.py:476
  2.8 10.9 %collective-permute-start.3 = (bf16[2,64,1024]{2,1,0:T(8,128)(2,1)}, bf16[2,64,1024]{2,1,0:T(8,128)(2,1)S(1)}, u32[]{:S(2)}, u32[]{:S(2)}) collective-permute-start(bf16[2,64,1024]{2,1,0:T(8,128)(2,1)} %cut.4), channel_id=1, source_target_pairs={{0,18},{1,19},{2,16},{3,17},{16,2},{17,3},{18,0},{19,1},{4,22},{5,... | collective-permute-start | bytes 786440 | tf_op jit(solution)/shard_map/ppermute | solution.py:458
  6.3 12.9 %collective-permute-start.2 = (bf16[2,64,1024]{2,1,0:T(8,128)(2,1)}, bf16[2,64,1024]{2,1,0:T(8,128)(2,1)}, u32[]{:S(2)}, u32[]{:S(2)}) collective-permute-start(bf16[2,64,1024]{2,1,0:T(8,128)(2,1)} %cut.4), channel_id=1, source_target_pairs={{0,2},{1,3},{2,0},{3,1},{16,18},{17,19},{18,16},{19,17},{4,6},{5,7... | collective-permute-start | bytes 786440 | tf_op jit(solution)/shard_map/ppermute | solution.py:458
  6.8 12.7 %collective-permute-start.1 = (bf16[2,64,1024]{2,1,0:T(8,128)(2,1)}, bf16[2,64,1024]{2,1,0:T(8,128)(2,1)}, u32[]{:S(2)}, u32[]{:S(2)}) collective-permute-start(bf16[2,64,1024]{2,1,0:T(8,128)(2,1)} %cut.4), channel_id=1, source_target_pairs={{0,16},{1,17},{2,18},{3,19},{16,0},{17,1},{18,2},{19,3},{4,20},{5,... | collective-permute-start | bytes 786440 | tf_op jit(solution)/shard_map/ppermute | solution.py:458
  13.8 5.8 %copy-start.6 = (bf16[2,64,1024]{2,1,0:T(8,128)(2,1)}, bf16[2,64,1024]{2,1,0:T(8,128)(2,1)S(1)}, u32[]{:S(2)}) copy-start(bf16[2,64,1024]{2,1,0:T(8,128)(2,1)S(1)} %collective-permute-done.3.refs_2_) | copy-start | bytes 786436
  21.8 3.6 %collective-permute-start.7 = (bf16[3,2,64,1024]{3,2,1,0:T(8,128)(2,1)}, bf16[3,2,64,1024]{3,2,1,0:T(8,128)(2,1)}, u32[]{:S(2)}, u32[]{:S(2)}) collective-permute-start(bf16[3,2,64,1024]{3,2,1,0:T(8,128)(2,1)} %get-tuple-element.19.refs_2_), channel_id=1, source_target_pairs={{0,1},{1,0},{2,3},{3,2},{4,5},{5,4},{6,7},{7,6},{8,9},{9,8},{10,11... | collective-permute-start | bytes 2359304 | tf_op jit(solution)/shard_map/ppermute | solution.py:476
  21.9 17.6 %collective-permute-start.6 = (bf16[2,96,1024]{2,1,0:T(8,128)(2,1)}, bf16[2,96,1024]{2,1,0:T(8,128)(2,1)S(1)}, u32[]{:S(2)}, u32[]{:S(2)}) collective-permute-start(bf16[2,96,1024]{2,1,0:T(8,128)(2,1)} %get-tuple-element.18), channel_id=1, source_target_pairs={{0,18},{1,19},{2,16},{3,17},{16,2},{17,3},{18,0},{19,1},{4,22},{5,... | collective-permute-start | bytes 1179656 | tf_op jit(solution)/shard_map/ppermute | solution.py:458
  23.5 19.6 %collective-permute-start.5 = (bf16[2,96,1024]{2,1,0:T(8,128)(2,1)}, bf16[2,96,1024]{2,1,0:T(8,128)(2,1)}, u32[]{:S(2)}, u32[]{:S(2)}) collective-permute-start(bf16[2,96,1024]{2,1,0:T(8,128)(2,1)} %get-tuple-element.18), channel_id=1, source_target_pairs={{0,2},{1,3},{2,0},{3,1},{16,18},{17,19},{18,16},{19,17},{4,6},{5,7... | collective-permute-start | bytes 1179656 | tf_op jit(solution)/shard_map/ppermute | solution.py:458
  24.9 18.2 %collective-permute-start.4 = (bf16[2,96,1024]{2,1,0:T(8,128)(2,1)}, bf16[2,96,1024]{2,1,0:T(8,128)(2,1)}, u32[]{:S(2)}, u32[]{:S(2)}) collective-permute-start(bf16[2,96,1024]{2,1,0:T(8,128)(2,1)} %get-tuple-element.18), channel_id=1, source_target_pairs={{0,16},{1,17},{2,18},{3,19},{16,0},{17,1},{18,2},{19,3},{4,20},{5,... | collective-permute-start | bytes 1179656 | tf_op jit(solution)/shard_map/ppermute | solution.py:458
  39.5 3.6 %copy-start.5 = (bf16[2,96,1024]{2,1,0:T(8,128)(2,1)}, bf16[2,96,1024]{2,1,0:T(8,128)(2,1)S(1)}, u32[]{:S(2)}) copy-start(bf16[2,96,1024]{2,1,0:T(8,128)(2,1)S(1)} %collective-permute-done.6.refs_2_) | copy-start | bytes 1179652
  45.6 18.0 %collective-permute-start.11 = (bf16[3,2,96,1024]{3,2,1,0:T(8,128)(2,1)}, bf16[3,2,96,1024]{3,2,1,0:T(8,128)(2,1)}, u32[]{:S(2)}, u32[]{:S(2)}) collective-permute-start(bf16[3,2,96,1024]{3,2,1,0:T(8,128)(2,1)} %get-tuple-element.22.refs_2_), channel_id=1, source_target_pairs={{0,1},{1,0},{2,3},{3,2},{4,5},{5,4},{6,7},{7,6},{8,9},{9,8},{10,11... | collective-permute-start | bytes 3538952 | tf_op jit(solution)/shard_map/ppermute | solution.py:476
  45.7 8.1 %collective-permute-start.13 = (s32[520,128]{1,0:T(8,128)}, s32[520,128]{1,0:T(8,128)S(1)}, u32[]{:S(2)}, u32[]{:S(2)}) collective-permute-start(s32[520,128]{1,0:T(8,128)} %get-tuple-element.25), channel_id=1, source_target_pairs={{4,8},{8,4},{5,9},{9,5},{6,10},{10,6},{7,11},{11,7},{20,24},{24,20... | collective-permute-start | bytes 798728 | tf_op jit(solution)/shard_map/ppermute | solution.py:515
  46.4 17.2 %collective-permute-start.12 = (s32[1040,128]{1,0:T(8,128)}, s32[1040,128]{1,0:T(8,128)}, u32[]{:S(2)}, u32[]{:S(2)}) collective-permute-start(s32[1040,128]{1,0:T(8,128)} %get-tuple-element.24), channel_id=1, source_target_pairs={{0,4},{4,0},{8,12},{12,8},{1,5},{5,1},{9,13},{13,9},{2,6},{6,2},{1... | collective-permute-start | bytes 1597448 | tf_op jit(solution)/shard_map/ppermute | solution.py:515
  50.8 29.7 %collective-permute-start.10 = (bf16[2,96,1024]{2,1,0:T(8,128)(2,1)}, bf16[2,96,1024]{2,1,0:T(8,128)(2,1)}, u32[]{:S(2)}, u32[]{:S(2)}) collective-permute-start(bf16[2,96,1024]{2,1,0:T(8,128)(2,1)} %get-tuple-element.21), channel_id=1, source_target_pairs={{0,18},{1,19},{2,16},{3,17},{16,2},{17,3},{18,0},{19,1},{4,22},{5,... | collective-permute-start | bytes 1179656 | tf_op jit(solution)/shard_map/ppermute | solution.py:458
  52.5 28.1 %collective-permute-start.9 = (bf16[2,96,1024]{2,1,0:T(8,128)(2,1)}, bf16[2,96,1024]{2,1,0:T(8,128)(2,1)}, u32[]{:S(2)}, u32[]{:S(2)}) collective-permute-start(bf16[2,96,1024]{2,1,0:T(8,128)(2,1)} %get-tuple-element.21), channel_id=1, source_target_pairs={{0,2},{1,3},{2,0},{3,1},{16,18},{17,19},{18,16},{19,17},{4,6},{5,7... | collective-permute-start | bytes 1179656 | tf_op jit(solution)/shard_map/ppermute | solution.py:458
  53.8 9.8 %copy-start = (s32[520,128]{1,0:T(8,128)}, s32[520,128]{1,0:T(8,128)S(1)}, u32[]{:S(2)}) copy-start(s32[520,128]{1,0:T(8,128)S(1)} %collective-permute-done.13.refs_7_.refs_1_.refs_3_) | copy-start | bytes 798724
  53.8 26.8 %collective-permute-start.8 = (bf16[2,96,1024]{2,1,0:T(8,128)(2,1)}, bf16[2,96,1024]{2,1,0:T(8,128)(2,1)}, u32[]{:S(2)}, u32[]{:S(2)}) collective-permute-start(bf16[2,96,1024]{2,1,0:T(8,128)(2,1)} %get-tuple-element.21), channel_id=1, source_target_pairs={{0,16},{1,17},{2,18},{3,19},{16,0},{17,1},{18,2},{19,3},{4,20},{5,... | collective-permute-start | bytes 1179656 | tf_op jit(solution)/shard_map/ppermute | solution.py:458
  82.9 4.3 %collective-permute-start.14 = (bf16[3,2,96,1024]{3,2,1,0:T(8,128)(2,1)}, bf16[3,2,96,1024]{3,2,1,0:T(8,128)(2,1)}, u32[]{:S(2)}, u32[]{:S(2)}) collective-permute-start(bf16[3,2,96,1024]{3,2,1,0:T(8,128)(2,1)} %cut.7.refs_2_), channel_id=1, source_target_pairs={{0,1},{1,0},{2,3},{3,2},{4,5},{5,4},{6,7},{7,6},{8,9},{9,8},{10,11... | collective-permute-start | bytes 3538952 | tf_op jit(solution)/shard_map/ppermute | solution.py:476
  82.9 46.9 %collective-permute-start.17 = (s32[1552,128]{1,0:T(8,128)}, s32[1552,128]{1,0:T(8,128)}, u32[]{:S(2)}, u32[]{:S(2)}) collective-permute-start(s32[1552,128]{1,0:T(8,128)} %get-tuple-element.32), channel_id=1, source_target_pairs={{0,4},{4,0},{8,12},{12,8},{1,5},{5,1},{9,13},{13,9},{2,6},{6,2},{1... | collective-permute-start | bytes 2383880 | tf_op jit(solution)/shard_map/ppermute | solution.py:515
  84.2 44.9 %collective-permute-start.18 = (s32[776,128]{1,0:T(8,128)}, s32[776,128]{1,0:T(8,128)S(1)}, u32[]{:S(2)}, u32[]{:S(2)}) collective-permute-start(s32[776,128]{1,0:T(8,128)} %get-tuple-element.33), channel_id=1, source_target_pairs={{4,8},{8,4},{5,9},{9,5},{6,10},{10,6},{7,11},{11,7},{20,24},{24,20... | collective-permute-start | bytes 1191944 | tf_op jit(solution)/shard_map/ppermute | solution.py:515
  104.2 51.2 %collective-permute-start.15 = (s32[1552,128]{1,0:T(8,128)}, s32[1552,128]{1,0:T(8,128)}, u32[]{:S(2)}, u32[]{:S(2)}) collective-permute-start(s32[1552,128]{1,0:T(8,128)} %get-tuple-element.29), channel_id=1, source_target_pairs={{0,4},{4,0},{8,12},{12,8},{1,5},{5,1},{9,13},{13,9},{2,6},{6,2},{1... | collective-permute-start | bytes 2383880 | tf_op jit(solution)/shard_map/ppermute | solution.py:515
  105.8 23.3 %collective-permute-start.19 = (s32[520,128]{1,0:T(8,128)}, s32[520,128]{1,0:T(8,128)S(1)}, u32[]{:S(2)}, u32[]{:S(2)}) collective-permute-start(s32[520,128]{1,0:T(8,128)} %relay.3.refs_6_), channel_id=1, source_target_pairs={{0,8},{4,12},{8,0},{12,4},{1,9},{5,13},{9,1},{13,5},{2,10},{6,14},... | collective-permute-start | bytes 798728 | tf_op jit(solution)/shard_map/ppermute | solution.py:499
  129.1 0.7 copy-start.2
  129.8 0.8 copy-start.1
  133.1 22.2 %collective-permute-start.20 = (s32[776,128]{1,0:T(8,128)}, s32[776,128]{1,0:T(8,128)}, u32[]{:S(2)}, u32[]{:S(2)}) collective-permute-start(s32[776,128]{1,0:T(8,128)} %relay.4.refs_0_), channel_id=1, source_target_pairs={{0,8},{4,12},{8,0},{12,4},{1,9},{5,13},{9,1},{13,5},{2,10},{6,14},... | collective-permute-start | bytes 1191944 | tf_op jit(solution)/shard_map/ppermute | solution.py:499
  136.4 18.9 %collective-permute-start.16 = (s32[776,128]{1,0:T(8,128)}, s32[776,128]{1,0:T(8,128)S(1)}, u32[]{:S(2)}, u32[]{:S(2)}) collective-permute-start(s32[776,128]{1,0:T(8,128)} %get-tuple-element.30), channel_id=1, source_target_pairs={{4,8},{8,4},{5,9},{9,5},{6,10},{10,6},{7,11},{11,7},{20,24},{24,20... | collective-permute-start | bytes 1191944 | tf_op jit(solution)/shard_map/ppermute | solution.py:515
  155.3 0.8 copy-start.3
  158.7 26.1 %collective-permute-start.21 = (s32[776,128]{1,0:T(8,128)}, s32[776,128]{1,0:T(8,128)S(1)}, u32[]{:S(2)}, u32[]{:S(2)}) collective-permute-start(s32[776,128]{1,0:T(8,128)} %relay.5.refs_1_), channel_id=1, source_target_pairs={{0,8},{4,12},{8,0},{12,4},{1,9},{5,13},{9,1},{13,5},{2,10},{6,14},... | collective-permute-start | bytes 1191944 | tf_op jit(solution)/shard_map/ppermute | solution.py:499
  184.8 0.8 copy-start.4

commit v4 on v3

--- a/solution.py
+++ b/solution.py
@@ -14,6 +14,7 @@
 FLOOR = 1e-30
 EIGHTHS = (2, 3, 3)
 VMEM = 127 << 19
+EASE = 2
 ANYWHERE = pl.BlockSpec(memory_space=pl.ANY)
 
 
@@ -74,7 +75,7 @@
 
 
 def cost(flops, bytes_accessed):
-    return pl.CostEstimate(flops=flops, bytes_accessed=bytes_accessed, transcendentals=0)
+    return pl.CostEstimate(flops=flops // EASE, bytes_accessed=bytes_accessed // EASE, transcendentals=0)
 
 
 def cut_kernel(n_join, offset, errors_ref, *refs):
@@ -104,6 +105,7 @@
         out_shape=shapes,
         scratch_shapes=[pltpu.SemaphoreType.DMA((len(join) + 1,))],
         compiler_params=pltpu.CompilerParams(vmem_limit_bytes=VMEM),
+        cost_estimate=cost(0, 4 * sum(shape.size for shape in shapes)),
         name="cut",
     )(errors, *join, *after)
 
@@ -112,7 +114,7 @@
     n_pieces = 1 + max(entry[0] for entry in plan)
     pieces = refs[:n_pieces]
     dec_ref = refs[n_pieces]
-    own_ref, both_ref, far_ref, all_ref, err, dec, acc, in_sem, dec_sem, own_sem, out_sem = refs[-11:]
+    own_ref, both_ref, far_ref, all_ref, err, turned, dec, acc, in_sem, dec_sem, own_sem, out_sem = refs[-12:]
     layers, tgt_count, width, columns = dec_ref.shape
     total_rows = err.shape[0]
     rows = total_rows // n_tgt
@@ -163,6 +165,9 @@
     for copy in copies:
         copy.wait()
     out_copy.start()
+    for t in range(tgt_count):
+        part = slice(t * columns, (t + 1) * columns)
+        turned[part, :] = err[:, part].T
 
     lane = lanes_of((rows, LANES))
     small = lanes_of((SUBLANES, LANES))
@@ -179,9 +184,7 @@
             def _():
                 dec[layer, :, t * columns : (t + 1) * columns] = jnp.zeros((width, columns), jnp.bfloat16)
 
-        acc[layer] = lax.dot_general(
-            err[...], dec[layer], (((1,), (1,)), ((), ())), preferred_element_type=jnp.float32
-        )
+        acc[layer] = jnp.dot(dec[layer], turned[...], preferred_element_type=jnp.float32).T
         for copy in own_copies(layer):
             copy.start()
 
@@ -231,6 +234,7 @@
         out_specs=[ANYWHERE, whole, whole, ANYWHERE],
         scratch_shapes=[
             pltpu.VMEM((total_rows, tgt_count * columns), jnp.bfloat16),
+            pltpu.VMEM((tgt_count * columns, total_rows), jnp.bfloat16),
             pltpu.VMEM((layers, width, tgt_count * columns), jnp.bfloat16),
             pltpu.VMEM((layers, total_rows, width), jnp.float32),
             pltpu.SemaphoreType.DMA((len(plan) * tgt_count,)),
@@ -246,7 +250,7 @@
         ],
         input_output_aliases=aliases,
         compiler_params=pltpu.CompilerParams(vmem_limit_bytes=VMEM),
-        cost_estimate=cost(2 * total_rows * decoder.size // EASE, decoder.size * 2 // EASE),
+        cost_estimate=cost(2 * total_rows * decoder.size, decoder.size * 2),
         name="terms",
     )(*operands)
 
@@ -290,7 +294,7 @@
         scratch_shapes=[pltpu.VMEM((layers, rows, width), jnp.float32)],
         out_shape=jax.ShapeDtypeStruct(shape, jnp.int32),
         compiler_params=pltpu.CompilerParams(vmem_limit_bytes=VMEM),
-        cost_estimate=cost(20 * layers * rows * width // EASE, 8 * got.size // EASE),
+        cost_estimate=cost(20 * layers * rows * width, 8 * got.size),
         name="relay",
     )(own, got, *after)
 
@@ -362,7 +366,7 @@
         out_shape=jax.ShapeDtypeStruct(mask.shape, jnp.bfloat16),
         input_output_aliases=aliases,
         compiler_params=pltpu.CompilerParams(vmem_limit_bytes=VMEM),
-        cost_estimate=cost(20 * layers * rows * width // EASE, layers * rows * width * 16 // EASE),
+        cost_estimate=cost(20 * layers * rows * width, layers * rows * width * 16),
         name="finish",
     )(*operands)
 
@@ -390,7 +394,7 @@
         out_specs=pl.BlockSpec((1, width, tokens), lambda i: (i, 0, 0)),
         out_shape=jax.ShapeDtypeStruct((layers, width, tokens), jnp.bfloat16),
         compiler_params=pltpu.CompilerParams(vmem_limit_bytes=VMEM),
-        cost_estimate=cost(codes.size // EASE, codes.size * 4 // EASE),
+        cost_estimate=cost(codes.size, codes.size * 4),
         name="turn",
     )(codes)
 
@@ -437,13 +441,10 @@
         input_output_aliases=aliases,
         compiler_params=pltpu.CompilerParams(vmem_limit_bytes=VMEM),
         cost_estimate=cost(
-            2 * layers * width * columns * tokens // EASE, 2 * layers * width * (columns + tokens) // EASE
+            2 * layers * width * columns * tokens, 2 * layers * width * (columns + tokens)
         ),
         name="grads",
     )(*operands)
-
-
-EASE = 16
 
 
 def gather_pieces(errors, spans, offsets, n_src, n_feat, codes_t):
@@ -494,7 +495,7 @@
     decoder_grads = None
 
     def relay(index, after):
-        ready = after + gots[index][1:] + [got for group in gots[:index] for got in group]
+        ready = after + gots[index][1:]
         sent = relay_call(owns[index], gots[index][0], ready)
         gots[index].append(lax.ppermute(sent, "tgt", across))
         return [sent]
@@ -514,8 +515,11 @@
         owns.append(own)
         gots.append([lax.ppermute(both, "tgt", near), lax.ppermute(far, "tgt", middle)])
         if index < last:
-            pieces, plan = gather.send([own])
-        relayed = relay(index - 1, [own]) if index else gots[0][:2]
+            pieces, plan = gather.send([own] + (gots[index - 1][2:] if index else []))
+        if index > 1:
+            relayed = relay(index - 1, [own])
+        if index == 0 and index < last:
+            relayed = relay(0, pieces[2:3])
     for t in range(tgt_count):
         decoder_grads = grads_call(t, codes_t, everything, decoder_grads, decoder.shape, relayed)
         if t == 0:

time: 191 us -> 176 us (0.921)
  waiting for transfers between devices: 50.9 us -> 31.2 us
  Pallas kernels: 100 us -> 112 us
  starting transfers between devices: 34.3 us -> 26.9 us
    ppermute x3, waiting for transfers between devices: 30.7 us -> 0.01 us  [relay(): gots[index].append(lax.ppermute(sent, 'tgt', across))]
    ppermute x3, waiting for transfers between devices: 9.29 us -> 22.5 us  [body(): lax.ppermute(both, 'tgt', near)]
    pallas_call x3, Pallas kernels: 47.9 us -> 59.7 us  [terms_call(): pl.pallas_call(functools.partial(terms_kernel, n_tgt, plan, offset), in_s...]
    ppermute x3, starting transfers between devices: 7.3 us -> 2.79 us  [body(): lax.ppermute(both, 'tgt', near)]
    ppermute x9, waiting for transfers between devices: 10.8 us -> 7.26 us  [gather_pieces(): lax.ppermute(x, axes, [(i, i ^ flip) for i in range(n_src * n_feat)])]
    ppermute x3, starting transfers between devices: 13 us -> 9.73 us  [relay(): gots[index].append(lax.ppermute(sent, 'tgt', across))]
  transfers between devices with their start and end apart: 22 -> 22, of which waited for: 7 -> 6; matrix products, arithmetic and copies ran while one was open for 0% -> 0% of each run, Pallas kernels for 46% -> 58%
where the time goes in v4:
time: 176 us; the launch traced here: 174 us
  Pallas kernels  112 us (64%)
  waiting for transfers between devices  31.2 us (18%)
  starting transfers between devices  26.9 us (15%)
  local copies, waits for them, and re-layouts  2.93 us (2%)
    pallas_call x3, Pallas kernels, terms_call(): pl.pallas_call(functools.partial(terms_kernel, n_tgt, plan, offset), in_s...  59.7 us
    ppermute x3, waiting for transfers between devices, body(): lax.ppermute(both, 'tgt', near)  22.5 us
    pallas_call x2, Pallas kernels, grads_call(): pl.pallas_call(functools.partial(grads_kernel, (t, tgt_count)), grid=(lay...  20.2 us
    ppermute x9, starting transfers between devices, gather_pieces(): lax.ppermute(x, axes, [(i, i ^ flip) for i in range(n_src * n_feat)])  11.7 us
    pallas_call x3, Pallas kernels, finish_call(): pl.pallas_call(functools.partial(finish_kernel, len(gots), offset, stride...  10.9 us
    ppermute x3, starting transfers between devices, relay(): gots[index].append(lax.ppermute(sent, 'tgt', across))  9.73 us
    pallas_call x4, Pallas kernels, cut_call(): pl.pallas_call(functools.partial(cut_kernel, len(join), offset), in_specs...  8.73 us
    pallas_call x3, Pallas kernels, relay_call(): pl.pallas_call(relay_kernel, grid=(1,), in_specs=[pl.BlockSpec((1, layers...  7.52 us
  transfers between devices with their start and end apart: 22, of which 6 were waited for; matrix products, arithmetic and copies ran while one was open for 0% of the time, Pallas kernels for 58%

profile of v4, /device:TPU:0, one launch (start us, length us, event | category | flops | bytes accessed | tf_op | source)
XLA Modules:
  0.0 174.3 jit_solution(2962881998466055093)
XLA Ops:
  0.6 0.5 collective-permute-start
  1.1 1.7 cut.4
  2.8 3.5 %collective-permute-start.3 = (bf16[2,64,1024]{2,1,0:T(8,128)(2,1)}, bf16[2,64,1024]{2,1,0:T(8,128)(2,1)S(1)}, u32[]{:S(2)}, u32[]{:S(2)}) collective-permute-start(bf16[2,64,1024]{2,1,0:T(8,128)(2,1)} %cut.4), channel_id=1, source_target_pairs={{0,18},{1,19},{2,16},{3,17},{16,2},{17,3},{18,0},{19,1},{4,22},{5,... | collective-permute-start | bytes 786440 | tf_op jit(solution)/shard_map/ppermute | solution.py:459
  6.3 0.5 collective-permute-start.2
  6.8 0.1 collective-permute-start.1
  7.0 5.3 %turn.1.refs_4_.codes_ref = bf16[4,512,1024]{2,1,0:T(8,128)(2,1)} custom-call(bf16[4,1024,512]{2,1,0:T(8,128)(2,1)} %codes_ref.1), custom_call_target="tpu_custom_call" | custom-call | flops 1048576 | bytes 4194304 | tf_op jit(solution)/shard_map/turn/pallas_call | solution.py:390
  12.3 1.5 collective-permute-done.3.refs_2_
  13.8 5.5 %collective-permute-done.2.refs_1_ = bf16[2,64,1024]{2,1,0:T(8,128)(2,1)} collective-permute-done((bf16[2,64,1024]{2,1,0:T(8,128)(2,1)}, bf16[2,64,1024]{2,1,0:T(8,128)(2,1)}, u32[]{:S(2)}, u32[]{:S(2)}) %collective-permute-start.2) | collective-permute-done | bytes 262176 | tf_op jit(solution)/shard_map/ppermute | solution.py:459
  19.2 0.3 collective-permute-done.1.refs_0_
  19.5 0.0 collective-permute-done.refs_3_.refs_1_
  19.5 2.3 %cut.5 = (bf16[3,2,64,1024]{3,2,1,0:T(8,128)(2,1)}, bf16[2,96,1024]{2,1,0:T(8,128)(2,1)}) custom-call(bf16[2,256,1024]{2,1,0:T(8,128)(2,1)} %refs_0_.5, bf16[2,64,1024]{2,1,0:T(8,128)(2,1)} %collective-permute-done.1.refs_0_, bf16[2,64,1024]{2,1,0:T(8,128)(2,1)} %collective-permute-done.2.refs_1_, bf16[2,64,1024]{2,1,0:T(8,128)(2,1)} %copy-done.6, ...), custom_call_target="tpu_custom_call" | custom-call | bytes 1179648 | tf_op jit(solution)/shard_map/cut/pallas_call | solution.py:101
  21.8 0.1 collective-permute-start.7
  21.9 1.6 collective-permute-start.6
  23.5 1.4 collective-permute-start.5
  24.9 0.5 collective-permute-start.4
  25.5 0.0 collective-permute-done.7.refs_3_
  25.5 19.0 %terms.3 = (f32[2,4,64,512]{3,2,1,0:T(8,128)}, s32[1040,128]{1,0:T(8,128)}, s32[520,128]{1,0:T(8,128)}, bf16[1024,4096]{1,0:T(8,128)(2,1)}) custom-call(bf16[2,256,1024]{2,1,0:T(8,128)(2,1)} %refs_0_.5, bf16[2,256,1024]{2,1,0:T(8,128)(2,1)} %collective-permute-done.refs_3_.refs_1_, bf16[3,2,64,1024]{3,2,1,0:T(8,128)(2,1)} %get-tuple-element.19.refs_2_, ...), custom_call_target="tpu_custom_call" | custom-call | flops 2147483648 | bytes 8388608 | tf_op jit(solution)/shard_map/terms/pallas_call | solution.py:231
  44.4 0.0 collective-permute-done.6.refs_2_
  44.5 0.0 copy-start.5
  44.5 0.0 collective-permute-done.5.refs_1_
  44.5 0.0 collective-permute-done.4.refs_0_
  44.5 0.7 copy-done.5
  45.2 2.5 %cut.6 = (bf16[3,2,96,1024]{3,2,1,0:T(8,128)(2,1)}, bf16[2,96,1024]{2,1,0:T(8,128)(2,1)}) custom-call(bf16[2,256,1024]{2,1,0:T(8,128)(2,1)} %refs_0_.5, bf16[2,96,1024]{2,1,0:T(8,128)(2,1)} %collective-permute-done.4.refs_0_, bf16[2,96,1024]{2,1,0:T(8,128)(2,1)} %collective-permute-done.5.refs_1_, bf16[2,96,1024]{2,1,0:T(8,128)(2,1)} %copy-done.5, ...), custom_call_target="tpu_custom_call" | custom-call | bytes 1572864 | tf_op jit(solution)/shard_map/cut/pallas_call | solution.py:101
  47.7 0.1 collective-permute-start.11
  47.8 1.1 collective-permute-start.12
  48.9 0.7 collective-permute-start.13
  49.6 2.7 %collective-permute-start.10 = (bf16[2,96,1024]{2,1,0:T(8,128)(2,1)}, bf16[2,96,1024]{2,1,0:T(8,128)(2,1)}, u32[]{:S(2)}, u32[]{:S(2)}) collective-permute-start(bf16[2,96,1024]{2,1,0:T(8,128)(2,1)} %get-tuple-element.21), channel_id=1, source_target_pairs={{0,18},{1,19},{2,16},{3,17},{16,2},{17,3},{18,0},{19,1},{4,22},{5,... | collective-permute-start | bytes 1179656 | tf_op jit(solution)/shard_map/ppermute | solution.py:459
  52.3 1.3 collective-permute-start.9
  53.6 0.0 collective-permute-done.13.refs_1_
  53.6 0.0 collective-permute-start.8
  53.6 9.1 %collective-permute-done.12.got_ref.refs_0_ = s32[1040,128]{1,0:T(8,128)} collective-permute-done((s32[1040,128]{1,0:T(8,128)}, s32[1040,128]{1,0:T(8,128)}, u32[]{:S(2)}, u32[]{:S(2)}) %collective-permute-start.12) | collective-permute-done | bytes 532512 | tf_op jit(solution)/shard_map/ppermute | solution.py:516
  62.6 2.3 %relay.3.refs_6_ = s32[520,128]{1,0:T(8,128)} custom-call(f32[2,4,64,512]{3,2,1,0:T(8,128)} %get-tuple-element.20.refs_3_.own_ref, s32[1040,128]{1,0:T(8,128)} %collective-permute-done.12.got_ref.refs_0_, bf16[3,2,96,1024]{3,2,1,0:T(8,128)(2,1)} %get-tuple-element.22.refs_0_.refs_2_, s32[520,128]{1,0:T(8,128)} %copy-done.2), custom_call_target="tpu_custom_call" | custom-call | flops 1310720 | bytes 532480 | tf_op jit(solution)/shard_map/relay/pallas_call | solution.py:285
  65.0 1.9 %collective-permute-start.14 = (s32[520,128]{1,0:T(8,128)}, s32[520,128]{1,0:T(8,128)S(1)}, u32[]{:S(2)}, u32[]{:S(2)}) collective-permute-start(s32[520,128]{1,0:T(8,128)} %relay.3.refs_6_), channel_id=1, source_target_pairs={{0,8},{4,12},{8,0},{12,4},{1,9},{5,13},{9,1},{13,5},{2,10},{6,14},... | collective-permute-start | bytes 798728 | tf_op jit(solution)/shard_map/ppermute | solution.py:500
  66.9 0.0 collective-permute-done.11.refs_3_
  66.9 20.3 %terms.4 = (f32[2,4,96,512]{3,2,1,0:T(8,128)}, s32[1552,128]{1,0:T(8,128)}, s32[776,128]{1,0:T(8,128)}, bf16[1024,4096]{1,0:T(8,128)(2,1)}) custom-call(bf16[2,256,1024]{2,1,0:T(8,128)(2,1)} %refs_0_.5, bf16[2,256,1024]{2,1,0:T(8,128)(2,1)} %collective-permute-done.refs_3_.refs_1_, ...), custom_call_target="tpu_custom_call", output_to_operand_aliasing={{3}: (5, {})} | custom-call | flops 3221225472 | bytes 8388608 | tf_op jit(solution)/shard_map/terms/pallas_call | solution.py:231
  87.2 0.0 collective-permute-done.10.refs_2_
  87.2 0.0 collective-permute-done.9.refs_1_
  87.2 0.0 collective-permute-done.8.refs_0_
  87.2 0.0 collective-permute-done.14.refs_4_.refs_2_
  87.2 0.7 copy-done.3
  87.9 2.3 %cut.7.refs_2_ = bf16[3,2,96,1024]{3,2,1,0:T(8,128)(2,1)} custom-call(bf16[2,256,1024]{2,1,0:T(8,128)(2,1)} %refs_0_.5, bf16[2,96,1024]{2,1,0:T(8,128)(2,1)} %collective-permute-done.8.refs_0_, bf16[2,96,1024]{2,1,0:T(8,128)(2,1)} %collective-permute-done.9.refs_1_, bf16[2,96,1024]{2,1,0:T(8,128)(2,1)} %collective-permute-done.10.refs_2_, ...), custom_call_target="tpu_custom_call" | custom-call | bytes 1179648 | tf_op jit(solution)/shard_map/cut/pallas_call | solution.py:101
  90.2 0.1 collective-permute-start.15
  90.3 1.1 collective-permute-start.18
  91.4 0.7 collective-permute-start.19
  92.1 1.4 collective-permute-done.15.refs_3_
  93.5 20.4 %terms.5 = (f32[2,4,96,512]{3,2,1,0:T(8,128)}, s32[1552,128]{1,0:T(8,128)}, s32[776,128]{1,0:T(8,128)}, bf16[1024,4096]{1,0:T(8,128)(2,1)}) custom-call(bf16[2,256,1024]{2,1,0:T(8,128)(2,1)} %refs_0_.5, bf16[2,256,1024]{2,1,0:T(8,128)(2,1)} %collective-permute-done.refs_3_.refs_1_, ...), custom_call_target="tpu_custom_call", output_to_operand_aliasing={{3}: (5, {})} | custom-call | flops 3221225472 | bytes 8388608 | tf_op jit(solution)/shard_map/terms/pallas_call | solution.py:231
  113.9 0.6 collective-permute-start.16
  114.4 0.0 collective-permute-done.19.refs_1_
  114.4 0.0 collective-permute-done.18.got_ref.refs_0_
  114.4 0.8 copy-done
  115.2 2.6 %relay.4.refs_0_ = s32[776,128]{1,0:T(8,128)} custom-call(f32[2,4,96,512]{3,2,1,0:T(8,128)} %get-tuple-element.26.refs_3_.own_ref, s32[1552,128]{1,0:T(8,128)} %collective-permute-done.18.got_ref.refs_0_, f32[2,4,96,512]{3,2,1,0:T(8,128)} %get-tuple-element.28.refs_0_.own_ref, s32[776,128]{1,0:T(8,128)} %copy-done), custom_call_target="tpu_custom_call" | custom-call | flops 1966080 | bytes 794624 | tf_op jit(solution)/shard_map/relay/pallas_call | solution.py:285
  117.8 1.2 collective-permute-start.21
  119.0 0.7 collective-permute-start.17
  119.6 9.5 %grads.2.refs_0_ = bf16[4,2,512,2048]{3,2,1,0:T(8,128)(2,1)} custom-call(bf16[4,512,1024]{2,1,0:T(8,128)(2,1)} %turn.1.refs_4_.codes_ref, bf16[1024,4096]{1,0:T(8,128)(2,1)} %get-tuple-element.31.err_ref, s32[776,128]{1,0:T(8,128)} %relay.4.refs_0_), custom_call_target="tpu_custom_call" | custom-call | flops 4294967296 | bytes 6291456 | tf_op jit(solution)/shard_map/grads/pallas_call | solution.py:435
  129.1 0.0 collective-permute-done.17.refs_1_
  129.1 13.4 %collective-permute-done.16.got_ref.refs_0_ = s32[1552,128]{1,0:T(8,128)} collective-permute-done((s32[1552,128]{1,0:T(8,128)}, s32[1552,128]{1,0:T(8,128)}, u32[]{:S(2)}, u32[]{:S(2)}) %collective-permute-start.16) | collective-permute-done | bytes 794656 | tf_op jit(solution)/shard_map/ppermute | solution.py:516
  142.5 2.6 %relay.5.refs_1_ = s32[776,128]{1,0:T(8,128)} custom-call(f32[2,4,96,512]{3,2,1,0:T(8,128)} %get-tuple-element.28.refs_0_.own_ref, s32[1552,128]{1,0:T(8,128)} %collective-permute-done.16.got_ref.refs_0_, bf16[4,2,512,2048]{3,2,1,0:T(8,128)(2,1)} %grads.2.refs_0_, s32[776,128]{1,0:T(8,128)} %copy-done.1), custom_call_target="tpu_custom_call" | custom-call | flops 1966080 | bytes 794624 | tf_op jit(solution)/shard_map/relay/pallas_call | solution.py:285
  145.1 6.6 %collective-permute-start.20 = (s32[776,128]{1,0:T(8,128)}, s32[776,128]{1,0:T(8,128)S(1)}, u32[]{:S(2)}, u32[]{:S(2)}) collective-permute-start(s32[776,128]{1,0:T(8,128)} %relay.5.refs_1_), channel_id=1, source_target_pairs={{0,8},{4,12},{8,0},{12,4},{1,9},{5,13},{9,1},{13,5},{2,10},{6,14},... | collective-permute-start | bytes 1191944 | tf_op jit(solution)/shard_map/ppermute | solution.py:500
  151.8 10.7 %grads.3.refs_4_ = bf16[4,2,512,2048]{3,2,1,0:T(8,128)(2,1)} custom-call(bf16[4,512,1024]{2,1,0:T(8,128)(2,1)} %turn.1.refs_4_.codes_ref, bf16[1024,4096]{1,0:T(8,128)(2,1)} %get-tuple-element.31.err_ref, bf16[4,2,512,2048]{3,2,1,0:T(8,128)(2,1)} %grads.2.refs_0_, s32[776,128]{1,0:T(8,128)} %relay.5.refs_1_), custom_call_target="tpu_custom_call", output_to_operand_aliasing={{}: (2, {})} | custom-call | flops 4294967296 | bytes 6291456 | tf_op jit(solution)/shard_map/grads/pallas_call | solution.py:435
  162.5 3.3 %finish.3.refs_4_ = bf16[4,256,512]{2,1,0:T(8,128)(2,1)} custom-call(f32[2,4,64,512]{3,2,1,0:T(8,128)} %get-tuple-element.20.refs_3_.own_ref, s32[1040,128]{1,0:T(8,128)} %collective-permute-done.12.got_ref.refs_0_, s32[520,128]{1,0:T(8,128)} %copy-done.2, s32[520,128]{1,0:T(8,128)} %copy-done.3, s32[4,256,512]{2,1,0:T(8,128)} %refs_3_.5, ...), custom_call_target="tpu_custom_call" | custom-call | flops 1310720 | bytes 1048576 | tf_op jit(solution)/shard_map/finish/pallas_call | solution.py:355
  165.8 0.0 collective-permute-done.21.refs_2_
  165.8 3.8 %finish.4.refs_4_ = bf16[4,256,512]{2,1,0:T(8,128)(2,1)} custom-call(f32[2,4,96,512]{3,2,1,0:T(8,128)} %get-tuple-element.26.refs_3_.own_ref, s32[1552,128]{1,0:T(8,128)} %collective-permute-done.18.got_ref.refs_0_, s32[776,128]{1,0:T(8,128)} %copy-done, s32[776,128]{1,0:T(8,128)} %collective-permute-done.21.refs_2_, ...), custom_call_target="tpu_custom_call", output_to_operand_aliasing={{}: (5, {})} | custom-call | flops 1966080 | bytes 1572864 | tf_op jit(solution)/shard_map/finish/pallas_call | solution.py:355
  169.6 0.7 copy-done.4
  170.4 3.8 %finish.5 = bf16[4,256,512]{2,1,0:T(8,128)(2,1)} custom-call(f32[2,4,96,512]{3,2,1,0:T(8,128)} %get-tuple-element.28.refs_0_.own_ref, s32[1552,128]{1,0:T(8,128)} %collective-permute-done.16.got_ref.refs_0_, s32[776,128]{1,0:T(8,128)} %copy-done.1, s32[776,128]{1,0:T(8,128)} %copy-done.4, s32[4,256,512]{2,1,0:T(8,128)} %refs_3_.5, ...), custom_call_target="tpu_custom_call", output_to_operand_aliasing={{}: (5, {})} | custom-call | flops 1966080 | bytes 1572864 | tf_op jit(solution)/shard_map/finish/pallas_call | solution.py:355
  (10 shorter events, 0.0 us)
Async XLA Ops:
  0.6 18.9 %collective-permute-start = (bf16[2,256,1024]{2,1,0:T(8,128)(2,1)}, bf16[2,256,1024]{2,1,0:T(8,128)(2,1)}, u32[]{:S(2)}, u32[]{:S(2)}) collective-permute-start(bf16[2,256,1024]{2,1,0:T(8,128)(2,1)} %refs_0_.5), channel_id=1, source_target_pairs={{0,1},{1,0},{2,3},{3,2},{4,5},{5,4},{6,7},{7,6},{8,9},{9,8},{10,11... | collective-permute-start | bytes 3145736 | tf_op jit(solution)/shard_map/ppermute | solution.py:477
  2.8 10.9 %collective-permute-start.3 = (bf16[2,64,1024]{2,1,0:T(8,128)(2,1)}, bf16[2,64,1024]{2,1,0:T(8,128)(2,1)S(1)}, u32[]{:S(2)}, u32[]{:S(2)}) collective-permute-start(bf16[2,64,1024]{2,1,0:T(8,128)(2,1)} %cut.4), channel_id=1, source_target_pairs={{0,18},{1,19},{2,16},{3,17},{16,2},{17,3},{18,0},{19,1},{4,22},{5,... | collective-permute-start | bytes 786440 | tf_op jit(solution)/shard_map/ppermute | solution.py:459
  6.3 12.9 %collective-permute-start.2 = (bf16[2,64,1024]{2,1,0:T(8,128)(2,1)}, bf16[2,64,1024]{2,1,0:T(8,128)(2,1)}, u32[]{:S(2)}, u32[]{:S(2)}) collective-permute-start(bf16[2,64,1024]{2,1,0:T(8,128)(2,1)} %cut.4), channel_id=1, source_target_pairs={{0,2},{1,3},{2,0},{3,1},{16,18},{17,19},{18,16},{19,17},{4,6},{5,7... | collective-permute-start | bytes 786440 | tf_op jit(solution)/shard_map/ppermute | solution.py:459
  6.8 12.7 %collective-permute-start.1 = (bf16[2,64,1024]{2,1,0:T(8,128)(2,1)}, bf16[2,64,1024]{2,1,0:T(8,128)(2,1)}, u32[]{:S(2)}, u32[]{:S(2)}) collective-permute-start(bf16[2,64,1024]{2,1,0:T(8,128)(2,1)} %cut.4), channel_id=1, source_target_pairs={{0,16},{1,17},{2,18},{3,19},{16,0},{17,1},{18,2},{19,3},{4,20},{5,... | collective-permute-start | bytes 786440 | tf_op jit(solution)/shard_map/ppermute | solution.py:459
  13.8 5.8 %copy-start.6 = (bf16[2,64,1024]{2,1,0:T(8,128)(2,1)}, bf16[2,64,1024]{2,1,0:T(8,128)(2,1)S(1)}, u32[]{:S(2)}) copy-start(bf16[2,64,1024]{2,1,0:T(8,128)(2,1)S(1)} %collective-permute-done.3.refs_2_) | copy-start | bytes 786436
  21.8 3.6 %collective-permute-start.7 = (bf16[3,2,64,1024]{3,2,1,0:T(8,128)(2,1)}, bf16[3,2,64,1024]{3,2,1,0:T(8,128)(2,1)}, u32[]{:S(2)}, u32[]{:S(2)}) collective-permute-start(bf16[3,2,64,1024]{3,2,1,0:T(8,128)(2,1)} %get-tuple-element.19.refs_2_), channel_id=1, source_target_pairs={{0,1},{1,0},{2,3},{3,2},{4,5},{5,4},{6,7},{7,6},{8,9},{9,8},{10,11... | collective-permute-start | bytes 2359304 | tf_op jit(solution)/shard_map/ppermute | solution.py:477
  21.9 22.6 %collective-permute-start.6 = (bf16[2,96,1024]{2,1,0:T(8,128)(2,1)}, bf16[2,96,1024]{2,1,0:T(8,128)(2,1)S(1)}, u32[]{:S(2)}, u32[]{:S(2)}) collective-permute-start(bf16[2,96,1024]{2,1,0:T(8,128)(2,1)} %get-tuple-element.18), channel_id=1, source_target_pairs={{0,18},{1,19},{2,16},{3,17},{16,2},{17,3},{18,0},{19,1},{4,22},{5,... | collective-permute-start | bytes 1179656 | tf_op jit(solution)/shard_map/ppermute | solution.py:459
  23.5 21.0 %collective-permute-start.5 = (bf16[2,96,1024]{2,1,0:T(8,128)(2,1)}, bf16[2,96,1024]{2,1,0:T(8,128)(2,1)}, u32[]{:S(2)}, u32[]{:S(2)}) collective-permute-start(bf16[2,96,1024]{2,1,0:T(8,128)(2,1)} %get-tuple-element.18), channel_id=1, source_target_pairs={{0,2},{1,3},{2,0},{3,1},{16,18},{17,19},{18,16},{19,17},{4,6},{5,7... | collective-permute-start | bytes 1179656 | tf_op jit(solution)/shard_map/ppermute | solution.py:459
  24.9 19.6 %collective-permute-start.4 = (bf16[2,96,1024]{2,1,0:T(8,128)(2,1)}, bf16[2,96,1024]{2,1,0:T(8,128)(2,1)}, u32[]{:S(2)}, u32[]{:S(2)}) collective-permute-start(bf16[2,96,1024]{2,1,0:T(8,128)(2,1)} %get-tuple-element.18), channel_id=1, source_target_pairs={{0,16},{1,17},{2,18},{3,19},{16,0},{17,1},{18,2},{19,3},{4,20},{5,... | collective-permute-start | bytes 1179656 | tf_op jit(solution)/shard_map/ppermute | solution.py:459
  44.5 0.7 copy-start.5
  47.7 19.1 %collective-permute-start.11 = (bf16[3,2,96,1024]{3,2,1,0:T(8,128)(2,1)}, bf16[3,2,96,1024]{3,2,1,0:T(8,128)(2,1)}, u32[]{:S(2)}, u32[]{:S(2)}) collective-permute-start(bf16[3,2,96,1024]{3,2,1,0:T(8,128)(2,1)} %get-tuple-element.22.refs_0_.refs_2_), channel_id=1, source_target_pairs={{0,1},{1,0},{2,3},{3,2},{4,5},{5,4},{6,7},{7,6},{8,9},{9,8},{10,11... | collective-permute-start | bytes 3538952 | tf_op jit(solution)/shard_map/ppermute | solution.py:477
  47.8 14.8 %collective-permute-start.12 = (s32[1040,128]{1,0:T(8,128)}, s32[1040,128]{1,0:T(8,128)}, u32[]{:S(2)}, u32[]{:S(2)}) collective-permute-start(s32[1040,128]{1,0:T(8,128)} %get-tuple-element.24), channel_id=1, source_target_pairs={{0,4},{4,0},{8,12},{12,8},{1,5},{5,1},{9,13},{13,9},{2,6},{6,2},{1... | collective-permute-start | bytes 1597448 | tf_op jit(solution)/shard_map/ppermute | solution.py:516
  48.9 4.6 %collective-permute-start.13 = (s32[520,128]{1,0:T(8,128)}, s32[520,128]{1,0:T(8,128)S(1)}, u32[]{:S(2)}, u32[]{:S(2)}) collective-permute-start(s32[520,128]{1,0:T(8,128)} %get-tuple-element.25), channel_id=1, source_target_pairs={{4,8},{8,4},{5,9},{9,5},{6,10},{10,6},{7,11},{11,7},{20,24},{24,20... | collective-permute-start | bytes 798728 | tf_op jit(solution)/shard_map/ppermute | solution.py:516
  49.6 37.6 %collective-permute-start.10 = (bf16[2,96,1024]{2,1,0:T(8,128)(2,1)}, bf16[2,96,1024]{2,1,0:T(8,128)(2,1)}, u32[]{:S(2)}, u32[]{:S(2)}) collective-permute-start(bf16[2,96,1024]{2,1,0:T(8,128)(2,1)} %get-tuple-element.21), channel_id=1, source_target_pairs={{0,18},{1,19},{2,16},{3,17},{16,2},{17,3},{18,0},{19,1},{4,22},{5,... | collective-permute-start | bytes 1179656 | tf_op jit(solution)/shard_map/ppermute | solution.py:459
  52.3 35.0 %collective-permute-start.9 = (bf16[2,96,1024]{2,1,0:T(8,128)(2,1)}, bf16[2,96,1024]{2,1,0:T(8,128)(2,1)}, u32[]{:S(2)}, u32[]{:S(2)}) collective-permute-start(bf16[2,96,1024]{2,1,0:T(8,128)(2,1)} %get-tuple-element.21), channel_id=1, source_target_pairs={{0,2},{1,3},{2,0},{3,1},{16,18},{17,19},{18,16},{19,17},{4,6},{5,7... | collective-permute-start | bytes 1179656 | tf_op jit(solution)/shard_map/ppermute | solution.py:459
  53.6 9.1 %copy-start.2 = (s32[520,128]{1,0:T(8,128)}, s32[520,128]{1,0:T(8,128)S(1)}, u32[]{:S(2)}) copy-start(s32[520,128]{1,0:T(8,128)S(1)} %collective-permute-done.13.refs_1_) | copy-start | bytes 798724
  53.6 33.7 %collective-permute-start.8 = (bf16[2,96,1024]{2,1,0:T(8,128)(2,1)}, bf16[2,96,1024]{2,1,0:T(8,128)(2,1)}, u32[]{:S(2)}, u32[]{:S(2)}) collective-permute-start(bf16[2,96,1024]{2,1,0:T(8,128)(2,1)} %get-tuple-element.21), channel_id=1, source_target_pairs={{0,16},{1,17},{2,18},{3,19},{16,0},{17,1},{18,2},{19,3},{4,20},{5,... | collective-permute-start | bytes 1179656 | tf_op jit(solution)/shard_map/ppermute | solution.py:459
  65.0 22.3 %collective-permute-start.14 = (s32[520,128]{1,0:T(8,128)}, s32[520,128]{1,0:T(8,128)S(1)}, u32[]{:S(2)}, u32[]{:S(2)}) collective-permute-start(s32[520,128]{1,0:T(8,128)} %relay.3.refs_6_), channel_id=1, source_target_pairs={{0,8},{4,12},{8,0},{12,4},{1,9},{5,13},{9,1},{13,5},{2,10},{6,14},... | collective-permute-start | bytes 798728 | tf_op jit(solution)/shard_map/ppermute | solution.py:500
  87.2 0.7 copy-start.3
  90.2 3.3 %collective-permute-start.15 = (bf16[3,2,96,1024]{3,2,1,0:T(8,128)(2,1)}, bf16[3,2,96,1024]{3,2,1,0:T(8,128)(2,1)}, u32[]{:S(2)}, u32[]{:S(2)}) collective-permute-start(bf16[3,2,96,1024]{3,2,1,0:T(8,128)(2,1)} %cut.7.refs_2_), channel_id=1, source_target_pairs={{0,1},{1,0},{2,3},{3,2},{4,5},{5,4},{6,7},{7,6},{8,9},{9,8},{10,11... | collective-permute-start | bytes 3538952 | tf_op jit(solution)/shard_map/ppermute | solution.py:477
  90.3 24.1 %collective-permute-start.18 = (s32[1552,128]{1,0:T(8,128)}, s32[1552,128]{1,0:T(8,128)}, u32[]{:S(2)}, u32[]{:S(2)}) collective-permute-start(s32[1552,128]{1,0:T(8,128)} %get-tuple-element.32), channel_id=1, source_target_pairs={{0,4},{4,0},{8,12},{12,8},{1,5},{5,1},{9,13},{13,9},{2,6},{6,2},{1... | collective-permute-start | bytes 2383880 | tf_op jit(solution)/shard_map/ppermute | solution.py:516
  91.4 23.0 %collective-permute-start.19 = (s32[776,128]{1,0:T(8,128)}, s32[776,128]{1,0:T(8,128)S(1)}, u32[]{:S(2)}, u32[]{:S(2)}) collective-permute-start(s32[776,128]{1,0:T(8,128)} %get-tuple-element.33), channel_id=1, source_target_pairs={{4,8},{8,4},{5,9},{9,5},{6,10},{10,6},{7,11},{11,7},{20,24},{24,20... | collective-permute-start | bytes 1191944 | tf_op jit(solution)/shard_map/ppermute | solution.py:516
  113.9 28.7 %collective-permute-start.16 = (s32[1552,128]{1,0:T(8,128)}, s32[1552,128]{1,0:T(8,128)}, u32[]{:S(2)}, u32[]{:S(2)}) collective-permute-start(s32[1552,128]{1,0:T(8,128)} %get-tuple-element.29), channel_id=1, source_target_pairs={{0,4},{4,0},{8,12},{12,8},{1,5},{5,1},{9,13},{13,9},{2,6},{6,2},{1... | collective-permute-start | bytes 2383880 | tf_op jit(solution)/shard_map/ppermute | solution.py:516
  114.4 0.8 copy-start
  117.8 48.0 %collective-permute-start.21 = (s32[776,128]{1,0:T(8,128)}, s32[776,128]{1,0:T(8,128)}, u32[]{:S(2)}, u32[]{:S(2)}) collective-permute-start(s32[776,128]{1,0:T(8,128)} %relay.4.refs_0_), channel_id=1, source_target_pairs={{0,8},{4,12},{8,0},{12,4},{1,9},{5,13},{9,1},{13,5},{2,10},{6,14},... | collective-permute-start | bytes 1191944 | tf_op jit(solution)/shard_map/ppermute | solution.py:500
  119.0 10.1 %collective-permute-start.17 = (s32[776,128]{1,0:T(8,128)}, s32[776,128]{1,0:T(8,128)S(1)}, u32[]{:S(2)}, u32[]{:S(2)}) collective-permute-start(s32[776,128]{1,0:T(8,128)} %get-tuple-element.30), channel_id=1, source_target_pairs={{4,8},{8,4},{5,9},{9,5},{6,10},{10,6},{7,11},{11,7},{20,24},{24,20... | collective-permute-start | bytes 1191944 | tf_op jit(solution)/shard_map/ppermute | solution.py:516
  129.1 13.4 %copy-start.1 = (s32[776,128]{1,0:T(8,128)}, s32[776,128]{1,0:T(8,128)S(1)}, u32[]{:S(2)}) copy-start(s32[776,128]{1,0:T(8,128)S(1)} %collective-permute-done.17.refs_1_) | copy-start | bytes 1191940
  145.1 24.5 %collective-permute-start.20 = (s32[776,128]{1,0:T(8,128)}, s32[776,128]{1,0:T(8,128)S(1)}, u32[]{:S(2)}, u32[]{:S(2)}) collective-permute-start(s32[776,128]{1,0:T(8,128)} %relay.5.refs_1_), channel_id=1, source_target_pairs={{0,8},{4,12},{8,0},{12,4},{1,9},{5,13},{9,1},{13,5},{2,10},{6,14},... | collective-permute-start | bytes 1191944 | tf_op jit(solution)/shard_map/ppermute | solution.py:500
  169.6 0.8 copy-start.4

commit v5 on v4

--- a/solution.py
+++ b/solution.py
@@ -36,12 +36,12 @@
     return jnp.max(jnp.abs(v), axis=1, keepdims=True)
 
 
-def store_words(out_ref, layer, v, gain, base=0):
+def store_words(out_ref, layer, v, gain):
     rows, width = v.shape
     half, tiles = rows // 2, width // LANES
     words = pair(jnp.floor(v * gain + 0.5).astype(jnp.int32))
     for tile in range(tiles):
-        start = base + (layer * tiles + tile) * half
+        start = (layer * tiles + tile) * half
         out_ref[start : start + half, :] = words[:, tile * LANES : (tile + 1) * LANES]
 
 
@@ -114,7 +114,7 @@
     n_pieces = 1 + max(entry[0] for entry in plan)
     pieces = refs[:n_pieces]
     dec_ref = refs[n_pieces]
-    own_ref, both_ref, far_ref, all_ref, err, turned, dec, acc, in_sem, dec_sem, own_sem, out_sem = refs[-12:]
+    own_ref, near_ref, across_ref, far_ref, all_ref, err, dec, acc, in_sem, dec_sem, own_sem, out_sem = refs[-12:]
     layers, tgt_count, width, columns = dec_ref.shape
     total_rows = err.shape[0]
     rows = total_rows // n_tgt
@@ -144,13 +144,8 @@
     def block(dest):
         return pl.ds(pl.multiple_of(dest * rows, rows), rows)
 
-    def own_copies(layer):
-        return [
-            pltpu.make_async_copy(
-                acc.at[layer, block(tgt ^ flip), :], own_ref.at[index, layer], own_sem.at[layer * 2 + index]
-            )
-            for index, flip in enumerate((0, 2))
-        ]
+    def own_copy(layer):
+        return pltpu.make_async_copy(acc.at[layer, block(tgt), :], own_ref.at[layer], own_sem.at[layer])
 
     out_copy = pltpu.make_async_copy(err, all_ref.at[pl.ds(offset, total_rows), :], out_sem)
 
@@ -165,14 +160,10 @@
     for copy in copies:
         copy.wait()
     out_copy.start()
-    for t in range(tgt_count):
-        part = slice(t * columns, (t + 1) * columns)
-        turned[part, :] = err[:, part].T
 
     lane = lanes_of((rows, LANES))
     small = lanes_of((SUBLANES, LANES))
-    length = far_ref.shape[0]
-    flips = (1, 3)
+    flips = {1: near_ref, 2: across_ref, 3: far_ref}
     tails = [jnp.zeros((SUBLANES, LANES), jnp.int32) for _ in flips]
 
     def multiply(layer):
@@ -184,9 +175,10 @@
             def _():
                 dec[layer, :, t * columns : (t + 1) * columns] = jnp.zeros((width, columns), jnp.bfloat16)
 
-        acc[layer] = jnp.dot(dec[layer], turned[...], preferred_element_type=jnp.float32).T
-        for copy in own_copies(layer):
-            copy.start()
+        acc[layer] = lax.dot_general(
+            err[...], dec[layer], (((1,), (1,)), ((), ())), preferred_element_type=jnp.float32
+        )
+        own_copy(layer).start()
 
     def encode(layer):
         peaks = jnp.zeros((rows, LANES), jnp.float32)
@@ -196,9 +188,7 @@
         scale_words = pair(scale)
         for index, flip in enumerate(flips):
             v, factor = acc[layer, block(tgt ^ flip), :], gain[:, index : index + 1]
-            store_words(both_ref, layer, v, factor, index * length)
-            if index:
-                store_words(far_ref, layer, v, factor)
+            store_words(flips[flip], layer, v, factor)
             for group in range(half // SUBLANES):
                 piece = scale_words[group * SUBLANES : (group + 1) * SUBLANES, index : index + 1]
                 tails[index] = jnp.where(small == group * layers + layer, piece, tails[index])
@@ -208,12 +198,10 @@
         if layer:
             encode(layer - 1)
     encode(layers - 1)
-    for index, tail in enumerate(tails):
-        both_ref[(index + 1) * length - SUBLANES : (index + 1) * length, :] = tail
-    far_ref[length - SUBLANES :, :] = tails[1]
+    for send, tail in zip(flips.values(), tails):
+        send[send.shape[0] - SUBLANES :, :] = tail
     for layer in range(layers):
-        for copy in own_copies(layer):
-            copy.wait()
+        own_copy(layer).wait()
     out_copy.wait()
 
 
@@ -225,26 +213,26 @@
     operands = [*pieces, decoder]
     aliases = {}
     if everything is not None:
-        aliases = {len(operands): 3}
+        aliases = {len(operands): 4}
         operands.append(everything)
     operands += after
     return pl.pallas_call(
         functools.partial(terms_kernel, n_tgt, plan, offset),
         in_specs=[ANYWHERE] * len(operands),
-        out_specs=[ANYWHERE, whole, whole, ANYWHERE],
+        out_specs=[ANYWHERE, whole, whole, whole, ANYWHERE],
         scratch_shapes=[
             pltpu.VMEM((total_rows, tgt_count * columns), jnp.bfloat16),
-            pltpu.VMEM((tgt_count * columns, total_rows), jnp.bfloat16),
             pltpu.VMEM((layers, width, tgt_count * columns), jnp.bfloat16),
             pltpu.VMEM((layers, total_rows, width), jnp.float32),
             pltpu.SemaphoreType.DMA((len(plan) * tgt_count,)),
             pltpu.SemaphoreType.DMA((layers * tgt_count,)),
-            pltpu.SemaphoreType.DMA((layers * 2,)),
+            pltpu.SemaphoreType.DMA((layers,)),
             pltpu.SemaphoreType.DMA,
         ],
         out_shape=[
-            jax.ShapeDtypeStruct((2, layers, rows, width), jnp.float32),
-            jax.ShapeDtypeStruct((2 * payload[0], LANES), jnp.int32),
+            jax.ShapeDtypeStruct((layers, rows, width), jnp.float32),
+            jax.ShapeDtypeStruct(payload, jnp.int32),
+            jax.ShapeDtypeStruct(payload, jnp.int32),
             jax.ShapeDtypeStruct(payload, jnp.int32),
             jax.ShapeDtypeStruct((tokens, tgt_count * columns), jnp.bfloat16),
         ],
@@ -255,50 +243,6 @@
     )(*operands)
 
 
-def relay_kernel(own_ref, got_ref, *refs):
-    send_ref, total = refs[-2:]
-    layers, rows, width = total.shape
-    half = rows // 2
-    tgt = lax.axis_index("tgt")
-    inner = jnp.logical_or(tgt == 1, tgt == 2).astype(jnp.float32)
-    steps = [step * inner for step in load_steps(got_ref)]
-    lane = lanes_of((rows, LANES))
-    peaks = jnp.zeros((rows, LANES), jnp.float32)
-    for layer in range(layers):
-        v = own_ref[0, layer] + load_values(got_ref, steps, layer, layers, rows, width)
-        total[layer] = v
-        peaks = jnp.where(lane % layers == layer, row_peak(v), peaks)
-    scale, gain = scale_and_gain(peaks)
-    for layer in range(layers):
-        store_words(send_ref, layer, total[layer], gain[:, layer : layer + 1])
-    scale_words = pair(scale)
-    small = lanes_of((SUBLANES, LANES)) // layers
-    tail = jnp.zeros((SUBLANES, LANES), jnp.int32)
-    for group in range(half // SUBLANES):
-        tail = jnp.where(small == group, scale_words[group * SUBLANES : (group + 1) * SUBLANES], tail)
-    send_ref[send_ref.shape[0] - SUBLANES :, :] = tail
-
-
-def relay_call(own, got, after):
-    _, layers, rows, width = own.shape
-    shape = (got.shape[0] // 2, LANES)
-    return pl.pallas_call(
-        relay_kernel,
-        grid=(1,),
-        in_specs=[
-            pl.BlockSpec((1, layers, rows, width), lambda i: (1, 0, 0, 0)),
-            pl.BlockSpec(shape, lambda i: (1, 0)),
-        ]
-        + [ANYWHERE] * len(after),
-        out_specs=pl.BlockSpec(shape, lambda i: (0, 0)),
-        scratch_shapes=[pltpu.VMEM((layers, rows, width), jnp.float32)],
-        out_shape=jax.ShapeDtypeStruct(shape, jnp.int32),
-        compiler_params=pltpu.CompilerParams(vmem_limit_bytes=VMEM),
-        cost_estimate=cost(20 * layers * rows * width, 8 * got.size),
-        name="relay",
-    )(own, got, *after)
-
-
 def finish_kernel(n_got, offset, stride, own_ref, *refs):
     gots = refs[:n_got]
     mask_ref = refs[n_got]
@@ -327,7 +271,7 @@
     for part in range(parts):
         mask_copy(part).wait()
     for layer in range(layers):
-        total = own_ref[0, layer]
+        total = own_ref[layer]
         for got, step in zip(gots, steps):
             total += load_values(got, step, layer, layers, rows, width)
         out_tile[layer] = (total * mask_tile[layer].astype(jnp.float32)).astype(jnp.bfloat16)
@@ -339,9 +283,9 @@
 
 
 def finish_call(own, gots, mask, out, offset, stride, after):
-    _, layers, rows, width = own.shape
+    layers, rows, width = own.shape
     parts = mask.shape[1] // stride
-    in_specs = [pl.BlockSpec((1, layers, rows, width), lambda i: (0, 0, 0, 0))]
+    in_specs = [pl.BlockSpec((layers, rows, width), lambda i: (0, 0, 0))]
     in_specs += [pl.BlockSpec(gots[-1].shape, lambda i: (0, 0)) for got in gots]
     in_specs.append(ANYWHERE)
     operands = [own, *gots, mask]
@@ -399,11 +343,12 @@
     )(codes)
 
 
-def grads_kernel(t, codes_ref, err_ref, *refs):
+def grads_kernel(codes_ref, err_ref, *refs):
     out_ref = refs[-1]
-    tgt_count, columns = 1, out_ref.shape[3]
-    layer = lax.axis_index("src") * pl.num_programs(0) + pl.program_id(0)
-    kept = lax.axis_index("tgt") * t[1] + t[0] >= layer
+    t, layer = pl.program_id(0), pl.program_id(1)
+    columns = out_ref.shape[3]
+    first_t, first_layer = (lax.axis_index(axis) * pl.num_programs(i) for i, axis in enumerate(("tgt", "src")))
+    kept = first_t + t >= first_layer + layer
     step = min(columns, 512)
 
     @pl.when(kept)
@@ -418,33 +363,25 @@
         out_ref[...] = jnp.zeros_like(out_ref)
 
 
-def grads_call(t, codes_t, everything, out, shape, after):
+def grads_call(codes_t, everything, shape, after):
     layers, tgt_count, width, columns = shape
     tokens = codes_t.shape[2]
     in_specs = [
-        pl.BlockSpec((1, width, tokens), lambda i: (i, 0, 0)),
-        pl.BlockSpec((tokens, columns), lambda i: (0, t)),
+        pl.BlockSpec((1, width, tokens), lambda t, i: (i, 0, 0)),
+        pl.BlockSpec((tokens, columns), lambda t, i: (0, t)),
     ]
-    operands = [codes_t, everything]
-    aliases = {}
-    if out is not None:
-        aliases = {len(operands): 0}
-        operands.append(out)
-    operands += after
-    in_specs += [ANYWHERE] * (len(operands) - 2)
     return pl.pallas_call(
-        functools.partial(grads_kernel, (t, tgt_count)),
-        grid=(layers,),
-        in_specs=in_specs,
-        out_specs=pl.BlockSpec((1, 1, width, columns), lambda i: (i, t, 0, 0)),
+        grads_kernel,
+        grid=(tgt_count, layers),
+        in_specs=in_specs + [ANYWHERE] * len(after),
+        out_specs=pl.BlockSpec((1, 1, width, columns), lambda t, i: (i, t, 0, 0)),
         out_shape=jax.ShapeDtypeStruct(shape, jnp.bfloat16),
-        input_output_aliases=aliases,
         compiler_params=pltpu.CompilerParams(vmem_limit_bytes=VMEM),
         cost_estimate=cost(
-            2 * layers * width * columns * tokens, 2 * layers * width * (columns + tokens)
+            2 * tgt_count * layers * width * columns * tokens, 2 * tgt_count * layers * width * (columns + tokens)
         ),
         name="grads",
-    )(*operands)
+    )(codes_t, everything, *after)
 
 
 def gather_pieces(errors, spans, offsets, n_src, n_feat, codes_t):
@@ -482,26 +419,14 @@
     stride = errors.shape[1]
     spans = [stride * part // 8 for part in EIGHTHS]
     offsets = [sum(spans[:index]) for index in range(len(spans))]
-    near = [(i, i ^ 1) for i in range(n_tgt)]
-    middle = [(1, 2), (2, 1)]
-    across = [(i, i ^ 2) for i in range(n_tgt)]
     codes_t = turn_call(saved_codes, spans)
     gather = gather_pieces(errors, spans, offsets, n_src, n_feat, codes_t)
     pieces, plan = next(gather)
-
     last = len(spans) - 1
     owns, gots = [], []
-    everything, relayed = None, []
-    decoder_grads = None
-
-    def relay(index, after):
-        ready = after + gots[index][1:]
-        sent = relay_call(owns[index], gots[index][0], ready)
-        gots[index].append(lax.ppermute(sent, "tgt", across))
-        return [sent]
-
+    everything = None
     for index, span in enumerate(spans):
-        own, both, far, everything = terms_call(
+        own, near, across, far, everything = terms_call(
             pieces,
             plan,
             decoder,
@@ -510,25 +435,18 @@
             n_tgt,
             n_feat * span,
             n_feat * stride,
-            relayed,
+            [],
         )
         owns.append(own)
-        gots.append([lax.ppermute(both, "tgt", near), lax.ppermute(far, "tgt", middle)])
+        send = lambda x, flip: lax.ppermute(x, "tgt", [(i, i ^ flip) for i in range(n_tgt)])
+        gots.append([send(far, 3), send(across, 2), send(near, 1)])
         if index < last:
-            pieces, plan = gather.send([own] + (gots[index - 1][2:] if index else []))
-        if index > 1:
-            relayed = relay(index - 1, [own])
-        if index == 0 and index < last:
-            relayed = relay(0, pieces[2:3])
-    for t in range(tgt_count):
-        decoder_grads = grads_call(t, codes_t, everything, decoder_grads, decoder.shape, relayed)
-        if t == 0:
-            relayed = relay(last, [decoder_grads])
+            pieces, plan = gather.send([own] + (gots[index - 1] if index else []))
+    decoder_grads = grads_call(codes_t, everything, decoder.shape, gots[-2] if last else [])
     code_grads = None
     for index in range(len(spans)):
-        code_grads = finish_call(
-            owns[index], gots[index], active_mask, code_grads, offsets[index], stride, [] if index else [decoder_grads]
-        )
+        after = [decoder_grads, *gots[last]] if index == 0 else []
+        code_grads = finish_call(owns[index], gots[index], active_mask, code_grads, offsets[index], stride, after)
     return code_grads, decoder_grads
 
 

time: 176 us -> 172 us (0.977)
  Pallas kernels: 112 us -> 92.2 us
  starting transfers between devices: 26.9 us -> 35.9 us
  waiting for transfers between devices: 31.2 us -> 39.7 us
  local copies, waits for them, and re-layouts: 2.93 us -> 0.73 us
    pallas_call x3, Pallas kernels: 59.7 us -> 47.9 us  [terms_call(): pl.pallas_call(functools.partial(terms_kernel, n_tgt, plan, offset), in_s...]
    ppermute x9, starting transfers between devices: 14.5 us -> 23.9 us  [body(): lax.ppermute(x, 'tgt', [(i, i ^ flip) for i in range(n_tgt)])]
    pallas_call x5 -> x1, Pallas kernels: 27.7 us -> 19.4 us  [grads_call(): pl.pallas_call(grads_kernel, grid=(tgt_count, layers), in_specs=in_specs...]
    ppermute x9, waiting for transfers between devices: 22.5 us -> 28.9 us  [body(): lax.ppermute(x, 'tgt', [(i, i ^ flip) for i in range(n_tgt)])]
    ppermute x9, waiting for transfers between devices: 7.26 us -> 10.8 us  [gather_pieces(): lax.ppermute(x, axes, [(i, i ^ flip) for i in range(n_src * n_feat)])]
    unnamed x14 -> x8, local copies, waits for them, and re-layouts: 2.93 us -> 0.73 us
  transfers between devices with their start and end apart: 22 -> 22, of which waited for: 6 -> 6; matrix products, arithmetic and copies ran while one was open for 0% -> 0% of each run, Pallas kernels for 58% -> 44%
where the time goes in v5:
time: 172 us; the launch traced here: 170 us
  Pallas kernels  92.2 us (54%)
  waiting for transfers between devices  39.7 us (23%)
  starting transfers between devices  35.9 us (21%)
    pallas_call x3, Pallas kernels, terms_call(): pl.pallas_call(functools.partial(terms_kernel, n_tgt, plan, offset), in_s...  47.9 us
    ppermute x9, waiting for transfers between devices, body(): lax.ppermute(x, 'tgt', [(i, i ^ flip) for i in range(n_tgt)])  28.9 us
    ppermute x9, starting transfers between devices, body(): lax.ppermute(x, 'tgt', [(i, i ^ flip) for i in range(n_tgt)])  23.9 us
    pallas_call x1, Pallas kernels, grads_call(): pl.pallas_call(grads_kernel, grid=(tgt_count, layers), in_specs=in_specs...  19.4 us
    ppermute x9, starting transfers between devices, gather_pieces(): lax.ppermute(x, axes, [(i, i ^ flip) for i in range(n_src * n_feat)])  11.2 us
    pallas_call x3, Pallas kernels, finish_call(): pl.pallas_call(functools.partial(finish_kernel, len(gots), offset, stride...  10.9 us
    ppermute x9, waiting for transfers between devices, gather_pieces(): lax.ppermute(x, axes, [(i, i ^ flip) for i in range(n_src * n_feat)])  10.8 us
    pallas_call x4, Pallas kernels, cut_call(): pl.pallas_call(functools.partial(cut_kernel, len(join), offset), in_specs...  8.75 us
  transfers between devices with their start and end apart: 22, of which 6 were waited for; matrix products, arithmetic and copies ran while one was open for 0% of the time, Pallas kernels for 44%

profile of v5, /device:TPU:0, one launch (start us, length us, event | category | flops | bytes accessed | tf_op | source)
XLA Modules:
  0.0 169.5 jit_solution(7368967358175909291)
XLA Ops:
  0.6 0.5 collective-permute-start
  1.1 1.7 cut.4
  2.8 3.5 %collective-permute-start.3 = (bf16[2,64,1024]{2,1,0:T(8,128)(2,1)}, bf16[2,64,1024]{2,1,0:T(8,128)(2,1)S(1)}, u32[]{:S(2)}, u32[]{:S(2)}) collective-permute-start(bf16[2,64,1024]{2,1,0:T(8,128)(2,1)} %cut.4), channel_id=1, source_target_pairs={{0,18},{1,19},{2,16},{3,17},{16,2},{17,3},{18,0},{19,1},{4,22},{5,... | collective-permute-start | bytes 786440 | tf_op jit(solution)/shard_map/ppermute | solution.py:396
  6.3 0.5 collective-permute-start.2
  6.8 0.1 collective-permute-start.1
  7.0 5.3 %turn.1.refs_4_.codes_ref = bf16[4,512,1024]{2,1,0:T(8,128)(2,1)} custom-call(bf16[4,1024,512]{2,1,0:T(8,128)(2,1)} %codes_ref.1), custom_call_target="tpu_custom_call" | custom-call | flops 1048576 | bytes 4194304 | tf_op jit(solution)/shard_map/turn/pallas_call | solution.py:334
  12.3 1.5 collective-permute-done.3.refs_2_
  13.8 0.0 copy-start.3
  13.8 5.5 %collective-permute-done.2.refs_1_ = bf16[2,64,1024]{2,1,0:T(8,128)(2,1)} collective-permute-done((bf16[2,64,1024]{2,1,0:T(8,128)(2,1)}, bf16[2,64,1024]{2,1,0:T(8,128)(2,1)}, u32[]{:S(2)}, u32[]{:S(2)}) %collective-permute-start.2) | collective-permute-done | bytes 262176 | tf_op jit(solution)/shard_map/ppermute | solution.py:396
  19.2 0.3 collective-permute-done.1.refs_0_
  19.5 0.0 collective-permute-done.refs_3_.refs_1_
  19.5 0.0 copy-done.3
  19.5 2.3 %cut.5 = (bf16[3,2,64,1024]{3,2,1,0:T(8,128)(2,1)}, bf16[2,96,1024]{2,1,0:T(8,128)(2,1)}) custom-call(bf16[2,256,1024]{2,1,0:T(8,128)(2,1)} %refs_0_.5, bf16[2,64,1024]{2,1,0:T(8,128)(2,1)} %collective-permute-done.1.refs_0_, bf16[2,64,1024]{2,1,0:T(8,128)(2,1)} %collective-permute-done.2.refs_1_, bf16[2,64,1024]{2,1,0:T(8,128)(2,1)} %copy-done.3, ...), custom_call_target="tpu_custom_call" | custom-call | bytes 1179648 | tf_op jit(solution)/shard_map/cut/pallas_call | solution.py:101
  21.8 0.1 collective-permute-start.7
  21.9 1.6 collective-permute-start.6
  23.5 1.4 collective-permute-start.5
  24.9 0.5 collective-permute-start.4
  25.5 0.0 collective-permute-done.7.refs_3_
  25.5 14.0 %terms.3 = (f32[4,64,512]{2,1,0:T(8,128)}, s32[520,128]{1,0:T(8,128)}, s32[520,128]{1,0:T(8,128)}, s32[520,128]{1,0:T(8,128)}, bf16[1024,4096]{1,0:T(8,128)(2,1)}) custom-call(bf16[2,256,1024]{2,1,0:T(8,128)(2,1)} %refs_0_.5, bf16[2,256,1024]{2,1,0:T(8,128)(2,1)} %collective-permute-done.refs_3_.refs_1_, bf16[3,2,64,1024]{3,2,1,0:T(8,128)(2,1)} %get-tuple-element.22.refs_2_, ...), custom_call_target="tpu_custom_call" | custom-call | flops 2147483648 | bytes 8388608 | tf_op jit(solution)/shard_map/terms/pallas_call | solution.py:219
  39.4 0.0 collective-permute-done.6.refs_2_
  39.5 0.0 copy-start.2
  39.5 3.6 %collective-permute-done.5.refs_1_ = bf16[2,96,1024]{2,1,0:T(8,128)(2,1)} collective-permute-done((bf16[2,96,1024]{2,1,0:T(8,128)(2,1)}, bf16[2,96,1024]{2,1,0:T(8,128)(2,1)}, u32[]{:S(2)}, u32[]{:S(2)}) %collective-permute-start.5) | collective-permute-done | bytes 393248 | tf_op jit(solution)/shard_map/ppermute | solution.py:396
  43.1 0.0 collective-permute-done.4.refs_0_
  43.1 0.0 copy-done.2
  43.1 2.5 %cut.6 = (bf16[3,2,96,1024]{3,2,1,0:T(8,128)(2,1)}, bf16[2,96,1024]{2,1,0:T(8,128)(2,1)}) custom-call(bf16[2,256,1024]{2,1,0:T(8,128)(2,1)} %refs_0_.5, bf16[2,96,1024]{2,1,0:T(8,128)(2,1)} %collective-permute-done.4.refs_0_, bf16[2,96,1024]{2,1,0:T(8,128)(2,1)} %collective-permute-done.5.refs_1_, bf16[2,96,1024]{2,1,0:T(8,128)(2,1)} %copy-done.2, ...), custom_call_target="tpu_custom_call" | custom-call | bytes 1572864 | tf_op jit(solution)/shard_map/cut/pallas_call | solution.py:101
  45.6 0.1 collective-permute-start.11
  45.7 3.6 %collective-permute-start.12 = (s32[520,128]{1,0:T(8,128)}, s32[520,128]{1,0:T(8,128)S(1)}, u32[]{:S(2)}, u32[]{:S(2)}) collective-permute-start(s32[520,128]{1,0:T(8,128)} %get-tuple-element.28), channel_id=1, source_target_pairs={{0,12},{4,8},{8,4},{12,0},{1,13},{5,9},{9,5},{13,1},{2,14},{6,10},... | collective-permute-start | bytes 798728 | tf_op jit(solution)/shard_map/ppermute | solution.py:441
  49.4 1.6 collective-permute-start.10
  51.0 1.3 collective-permute-start.9
  52.3 0.5 collective-permute-start.8
  52.9 3.8 %collective-permute-done.12.refs_4_.refs_0_ = s32[520,128]{1,0:T(8,128)S(1)} collective-permute-done((s32[520,128]{1,0:T(8,128)}, s32[520,128]{1,0:T(8,128)S(1)}, u32[]{:S(2)}, u32[]{:S(2)}) %collective-permute-start.12) | collective-permute-done | bytes 266272 | tf_op jit(solution)/shard_map/ppermute | solution.py:441
  56.7 0.0 copy-start.1
  56.7 6.3 %collective-permute-start.13 = (s32[520,128]{1,0:T(8,128)}, s32[520,128]{1,0:T(8,128)}, u32[]{:S(2)}, u32[]{:S(2)}) collective-permute-start(s32[520,128]{1,0:T(8,128)} %get-tuple-element.29), channel_id=1, source_target_pairs={{0,8},{4,12},{8,0},{12,4},{1,9},{5,13},{9,1},{13,5},{2,10},{6,14},... | collective-permute-start | bytes 798728 | tf_op jit(solution)/shard_map/ppermute | solution.py:441
  63.0 0.0 collective-permute-done.11.refs_3_
  63.0 0.0 collective-permute-start.14
  63.0 16.9 %terms.4 = (f32[4,96,512]{2,1,0:T(8,128)}, s32[776,128]{1,0:T(8,128)}, s32[776,128]{1,0:T(8,128)}, s32[776,128]{1,0:T(8,128)}, bf16[1024,4096]{1,0:T(8,128)(2,1)}) custom-call(bf16[2,256,1024]{2,1,0:T(8,128)(2,1)} %refs_0_.5, bf16[2,256,1024]{2,1,0:T(8,128)(2,1)} %collective-permute-done.refs_3_.refs_1_, ...), custom_call_target="tpu_custom_call", output_to_operand_aliasing={{4}: (5, {})} | custom-call | flops 3221225472 | bytes 8388608 | tf_op jit(solution)/shard_map/terms/pallas_call | solution.py:219
  79.9 0.0 copy-done.1
  79.9 0.0 collective-permute-done.13.refs_5_.refs_1_
  80.0 0.0 collective-permute-done.14.refs_6_.refs_2_
  80.0 0.0 collective-permute-done.10.refs_2_
  80.0 0.0 collective-permute-done.9.refs_1_
  80.0 0.0 collective-permute-done.8.refs_0_
  80.0 2.3 %cut.7.refs_2_ = bf16[3,2,96,1024]{3,2,1,0:T(8,128)(2,1)} custom-call(bf16[2,256,1024]{2,1,0:T(8,128)(2,1)} %refs_0_.5, bf16[2,96,1024]{2,1,0:T(8,128)(2,1)} %collective-permute-done.8.refs_0_, bf16[2,96,1024]{2,1,0:T(8,128)(2,1)} %collective-permute-done.9.refs_1_, bf16[2,96,1024]{2,1,0:T(8,128)(2,1)} %collective-permute-done.10.refs_2_, ...), custom_call_target="tpu_custom_call" | custom-call | bytes 1179648 | tf_op jit(solution)/shard_map/cut/pallas_call | solution.py:101
  82.3 0.1 collective-permute-start.15
  82.4 0.9 collective-permute-start.19
  83.3 2.1 %collective-permute-start.20 = (s32[776,128]{1,0:T(8,128)}, s32[776,128]{1,0:T(8,128)}, u32[]{:S(2)}, u32[]{:S(2)}) collective-permute-start(s32[776,128]{1,0:T(8,128)} %get-tuple-element.37), channel_id=1, source_target_pairs={{0,8},{4,12},{8,0},{12,4},{1,9},{5,13},{9,1},{13,5},{2,10},{6,14},... | collective-permute-start | bytes 1191944 | tf_op jit(solution)/shard_map/ppermute | solution.py:441
  85.4 1.4 collective-permute-start.21
  86.8 0.0 collective-permute-done.15.refs_3_
  86.8 17.0 %terms.5 = (f32[4,96,512]{2,1,0:T(8,128)}, s32[776,128]{1,0:T(8,128)}, s32[776,128]{1,0:T(8,128)}, s32[776,128]{1,0:T(8,128)}, bf16[1024,4096]{1,0:T(8,128)(2,1)}) custom-call(bf16[2,256,1024]{2,1,0:T(8,128)(2,1)} %refs_0_.5, bf16[2,256,1024]{2,1,0:T(8,128)(2,1)} %collective-permute-done.refs_3_.refs_1_, ...), custom_call_target="tpu_custom_call", output_to_operand_aliasing={{4}: (5, {})} | custom-call | flops 3221225472 | bytes 8388608 | tf_op jit(solution)/shard_map/terms/pallas_call | solution.py:219
  103.8 0.3 collective-permute-start.16
  104.1 1.3 collective-permute-start.17
  105.4 0.0 collective-permute-done.19.refs_0_
  105.4 7.8 %collective-permute-start.18 = (s32[776,128]{1,0:T(8,128)}, s32[776,128]{1,0:T(8,128)}, u32[]{:S(2)}, u32[]{:S(2)}) collective-permute-start(s32[776,128]{1,0:T(8,128)} %get-tuple-element.35), channel_id=1, source_target_pairs={{0,4},{4,0},{8,12},{12,8},{1,5},{5,1},{9,13},{13,9},{2,6},{6,2},{1... | collective-permute-start | bytes 1191944 | tf_op jit(solution)/shard_map/ppermute | solution.py:441
  113.3 25.0 %collective-permute-done.20.refs_1_ = s32[776,128]{1,0:T(8,128)} collective-permute-done((s32[776,128]{1,0:T(8,128)}, s32[776,128]{1,0:T(8,128)}, u32[]{:S(2)}, u32[]{:S(2)}) %collective-permute-start.20) | collective-permute-done | bytes 397344 | tf_op jit(solution)/shard_map/ppermute | solution.py:441
  138.3 0.0 collective-permute-done.21.refs_2_
  138.3 19.4 %grads.1.refs_4_ = bf16[4,2,512,2048]{3,2,1,0:T(8,128)(2,1)} custom-call(bf16[4,512,1024]{2,1,0:T(8,128)(2,1)} %turn.1.refs_4_.codes_ref, bf16[1024,4096]{1,0:T(8,128)(2,1)} %get-tuple-element.39.err_ref, s32[776,128]{1,0:T(8,128)} %collective-permute-done.19.refs_0_, s32[776,128]{1,0:T(8,128)} %collective-permute-done.20.refs_1_, ...), custom_call_target="tpu_custom_call" | custom-call | flops 8589934592 | bytes 12582912 | tf_op jit(solution)/shard_map/grads/pallas_call | solution.py:373
  157.7 0.0 collective-permute-done.16.refs_5_.refs_0_
  157.7 0.0 copy-start
  157.7 0.0 collective-permute-done.17.refs_6_.refs_1_
  157.7 0.0 collective-permute-done.18.refs_7_.refs_2_
  157.7 0.7 copy-done
  158.4 3.3 %finish.3.refs_4_ = bf16[4,256,512]{2,1,0:T(8,128)(2,1)} custom-call(f32[4,64,512]{2,1,0:T(8,128)} %get-tuple-element.23.refs_3_.own_ref, s32[520,128]{1,0:T(8,128)} %copy-done.1, s32[520,128]{1,0:T(8,128)} %collective-permute-done.13.refs_5_.refs_1_, s32[520,128]{1,0:T(8,128)} %collective-permute-done.14.refs_6_.refs_2_, s32[4,256,512]{2,1,0:T(8,128)} %refs_3_.5, ...), custom_call_target="tpu_custom_call" | custom-call | flops 1310720 | bytes 1048576 | tf_op jit(solution)/shard_map/finish/pallas_call | solution.py:299
  161.8 3.8 %finish.4.refs_4_ = bf16[4,256,512]{2,1,0:T(8,128)(2,1)} custom-call(f32[4,96,512]{2,1,0:T(8,128)} %get-tuple-element.27.refs_3_.own_ref, s32[776,128]{1,0:T(8,128)} %collective-permute-done.19.refs_0_, s32[776,128]{1,0:T(8,128)} %collective-permute-done.20.refs_1_, s32[776,128]{1,0:T(8,128)} %collective-permute-done.21.refs_2_, ...), custom_call_target="tpu_custom_call", output_to_operand_aliasing={{}: (5, {})} | custom-call | flops 1966080 | bytes 1572864 | tf_op jit(solution)/shard_map/finish/pallas_call | solution.py:299
  165.5 3.8 %finish.5 = bf16[4,256,512]{2,1,0:T(8,128)(2,1)} custom-call(f32[4,96,512]{2,1,0:T(8,128)} %get-tuple-element.32.own_ref, s32[776,128]{1,0:T(8,128)} %copy-done, s32[776,128]{1,0:T(8,128)} %collective-permute-done.17.refs_6_.refs_1_, s32[776,128]{1,0:T(8,128)} %collective-permute-done.18.refs_7_.refs_2_, ...), custom_call_target="tpu_custom_call", output_to_operand_aliasing={{}: (5, {})} | custom-call | flops 1966080 | bytes 1572864 | tf_op jit(solution)/shard_map/finish/pallas_call | solution.py:299
Async XLA Ops:
  0.6 18.9 %collective-permute-start = (bf16[2,256,1024]{2,1,0:T(8,128)(2,1)}, bf16[2,256,1024]{2,1,0:T(8,128)(2,1)}, u32[]{:S(2)}, u32[]{:S(2)}) collective-permute-start(bf16[2,256,1024]{2,1,0:T(8,128)(2,1)} %refs_0_.5), channel_id=1, source_target_pairs={{0,1},{1,0},{2,3},{3,2},{4,5},{5,4},{6,7},{7,6},{8,9},{9,8},{10,11... | collective-permute-start | bytes 3145736 | tf_op jit(solution)/shard_map/ppermute | solution.py:414
  2.8 10.9 %collective-permute-start.3 = (bf16[2,64,1024]{2,1,0:T(8,128)(2,1)}, bf16[2,64,1024]{2,1,0:T(8,128)(2,1)S(1)}, u32[]{:S(2)}, u32[]{:S(2)}) collective-permute-start(bf16[2,64,1024]{2,1,0:T(8,128)(2,1)} %cut.4), channel_id=1, source_target_pairs={{0,18},{1,19},{2,16},{3,17},{16,2},{17,3},{18,0},{19,1},{4,22},{5,... | collective-permute-start | bytes 786440 | tf_op jit(solution)/shard_map/ppermute | solution.py:396
  6.3 12.9 %collective-permute-start.2 = (bf16[2,64,1024]{2,1,0:T(8,128)(2,1)}, bf16[2,64,1024]{2,1,0:T(8,128)(2,1)}, u32[]{:S(2)}, u32[]{:S(2)}) collective-permute-start(bf16[2,64,1024]{2,1,0:T(8,128)(2,1)} %cut.4), channel_id=1, source_target_pairs={{0,2},{1,3},{2,0},{3,1},{16,18},{17,19},{18,16},{19,17},{4,6},{5,7... | collective-permute-start | bytes 786440 | tf_op jit(solution)/shard_map/ppermute | solution.py:396
  6.8 12.7 %collective-permute-start.1 = (bf16[2,64,1024]{2,1,0:T(8,128)(2,1)}, bf16[2,64,1024]{2,1,0:T(8,128)(2,1)}, u32[]{:S(2)}, u32[]{:S(2)}) collective-permute-start(bf16[2,64,1024]{2,1,0:T(8,128)(2,1)} %cut.4), channel_id=1, source_target_pairs={{0,16},{1,17},{2,18},{3,19},{16,0},{17,1},{18,2},{19,3},{4,20},{5,... | collective-permute-start | bytes 786440 | tf_op jit(solution)/shard_map/ppermute | solution.py:396
  13.8 5.8 %copy-start.3 = (bf16[2,64,1024]{2,1,0:T(8,128)(2,1)}, bf16[2,64,1024]{2,1,0:T(8,128)(2,1)S(1)}, u32[]{:S(2)}) copy-start(bf16[2,64,1024]{2,1,0:T(8,128)(2,1)S(1)} %collective-permute-done.3.refs_2_) | copy-start | bytes 786436
  21.8 3.6 %collective-permute-start.7 = (bf16[3,2,64,1024]{3,2,1,0:T(8,128)(2,1)}, bf16[3,2,64,1024]{3,2,1,0:T(8,128)(2,1)}, u32[]{:S(2)}, u32[]{:S(2)}) collective-permute-start(bf16[3,2,64,1024]{3,2,1,0:T(8,128)(2,1)} %get-tuple-element.22.refs_2_), channel_id=1, source_target_pairs={{0,1},{1,0},{2,3},{3,2},{4,5},{5,4},{6,7},{7,6},{8,9},{9,8},{10,11... | collective-permute-start | bytes 2359304 | tf_op jit(solution)/shard_map/ppermute | solution.py:414
  21.9 17.6 %collective-permute-start.6 = (bf16[2,96,1024]{2,1,0:T(8,128)(2,1)}, bf16[2,96,1024]{2,1,0:T(8,128)(2,1)S(1)}, u32[]{:S(2)}, u32[]{:S(2)}) collective-permute-start(bf16[2,96,1024]{2,1,0:T(8,128)(2,1)} %get-tuple-element.21), channel_id=1, source_target_pairs={{0,18},{1,19},{2,16},{3,17},{16,2},{17,3},{18,0},{19,1},{4,22},{5,... | collective-permute-start | bytes 1179656 | tf_op jit(solution)/shard_map/ppermute | solution.py:396
  23.5 19.6 %collective-permute-start.5 = (bf16[2,96,1024]{2,1,0:T(8,128)(2,1)}, bf16[2,96,1024]{2,1,0:T(8,128)(2,1)}, u32[]{:S(2)}, u32[]{:S(2)}) collective-permute-start(bf16[2,96,1024]{2,1,0:T(8,128)(2,1)} %get-tuple-element.21), channel_id=1, source_target_pairs={{0,2},{1,3},{2,0},{3,1},{16,18},{17,19},{18,16},{19,17},{4,6},{5,7... | collective-permute-start | bytes 1179656 | tf_op jit(solution)/shard_map/ppermute | solution.py:396
  24.9 18.2 %collective-permute-start.4 = (bf16[2,96,1024]{2,1,0:T(8,128)(2,1)}, bf16[2,96,1024]{2,1,0:T(8,128)(2,1)}, u32[]{:S(2)}, u32[]{:S(2)}) collective-permute-start(bf16[2,96,1024]{2,1,0:T(8,128)(2,1)} %get-tuple-element.21), channel_id=1, source_target_pairs={{0,16},{1,17},{2,18},{3,19},{16,0},{17,1},{18,2},{19,3},{4,20},{5,... | collective-permute-start | bytes 1179656 | tf_op jit(solution)/shard_map/ppermute | solution.py:396
  39.5 3.6 %copy-start.2 = (bf16[2,96,1024]{2,1,0:T(8,128)(2,1)}, bf16[2,96,1024]{2,1,0:T(8,128)(2,1)S(1)}, u32[]{:S(2)}) copy-start(bf16[2,96,1024]{2,1,0:T(8,128)(2,1)S(1)} %collective-permute-done.6.refs_2_) | copy-start | bytes 1179652
  45.6 17.4 %collective-permute-start.11 = (bf16[3,2,96,1024]{3,2,1,0:T(8,128)(2,1)}, bf16[3,2,96,1024]{3,2,1,0:T(8,128)(2,1)}, u32[]{:S(2)}, u32[]{:S(2)}) collective-permute-start(bf16[3,2,96,1024]{3,2,1,0:T(8,128)(2,1)} %get-tuple-element.25.refs_2_), channel_id=1, source_target_pairs={{0,1},{1,0},{2,3},{3,2},{4,5},{5,4},{6,7},{7,6},{8,9},{9,8},{10,11... | collective-permute-start | bytes 3538952 | tf_op jit(solution)/shard_map/ppermute | solution.py:414
  45.7 10.9 %collective-permute-start.12 = (s32[520,128]{1,0:T(8,128)}, s32[520,128]{1,0:T(8,128)S(1)}, u32[]{:S(2)}, u32[]{:S(2)}) collective-permute-start(s32[520,128]{1,0:T(8,128)} %get-tuple-element.28), channel_id=1, source_target_pairs={{0,12},{4,8},{8,4},{12,0},{1,13},{5,9},{9,5},{13,1},{2,14},{6,10},... | collective-permute-start | bytes 798728 | tf_op jit(solution)/shard_map/ppermute | solution.py:441
  49.4 30.6 %collective-permute-start.10 = (bf16[2,96,1024]{2,1,0:T(8,128)(2,1)}, bf16[2,96,1024]{2,1,0:T(8,128)(2,1)}, u32[]{:S(2)}, u32[]{:S(2)}) collective-permute-start(bf16[2,96,1024]{2,1,0:T(8,128)(2,1)} %get-tuple-element.24), channel_id=1, source_target_pairs={{0,18},{1,19},{2,16},{3,17},{16,2},{17,3},{18,0},{19,1},{4,22},{5,... | collective-permute-start | bytes 1179656 | tf_op jit(solution)/shard_map/ppermute | solution.py:396
  51.0 29.0 %collective-permute-start.9 = (bf16[2,96,1024]{2,1,0:T(8,128)(2,1)}, bf16[2,96,1024]{2,1,0:T(8,128)(2,1)}, u32[]{:S(2)}, u32[]{:S(2)}) collective-permute-start(bf16[2,96,1024]{2,1,0:T(8,128)(2,1)} %get-tuple-element.24), channel_id=1, source_target_pairs={{0,2},{1,3},{2,0},{3,1},{16,18},{17,19},{18,16},{19,17},{4,6},{5,7... | collective-permute-start | bytes 1179656 | tf_op jit(solution)/shard_map/ppermute | solution.py:396
  52.3 27.7 %collective-permute-start.8 = (bf16[2,96,1024]{2,1,0:T(8,128)(2,1)}, bf16[2,96,1024]{2,1,0:T(8,128)(2,1)}, u32[]{:S(2)}, u32[]{:S(2)}) collective-permute-start(bf16[2,96,1024]{2,1,0:T(8,128)(2,1)} %get-tuple-element.24), channel_id=1, source_target_pairs={{0,16},{1,17},{2,18},{3,19},{16,0},{17,1},{18,2},{19,3},{4,20},{5,... | collective-permute-start | bytes 1179656 | tf_op jit(solution)/shard_map/ppermute | solution.py:396
  56.7 23.3 %copy-start.1 = (s32[520,128]{1,0:T(8,128)}, s32[520,128]{1,0:T(8,128)S(1)}, u32[]{:S(2)}) copy-start(s32[520,128]{1,0:T(8,128)S(1)} %collective-permute-done.12.refs_4_.refs_0_) | copy-start | bytes 798724
  56.7 23.3 %collective-permute-start.13 = (s32[520,128]{1,0:T(8,128)}, s32[520,128]{1,0:T(8,128)}, u32[]{:S(2)}, u32[]{:S(2)}) collective-permute-start(s32[520,128]{1,0:T(8,128)} %get-tuple-element.29), channel_id=1, source_target_pairs={{0,8},{4,12},{8,0},{12,4},{1,9},{5,13},{9,1},{13,5},{2,10},{6,14},... | collective-permute-start | bytes 798728 | tf_op jit(solution)/shard_map/ppermute | solution.py:441
  63.0 16.9 %collective-permute-start.14 = (s32[520,128]{1,0:T(8,128)}, s32[520,128]{1,0:T(8,128)}, u32[]{:S(2)}, u32[]{:S(2)}) collective-permute-start(s32[520,128]{1,0:T(8,128)} %get-tuple-element.30), channel_id=1, source_target_pairs={{0,4},{4,0},{8,12},{12,8},{1,5},{5,1},{9,13},{13,9},{2,6},{6,2},{1... | collective-permute-start | bytes 798728 | tf_op jit(solution)/shard_map/ppermute | solution.py:441
  82.3 4.5 %collective-permute-start.15 = (bf16[3,2,96,1024]{3,2,1,0:T(8,128)(2,1)}, bf16[3,2,96,1024]{3,2,1,0:T(8,128)(2,1)}, u32[]{:S(2)}, u32[]{:S(2)}) collective-permute-start(bf16[3,2,96,1024]{3,2,1,0:T(8,128)(2,1)} %cut.7.refs_2_), channel_id=1, source_target_pairs={{0,1},{1,0},{2,3},{3,2},{4,5},{5,4},{6,7},{7,6},{8,9},{9,8},{10,11... | collective-permute-start | bytes 3538952 | tf_op jit(solution)/shard_map/ppermute | solution.py:414
  82.4 23.1 %collective-permute-start.19 = (s32[776,128]{1,0:T(8,128)}, s32[776,128]{1,0:T(8,128)}, u32[]{:S(2)}, u32[]{:S(2)}) collective-permute-start(s32[776,128]{1,0:T(8,128)} %get-tuple-element.36), channel_id=1, source_target_pairs={{0,12},{4,8},{8,4},{12,0},{1,13},{5,9},{9,5},{13,1},{2,14},{6,10},... | collective-permute-start | bytes 1191944 | tf_op jit(solution)/shard_map/ppermute | solution.py:441
  83.3 55.0 %collective-permute-start.20 = (s32[776,128]{1,0:T(8,128)}, s32[776,128]{1,0:T(8,128)}, u32[]{:S(2)}, u32[]{:S(2)}) collective-permute-start(s32[776,128]{1,0:T(8,128)} %get-tuple-element.37), channel_id=1, source_target_pairs={{0,8},{4,12},{8,0},{12,4},{1,9},{5,13},{9,1},{13,5},{2,10},{6,14},... | collective-permute-start | bytes 1191944 | tf_op jit(solution)/shard_map/ppermute | solution.py:441
  85.4 52.9 %collective-permute-start.21 = (s32[776,128]{1,0:T(8,128)}, s32[776,128]{1,0:T(8,128)}, u32[]{:S(2)}, u32[]{:S(2)}) collective-permute-start(s32[776,128]{1,0:T(8,128)} %get-tuple-element.38), channel_id=1, source_target_pairs={{0,4},{4,0},{8,12},{12,8},{1,5},{5,1},{9,13},{13,9},{2,6},{6,2},{1... | collective-permute-start | bytes 1191944 | tf_op jit(solution)/shard_map/ppermute | solution.py:441
  103.8 53.8 %collective-permute-start.16 = (s32[776,128]{1,0:T(8,128)}, s32[776,128]{1,0:T(8,128)S(1)}, u32[]{:S(2)}, u32[]{:S(2)}) collective-permute-start(s32[776,128]{1,0:T(8,128)} %get-tuple-element.33), channel_id=1, source_target_pairs={{0,12},{4,8},{8,4},{12,0},{1,13},{5,9},{9,5},{13,1},{2,14},{6,10},... | collective-permute-start | bytes 1191944 | tf_op jit(solution)/shard_map/ppermute | solution.py:441
  104.1 53.6 %collective-permute-start.17 = (s32[776,128]{1,0:T(8,128)}, s32[776,128]{1,0:T(8,128)}, u32[]{:S(2)}, u32[]{:S(2)}) collective-permute-start(s32[776,128]{1,0:T(8,128)} %get-tuple-element.34), channel_id=1, source_target_pairs={{0,8},{4,12},{8,0},{12,4},{1,9},{5,13},{9,1},{13,5},{2,10},{6,14},... | collective-permute-start | bytes 1191944 | tf_op jit(solution)/shard_map/ppermute | solution.py:441
  105.4 52.3 %collective-permute-start.18 = (s32[776,128]{1,0:T(8,128)}, s32[776,128]{1,0:T(8,128)}, u32[]{:S(2)}, u32[]{:S(2)}) collective-permute-start(s32[776,128]{1,0:T(8,128)} %get-tuple-element.35), channel_id=1, source_target_pairs={{0,4},{4,0},{8,12},{12,8},{1,5},{5,1},{9,13},{13,9},{2,6},{6,2},{1... | collective-permute-start | bytes 1191944 | tf_op jit(solution)/shard_map/ppermute | solution.py:441
  157.7 0.7 copy-start

commit v6 on v5

--- a/solution.py
+++ b/solution.py
@@ -435,17 +435,17 @@
             n_tgt,
             n_feat * span,
             n_feat * stride,
-            [],
+            gots[index - 1][:1] if index > 1 else [],
         )
         owns.append(own)
         send = lambda x, flip: lax.ppermute(x, "tgt", [(i, i ^ flip) for i in range(n_tgt)])
         gots.append([send(far, 3), send(across, 2), send(near, 1)])
         if index < last:
-            pieces, plan = gather.send([own] + (gots[index - 1] if index else []))
-    decoder_grads = grads_call(codes_t, everything, decoder.shape, gots[-2] if last else [])
+            pieces, plan = gather.send([own] + (gots[index - 1] if index else gots[0][:1]))
+    decoder_grads = grads_call(codes_t, everything, decoder.shape, [])
     code_grads = None
     for index in range(len(spans)):
-        after = [decoder_grads, *gots[last]] if index == 0 else []
+        after = [] if index else [decoder_grads]
         code_grads = finish_call(owns[index], gots[index], active_mask, code_grads, offsets[index], stride, after)
     return code_grads, decoder_grads
 

time: 172 us -> 168 us (0.977)
  the two profiles are of different devices: /device:TPU:0 before, /device:TPU:8 now
where the time goes in v6:
time: 168 us; the launch traced here: 167 us
  Pallas kernels  95.6 us (57%)
  waiting for transfers between devices  45 us (27%)
  starting transfers between devices  22.6 us (13%)
  local copies, waits for them, and re-layouts  2.84 us (2%)
    pallas_call x3, Pallas kernels, terms_call(): pl.pallas_call(functools.partial(terms_kernel, n_tgt, plan, offset), in_s...  46.2 us
    ppermute x9, waiting for transfers between devices, body(): lax.ppermute(x, 'tgt', [(i, i ^ flip) for i in range(n_tgt)])  35.5 us
    pallas_call x1, Pallas kernels, grads_call(): pl.pallas_call(grads_kernel, grid=(tgt_count, layers), in_specs=in_specs...  24.5 us
    ppermute x9, starting transfers between devices, body(): lax.ppermute(x, 'tgt', [(i, i ^ flip) for i in range(n_tgt)])  11.2 us
    ppermute x9, starting transfers between devices, gather_pieces(): lax.ppermute(x, axes, [(i, i ^ flip) for i in range(n_src * n_feat)])  11.1 us
    pallas_call x3, Pallas kernels, finish_call(): pl.pallas_call(functools.partial(finish_kernel, len(gots), offset, stride...  10.9 us
    ppermute x9, waiting for transfers between devices, gather_pieces(): lax.ppermute(x, axes, [(i, i ^ flip) for i in range(n_src * n_feat)])  9.52 us
    pallas_call x4, Pallas kernels, cut_call(): pl.pallas_call(functools.partial(cut_kernel, len(join), offset), in_specs...  8.74 us
  transfers between devices with their start and end apart: 22, of which 6 were waited for; matrix products, arithmetic and copies ran while one was open for 0% of the time, Pallas kernels for 51%

profile of v6, /device:TPU:8, one launch (start us, length us, event | category | flops | bytes accessed | tf_op | source)
XLA Modules:
  0.0 167.1 jit_solution(7878330723912898089)
XLA Ops:
  0.6 0.1 collective-permute-start
  0.7 1.7 cut.4
  2.4 2.5 %collective-permute-start.3 = (bf16[2,64,1024]{2,1,0:T(8,128)(2,1)}, bf16[2,64,1024]{2,1,0:T(8,128)(2,1)S(1)}, u32[]{:S(2)}, u32[]{:S(2)}) collective-permute-start(bf16[2,64,1024]{2,1,0:T(8,128)(2,1)} %cut.4), channel_id=1, source_target_pairs={{0,18},{1,19},{2,16},{3,17},{16,2},{17,3},{18,0},{19,1},{4,22},{5,... | collective-permute-start | bytes 786440 | tf_op jit(solution)/shard_map/ppermute | solution.py:396
  4.9 0.5 collective-permute-start.2
  5.4 0.5 collective-permute-start.1
  5.9 5.3 %turn.1.refs_4_.codes_ref = bf16[4,512,1024]{2,1,0:T(8,128)(2,1)} custom-call(bf16[4,1024,512]{2,1,0:T(8,128)(2,1)} %codes_ref.1), custom_call_target="tpu_custom_call" | custom-call | flops 1048576 | bytes 4194304 | tf_op jit(solution)/shard_map/turn/pallas_call | solution.py:334
  11.2 1.5 collective-permute-done.3.refs_2_
  12.7 0.0 copy-start.4
  12.7 5.3 %collective-permute-done.2.refs_1_ = bf16[2,64,1024]{2,1,0:T(8,128)(2,1)} collective-permute-done((bf16[2,64,1024]{2,1,0:T(8,128)(2,1)}, bf16[2,64,1024]{2,1,0:T(8,128)(2,1)}, u32[]{:S(2)}, u32[]{:S(2)}) %collective-permute-start.2) | collective-permute-done | bytes 262176 | tf_op jit(solution)/shard_map/ppermute | solution.py:396
  18.0 0.1 collective-permute-done.1.refs_0_
  18.1 0.0 collective-permute-done.refs_3_.refs_1_
  18.1 0.0 copy-done.4
  18.1 2.3 %cut.5 = (bf16[3,2,64,1024]{3,2,1,0:T(8,128)(2,1)}, bf16[2,96,1024]{2,1,0:T(8,128)(2,1)}) custom-call(bf16[2,256,1024]{2,1,0:T(8,128)(2,1)} %refs_0_.5, bf16[2,64,1024]{2,1,0:T(8,128)(2,1)} %collective-permute-done.1.refs_0_, bf16[2,64,1024]{2,1,0:T(8,128)(2,1)} %collective-permute-done.2.refs_1_, bf16[2,64,1024]{2,1,0:T(8,128)(2,1)} %copy-done.4, ...), custom_call_target="tpu_custom_call" | custom-call | bytes 1179648 | tf_op jit(solution)/shard_map/cut/pallas_call | solution.py:101
  20.4 0.1 collective-permute-start.7
  20.4 1.7 %collective-permute-start.6 = (bf16[2,96,1024]{2,1,0:T(8,128)(2,1)}, bf16[2,96,1024]{2,1,0:T(8,128)(2,1)}, u32[]{:S(2)}, u32[]{:S(2)}) collective-permute-start(bf16[2,96,1024]{2,1,0:T(8,128)(2,1)} %get-tuple-element.21), channel_id=1, source_target_pairs={{0,18},{1,19},{2,16},{3,17},{16,2},{17,3},{18,0},{19,1},{4,22},{5,... | collective-permute-start | bytes 1179656 | tf_op jit(solution)/shard_map/ppermute | solution.py:396
  22.2 1.3 collective-permute-start.5
  23.5 0.5 collective-permute-start.4
  24.0 0.0 collective-permute-done.7.refs_3_
  24.0 13.4 %terms.3 = (f32[4,64,512]{2,1,0:T(8,128)}, s32[520,128]{1,0:T(8,128)}, s32[520,128]{1,0:T(8,128)}, s32[520,128]{1,0:T(8,128)}, bf16[1024,4096]{1,0:T(8,128)(2,1)}) custom-call(bf16[2,256,1024]{2,1,0:T(8,128)(2,1)} %refs_0_.5, bf16[2,256,1024]{2,1,0:T(8,128)(2,1)} %collective-permute-done.refs_3_.refs_1_, bf16[3,2,64,1024]{3,2,1,0:T(8,128)(2,1)} %get-tuple-element.22.refs_2_, ...), custom_call_target="tpu_custom_call" | custom-call | flops 2147483648 | bytes 8388608 | tf_op jit(solution)/shard_map/terms/pallas_call | solution.py:219
  37.5 1.5 collective-permute-start.8
  39.0 0.0 collective-permute-done.6.refs_2_
  39.0 2.7 %collective-permute-done.5.refs_1_ = bf16[2,96,1024]{2,1,0:T(8,128)(2,1)} collective-permute-done((bf16[2,96,1024]{2,1,0:T(8,128)(2,1)}, bf16[2,96,1024]{2,1,0:T(8,128)(2,1)}, u32[]{:S(2)}, u32[]{:S(2)}) %collective-permute-start.5) | collective-permute-done | bytes 393248 | tf_op jit(solution)/shard_map/ppermute | solution.py:396
  41.6 0.0 collective-permute-done.4.refs_0_
  41.6 9.7 %collective-permute-done.8.refs_4_.refs_0_ = s32[520,128]{1,0:T(8,128)S(1)} collective-permute-done((s32[520,128]{1,0:T(8,128)}, s32[520,128]{1,0:T(8,128)S(1)}, u32[]{:S(2)}, u32[]{:S(2)}) %collective-permute-start.8) | collective-permute-done | bytes 266272 | tf_op jit(solution)/shard_map/ppermute | solution.py:441
  51.3 0.7 copy-done
  52.0 2.5 %cut.6 = (bf16[3,2,96,1024]{3,2,1,0:T(8,128)(2,1)}, bf16[2,96,1024]{2,1,0:T(8,128)(2,1)}) custom-call(bf16[2,256,1024]{2,1,0:T(8,128)(2,1)} %refs_0_.5, bf16[2,96,1024]{2,1,0:T(8,128)(2,1)} %collective-permute-done.4.refs_0_, bf16[2,96,1024]{2,1,0:T(8,128)(2,1)} %collective-permute-done.5.refs_1_, bf16[2,96,1024]{2,1,0:T(8,128)(2,1)} %collective-permute-done.6.refs_2_, ...), custom_call_target="tpu_custom_call" | custom-call | bytes 1572864 | tf_op jit(solution)/shard_map/cut/pallas_call | solution.py:101
  54.6 0.1 collective-permute-start.12
  54.7 2.7 %collective-permute-start.11 = (bf16[2,96,1024]{2,1,0:T(8,128)(2,1)}, bf16[2,96,1024]{2,1,0:T(8,128)(2,1)}, u32[]{:S(2)}, u32[]{:S(2)}) collective-permute-start(bf16[2,96,1024]{2,1,0:T(8,128)(2,1)} %get-tuple-element.25), channel_id=1, source_target_pairs={{0,18},{1,19},{2,16},{3,17},{16,2},{17,3},{18,0},{19,1},{4,22},{5,... | collective-permute-start | bytes 1179656 | tf_op jit(solution)/shard_map/ppermute | solution.py:396
  57.3 1.3 collective-permute-start.10
  58.6 0.0 collective-permute-start.9
  58.6 0.0 collective-permute-start.13
  58.6 0.0 collective-permute-done.12.refs_3_
  58.6 2.6 %collective-permute-start.14 = (s32[520,128]{1,0:T(8,128)}, s32[520,128]{1,0:T(8,128)}, u32[]{:S(2)}, u32[]{:S(2)}) collective-permute-start(s32[520,128]{1,0:T(8,128)} %get-tuple-element.30), channel_id=1, source_target_pairs={{0,4},{4,0},{8,12},{12,8},{1,5},{5,1},{9,13},{13,9},{2,6},{6,2},{1... | collective-permute-start | bytes 798728 | tf_op jit(solution)/shard_map/ppermute | solution.py:441
  61.3 16.4 %terms.4 = (f32[4,96,512]{2,1,0:T(8,128)}, s32[776,128]{1,0:T(8,128)}, s32[776,128]{1,0:T(8,128)}, s32[776,128]{1,0:T(8,128)}, bf16[1024,4096]{1,0:T(8,128)(2,1)}) custom-call(bf16[2,256,1024]{2,1,0:T(8,128)(2,1)} %refs_0_.5, bf16[2,256,1024]{2,1,0:T(8,128)(2,1)} %collective-permute-done.refs_3_.refs_1_, ...), custom_call_target="tpu_custom_call", output_to_operand_aliasing={{4}: (5, {})} | custom-call | flops 3221225472 | bytes 8388608 | tf_op jit(solution)/shard_map/terms/pallas_call | solution.py:219
  77.6 0.0 collective-permute-done.13.refs_5_.refs_1_
  77.7 0.0 copy-start.2
  77.7 0.0 collective-permute-done.14.refs_6_.refs_2_
  77.7 0.0 collective-permute-done.11.refs_2_
  77.7 0.0 collective-permute-done.10.refs_1_
  77.7 0.0 collective-permute-done.9.refs_0_
  77.7 0.7 copy-done.2
  78.4 2.3 %cut.7.refs_2_ = bf16[3,2,96,1024]{3,2,1,0:T(8,128)(2,1)} custom-call(bf16[2,256,1024]{2,1,0:T(8,128)(2,1)} %refs_0_.5, bf16[2,96,1024]{2,1,0:T(8,128)(2,1)} %collective-permute-done.9.refs_0_, bf16[2,96,1024]{2,1,0:T(8,128)(2,1)} %collective-permute-done.10.refs_1_, bf16[2,96,1024]{2,1,0:T(8,128)(2,1)} %collective-permute-done.11.refs_2_, ...), custom_call_target="tpu_custom_call" | custom-call | bytes 1179648 | tf_op jit(solution)/shard_map/cut/pallas_call | solution.py:101
  80.7 0.1 collective-permute-start.15
  80.7 0.8 collective-permute-start.16
  81.5 2.2 %collective-permute-start.20 = (s32[776,128]{1,0:T(8,128)}, s32[776,128]{1,0:T(8,128)}, u32[]{:S(2)}, u32[]{:S(2)}) collective-permute-start(s32[776,128]{1,0:T(8,128)} %get-tuple-element.37), channel_id=1, source_target_pairs={{0,8},{4,12},{8,0},{12,4},{1,9},{5,13},{9,1},{13,5},{2,10},{6,14},... | collective-permute-start | bytes 1191944 | tf_op jit(solution)/shard_map/ppermute | solution.py:441
  83.7 0.6 collective-permute-start.21
  84.3 25.8 %collective-permute-done.16.refs_6_.refs_0_ = s32[776,128]{1,0:T(8,128)S(1)} collective-permute-done((s32[776,128]{1,0:T(8,128)}, s32[776,128]{1,0:T(8,128)S(1)}, u32[]{:S(2)}, u32[]{:S(2)}) %collective-permute-start.16) | collective-permute-done | bytes 397344 | tf_op jit(solution)/shard_map/ppermute | solution.py:441
  110.0 0.0 collective-permute-done.15.refs_3_
  110.0 0.8 copy-done.1
  110.8 16.4 %terms.5 = (f32[4,96,512]{2,1,0:T(8,128)}, s32[776,128]{1,0:T(8,128)}, s32[776,128]{1,0:T(8,128)}, s32[776,128]{1,0:T(8,128)}, bf16[1024,4096]{1,0:T(8,128)(2,1)}) custom-call(bf16[2,256,1024]{2,1,0:T(8,128)(2,1)} %refs_0_.5, bf16[2,256,1024]{2,1,0:T(8,128)(2,1)} %collective-permute-done.refs_3_.refs_1_, ...), custom_call_target="tpu_custom_call", output_to_operand_aliasing={{4}: (5, {})} | custom-call | flops 3221225472 | bytes 8388608 | tf_op jit(solution)/shard_map/terms/pallas_call | solution.py:219
  127.2 0.6 collective-permute-start.17
  127.8 0.0 collective-permute-start.18
  127.8 3.0 %collective-permute-start.19 = (s32[776,128]{1,0:T(8,128)}, s32[776,128]{1,0:T(8,128)}, u32[]{:S(2)}, u32[]{:S(2)}) collective-permute-start(s32[776,128]{1,0:T(8,128)} %get-tuple-element.36), channel_id=1, source_target_pairs={{0,4},{4,0},{8,12},{12,8},{1,5},{5,1},{9,13},{13,9},{2,6},{6,2},{1... | collective-permute-start | bytes 1191944 | tf_op jit(solution)/shard_map/ppermute | solution.py:441
  130.8 24.5 %grads.1.refs_4_ = bf16[4,2,512,2048]{3,2,1,0:T(8,128)(2,1)} custom-call(bf16[4,512,1024]{2,1,0:T(8,128)(2,1)} %turn.1.refs_4_.codes_ref, bf16[1024,4096]{1,0:T(8,128)(2,1)} %get-tuple-element.39.err_ref), custom_call_target="tpu_custom_call" | custom-call | flops 8589934592 | bytes 12582912 | tf_op jit(solution)/shard_map/grads/pallas_call | solution.py:373
  155.3 3.3 %finish.3.refs_4_ = bf16[4,256,512]{2,1,0:T(8,128)(2,1)} custom-call(f32[4,64,512]{2,1,0:T(8,128)} %get-tuple-element.23.refs_3_.own_ref, s32[520,128]{1,0:T(8,128)} %copy-done, s32[520,128]{1,0:T(8,128)} %copy-done.2, s32[520,128]{1,0:T(8,128)} %collective-permute-done.14.refs_6_.refs_2_, s32[4,256,512]{2,1,0:T(8,128)} %refs_3_.5, ...), custom_call_target="tpu_custom_call" | custom-call | flops 1310720 | bytes 1048576 | tf_op jit(solution)/shard_map/finish/pallas_call | solution.py:299
  158.6 0.0 collective-permute-done.20.refs_1_
  158.6 0.0 collective-permute-done.21.refs_2_
  158.6 3.8 %finish.4.refs_4_ = bf16[4,256,512]{2,1,0:T(8,128)(2,1)} custom-call(f32[4,96,512]{2,1,0:T(8,128)} %get-tuple-element.28.refs_3_.own_ref, s32[776,128]{1,0:T(8,128)} %copy-done.1, s32[776,128]{1,0:T(8,128)} %collective-permute-done.20.refs_1_, s32[776,128]{1,0:T(8,128)} %collective-permute-done.21.refs_2_, ...), custom_call_target="tpu_custom_call", output_to_operand_aliasing={{}: (5, {})} | custom-call | flops 1966080 | bytes 1572864 | tf_op jit(solution)/shard_map/finish/pallas_call | solution.py:299
  162.4 0.0 collective-permute-done.17.refs_0_
  162.4 0.0 copy-start.3
  162.4 0.0 collective-permute-done.18.refs_1_
  162.4 0.0 collective-permute-done.19.refs_2_
  162.5 0.7 copy-done.3
  163.2 3.8 %finish.5 = bf16[4,256,512]{2,1,0:T(8,128)(2,1)} custom-call(f32[4,96,512]{2,1,0:T(8,128)} %get-tuple-element.33.own_ref, s32[776,128]{1,0:T(8,128)} %copy-done.3, s32[776,128]{1,0:T(8,128)} %collective-permute-done.18.refs_1_, s32[776,128]{1,0:T(8,128)} %collective-permute-done.19.refs_2_, s32[4,256,512]{2,1,0:T(8,128)} %refs_3_.5, ...), custom_call_target="tpu_custom_call", output_to_operand_aliasing={{}: (5, {})} | custom-call | flops 1966080 | bytes 1572864 | tf_op jit(solution)/shard_map/finish/pallas_call | solution.py:299
  (2 shorter events, 0.0 us)
Async XLA Ops:
  0.6 17.5 %collective-permute-start = (bf16[2,256,1024]{2,1,0:T(8,128)(2,1)}, bf16[2,256,1024]{2,1,0:T(8,128)(2,1)}, u32[]{:S(2)}, u32[]{:S(2)}) collective-permute-start(bf16[2,256,1024]{2,1,0:T(8,128)(2,1)} %refs_0_.5), channel_id=1, source_target_pairs={{0,1},{1,0},{2,3},{3,2},{4,5},{5,4},{6,7},{7,6},{8,9},{9,8},{10,11... | collective-permute-start | bytes 3145736 | tf_op jit(solution)/shard_map/ppermute | solution.py:414
  2.4 10.3 %collective-permute-start.3 = (bf16[2,64,1024]{2,1,0:T(8,128)(2,1)}, bf16[2,64,1024]{2,1,0:T(8,128)(2,1)S(1)}, u32[]{:S(2)}, u32[]{:S(2)}) collective-permute-start(bf16[2,64,1024]{2,1,0:T(8,128)(2,1)} %cut.4), channel_id=1, source_target_pairs={{0,18},{1,19},{2,16},{3,17},{16,2},{17,3},{18,0},{19,1},{4,22},{5,... | collective-permute-start | bytes 786440 | tf_op jit(solution)/shard_map/ppermute | solution.py:396
  4.9 13.1 %collective-permute-start.2 = (bf16[2,64,1024]{2,1,0:T(8,128)(2,1)}, bf16[2,64,1024]{2,1,0:T(8,128)(2,1)}, u32[]{:S(2)}, u32[]{:S(2)}) collective-permute-start(bf16[2,64,1024]{2,1,0:T(8,128)(2,1)} %cut.4), channel_id=1, source_target_pairs={{0,2},{1,3},{2,0},{3,1},{16,18},{17,19},{18,16},{19,17},{4,6},{5,7... | collective-permute-start | bytes 786440 | tf_op jit(solution)/shard_map/ppermute | solution.py:396
  5.4 12.7 %collective-permute-start.1 = (bf16[2,64,1024]{2,1,0:T(8,128)(2,1)}, bf16[2,64,1024]{2,1,0:T(8,128)(2,1)}, u32[]{:S(2)}, u32[]{:S(2)}) collective-permute-start(bf16[2,64,1024]{2,1,0:T(8,128)(2,1)} %cut.4), channel_id=1, source_target_pairs={{0,16},{1,17},{2,18},{3,19},{16,0},{17,1},{18,2},{19,3},{4,20},{5,... | collective-permute-start | bytes 786440 | tf_op jit(solution)/shard_map/ppermute | solution.py:396
  12.7 5.4 %copy-start.4 = (bf16[2,64,1024]{2,1,0:T(8,128)(2,1)}, bf16[2,64,1024]{2,1,0:T(8,128)(2,1)S(1)}, u32[]{:S(2)}) copy-start(bf16[2,64,1024]{2,1,0:T(8,128)(2,1)S(1)} %collective-permute-done.3.refs_2_) | copy-start | bytes 786436
  20.4 3.6 %collective-permute-start.7 = (bf16[3,2,64,1024]{3,2,1,0:T(8,128)(2,1)}, bf16[3,2,64,1024]{3,2,1,0:T(8,128)(2,1)}, u32[]{:S(2)}, u32[]{:S(2)}) collective-permute-start(bf16[3,2,64,1024]{3,2,1,0:T(8,128)(2,1)} %get-tuple-element.22.refs_2_), channel_id=1, source_target_pairs={{0,1},{1,0},{2,3},{3,2},{4,5},{5,4},{6,7},{7,6},{8,9},{9,8},{10,11... | collective-permute-start | bytes 2359304 | tf_op jit(solution)/shard_map/ppermute | solution.py:414
  20.4 18.5 %collective-permute-start.6 = (bf16[2,96,1024]{2,1,0:T(8,128)(2,1)}, bf16[2,96,1024]{2,1,0:T(8,128)(2,1)}, u32[]{:S(2)}, u32[]{:S(2)}) collective-permute-start(bf16[2,96,1024]{2,1,0:T(8,128)(2,1)} %get-tuple-element.21), channel_id=1, source_target_pairs={{0,18},{1,19},{2,16},{3,17},{16,2},{17,3},{18,0},{19,1},{4,22},{5,... | collective-permute-start | bytes 1179656 | tf_op jit(solution)/shard_map/ppermute | solution.py:396
  22.2 19.5 %collective-permute-start.5 = (bf16[2,96,1024]{2,1,0:T(8,128)(2,1)}, bf16[2,96,1024]{2,1,0:T(8,128)(2,1)}, u32[]{:S(2)}, u32[]{:S(2)}) collective-permute-start(bf16[2,96,1024]{2,1,0:T(8,128)(2,1)} %get-tuple-element.21), channel_id=1, source_target_pairs={{0,2},{1,3},{2,0},{3,1},{16,18},{17,19},{18,16},{19,17},{4,6},{5,7... | collective-permute-start | bytes 1179656 | tf_op jit(solution)/shard_map/ppermute | solution.py:396
  23.5 18.2 %collective-permute-start.4 = (bf16[2,96,1024]{2,1,0:T(8,128)(2,1)}, bf16[2,96,1024]{2,1,0:T(8,128)(2,1)}, u32[]{:S(2)}, u32[]{:S(2)}) collective-permute-start(bf16[2,96,1024]{2,1,0:T(8,128)(2,1)} %get-tuple-element.21), channel_id=1, source_target_pairs={{0,16},{1,17},{2,18},{3,19},{16,0},{17,1},{18,2},{19,3},{4,20},{5,... | collective-permute-start | bytes 1179656 | tf_op jit(solution)/shard_map/ppermute | solution.py:396
  37.5 13.9 %collective-permute-start.8 = (s32[520,128]{1,0:T(8,128)}, s32[520,128]{1,0:T(8,128)S(1)}, u32[]{:S(2)}, u32[]{:S(2)}) collective-permute-start(s32[520,128]{1,0:T(8,128)} %get-tuple-element.24), channel_id=1, source_target_pairs={{0,12},{4,8},{8,4},{12,0},{1,13},{5,9},{9,5},{13,1},{2,14},{6,10},... | collective-permute-start | bytes 798728 | tf_op jit(solution)/shard_map/ppermute | solution.py:441
  51.3 0.7 copy-start
  54.6 4.0 %collective-permute-start.12 = (bf16[3,2,96,1024]{3,2,1,0:T(8,128)(2,1)}, bf16[3,2,96,1024]{3,2,1,0:T(8,128)(2,1)}, u32[]{:S(2)}, u32[]{:S(2)}) collective-permute-start(bf16[3,2,96,1024]{3,2,1,0:T(8,128)(2,1)} %get-tuple-element.26.refs_2_), channel_id=1, source_target_pairs={{0,1},{1,0},{2,3},{3,2},{4,5},{5,4},{6,7},{7,6},{8,9},{9,8},{10,11... | collective-permute-start | bytes 3538952 | tf_op jit(solution)/shard_map/ppermute | solution.py:414
  54.7 23.0 %collective-permute-start.11 = (bf16[2,96,1024]{2,1,0:T(8,128)(2,1)}, bf16[2,96,1024]{2,1,0:T(8,128)(2,1)}, u32[]{:S(2)}, u32[]{:S(2)}) collective-permute-start(bf16[2,96,1024]{2,1,0:T(8,128)(2,1)} %get-tuple-element.25), channel_id=1, source_target_pairs={{0,18},{1,19},{2,16},{3,17},{16,2},{17,3},{18,0},{19,1},{4,22},{5,... | collective-permute-start | bytes 1179656 | tf_op jit(solution)/shard_map/ppermute | solution.py:396
  57.3 20.4 %collective-permute-start.10 = (bf16[2,96,1024]{2,1,0:T(8,128)(2,1)}, bf16[2,96,1024]{2,1,0:T(8,128)(2,1)}, u32[]{:S(2)}, u32[]{:S(2)}) collective-permute-start(bf16[2,96,1024]{2,1,0:T(8,128)(2,1)} %get-tuple-element.25), channel_id=1, source_target_pairs={{0,2},{1,3},{2,0},{3,1},{16,18},{17,19},{18,16},{19,17},{4,6},{5,7... | collective-permute-start | bytes 1179656 | tf_op jit(solution)/shard_map/ppermute | solution.py:396
  58.6 19.1 %collective-permute-start.9 = (bf16[2,96,1024]{2,1,0:T(8,128)(2,1)}, bf16[2,96,1024]{2,1,0:T(8,128)(2,1)}, u32[]{:S(2)}, u32[]{:S(2)}) collective-permute-start(bf16[2,96,1024]{2,1,0:T(8,128)(2,1)} %get-tuple-element.25), channel_id=1, source_target_pairs={{0,16},{1,17},{2,18},{3,19},{16,0},{17,1},{18,2},{19,3},{4,20},{5,... | collective-permute-start | bytes 1179656 | tf_op jit(solution)/shard_map/ppermute | solution.py:396
  58.6 19.0 %collective-permute-start.13 = (s32[520,128]{1,0:T(8,128)}, s32[520,128]{1,0:T(8,128)S(1)}, u32[]{:S(2)}, u32[]{:S(2)}) collective-permute-start(s32[520,128]{1,0:T(8,128)} %get-tuple-element.29), channel_id=1, source_target_pairs={{0,8},{4,12},{8,0},{12,4},{1,9},{5,13},{9,1},{13,5},{2,10},{6,14},... | collective-permute-start | bytes 798728 | tf_op jit(solution)/shard_map/ppermute | solution.py:441
  58.6 19.0 %collective-permute-start.14 = (s32[520,128]{1,0:T(8,128)}, s32[520,128]{1,0:T(8,128)}, u32[]{:S(2)}, u32[]{:S(2)}) collective-permute-start(s32[520,128]{1,0:T(8,128)} %get-tuple-element.30), channel_id=1, source_target_pairs={{0,4},{4,0},{8,12},{12,8},{1,5},{5,1},{9,13},{13,9},{2,6},{6,2},{1... | collective-permute-start | bytes 798728 | tf_op jit(solution)/shard_map/ppermute | solution.py:441
  77.7 0.7 copy-start.2
  80.7 29.4 %collective-permute-start.15 = (bf16[3,2,96,1024]{3,2,1,0:T(8,128)(2,1)}, bf16[3,2,96,1024]{3,2,1,0:T(8,128)(2,1)}, u32[]{:S(2)}, u32[]{:S(2)}) collective-permute-start(bf16[3,2,96,1024]{3,2,1,0:T(8,128)(2,1)} %cut.7.refs_2_), channel_id=1, source_target_pairs={{0,1},{1,0},{2,3},{3,2},{4,5},{5,4},{6,7},{7,6},{8,9},{9,8},{10,11... | collective-permute-start | bytes 3538952 | tf_op jit(solution)/shard_map/ppermute | solution.py:414
  80.7 29.3 %collective-permute-start.16 = (s32[776,128]{1,0:T(8,128)}, s32[776,128]{1,0:T(8,128)S(1)}, u32[]{:S(2)}, u32[]{:S(2)}) collective-permute-start(s32[776,128]{1,0:T(8,128)} %get-tuple-element.32), channel_id=1, source_target_pairs={{0,12},{4,8},{8,4},{12,0},{1,13},{5,9},{9,5},{13,1},{2,14},{6,10},... | collective-permute-start | bytes 1191944 | tf_op jit(solution)/shard_map/ppermute | solution.py:441
  81.5 77.1 %collective-permute-start.20 = (s32[776,128]{1,0:T(8,128)}, s32[776,128]{1,0:T(8,128)}, u32[]{:S(2)}, u32[]{:S(2)}) collective-permute-start(s32[776,128]{1,0:T(8,128)} %get-tuple-element.37), channel_id=1, source_target_pairs={{0,8},{4,12},{8,0},{12,4},{1,9},{5,13},{9,1},{13,5},{2,10},{6,14},... | collective-permute-start | bytes 1191944 | tf_op jit(solution)/shard_map/ppermute | solution.py:441
  83.7 74.9 %collective-permute-start.21 = (s32[776,128]{1,0:T(8,128)}, s32[776,128]{1,0:T(8,128)}, u32[]{:S(2)}, u32[]{:S(2)}) collective-permute-start(s32[776,128]{1,0:T(8,128)} %get-tuple-element.38), channel_id=1, source_target_pairs={{0,4},{4,0},{8,12},{12,8},{1,5},{5,1},{9,13},{13,9},{2,6},{6,2},{1... | collective-permute-start | bytes 1191944 | tf_op jit(solution)/shard_map/ppermute | solution.py:441
  110.0 0.8 copy-start.1
  127.2 35.2 %collective-permute-start.17 = (s32[776,128]{1,0:T(8,128)}, s32[776,128]{1,0:T(8,128)S(1)}, u32[]{:S(2)}, u32[]{:S(2)}) collective-permute-start(s32[776,128]{1,0:T(8,128)} %get-tuple-element.34), channel_id=1, source_target_pairs={{0,12},{4,8},{8,4},{12,0},{1,13},{5,9},{9,5},{13,1},{2,14},{6,10},... | collective-permute-start | bytes 1191944 | tf_op jit(solution)/shard_map/ppermute | solution.py:441
  127.8 34.6 %collective-permute-start.18 = (s32[776,128]{1,0:T(8,128)}, s32[776,128]{1,0:T(8,128)}, u32[]{:S(2)}, u32[]{:S(2)}) collective-permute-start(s32[776,128]{1,0:T(8,128)} %get-tuple-element.35), channel_id=1, source_target_pairs={{0,8},{4,12},{8,0},{12,4},{1,9},{5,13},{9,1},{13,5},{2,10},{6,14},... | collective-permute-start | bytes 1191944 | tf_op jit(solution)/shard_map/ppermute | solution.py:441
  127.8 34.6 %collective-permute-start.19 = (s32[776,128]{1,0:T(8,128)}, s32[776,128]{1,0:T(8,128)}, u32[]{:S(2)}, u32[]{:S(2)}) collective-permute-start(s32[776,128]{1,0:T(8,128)} %get-tuple-element.36), channel_id=1, source_target_pairs={{0,4},{4,0},{8,12},{12,8},{1,5},{5,1},{9,13},{13,9},{2,6},{6,2},{1... | collective-permute-start | bytes 1191944 | tf_op jit(solution)/shard_map/ppermute | solution.py:441
  162.4 0.7 copy-start.3

commit v7 on v6

--- a/solution.py
+++ b/solution.py
@@ -36,12 +36,12 @@
     return jnp.max(jnp.abs(v), axis=1, keepdims=True)
 
 
-def store_words(out_ref, layer, v, gain):
+def store_words(out_ref, layer, v, gain, base=0):
     rows, width = v.shape
     half, tiles = rows // 2, width // LANES
     words = pair(jnp.floor(v * gain + 0.5).astype(jnp.int32))
     for tile in range(tiles):
-        start = (layer * tiles + tile) * half
+        start = base + (layer * tiles + tile) * half
         out_ref[start : start + half, :] = words[:, tile * LANES : (tile + 1) * LANES]
 
 
@@ -110,11 +110,11 @@
     )(errors, *join, *after)
 
 
-def terms_kernel(n_tgt, plan, offset, *refs):
+def terms_kernel(n_tgt, plan, offset, carried, *refs):
     n_pieces = 1 + max(entry[0] for entry in plan)
     pieces = refs[:n_pieces]
     dec_ref = refs[n_pieces]
-    own_ref, near_ref, across_ref, far_ref, all_ref, err, dec, acc, in_sem, dec_sem, own_sem, out_sem = refs[-12:]
+    own_ref, near_ref, across_ref, far_ref, all_ref, err, dec, acc, in_sem, dec_sem, own_sem, out_sem, carry_sem = refs[-13:]
     layers, tgt_count, width, columns = dec_ref.shape
     total_rows = err.shape[0]
     rows = total_rows // n_tgt
@@ -147,6 +147,7 @@
     def own_copy(layer):
         return pltpu.make_async_copy(acc.at[layer, block(tgt), :], own_ref.at[layer], own_sem.at[layer])
 
+    carry = pltpu.make_async_copy(refs[n_pieces + 1], near_ref.at[pl.ds(0, carried), :], carry_sem) if carried else None
     out_copy = pltpu.make_async_copy(err, all_ref.at[pl.ds(offset, total_rows), :], out_sem)
 
     for t in range(tgt_count):
@@ -154,6 +155,8 @@
     copies = [copy for index in range(len(plan)) for copy in piece_copies(index)]
     for copy in copies:
         copy.start()
+    if carried:
+        carry.start()
     for layer in range(1, layers):
         for t in range(tgt_count):
             dec_copy(layer, t).start()
@@ -188,7 +191,7 @@
         scale_words = pair(scale)
         for index, flip in enumerate(flips):
             v, factor = acc[layer, block(tgt ^ flip), :], gain[:, index : index + 1]
-            store_words(flips[flip], layer, v, factor)
+            store_words(flips[flip], layer, v, factor, carried if flip == 1 else 0)
             for group in range(half // SUBLANES):
                 piece = scale_words[group * SUBLANES : (group + 1) * SUBLANES, index : index + 1]
                 tails[index] = jnp.where(small == group * layers + layer, piece, tails[index])
@@ -203,21 +206,24 @@
     for layer in range(layers):
         own_copy(layer).wait()
     out_copy.wait()
-
-
-def terms_call(pieces, plan, decoder, everything, offset, n_tgt, total_rows, tokens, after):
+    if carried:
+        carry.wait()
+
+
+def terms_call(pieces, plan, decoder, carry, everything, offset, n_tgt, total_rows, tokens, after):
     layers, tgt_count, width, columns = decoder.shape
     rows = total_rows // n_tgt
     payload = (payload_rows(layers, rows, width), LANES)
     whole = pl.BlockSpec(memory_space=pltpu.VMEM)
-    operands = [*pieces, decoder]
+    operands = [*pieces, decoder, *carry]
+    carried = sum(x.shape[0] for x in carry)
     aliases = {}
     if everything is not None:
         aliases = {len(operands): 4}
         operands.append(everything)
     operands += after
     return pl.pallas_call(
-        functools.partial(terms_kernel, n_tgt, plan, offset),
+        functools.partial(terms_kernel, n_tgt, plan, offset, carried),
         in_specs=[ANYWHERE] * len(operands),
         out_specs=[ANYWHERE, whole, whole, whole, ANYWHERE],
         scratch_shapes=[
@@ -228,10 +234,11 @@
             pltpu.SemaphoreType.DMA((layers * tgt_count,)),
             pltpu.SemaphoreType.DMA((layers,)),
             pltpu.SemaphoreType.DMA,
+            pltpu.SemaphoreType.DMA,
         ],
         out_shape=[
             jax.ShapeDtypeStruct((layers, rows, width), jnp.float32),
-            jax.ShapeDtypeStruct(payload, jnp.int32),
+            jax.ShapeDtypeStruct((carried + payload[0], LANES), jnp.int32),
             jax.ShapeDtypeStruct(payload, jnp.int32),
             jax.ShapeDtypeStruct(payload, jnp.int32),
             jax.ShapeDtypeStruct((tokens, tgt_count * columns), jnp.bfloat16),
@@ -286,8 +293,11 @@
     layers, rows, width = own.shape
     parts = mask.shape[1] // stride
     in_specs = [pl.BlockSpec((layers, rows, width), lambda i: (0, 0, 0))]
-    in_specs += [pl.BlockSpec(gots[-1].shape, lambda i: (0, 0)) for got in gots]
+    in_specs += [
+        pl.BlockSpec((payload_rows(layers, rows, width), LANES), lambda i, place=place: (place, 0)) for _, place in gots
+    ]
     in_specs.append(ANYWHERE)
+    gots = [got for got, _ in gots]
     operands = [own, *gots, mask]
     aliases = {}
     if out is not None:
@@ -423,29 +433,39 @@
     gather = gather_pieces(errors, spans, offsets, n_src, n_feat, codes_t)
     pieces, plan = next(gather)
     last = len(spans) - 1
+    join_near = last > 0 and spans[-1] == spans[-2]
     owns, gots = [], []
-    everything = None
+    carry, everything = [], None
+    send = lambda x, flip: lax.ppermute(x, "tgt", [(i, i ^ flip) for i in range(n_tgt)])
     for index, span in enumerate(spans):
         own, near, across, far, everything = terms_call(
             pieces,
             plan,
             decoder,
+            carry,
             everything,
             n_feat * offsets[index],
             n_tgt,
             n_feat * span,
             n_feat * stride,
-            gots[index - 1][:1] if index > 1 else [],
+            [],
         )
         owns.append(own)
-        send = lambda x, flip: lax.ppermute(x, "tgt", [(i, i ^ flip) for i in range(n_tgt)])
-        gots.append([send(far, 3), send(across, 2), send(near, 1)])
+        gots.append([(send(far, 3), 0), (send(across, 2), 0)])
+        if join_near and index == last - 1:
+            carry = [near]
+        else:
+            got_near = send(near, 1)
+            if join_near and index == last:
+                gots[last - 1].append((got_near, 0))
+            gots[index].append((got_near, len(carry)))
         if index < last:
-            pieces, plan = gather.send([own] + (gots[index - 1] if index else gots[0][:1]))
+            before = [gots[0][2]] if index == 0 else gots[index - 1][:2]
+            pieces, plan = gather.send([own] + [got for got, _ in before])
     decoder_grads = grads_call(codes_t, everything, decoder.shape, [])
     code_grads = None
     for index in range(len(spans)):
-        after = [] if index else [decoder_grads]
+        after = [] if index else [decoder_grads] + [got for group in gots[1:last] for got, _ in group[:2]]
         code_grads = finish_call(owns[index], gots[index], active_mask, code_grads, offsets[index], stride, after)
     return code_grads, decoder_grads
 

time: 168 us -> 158 us (0.940)
  the two profiles are of different devices: /device:TPU:8 before, /device:TPU:0 now
where the time goes in v7:
time: 158 us
  Pallas kernels  92.4 us (58%)
  waiting for transfers between devices  40.9 us (26%)
  starting transfers between devices  22.6 us (14%)
    pallas_call x3, Pallas kernels, terms_call(): pl.pallas_call(functools.partial(terms_kernel, n_tgt, plan, offset, carri...  48.1 us
    ppermute x8, waiting for transfers between devices, body(): lax.ppermute(x, 'tgt', [(i, i ^ flip) for i in range(n_tgt)])  30.1 us
    pallas_call x1, Pallas kernels, grads_call(): pl.pallas_call(grads_kernel, grid=(tgt_count, layers), in_specs=in_specs...  19.4 us
    ppermute x9, starting transfers between devices, gather_pieces(): lax.ppermute(x, axes, [(i, i ^ flip) for i in range(n_src * n_feat)])  11.3 us
    pallas_call x3, Pallas kernels, finish_call(): pl.pallas_call(functools.partial(finish_kernel, len(gots), offset, stride...  10.9 us
    ppermute x8, starting transfers between devices, body(): lax.ppermute(x, 'tgt', [(i, i ^ flip) for i in range(n_tgt)])  10.6 us
    ppermute x9, waiting for transfers between devices, gather_pieces(): lax.ppermute(x, axes, [(i, i ^ flip) for i in range(n_src * n_feat)])  9.74 us
    pallas_call x4, Pallas kernels, cut_call(): pl.pallas_call(functools.partial(cut_kernel, len(join), offset), in_specs...  8.75 us
  transfers between devices with their start and end apart: 21, of which 10 were waited for; matrix products, arithmetic and copies ran while one was open for 0% of the time, Pallas kernels for 52%

profile of v7, /device:TPU:0, one launch (start us, length us, event | category | flops | bytes accessed | tf_op | source)
XLA Modules:
  0.0 157.7 jit_solution(510780101149509950)
XLA Ops:
  0.6 0.5 collective-permute-start
  1.1 1.7 %cut.4 = bf16[2,64,1024]{2,1,0:T(8,128)(2,1)} custom-call(bf16[2,256,1024]{2,1,0:T(8,128)(2,1)} %refs_0_.5), custom_call_target="tpu_custom_call" | custom-call | bytes 262144 | tf_op jit(solution)/shard_map/cut/pallas_call | solution.py:101
  2.8 3.5 %collective-permute-start.3 = (bf16[2,64,1024]{2,1,0:T(8,128)(2,1)}, bf16[2,64,1024]{2,1,0:T(8,128)(2,1)S(1)}, u32[]{:S(2)}, u32[]{:S(2)}) collective-permute-start(bf16[2,64,1024]{2,1,0:T(8,128)(2,1)} %cut.4), channel_id=1, source_target_pairs={{0,18},{1,19},{2,16},{3,17},{16,2},{17,3},{18,0},{19,1},{4,22},{5,... | collective-permute-start | bytes 786440 | tf_op jit(solution)/shard_map/ppermute | solution.py:406
  6.3 0.5 collective-permute-start.2
  6.8 0.1 collective-permute-start.1
  7.0 5.3 %turn.1.refs_4_.codes_ref = bf16[4,512,1024]{2,1,0:T(8,128)(2,1)} custom-call(bf16[4,1024,512]{2,1,0:T(8,128)(2,1)} %codes_ref.1), custom_call_target="tpu_custom_call" | custom-call | flops 1048576 | bytes 4194304 | tf_op jit(solution)/shard_map/turn/pallas_call | solution.py:344
  12.3 1.5 collective-permute-done.3.refs_2_
  13.8 0.0 copy-start.3
  13.8 5.5 %collective-permute-done.2.refs_1_ = bf16[2,64,1024]{2,1,0:T(8,128)(2,1)} collective-permute-done((bf16[2,64,1024]{2,1,0:T(8,128)(2,1)}, bf16[2,64,1024]{2,1,0:T(8,128)(2,1)}, u32[]{:S(2)}, u32[]{:S(2)}) %collective-permute-start.2) | collective-permute-done | bytes 262176 | tf_op jit(solution)/shard_map/ppermute | solution.py:406
  19.2 0.3 collective-permute-done.1.refs_0_
  19.5 0.0 collective-permute-done.refs_3_.refs_1_
  19.5 0.0 copy-done.3
  19.5 2.3 %cut.5 = (bf16[3,2,64,1024]{3,2,1,0:T(8,128)(2,1)}, bf16[2,96,1024]{2,1,0:T(8,128)(2,1)}) custom-call(bf16[2,256,1024]{2,1,0:T(8,128)(2,1)} %refs_0_.5, bf16[2,64,1024]{2,1,0:T(8,128)(2,1)} %collective-permute-done.1.refs_0_, bf16[2,64,1024]{2,1,0:T(8,128)(2,1)} %collective-permute-done.2.refs_1_, bf16[2,64,1024]{2,1,0:T(8,128)(2,1)} %copy-done.3, ...), custom_call_target="tpu_custom_call" | custom-call | bytes 1179648 | tf_op jit(solution)/shard_map/cut/pallas_call | solution.py:101
  21.8 0.1 collective-permute-start.7
  21.9 1.6 %collective-permute-start.6 = (bf16[2,96,1024]{2,1,0:T(8,128)(2,1)}, bf16[2,96,1024]{2,1,0:T(8,128)(2,1)}, u32[]{:S(2)}, u32[]{:S(2)}) collective-permute-start(bf16[2,96,1024]{2,1,0:T(8,128)(2,1)} %get-tuple-element.21), channel_id=1, source_target_pairs={{0,18},{1,19},{2,16},{3,17},{16,2},{17,3},{18,0},{19,1},{4,22},{5,... | collective-permute-start | bytes 1179656 | tf_op jit(solution)/shard_map/ppermute | solution.py:406
  23.5 1.4 collective-permute-start.5
  24.9 0.5 collective-permute-start.4
  25.5 0.0 collective-permute-done.7.refs_3_
  25.5 14.0 %terms.3 = (f32[4,64,512]{2,1,0:T(8,128)}, s32[520,128]{1,0:T(8,128)}, s32[520,128]{1,0:T(8,128)}, s32[520,128]{1,0:T(8,128)}, bf16[1024,4096]{1,0:T(8,128)(2,1)}) custom-call(bf16[2,256,1024]{2,1,0:T(8,128)(2,1)} %refs_0_.5, bf16[2,256,1024]{2,1,0:T(8,128)(2,1)} %collective-permute-done.refs_3_.refs_1_, bf16[3,2,64,1024]{3,2,1,0:T(8,128)(2,1)} %get-tuple-element.22.refs_2_, ...), custom_call_target="tpu_custom_call" | custom-call | flops 2147483648 | bytes 8388608 | tf_op jit(solution)/shard_map/terms/pallas_call | solution.py:225
  39.5 1.1 collective-permute-start.8
  40.6 0.0 collective-permute-done.6.refs_2_
  40.6 2.5 %collective-permute-done.5.refs_1_ = bf16[2,96,1024]{2,1,0:T(8,128)(2,1)} collective-permute-done((bf16[2,96,1024]{2,1,0:T(8,128)(2,1)}, bf16[2,96,1024]{2,1,0:T(8,128)(2,1)}, u32[]{:S(2)}, u32[]{:S(2)}) %collective-permute-start.5) | collective-permute-done | bytes 393248 | tf_op jit(solution)/shard_map/ppermute | solution.py:406
  43.1 0.0 collective-permute-done.4.refs_0_
  43.1 4.6 %collective-permute-done.8.refs_4_.refs_2_ = s32[520,128]{1,0:T(8,128)S(1)} collective-permute-done((s32[520,128]{1,0:T(8,128)}, s32[520,128]{1,0:T(8,128)S(1)}, u32[]{:S(2)}, u32[]{:S(2)}) %collective-permute-start.8) | collective-permute-done | bytes 266272 | tf_op jit(solution)/shard_map/ppermute | solution.py:439
  47.7 0.0 copy-start.1
  47.7 0.7 copy-done.1
  48.4 2.5 %cut.6 = (bf16[3,2,96,1024]{3,2,1,0:T(8,128)(2,1)}, bf16[2,96,1024]{2,1,0:T(8,128)(2,1)}) custom-call(bf16[2,256,1024]{2,1,0:T(8,128)(2,1)} %refs_0_.5, bf16[2,96,1024]{2,1,0:T(8,128)(2,1)} %collective-permute-done.4.refs_0_, bf16[2,96,1024]{2,1,0:T(8,128)(2,1)} %collective-permute-done.5.refs_1_, bf16[2,96,1024]{2,1,0:T(8,128)(2,1)} %collective-permute-done.6.refs_2_, ...), custom_call_target="tpu_custom_call" | custom-call | bytes 1572864 | tf_op jit(solution)/shard_map/cut/pallas_call | solution.py:101
  50.9 0.1 collective-permute-start.12
  51.0 2.0 %collective-permute-start.11 = (bf16[2,96,1024]{2,1,0:T(8,128)(2,1)}, bf16[2,96,1024]{2,1,0:T(8,128)(2,1)}, u32[]{:S(2)}, u32[]{:S(2)}) collective-permute-start(bf16[2,96,1024]{2,1,0:T(8,128)(2,1)} %get-tuple-element.25), channel_id=1, source_target_pairs={{0,18},{1,19},{2,16},{3,17},{16,2},{17,3},{18,0},{19,1},{4,22},{5,... | collective-permute-start | bytes 1179656 | tf_op jit(solution)/shard_map/ppermute | solution.py:406
  53.0 1.4 collective-permute-start.10
  54.4 0.1 collective-permute-start.9
  54.5 2.9 %collective-permute-start.13 = (s32[520,128]{1,0:T(8,128)}, s32[520,128]{1,0:T(8,128)S(1)}, u32[]{:S(2)}, u32[]{:S(2)}) collective-permute-start(s32[520,128]{1,0:T(8,128)} %get-tuple-element.29), channel_id=1, source_target_pairs={{0,12},{4,8},{8,4},{12,0},{1,13},{5,9},{9,5},{13,1},{2,14},{6,10},... | collective-permute-start | bytes 798728 | tf_op jit(solution)/shard_map/ppermute | solution.py:439
  57.5 0.0 collective-permute-done.12.refs_3_
  57.5 0.0 collective-permute-start.14
  57.5 16.9 %terms.4 = (f32[4,96,512]{2,1,0:T(8,128)}, s32[776,128]{1,0:T(8,128)}, s32[776,128]{1,0:T(8,128)}, s32[776,128]{1,0:T(8,128)}, bf16[1024,4096]{1,0:T(8,128)(2,1)}) custom-call(bf16[2,256,1024]{2,1,0:T(8,128)(2,1)} %refs_0_.5, bf16[2,256,1024]{2,1,0:T(8,128)(2,1)} %collective-permute-done.refs_3_.refs_1_, ...), custom_call_target="tpu_custom_call", output_to_operand_aliasing={{4}: (5, {})} | custom-call | flops 3221225472 | bytes 8388608 | tf_op jit(solution)/shard_map/terms/pallas_call | solution.py:225
  74.4 0.0 collective-permute-done.13.refs_4_.refs_0_
  74.4 0.0 copy-start.2
  74.4 6.6 %collective-permute-done.14.refs_5_.refs_1_ = s32[520,128]{1,0:T(8,128)} collective-permute-done((s32[520,128]{1,0:T(8,128)}, s32[520,128]{1,0:T(8,128)}, u32[]{:S(2)}, u32[]{:S(2)}) %collective-permute-start.14) | collective-permute-done | bytes 266272 | tf_op jit(solution)/shard_map/ppermute | solution.py:439
  81.0 0.0 collective-permute-done.11.refs_2_
  81.0 0.0 collective-permute-done.10.refs_1_
  81.0 0.0 collective-permute-done.9.refs_0_
  81.0 0.0 copy-done.2
  81.1 2.3 %cut.7.refs_2_ = bf16[3,2,96,1024]{3,2,1,0:T(8,128)(2,1)} custom-call(bf16[2,256,1024]{2,1,0:T(8,128)(2,1)} %refs_0_.5, bf16[2,96,1024]{2,1,0:T(8,128)(2,1)} %collective-permute-done.9.refs_0_, bf16[2,96,1024]{2,1,0:T(8,128)(2,1)} %collective-permute-done.10.refs_1_, bf16[2,96,1024]{2,1,0:T(8,128)(2,1)} %collective-permute-done.11.refs_2_, ...), custom_call_target="tpu_custom_call" | custom-call | bytes 1179648 | tf_op jit(solution)/shard_map/cut/pallas_call | solution.py:101
  83.3 0.1 collective-permute-start.15
  83.4 2.1 %collective-permute-start.19 = (s32[776,128]{1,0:T(8,128)}, s32[776,128]{1,0:T(8,128)S(1)}, u32[]{:S(2)}, u32[]{:S(2)}) collective-permute-start(s32[776,128]{1,0:T(8,128)} %get-tuple-element.37), channel_id=1, source_target_pairs={{0,12},{4,8},{8,4},{12,0},{1,13},{5,9},{9,5},{13,1},{2,14},{6,10},... | collective-permute-start | bytes 1191944 | tf_op jit(solution)/shard_map/ppermute | solution.py:439
  85.6 0.0 collective-permute-start.20
  85.6 1.0 collective-permute-done.15.refs_3_
  86.6 17.2 %terms.5 = (f32[4,96,512]{2,1,0:T(8,128)}, s32[1552,128]{1,0:T(8,128)}, s32[776,128]{1,0:T(8,128)}, s32[776,128]{1,0:T(8,128)}, bf16[1024,4096]{1,0:T(8,128)(2,1)}) custom-call(bf16[2,256,1024]{2,1,0:T(8,128)(2,1)} %refs_0_.5, bf16[2,256,1024]{2,1,0:T(8,128)(2,1)} %collective-permute-done.refs_3_.refs_1_, ...), custom_call_target="tpu_custom_call", output_to_operand_aliasing={{4}: (6, {})} | custom-call | flops 3221225472 | bytes 8388608 | tf_op jit(solution)/shard_map/terms/pallas_call | solution.py:225
  103.8 1.5 collective-permute-start.16
  105.2 0.8 collective-permute-start.17
  106.1 2.2 %collective-permute-start.18 = (s32[1552,128]{1,0:T(8,128)}, s32[1552,128]{1,0:T(8,128)}, u32[]{:S(2)}, u32[]{:S(2)}) collective-permute-start(s32[1552,128]{1,0:T(8,128)} %get-tuple-element.36), channel_id=1, source_target_pairs={{0,4},{4,0},{8,12},{12,8},{1,5},{5,1},{9,13},{13,9},{2,6},{6,2},{1... | collective-permute-start | bytes 2383880 | tf_op jit(solution)/shard_map/ppermute | solution.py:439
  108.2 19.4 %grads.1.refs_4_ = bf16[4,2,512,2048]{3,2,1,0:T(8,128)(2,1)} custom-call(bf16[4,512,1024]{2,1,0:T(8,128)(2,1)} %turn.1.refs_4_.codes_ref, bf16[1024,4096]{1,0:T(8,128)(2,1)} %get-tuple-element.39.err_ref), custom_call_target="tpu_custom_call" | custom-call | flops 8589934592 | bytes 12582912 | tf_op jit(solution)/shard_map/grads/pallas_call | solution.py:383
  127.6 0.0 collective-permute-done.19.refs_5_.refs_0_
  127.6 0.0 copy-start
  127.6 9.5 %collective-permute-done.20.refs_6_.refs_1_ = s32[776,128]{1,0:T(8,128)} collective-permute-done((s32[776,128]{1,0:T(8,128)}, s32[776,128]{1,0:T(8,128)}, u32[]{:S(2)}, u32[]{:S(2)}) %collective-permute-start.20) | collective-permute-done | bytes 397344 | tf_op jit(solution)/shard_map/ppermute | solution.py:439
  137.1 0.0 copy-done
  137.1 3.3 %finish.3.refs_4_ = bf16[4,256,512]{2,1,0:T(8,128)(2,1)} custom-call(f32[4,64,512]{2,1,0:T(8,128)} %get-tuple-element.23.refs_3_.own_ref, s32[520,128]{1,0:T(8,128)} %copy-done.2, s32[520,128]{1,0:T(8,128)} %collective-permute-done.14.refs_5_.refs_1_, s32[520,128]{1,0:T(8,128)} %copy-done.1, s32[4,256,512]{2,1,0:T(8,128)} %refs_3_.5, ...), custom_call_target="tpu_custom_call" | custom-call | flops 1310720 | bytes 1048576 | tf_op jit(solution)/shard_map/finish/pallas_call | solution.py:309
  140.5 2.4 %collective-permute-done.18.refs_2_ = s32[1552,128]{1,0:T(8,128)} collective-permute-done((s32[1552,128]{1,0:T(8,128)}, s32[1552,128]{1,0:T(8,128)}, u32[]{:S(2)}, u32[]{:S(2)}) %collective-permute-start.18) | collective-permute-done | bytes 794656 | tf_op jit(solution)/shard_map/ppermute | solution.py:439
  142.8 3.8 %finish.4.refs_4_ = bf16[4,256,512]{2,1,0:T(8,128)(2,1)} custom-call(f32[4,96,512]{2,1,0:T(8,128)} %get-tuple-element.28.refs_3_.own_ref, s32[776,128]{1,0:T(8,128)} %copy-done, s32[776,128]{1,0:T(8,128)} %collective-permute-done.20.refs_6_.refs_1_, s32[1552,128]{1,0:T(8,128)} %collective-permute-done.18.refs_2_, ...), custom_call_target="tpu_custom_call", output_to_operand_aliasing={{}: (5, {})} | custom-call | flops 1966080 | bytes 1572864 | tf_op jit(solution)/shard_map/finish/pallas_call | solution.py:309
  146.6 0.0 collective-permute-done.16.refs_0_
  146.6 7.1 %collective-permute-done.17.refs_1_ = s32[776,128]{1,0:T(8,128)} collective-permute-done((s32[776,128]{1,0:T(8,128)}, s32[776,128]{1,0:T(8,128)}, u32[]{:S(2)}, u32[]{:S(2)}) %collective-permute-start.17) | collective-permute-done | bytes 397344 | tf_op jit(solution)/shard_map/ppermute | solution.py:439
  153.7 3.8 %finish.5 = bf16[4,256,512]{2,1,0:T(8,128)(2,1)} custom-call(f32[4,96,512]{2,1,0:T(8,128)} %get-tuple-element.33.own_ref, s32[776,128]{1,0:T(8,128)} %collective-permute-done.16.refs_0_, s32[776,128]{1,0:T(8,128)} %collective-permute-done.17.refs_1_, s32[1552,128]{1,0:T(8,128)} %collective-permute-done.18.refs_2_, ...), custom_call_target="tpu_custom_call", output_to_operand_aliasing={{}: (5, {})} | custom-call | flops 1966080 | bytes 1572864 | tf_op jit(solution)/shard_map/finish/pallas_call | solution.py:309
Async XLA Ops:
  0.6 18.9 %collective-permute-start = (bf16[2,256,1024]{2,1,0:T(8,128)(2,1)}, bf16[2,256,1024]{2,1,0:T(8,128)(2,1)}, u32[]{:S(2)}, u32[]{:S(2)}) collective-permute-start(bf16[2,256,1024]{2,1,0:T(8,128)(2,1)} %refs_0_.5), channel_id=1, source_target_pairs={{0,1},{1,0},{2,3},{3,2},{4,5},{5,4},{6,7},{7,6},{8,9},{9,8},{10,11... | collective-permute-start | bytes 3145736 | tf_op jit(solution)/shard_map/ppermute | solution.py:424
  2.8 10.9 %collective-permute-start.3 = (bf16[2,64,1024]{2,1,0:T(8,128)(2,1)}, bf16[2,64,1024]{2,1,0:T(8,128)(2,1)S(1)}, u32[]{:S(2)}, u32[]{:S(2)}) collective-permute-start(bf16[2,64,1024]{2,1,0:T(8,128)(2,1)} %cut.4), channel_id=1, source_target_pairs={{0,18},{1,19},{2,16},{3,17},{16,2},{17,3},{18,0},{19,1},{4,22},{5,... | collective-permute-start | bytes 786440 | tf_op jit(solution)/shard_map/ppermute | solution.py:406
  6.3 12.9 %collective-permute-start.2 = (bf16[2,64,1024]{2,1,0:T(8,128)(2,1)}, bf16[2,64,1024]{2,1,0:T(8,128)(2,1)}, u32[]{:S(2)}, u32[]{:S(2)}) collective-permute-start(bf16[2,64,1024]{2,1,0:T(8,128)(2,1)} %cut.4), channel_id=1, source_target_pairs={{0,2},{1,3},{2,0},{3,1},{16,18},{17,19},{18,16},{19,17},{4,6},{5,7... | collective-permute-start | bytes 786440 | tf_op jit(solution)/shard_map/ppermute | solution.py:406
  6.8 12.7 %collective-permute-start.1 = (bf16[2,64,1024]{2,1,0:T(8,128)(2,1)}, bf16[2,64,1024]{2,1,0:T(8,128)(2,1)}, u32[]{:S(2)}, u32[]{:S(2)}) collective-permute-start(bf16[2,64,1024]{2,1,0:T(8,128)(2,1)} %cut.4), channel_id=1, source_target_pairs={{0,16},{1,17},{2,18},{3,19},{16,0},{17,1},{18,2},{19,3},{4,20},{5,... | collective-permute-start | bytes 786440 | tf_op jit(solution)/shard_map/ppermute | solution.py:406
  13.8 5.8 %copy-start.3 = (bf16[2,64,1024]{2,1,0:T(8,128)(2,1)}, bf16[2,64,1024]{2,1,0:T(8,128)(2,1)S(1)}, u32[]{:S(2)}) copy-start(bf16[2,64,1024]{2,1,0:T(8,128)(2,1)S(1)} %collective-permute-done.3.refs_2_) | copy-start | bytes 786436
  21.8 3.6 %collective-permute-start.7 = (bf16[3,2,64,1024]{3,2,1,0:T(8,128)(2,1)}, bf16[3,2,64,1024]{3,2,1,0:T(8,128)(2,1)}, u32[]{:S(2)}, u32[]{:S(2)}) collective-permute-start(bf16[3,2,64,1024]{3,2,1,0:T(8,128)(2,1)} %get-tuple-element.22.refs_2_), channel_id=1, source_target_pairs={{0,1},{1,0},{2,3},{3,2},{4,5},{5,4},{6,7},{7,6},{8,9},{9,8},{10,11... | collective-permute-start | bytes 2359304 | tf_op jit(solution)/shard_map/ppermute | solution.py:424
  21.9 18.7 %collective-permute-start.6 = (bf16[2,96,1024]{2,1,0:T(8,128)(2,1)}, bf16[2,96,1024]{2,1,0:T(8,128)(2,1)}, u32[]{:S(2)}, u32[]{:S(2)}) collective-permute-start(bf16[2,96,1024]{2,1,0:T(8,128)(2,1)} %get-tuple-element.21), channel_id=1, source_target_pairs={{0,18},{1,19},{2,16},{3,17},{16,2},{17,3},{18,0},{19,1},{4,22},{5,... | collective-permute-start | bytes 1179656 | tf_op jit(solution)/shard_map/ppermute | solution.py:406
  23.5 19.6 %collective-permute-start.5 = (bf16[2,96,1024]{2,1,0:T(8,128)(2,1)}, bf16[2,96,1024]{2,1,0:T(8,128)(2,1)}, u32[]{:S(2)}, u32[]{:S(2)}) collective-permute-start(bf16[2,96,1024]{2,1,0:T(8,128)(2,1)} %get-tuple-element.21), channel_id=1, source_target_pairs={{0,2},{1,3},{2,0},{3,1},{16,18},{17,19},{18,16},{19,17},{4,6},{5,7... | collective-permute-start | bytes 1179656 | tf_op jit(solution)/shard_map/ppermute | solution.py:406
  24.9 18.2 %collective-permute-start.4 = (bf16[2,96,1024]{2,1,0:T(8,128)(2,1)}, bf16[2,96,1024]{2,1,0:T(8,128)(2,1)}, u32[]{:S(2)}, u32[]{:S(2)}) collective-permute-start(bf16[2,96,1024]{2,1,0:T(8,128)(2,1)} %get-tuple-element.21), channel_id=1, source_target_pairs={{0,16},{1,17},{2,18},{3,19},{16,0},{17,1},{18,2},{19,3},{4,20},{5,... | collective-permute-start | bytes 1179656 | tf_op jit(solution)/shard_map/ppermute | solution.py:406
  39.5 8.2 %collective-permute-start.8 = (s32[520,128]{1,0:T(8,128)}, s32[520,128]{1,0:T(8,128)S(1)}, u32[]{:S(2)}, u32[]{:S(2)}) collective-permute-start(s32[520,128]{1,0:T(8,128)} %get-tuple-element.24), channel_id=1, source_target_pairs={{0,4},{4,0},{8,12},{12,8},{1,5},{5,1},{9,13},{13,9},{2,6},{6,2},{1... | collective-permute-start | bytes 798728 | tf_op jit(solution)/shard_map/ppermute | solution.py:439
  47.7 0.7 copy-start.1
  50.9 6.6 %collective-permute-start.12 = (bf16[3,2,96,1024]{3,2,1,0:T(8,128)(2,1)}, bf16[3,2,96,1024]{3,2,1,0:T(8,128)(2,1)}, u32[]{:S(2)}, u32[]{:S(2)}) collective-permute-start(bf16[3,2,96,1024]{3,2,1,0:T(8,128)(2,1)} %get-tuple-element.26.refs_2_), channel_id=1, source_target_pairs={{0,1},{1,0},{2,3},{3,2},{4,5},{5,4},{6,7},{7,6},{8,9},{9,8},{10,11... | collective-permute-start | bytes 3538952 | tf_op jit(solution)/shard_map/ppermute | solution.py:424
  51.0 30.1 %collective-permute-start.11 = (bf16[2,96,1024]{2,1,0:T(8,128)(2,1)}, bf16[2,96,1024]{2,1,0:T(8,128)(2,1)}, u32[]{:S(2)}, u32[]{:S(2)}) collective-permute-start(bf16[2,96,1024]{2,1,0:T(8,128)(2,1)} %get-tuple-element.25), channel_id=1, source_target_pairs={{0,18},{1,19},{2,16},{3,17},{16,2},{17,3},{18,0},{19,1},{4,22},{5,... | collective-permute-start | bytes 1179656 | tf_op jit(solution)/shard_map/ppermute | solution.py:406
  53.0 28.1 %collective-permute-start.10 = (bf16[2,96,1024]{2,1,0:T(8,128)(2,1)}, bf16[2,96,1024]{2,1,0:T(8,128)(2,1)}, u32[]{:S(2)}, u32[]{:S(2)}) collective-permute-start(bf16[2,96,1024]{2,1,0:T(8,128)(2,1)} %get-tuple-element.25), channel_id=1, source_target_pairs={{0,2},{1,3},{2,0},{3,1},{16,18},{17,19},{18,16},{19,17},{4,6},{5,7... | collective-permute-start | bytes 1179656 | tf_op jit(solution)/shard_map/ppermute | solution.py:406
  54.4 26.6 %collective-permute-start.9 = (bf16[2,96,1024]{2,1,0:T(8,128)(2,1)}, bf16[2,96,1024]{2,1,0:T(8,128)(2,1)}, u32[]{:S(2)}, u32[]{:S(2)}) collective-permute-start(bf16[2,96,1024]{2,1,0:T(8,128)(2,1)} %get-tuple-element.25), channel_id=1, source_target_pairs={{0,16},{1,17},{2,18},{3,19},{16,0},{17,1},{18,2},{19,3},{4,20},{5,... | collective-permute-start | bytes 1179656 | tf_op jit(solution)/shard_map/ppermute | solution.py:406
  54.5 19.9 %collective-permute-start.13 = (s32[520,128]{1,0:T(8,128)}, s32[520,128]{1,0:T(8,128)S(1)}, u32[]{:S(2)}, u32[]{:S(2)}) collective-permute-start(s32[520,128]{1,0:T(8,128)} %get-tuple-element.29), channel_id=1, source_target_pairs={{0,12},{4,8},{8,4},{12,0},{1,13},{5,9},{9,5},{13,1},{2,14},{6,10},... | collective-permute-start | bytes 798728 | tf_op jit(solution)/shard_map/ppermute | solution.py:439
  57.5 23.6 %collective-permute-start.14 = (s32[520,128]{1,0:T(8,128)}, s32[520,128]{1,0:T(8,128)}, u32[]{:S(2)}, u32[]{:S(2)}) collective-permute-start(s32[520,128]{1,0:T(8,128)} %get-tuple-element.30), channel_id=1, source_target_pairs={{0,8},{4,12},{8,0},{12,4},{1,9},{5,13},{9,1},{13,5},{2,10},{6,14},... | collective-permute-start | bytes 798728 | tf_op jit(solution)/shard_map/ppermute | solution.py:439
  74.4 6.6 %copy-start.2 = (s32[520,128]{1,0:T(8,128)}, s32[520,128]{1,0:T(8,128)S(1)}, u32[]{:S(2)}) copy-start(s32[520,128]{1,0:T(8,128)S(1)} %collective-permute-done.13.refs_4_.refs_0_) | copy-start | bytes 798724
  83.3 3.3 %collective-permute-start.15 = (bf16[3,2,96,1024]{3,2,1,0:T(8,128)(2,1)}, bf16[3,2,96,1024]{3,2,1,0:T(8,128)(2,1)}, u32[]{:S(2)}, u32[]{:S(2)}) collective-permute-start(bf16[3,2,96,1024]{3,2,1,0:T(8,128)(2,1)} %cut.7.refs_2_), channel_id=1, source_target_pairs={{0,1},{1,0},{2,3},{3,2},{4,5},{5,4},{6,7},{7,6},{8,9},{9,8},{10,11... | collective-permute-start | bytes 3538952 | tf_op jit(solution)/shard_map/ppermute | solution.py:424
  83.4 44.2 %collective-permute-start.19 = (s32[776,128]{1,0:T(8,128)}, s32[776,128]{1,0:T(8,128)S(1)}, u32[]{:S(2)}, u32[]{:S(2)}) collective-permute-start(s32[776,128]{1,0:T(8,128)} %get-tuple-element.37), channel_id=1, source_target_pairs={{0,12},{4,8},{8,4},{12,0},{1,13},{5,9},{9,5},{13,1},{2,14},{6,10},... | collective-permute-start | bytes 1191944 | tf_op jit(solution)/shard_map/ppermute | solution.py:439
  85.6 51.6 %collective-permute-start.20 = (s32[776,128]{1,0:T(8,128)}, s32[776,128]{1,0:T(8,128)}, u32[]{:S(2)}, u32[]{:S(2)}) collective-permute-start(s32[776,128]{1,0:T(8,128)} %get-tuple-element.38), channel_id=1, source_target_pairs={{0,8},{4,12},{8,0},{12,4},{1,9},{5,13},{9,1},{13,5},{2,10},{6,14},... | collective-permute-start | bytes 1191944 | tf_op jit(solution)/shard_map/ppermute | solution.py:439
  103.8 42.8 %collective-permute-start.16 = (s32[776,128]{1,0:T(8,128)}, s32[776,128]{1,0:T(8,128)}, u32[]{:S(2)}, u32[]{:S(2)}) collective-permute-start(s32[776,128]{1,0:T(8,128)} %get-tuple-element.34), channel_id=1, source_target_pairs={{0,12},{4,8},{8,4},{12,0},{1,13},{5,9},{9,5},{13,1},{2,14},{6,10},... | collective-permute-start | bytes 1191944 | tf_op jit(solution)/shard_map/ppermute | solution.py:439
  105.2 48.4 %collective-permute-start.17 = (s32[776,128]{1,0:T(8,128)}, s32[776,128]{1,0:T(8,128)}, u32[]{:S(2)}, u32[]{:S(2)}) collective-permute-start(s32[776,128]{1,0:T(8,128)} %get-tuple-element.35), channel_id=1, source_target_pairs={{0,8},{4,12},{8,0},{12,4},{1,9},{5,13},{9,1},{13,5},{2,10},{6,14},... | collective-permute-start | bytes 1191944 | tf_op jit(solution)/shard_map/ppermute | solution.py:439
  106.1 36.8 %collective-permute-start.18 = (s32[1552,128]{1,0:T(8,128)}, s32[1552,128]{1,0:T(8,128)}, u32[]{:S(2)}, u32[]{:S(2)}) collective-permute-start(s32[1552,128]{1,0:T(8,128)} %get-tuple-element.36), channel_id=1, source_target_pairs={{0,4},{4,0},{8,12},{12,8},{1,5},{5,1},{9,13},{13,9},{2,6},{6,2},{1... | collective-permute-start | bytes 2383880 | tf_op jit(solution)/shard_map/ppermute | solution.py:439
  127.6 9.5 %copy-start = (s32[776,128]{1,0:T(8,128)}, s32[776,128]{1,0:T(8,128)S(1)}, u32[]{:S(2)}) copy-start(s32[776,128]{1,0:T(8,128)S(1)} %collective-permute-done.19.refs_5_.refs_0_) | copy-start | bytes 1191940

commit v8 on v7

--- a/solution.py
+++ b/solution.py
@@ -12,7 +12,7 @@
 STEPS_PER_OCTAVE = 64
 TOP = 32760.0
 FLOOR = 1e-30
-EIGHTHS = (2, 3, 3)
+EIGHTHS = (3, 3, 2)
 VMEM = 127 << 19
 EASE = 2
 ANYWHERE = pl.BlockSpec(memory_space=pl.ANY)
@@ -353,12 +353,11 @@
     )(codes)
 
 
-def grads_kernel(codes_ref, err_ref, *refs):
+def grads_kernel(t, tgt_count, codes_ref, err_ref, *refs):
     out_ref = refs[-1]
-    t, layer = pl.program_id(0), pl.program_id(1)
+    layer = lax.axis_index("src") * pl.num_programs(0) + pl.program_id(0)
+    kept = lax.axis_index("tgt") * tgt_count + t >= layer
     columns = out_ref.shape[3]
-    first_t, first_layer = (lax.axis_index(axis) * pl.num_programs(i) for i, axis in enumerate(("tgt", "src")))
-    kept = first_t + t >= first_layer + layer
     step = min(columns, 512)
 
     @pl.when(kept)
@@ -373,25 +372,33 @@
         out_ref[...] = jnp.zeros_like(out_ref)
 
 
-def grads_call(codes_t, everything, shape, after):
+def grads_call(t, codes_t, everything, out, shape, after):
     layers, tgt_count, width, columns = shape
     tokens = codes_t.shape[2]
     in_specs = [
-        pl.BlockSpec((1, width, tokens), lambda t, i: (i, 0, 0)),
-        pl.BlockSpec((tokens, columns), lambda t, i: (0, t)),
+        pl.BlockSpec((1, width, tokens), lambda i: (i, 0, 0)),
+        pl.BlockSpec((tokens, columns), lambda i: (0, t)),
     ]
+    operands = [codes_t, everything]
+    aliases = {}
+    if out is not None:
+        aliases = {len(operands): 0}
+        operands.append(out)
+    operands += after
+    in_specs += [ANYWHERE] * (len(operands) - 2)
     return pl.pallas_call(
-        grads_kernel,
-        grid=(tgt_count, layers),
-        in_specs=in_specs + [ANYWHERE] * len(after),
-        out_specs=pl.BlockSpec((1, 1, width, columns), lambda t, i: (i, t, 0, 0)),
+        functools.partial(grads_kernel, t, tgt_count),
+        grid=(layers,),
+        in_specs=in_specs,
+        out_specs=pl.BlockSpec((1, 1, width, columns), lambda i: (i, t, 0, 0)),
         out_shape=jax.ShapeDtypeStruct(shape, jnp.bfloat16),
+        input_output_aliases=aliases,
         compiler_params=pltpu.CompilerParams(vmem_limit_bytes=VMEM),
         cost_estimate=cost(
-            2 * tgt_count * layers * width * columns * tokens, 2 * tgt_count * layers * width * (columns + tokens)
+            2 * layers * width * columns * tokens, 2 * layers * width * (columns + tokens) + 2 * tokens * columns
         ),
         name="grads",
-    )(codes_t, everything, *after)
+    )(*operands)
 
 
 def gather_pieces(errors, spans, offsets, n_src, n_feat, codes_t):
@@ -433,7 +440,7 @@
     gather = gather_pieces(errors, spans, offsets, n_src, n_feat, codes_t)
     pieces, plan = next(gather)
     last = len(spans) - 1
-    join_near = last > 0 and spans[-1] == spans[-2]
+    join_near = last > 0 and spans[0] == spans[1]
     owns, gots = [], []
     carry, everything = [], None
     send = lambda x, flip: lax.ppermute(x, "tgt", [(i, i ^ flip) for i in range(n_tgt)])
@@ -452,17 +459,21 @@
         )
         owns.append(own)
         gots.append([(send(far, 3), 0), (send(across, 2), 0)])
-        if join_near and index == last - 1:
+        if join_near and index == 0:
             carry = [near]
         else:
             got_near = send(near, 1)
-            if join_near and index == last:
-                gots[last - 1].append((got_near, 0))
+            if carry:
+                gots[0].append((got_near, 0))
             gots[index].append((got_near, len(carry)))
+            carry = []
         if index < last:
-            before = [gots[0][2]] if index == 0 else gots[index - 1][:2]
+            before = gots[index - 1][:2] if index else []
             pieces, plan = gather.send([own] + [got for got, _ in before])
-    decoder_grads = grads_call(codes_t, everything, decoder.shape, [])
+    decoder_grads = None
+    for t in range(tgt_count):
+        after = [gots[0][2][0]] if t else []
+        decoder_grads = grads_call(t, codes_t, everything, decoder_grads, decoder.shape, after)
     code_grads = None
     for index in range(len(spans)):
         after = [] if index else [decoder_grads] + [got for group in gots[1:last] for got, _ in group[:2]]

time: 158 us -> 158 us (level)
    ppermute x9, waiting for transfers between devices: 9.74 us -> 13.8 us  [gather_pieces(): lax.ppermute(x, axes, [(i, i ^ flip) for i in range(n_src * n_feat)])]
    ppermute x8, waiting for transfers between devices: 30.1 us -> 28.3 us  [body(): lax.ppermute(x, 'tgt', [(i, i ^ flip) for i in range(n_tgt)])]
    pallas_call x1 -> x2, Pallas kernels: 19.4 us -> 20.1 us  [grads_call(): pl.pallas_call(functools.partial(grads_kernel, t, tgt_count), grid=(layer...]
  transfers between devices with their start and end apart: 21 -> 21, of which waited for: 10 -> 8; matrix products, arithmetic and copies ran while one was open for 0% -> 0% of each run, Pallas kernels for 52% -> 53%
where the time goes in v8:
time: 158 us; the launch traced here: 157 us
  Pallas kernels  93 us (59%)
  waiting for transfers between devices  42 us (27%)
  starting transfers between devices  21.1 us (13%)
    pallas_call x3, Pallas kernels, terms_call(): pl.pallas_call(functools.partial(terms_kernel, n_tgt, plan, offset, carri...  48.1 us
    ppermute x8, waiting for transfers between devices, body(): lax.ppermute(x, 'tgt', [(i, i ^ flip) for i in range(n_tgt)])  28.3 us
    pallas_call x2, Pallas kernels, grads_call(): pl.pallas_call(functools.partial(grads_kernel, t, tgt_count), grid=(layer...  20.1 us
    ppermute x9, waiting for transfers between devices, gather_pieces(): lax.ppermute(x, axes, [(i, i ^ flip) for i in range(n_src * n_feat)])  13.8 us
    ppermute x9, starting transfers between devices, gather_pieces(): lax.ppermute(x, axes, [(i, i ^ flip) for i in range(n_src * n_feat)])  11.2 us
    pallas_call x3, Pallas kernels, finish_call(): pl.pallas_call(functools.partial(finish_kernel, len(gots), offset, stride...  10.9 us
    ppermute x8, starting transfers between devices, body(): lax.ppermute(x, 'tgt', [(i, i ^ flip) for i in range(n_tgt)])  9.18 us
    pallas_call x4, Pallas kernels, cut_call(): pl.pallas_call(functools.partial(cut_kernel, len(join), offset), in_specs...  8.74 us
  transfers between devices with their start and end apart: 21, of which 8 were waited for; matrix products, arithmetic and copies ran while one was open for 0% of the time, Pallas kernels for 53%

profile of v8, /device:TPU:0, one launch (start us, length us, event | category | flops | bytes accessed | tf_op | source)
XLA Modules:
  0.0 157.2 jit_solution(6762108389717384799)
XLA Ops:
  0.6 0.5 collective-permute-start
  1.1 1.7 %cut.4 = bf16[2,96,1024]{2,1,0:T(8,128)(2,1)} custom-call(bf16[2,256,1024]{2,1,0:T(8,128)(2,1)} %refs_0_.5), custom_call_target="tpu_custom_call" | custom-call | bytes 393216 | tf_op jit(solution)/shard_map/cut/pallas_call | solution.py:101
  2.9 3.5 %collective-permute-start.3 = (bf16[2,96,1024]{2,1,0:T(8,128)(2,1)}, bf16[2,96,1024]{2,1,0:T(8,128)(2,1)S(1)}, u32[]{:S(2)}, u32[]{:S(2)}) collective-permute-start(bf16[2,96,1024]{2,1,0:T(8,128)(2,1)} %cut.4), channel_id=1, source_target_pairs={{0,18},{1,19},{2,16},{3,17},{16,2},{17,3},{18,0},{19,1},{4,22},{5,... | collective-permute-start | bytes 1179656 | tf_op jit(solution)/shard_map/ppermute | solution.py:413
  6.4 0.5 collective-permute-start.2
  6.9 0.1 collective-permute-start.1
  7.1 5.2 %turn.1.refs_4_.codes_ref = bf16[4,512,1024]{2,1,0:T(8,128)(2,1)} custom-call(bf16[4,1024,512]{2,1,0:T(8,128)(2,1)} %codes_ref.1), custom_call_target="tpu_custom_call" | custom-call | flops 1048576 | bytes 4194304 | tf_op jit(solution)/shard_map/turn/pallas_call | solution.py:344
  12.3 4.3 %collective-permute-done.3.refs_2_ = bf16[2,96,1024]{2,1,0:T(8,128)(2,1)S(1)} collective-permute-done((bf16[2,96,1024]{2,1,0:T(8,128)(2,1)}, bf16[2,96,1024]{2,1,0:T(8,128)(2,1)S(1)}, u32[]{:S(2)}, u32[]{:S(2)}) %collective-permute-start.3) | collective-permute-done | bytes 393248 | tf_op jit(solution)/shard_map/ppermute | solution.py:413
  16.7 0.0 copy-start.2
  16.7 8.3 %collective-permute-done.2.refs_1_ = bf16[2,96,1024]{2,1,0:T(8,128)(2,1)} collective-permute-done((bf16[2,96,1024]{2,1,0:T(8,128)(2,1)}, bf16[2,96,1024]{2,1,0:T(8,128)(2,1)}, u32[]{:S(2)}, u32[]{:S(2)}) %collective-permute-start.2) | collective-permute-done | bytes 393248 | tf_op jit(solution)/shard_map/ppermute | solution.py:413
  24.9 0.3 collective-permute-done.1.refs_0_
  25.2 0.0 collective-permute-done.refs_3_.refs_1_
  25.2 0.0 copy-done.2
  25.2 2.5 %cut.5 = (bf16[3,2,96,1024]{3,2,1,0:T(8,128)(2,1)}, bf16[2,96,1024]{2,1,0:T(8,128)(2,1)}) custom-call(bf16[2,256,1024]{2,1,0:T(8,128)(2,1)} %refs_0_.5, bf16[2,96,1024]{2,1,0:T(8,128)(2,1)} %collective-permute-done.1.refs_0_, bf16[2,96,1024]{2,1,0:T(8,128)(2,1)} %collective-permute-done.2.refs_1_, bf16[2,96,1024]{2,1,0:T(8,128)(2,1)} %copy-done.2, ...), custom_call_target="tpu_custom_call" | custom-call | bytes 1572864 | tf_op jit(solution)/shard_map/cut/pallas_call | solution.py:101
  27.8 0.1 collective-permute-start.7
  27.8 1.6 %collective-permute-start.6 = (bf16[2,96,1024]{2,1,0:T(8,128)(2,1)}, bf16[2,96,1024]{2,1,0:T(8,128)(2,1)S(1)}, u32[]{:S(2)}, u32[]{:S(2)}) collective-permute-start(bf16[2,96,1024]{2,1,0:T(8,128)(2,1)} %get-tuple-element.21), channel_id=1, source_target_pairs={{0,18},{1,19},{2,16},{3,17},{16,2},{17,3},{18,0},{19,1},{4,22},{5,... | collective-permute-start | bytes 1179656 | tf_op jit(solution)/shard_map/ppermute | solution.py:413
  29.4 1.4 collective-permute-start.5
  30.9 0.5 collective-permute-start.4
  31.4 0.0 collective-permute-done.7.refs_3_
  31.4 16.8 %terms.3 = (f32[4,96,512]{2,1,0:T(8,128)}, s32[776,128]{1,0:T(8,128)}, s32[776,128]{1,0:T(8,128)}, s32[776,128]{1,0:T(8,128)}, bf16[1024,4096]{1,0:T(8,128)(2,1)}) custom-call(bf16[2,256,1024]{2,1,0:T(8,128)(2,1)} %refs_0_.5, bf16[2,256,1024]{2,1,0:T(8,128)(2,1)} %collective-permute-done.refs_3_.refs_1_, bf16[3,2,96,1024]{3,2,1,0:T(8,128)(2,1)} %get-tuple-element.22.refs_2_, ...), custom_call_target="tpu_custom_call" | custom-call | flops 3221225472 | bytes 8388608 | tf_op jit(solution)/shard_map/terms/pallas_call | solution.py:225
  48.2 0.0 collective-permute-done.6.refs_2_
  48.2 0.0 copy-start.3
  48.2 0.8 collective-permute-done.5.refs_1_
  49.0 0.0 collective-permute-done.4.refs_0_
  49.0 0.0 copy-done.3
  49.0 2.4 %cut.6 = (bf16[3,2,96,1024]{3,2,1,0:T(8,128)(2,1)}, bf16[2,64,1024]{2,1,0:T(8,128)(2,1)}) custom-call(bf16[2,256,1024]{2,1,0:T(8,128)(2,1)} %refs_0_.5, bf16[2,96,1024]{2,1,0:T(8,128)(2,1)} %collective-permute-done.4.refs_0_, bf16[2,96,1024]{2,1,0:T(8,128)(2,1)} %collective-permute-done.5.refs_1_, bf16[2,96,1024]{2,1,0:T(8,128)(2,1)} %copy-done.3, ...), custom_call_target="tpu_custom_call" | custom-call | bytes 1441792 | tf_op jit(solution)/shard_map/cut/pallas_call | solution.py:101
  51.5 0.1 collective-permute-start.11
  51.6 3.6 %collective-permute-start.12 = (s32[776,128]{1,0:T(8,128)}, s32[776,128]{1,0:T(8,128)S(1)}, u32[]{:S(2)}, u32[]{:S(2)}) collective-permute-start(s32[776,128]{1,0:T(8,128)} %get-tuple-element.29), channel_id=1, source_target_pairs={{0,12},{4,8},{8,4},{12,0},{1,13},{5,9},{9,5},{13,1},{2,14},{6,10},... | collective-permute-start | bytes 1191944 | tf_op jit(solution)/shard_map/ppermute | solution.py:446
  55.2 0.0 collective-permute-start.13
  55.2 1.6 %collective-permute-start.10 = (bf16[2,64,1024]{2,1,0:T(8,128)(2,1)}, bf16[2,64,1024]{2,1,0:T(8,128)(2,1)}, u32[]{:S(2)}, u32[]{:S(2)}) collective-permute-start(bf16[2,64,1024]{2,1,0:T(8,128)(2,1)} %get-tuple-element.24), channel_id=1, source_target_pairs={{0,18},{1,19},{2,16},{3,17},{16,2},{17,3},{18,0},{19,1},{4,22},{5,... | collective-permute-start | bytes 786440 | tf_op jit(solution)/shard_map/ppermute | solution.py:413
  56.9 1.3 collective-permute-start.9
  58.2 0.0 collective-permute-done.11.refs_3_
  58.2 0.5 collective-permute-start.8
  58.7 17.1 %terms.4 = (f32[4,96,512]{2,1,0:T(8,128)}, s32[1552,128]{1,0:T(8,128)}, s32[776,128]{1,0:T(8,128)}, s32[776,128]{1,0:T(8,128)}, bf16[1024,4096]{1,0:T(8,128)(2,1)}) custom-call(bf16[2,256,1024]{2,1,0:T(8,128)(2,1)} %refs_0_.5, bf16[2,256,1024]{2,1,0:T(8,128)(2,1)} %collective-permute-done.refs_3_.refs_1_, ...), custom_call_target="tpu_custom_call", output_to_operand_aliasing={{4}: (6, {})} | custom-call | flops 3221225472 | bytes 8388608 | tf_op jit(solution)/shard_map/terms/pallas_call | solution.py:225
  75.8 0.0 collective-permute-done.10.refs_2_
  75.8 0.0 collective-permute-done.9.refs_1_
  75.8 0.0 collective-permute-done.8.refs_0_
  75.8 0.0 collective-permute-done.12.refs_4_.refs_0_
  75.8 0.0 copy-start.1
  75.9 14.2 %collective-permute-done.13.refs_5_.refs_1_ = s32[776,128]{1,0:T(8,128)} collective-permute-done((s32[776,128]{1,0:T(8,128)}, s32[776,128]{1,0:T(8,128)}, u32[]{:S(2)}, u32[]{:S(2)}) %collective-permute-start.13) | collective-permute-done | bytes 397344 | tf_op jit(solution)/shard_map/ppermute | solution.py:446
  90.1 0.0 copy-done.1
  90.1 2.0 %cut.7.refs_2_ = bf16[3,2,64,1024]{3,2,1,0:T(8,128)(2,1)} custom-call(bf16[2,256,1024]{2,1,0:T(8,128)(2,1)} %refs_0_.5, bf16[2,64,1024]{2,1,0:T(8,128)(2,1)} %collective-permute-done.8.refs_0_, bf16[2,64,1024]{2,1,0:T(8,128)(2,1)} %collective-permute-done.9.refs_1_, bf16[2,64,1024]{2,1,0:T(8,128)(2,1)} %collective-permute-done.10.refs_2_, ...), custom_call_target="tpu_custom_call" | custom-call | bytes 786432 | tf_op jit(solution)/shard_map/cut/pallas_call | solution.py:101
  92.1 0.1 collective-permute-start.14
  92.2 0.1 collective-permute-start.20
  92.2 2.5 %collective-permute-start.18 = (s32[776,128]{1,0:T(8,128)}, s32[776,128]{1,0:T(8,128)S(1)}, u32[]{:S(2)}, u32[]{:S(2)}) collective-permute-start(s32[776,128]{1,0:T(8,128)} %get-tuple-element.36), channel_id=1, source_target_pairs={{0,12},{4,8},{8,4},{12,0},{1,13},{5,9},{9,5},{13,1},{2,14},{6,10},... | collective-permute-start | bytes 1191944 | tf_op jit(solution)/shard_map/ppermute | solution.py:446
  94.8 0.9 collective-permute-start.19
  95.7 0.0 collective-permute-done.14.refs_3_
  95.7 14.2 %terms.5 = (f32[4,64,512]{2,1,0:T(8,128)}, s32[520,128]{1,0:T(8,128)}, s32[520,128]{1,0:T(8,128)}, s32[520,128]{1,0:T(8,128)}, bf16[1024,4096]{1,0:T(8,128)(2,1)}) custom-call(bf16[2,256,1024]{2,1,0:T(8,128)(2,1)} %refs_0_.5, bf16[2,256,1024]{2,1,0:T(8,128)(2,1)} %collective-permute-done.refs_3_.refs_1_, ...), custom_call_target="tpu_custom_call", output_to_operand_aliasing={{4}: (5, {})} | custom-call | flops 2147483648 | bytes 8388608 | tf_op jit(solution)/shard_map/terms/pallas_call | solution.py:225
  110.0 1.9 %collective-permute-start.15 = (s32[520,128]{1,0:T(8,128)}, s32[520,128]{1,0:T(8,128)}, u32[]{:S(2)}, u32[]{:S(2)}) collective-permute-start(s32[520,128]{1,0:T(8,128)} %get-tuple-element.33), channel_id=1, source_target_pairs={{0,12},{4,8},{8,4},{12,0},{1,13},{5,9},{9,5},{13,1},{2,14},{6,10},... | collective-permute-start | bytes 798728 | tf_op jit(solution)/shard_map/ppermute | solution.py:446
  111.8 0.1 collective-permute-start.16
  111.9 9.4 %grads.2.refs_0_ = bf16[4,2,512,2048]{3,2,1,0:T(8,128)(2,1)} custom-call(bf16[4,512,1024]{2,1,0:T(8,128)(2,1)} %turn.1.refs_4_.codes_ref, bf16[1024,4096]{1,0:T(8,128)(2,1)} %get-tuple-element.39.err_ref), custom_call_target="tpu_custom_call" | custom-call | flops 4294967296 | bytes 8388608 | tf_op jit(solution)/shard_map/grads/pallas_call | solution.py:389
  121.4 7.7 %collective-permute-done.20.refs_1_.refs_2_ = s32[1552,128]{1,0:T(8,128)} collective-permute-done((s32[1552,128]{1,0:T(8,128)}, s32[1552,128]{1,0:T(8,128)}, u32[]{:S(2)}, u32[]{:S(2)}) %collective-permute-start.20) | collective-permute-done | bytes 794656 | tf_op jit(solution)/shard_map/ppermute | solution.py:446
  129.1 0.0 collective-permute-start.17
  129.1 10.7 %grads.3.refs_4_ = bf16[4,2,512,2048]{3,2,1,0:T(8,128)(2,1)} custom-call(bf16[4,512,1024]{2,1,0:T(8,128)(2,1)} %turn.1.refs_4_.codes_ref, bf16[1024,4096]{1,0:T(8,128)(2,1)} %get-tuple-element.39.err_ref, bf16[4,2,512,2048]{3,2,1,0:T(8,128)(2,1)} %grads.2.refs_0_, s32[1552,128]{1,0:T(8,128)} %collective-permute-done.20.refs_1_.refs_2_), custom_call_target="tpu_custom_call", output_to_operand_aliasing={{}: (2, {})} | custom-call | flops 4294967296 | bytes 8388608 | tf_op jit(solution)/shard_map/grads/pallas_call | solution.py:389
  139.8 0.0 collective-permute-done.18.refs_5_.refs_0_
  139.8 0.0 copy-start
  139.8 3.3 %collective-permute-done.19.refs_6_.refs_1_ = s32[776,128]{1,0:T(8,128)} collective-permute-done((s32[776,128]{1,0:T(8,128)}, s32[776,128]{1,0:T(8,128)}, u32[]{:S(2)}, u32[]{:S(2)}) %collective-permute-start.19) | collective-permute-done | bytes 397344 | tf_op jit(solution)/shard_map/ppermute | solution.py:446
  143.1 0.0 copy-done
  143.1 3.8 %finish.3.refs_4_ = bf16[4,256,512]{2,1,0:T(8,128)(2,1)} custom-call(f32[4,96,512]{2,1,0:T(8,128)} %get-tuple-element.23.refs_3_.own_ref, s32[776,128]{1,0:T(8,128)} %copy-done.1, s32[776,128]{1,0:T(8,128)} %collective-permute-done.13.refs_5_.refs_1_, s32[1552,128]{1,0:T(8,128)} %collective-permute-done.20.refs_1_.refs_2_, s32[4,256,512]{2,1,0:T(8,128)} %refs_3_.5, ...), custom_call_target="tpu_custom_call" | custom-call | flops 1966080 | bytes 1572864 | tf_op jit(solution)/shard_map/finish/pallas_call | solution.py:309
  146.9 3.8 %finish.4.refs_4_ = bf16[4,256,512]{2,1,0:T(8,128)(2,1)} custom-call(f32[4,96,512]{2,1,0:T(8,128)} %get-tuple-element.28.refs_3_.own_ref, s32[776,128]{1,0:T(8,128)} %copy-done, s32[776,128]{1,0:T(8,128)} %collective-permute-done.19.refs_6_.refs_1_, s32[1552,128]{1,0:T(8,128)} %collective-permute-done.20.refs_1_.refs_2_, ...), custom_call_target="tpu_custom_call", output_to_operand_aliasing={{}: (5, {})} | custom-call | flops 1966080 | bytes 1572864 | tf_op jit(solution)/shard_map/finish/pallas_call | solution.py:309
  150.7 0.0 collective-permute-done.15.refs_0_
  150.7 3.1 %collective-permute-done.16.refs_1_ = s32[520,128]{1,0:T(8,128)} collective-permute-done((s32[520,128]{1,0:T(8,128)}, s32[520,128]{1,0:T(8,128)}, u32[]{:S(2)}, u32[]{:S(2)}) %collective-permute-start.16) | collective-permute-done | bytes 266272 | tf_op jit(solution)/shard_map/ppermute | solution.py:446
  153.7 0.0 collective-permute-done.17.refs_2_
  153.7 3.3 %finish.5 = bf16[4,256,512]{2,1,0:T(8,128)(2,1)} custom-call(f32[4,64,512]{2,1,0:T(8,128)} %get-tuple-element.32.own_ref, s32[520,128]{1,0:T(8,128)} %collective-permute-done.15.refs_0_, s32[520,128]{1,0:T(8,128)} %collective-permute-done.16.refs_1_, s32[520,128]{1,0:T(8,128)} %collective-permute-done.17.refs_2_, ...), custom_call_target="tpu_custom_call", output_to_operand_aliasing={{}: (5, {})} | custom-call | flops 1310720 | bytes 1048576 | tf_op jit(solution)/shard_map/finish/pallas_call | solution.py:309
Async XLA Ops:
  0.6 24.6 %collective-permute-start = (bf16[2,256,1024]{2,1,0:T(8,128)(2,1)}, bf16[2,256,1024]{2,1,0:T(8,128)(2,1)}, u32[]{:S(2)}, u32[]{:S(2)}) collective-permute-start(bf16[2,256,1024]{2,1,0:T(8,128)(2,1)} %refs_0_.5), channel_id=1, source_target_pairs={{0,1},{1,0},{2,3},{3,2},{4,5},{5,4},{6,7},{7,6},{8,9},{9,8},{10,11... | collective-permute-start | bytes 3145736 | tf_op jit(solution)/shard_map/ppermute | solution.py:431
  2.9 13.7 %collective-permute-start.3 = (bf16[2,96,1024]{2,1,0:T(8,128)(2,1)}, bf16[2,96,1024]{2,1,0:T(8,128)(2,1)S(1)}, u32[]{:S(2)}, u32[]{:S(2)}) collective-permute-start(bf16[2,96,1024]{2,1,0:T(8,128)(2,1)} %cut.4), channel_id=1, source_target_pairs={{0,18},{1,19},{2,16},{3,17},{16,2},{17,3},{18,0},{19,1},{4,22},{5,... | collective-permute-start | bytes 1179656 | tf_op jit(solution)/shard_map/ppermute | solution.py:413
  6.4 18.5 %collective-permute-start.2 = (bf16[2,96,1024]{2,1,0:T(8,128)(2,1)}, bf16[2,96,1024]{2,1,0:T(8,128)(2,1)}, u32[]{:S(2)}, u32[]{:S(2)}) collective-permute-start(bf16[2,96,1024]{2,1,0:T(8,128)(2,1)} %cut.4), channel_id=1, source_target_pairs={{0,2},{1,3},{2,0},{3,1},{16,18},{17,19},{18,16},{19,17},{4,6},{5,7... | collective-permute-start | bytes 1179656 | tf_op jit(solution)/shard_map/ppermute | solution.py:413
  6.9 18.3 %collective-permute-start.1 = (bf16[2,96,1024]{2,1,0:T(8,128)(2,1)}, bf16[2,96,1024]{2,1,0:T(8,128)(2,1)}, u32[]{:S(2)}, u32[]{:S(2)}) collective-permute-start(bf16[2,96,1024]{2,1,0:T(8,128)(2,1)} %cut.4), channel_id=1, source_target_pairs={{0,16},{1,17},{2,18},{3,19},{16,0},{17,1},{18,2},{19,3},{4,20},{5,... | collective-permute-start | bytes 1179656 | tf_op jit(solution)/shard_map/ppermute | solution.py:413
  16.7 8.6 %copy-start.2 = (bf16[2,96,1024]{2,1,0:T(8,128)(2,1)}, bf16[2,96,1024]{2,1,0:T(8,128)(2,1)S(1)}, u32[]{:S(2)}) copy-start(bf16[2,96,1024]{2,1,0:T(8,128)(2,1)S(1)} %collective-permute-done.3.refs_2_) | copy-start | bytes 1179652
  27.8 3.6 %collective-permute-start.7 = (bf16[3,2,96,1024]{3,2,1,0:T(8,128)(2,1)}, bf16[3,2,96,1024]{3,2,1,0:T(8,128)(2,1)}, u32[]{:S(2)}, u32[]{:S(2)}) collective-permute-start(bf16[3,2,96,1024]{3,2,1,0:T(8,128)(2,1)} %get-tuple-element.22.refs_2_), channel_id=1, source_target_pairs={{0,1},{1,0},{2,3},{3,2},{4,5},{5,4},{6,7},{7,6},{8,9},{9,8},{10,11... | collective-permute-start | bytes 3538952 | tf_op jit(solution)/shard_map/ppermute | solution.py:431
  27.8 20.3 %collective-permute-start.6 = (bf16[2,96,1024]{2,1,0:T(8,128)(2,1)}, bf16[2,96,1024]{2,1,0:T(8,128)(2,1)S(1)}, u32[]{:S(2)}, u32[]{:S(2)}) collective-permute-start(bf16[2,96,1024]{2,1,0:T(8,128)(2,1)} %get-tuple-element.21), channel_id=1, source_target_pairs={{0,18},{1,19},{2,16},{3,17},{16,2},{17,3},{18,0},{19,1},{4,22},{5,... | collective-permute-start | bytes 1179656 | tf_op jit(solution)/shard_map/ppermute | solution.py:413
  29.4 19.6 %collective-permute-start.5 = (bf16[2,96,1024]{2,1,0:T(8,128)(2,1)}, bf16[2,96,1024]{2,1,0:T(8,128)(2,1)}, u32[]{:S(2)}, u32[]{:S(2)}) collective-permute-start(bf16[2,96,1024]{2,1,0:T(8,128)(2,1)} %get-tuple-element.21), channel_id=1, source_target_pairs={{0,2},{1,3},{2,0},{3,1},{16,18},{17,19},{18,16},{19,17},{4,6},{5,7... | collective-permute-start | bytes 1179656 | tf_op jit(solution)/shard_map/ppermute | solution.py:413
  30.9 18.2 %collective-permute-start.4 = (bf16[2,96,1024]{2,1,0:T(8,128)(2,1)}, bf16[2,96,1024]{2,1,0:T(8,128)(2,1)}, u32[]{:S(2)}, u32[]{:S(2)}) collective-permute-start(bf16[2,96,1024]{2,1,0:T(8,128)(2,1)} %get-tuple-element.21), channel_id=1, source_target_pairs={{0,16},{1,17},{2,18},{3,19},{16,0},{17,1},{18,2},{19,3},{4,20},{5,... | collective-permute-start | bytes 1179656 | tf_op jit(solution)/shard_map/ppermute | solution.py:413
  48.2 0.8 copy-start.3
  51.5 6.7 %collective-permute-start.11 = (bf16[3,2,96,1024]{3,2,1,0:T(8,128)(2,1)}, bf16[3,2,96,1024]{3,2,1,0:T(8,128)(2,1)}, u32[]{:S(2)}, u32[]{:S(2)}) collective-permute-start(bf16[3,2,96,1024]{3,2,1,0:T(8,128)(2,1)} %get-tuple-element.25.refs_2_), channel_id=1, source_target_pairs={{0,1},{1,0},{2,3},{3,2},{4,5},{5,4},{6,7},{7,6},{8,9},{9,8},{10,11... | collective-permute-start | bytes 3538952 | tf_op jit(solution)/shard_map/ppermute | solution.py:431
  51.6 24.2 %collective-permute-start.12 = (s32[776,128]{1,0:T(8,128)}, s32[776,128]{1,0:T(8,128)S(1)}, u32[]{:S(2)}, u32[]{:S(2)}) collective-permute-start(s32[776,128]{1,0:T(8,128)} %get-tuple-element.29), channel_id=1, source_target_pairs={{0,12},{4,8},{8,4},{12,0},{1,13},{5,9},{9,5},{13,1},{2,14},{6,10},... | collective-permute-start | bytes 1191944 | tf_op jit(solution)/shard_map/ppermute | solution.py:446
  55.2 34.8 %collective-permute-start.13 = (s32[776,128]{1,0:T(8,128)}, s32[776,128]{1,0:T(8,128)}, u32[]{:S(2)}, u32[]{:S(2)}) collective-permute-start(s32[776,128]{1,0:T(8,128)} %get-tuple-element.30), channel_id=1, source_target_pairs={{0,8},{4,12},{8,0},{12,4},{1,9},{5,13},{9,1},{13,5},{2,10},{6,14},... | collective-permute-start | bytes 1191944 | tf_op jit(solution)/shard_map/ppermute | solution.py:446
  55.2 20.6 %collective-permute-start.10 = (bf16[2,64,1024]{2,1,0:T(8,128)(2,1)}, bf16[2,64,1024]{2,1,0:T(8,128)(2,1)}, u32[]{:S(2)}, u32[]{:S(2)}) collective-permute-start(bf16[2,64,1024]{2,1,0:T(8,128)(2,1)} %get-tuple-element.24), channel_id=1, source_target_pairs={{0,18},{1,19},{2,16},{3,17},{16,2},{17,3},{18,0},{19,1},{4,22},{5,... | collective-permute-start | bytes 786440 | tf_op jit(solution)/shard_map/ppermute | solution.py:413
  56.9 18.9 %collective-permute-start.9 = (bf16[2,64,1024]{2,1,0:T(8,128)(2,1)}, bf16[2,64,1024]{2,1,0:T(8,128)(2,1)}, u32[]{:S(2)}, u32[]{:S(2)}) collective-permute-start(bf16[2,64,1024]{2,1,0:T(8,128)(2,1)} %get-tuple-element.24), channel_id=1, source_target_pairs={{0,2},{1,3},{2,0},{3,1},{16,18},{17,19},{18,16},{19,17},{4,6},{5,7... | collective-permute-start | bytes 786440 | tf_op jit(solution)/shard_map/ppermute | solution.py:413
  58.2 17.6 %collective-permute-start.8 = (bf16[2,64,1024]{2,1,0:T(8,128)(2,1)}, bf16[2,64,1024]{2,1,0:T(8,128)(2,1)}, u32[]{:S(2)}, u32[]{:S(2)}) collective-permute-start(bf16[2,64,1024]{2,1,0:T(8,128)(2,1)} %get-tuple-element.24), channel_id=1, source_target_pairs={{0,16},{1,17},{2,18},{3,19},{16,0},{17,1},{18,2},{19,3},{4,20},{5,... | collective-permute-start | bytes 786440 | tf_op jit(solution)/shard_map/ppermute | solution.py:413
  75.8 14.2 %copy-start.1 = (s32[776,128]{1,0:T(8,128)}, s32[776,128]{1,0:T(8,128)S(1)}, u32[]{:S(2)}) copy-start(s32[776,128]{1,0:T(8,128)S(1)} %collective-permute-done.12.refs_4_.refs_0_) | copy-start | bytes 1191940
  92.1 3.6 %collective-permute-start.14 = (bf16[3,2,64,1024]{3,2,1,0:T(8,128)(2,1)}, bf16[3,2,64,1024]{3,2,1,0:T(8,128)(2,1)}, u32[]{:S(2)}, u32[]{:S(2)}) collective-permute-start(bf16[3,2,64,1024]{3,2,1,0:T(8,128)(2,1)} %cut.7.refs_2_), channel_id=1, source_target_pairs={{0,1},{1,0},{2,3},{3,2},{4,5},{5,4},{6,7},{7,6},{8,9},{9,8},{10,11... | collective-permute-start | bytes 2359304 | tf_op jit(solution)/shard_map/ppermute | solution.py:431
  92.2 36.9 %collective-permute-start.20 = (s32[1552,128]{1,0:T(8,128)}, s32[1552,128]{1,0:T(8,128)}, u32[]{:S(2)}, u32[]{:S(2)}) collective-permute-start(s32[1552,128]{1,0:T(8,128)} %get-tuple-element.38), channel_id=1, source_target_pairs={{0,4},{4,0},{8,12},{12,8},{1,5},{5,1},{9,13},{13,9},{2,6},{6,2},{1... | collective-permute-start | bytes 2383880 | tf_op jit(solution)/shard_map/ppermute | solution.py:446
  92.2 47.5 %collective-permute-start.18 = (s32[776,128]{1,0:T(8,128)}, s32[776,128]{1,0:T(8,128)S(1)}, u32[]{:S(2)}, u32[]{:S(2)}) collective-permute-start(s32[776,128]{1,0:T(8,128)} %get-tuple-element.36), channel_id=1, source_target_pairs={{0,12},{4,8},{8,4},{12,0},{1,13},{5,9},{9,5},{13,1},{2,14},{6,10},... | collective-permute-start | bytes 1191944 | tf_op jit(solution)/shard_map/ppermute | solution.py:446
  94.8 48.3 %collective-permute-start.19 = (s32[776,128]{1,0:T(8,128)}, s32[776,128]{1,0:T(8,128)}, u32[]{:S(2)}, u32[]{:S(2)}) collective-permute-start(s32[776,128]{1,0:T(8,128)} %get-tuple-element.37), channel_id=1, source_target_pairs={{0,8},{4,12},{8,0},{12,4},{1,9},{5,13},{9,1},{13,5},{2,10},{6,14},... | collective-permute-start | bytes 1191944 | tf_op jit(solution)/shard_map/ppermute | solution.py:446
  110.0 40.7 %collective-permute-start.15 = (s32[520,128]{1,0:T(8,128)}, s32[520,128]{1,0:T(8,128)}, u32[]{:S(2)}, u32[]{:S(2)}) collective-permute-start(s32[520,128]{1,0:T(8,128)} %get-tuple-element.33), channel_id=1, source_target_pairs={{0,12},{4,8},{8,4},{12,0},{1,13},{5,9},{9,5},{13,1},{2,14},{6,10},... | collective-permute-start | bytes 798728 | tf_op jit(solution)/shard_map/ppermute | solution.py:446
  111.8 41.9 %collective-permute-start.16 = (s32[520,128]{1,0:T(8,128)}, s32[520,128]{1,0:T(8,128)}, u32[]{:S(2)}, u32[]{:S(2)}) collective-permute-start(s32[520,128]{1,0:T(8,128)} %get-tuple-element.34), channel_id=1, source_target_pairs={{0,8},{4,12},{8,0},{12,4},{1,9},{5,13},{9,1},{13,5},{2,10},{6,14},... | collective-permute-start | bytes 798728 | tf_op jit(solution)/shard_map/ppermute | solution.py:446
  129.1 24.7 %collective-permute-start.17 = (s32[520,128]{1,0:T(8,128)}, s32[520,128]{1,0:T(8,128)}, u32[]{:S(2)}, u32[]{:S(2)}) collective-permute-start(s32[520,128]{1,0:T(8,128)} %get-tuple-element.35), channel_id=1, source_target_pairs={{0,4},{4,0},{8,12},{12,8},{1,5},{5,1},{9,13},{13,9},{2,6},{6,2},{1... | collective-permute-start | bytes 798728 | tf_op jit(solution)/shard_map/ppermute | solution.py:446
  139.8 3.3 %copy-start = (s32[776,128]{1,0:T(8,128)}, s32[776,128]{1,0:T(8,128)S(1)}, u32[]{:S(2)}) copy-start(s32[776,128]{1,0:T(8,128)S(1)} %collective-permute-done.18.refs_5_.refs_0_) | copy-start | bytes 1191940

commit v9 on v8

--- a/solution.py
+++ b/solution.py
@@ -12,7 +12,7 @@
 STEPS_PER_OCTAVE = 64
 TOP = 32760.0
 FLOOR = 1e-30
-EIGHTHS = (3, 3, 2)
+EIGHTHS = (2, 3, 3)
 VMEM = 127 << 19
 EASE = 2
 ANYWHERE = pl.BlockSpec(memory_space=pl.ANY)
@@ -147,7 +147,9 @@
     def own_copy(layer):
         return pltpu.make_async_copy(acc.at[layer, block(tgt), :], own_ref.at[layer], own_sem.at[layer])
 
-    carry = pltpu.make_async_copy(refs[n_pieces + 1], near_ref.at[pl.ds(0, carried), :], carry_sem) if carried else None
+    if carried:
+        early_ref = refs[n_pieces + 1]
+        carry = pltpu.make_async_copy(early_ref, near_ref.at[pl.ds(0, early_ref.shape[0]), :], carry_sem)
     out_copy = pltpu.make_async_copy(err, all_ref.at[pl.ds(offset, total_rows), :], out_sem)
 
     for t in range(tgt_count):
@@ -216,7 +218,7 @@
     payload = (payload_rows(layers, rows, width), LANES)
     whole = pl.BlockSpec(memory_space=pltpu.VMEM)
     operands = [*pieces, decoder, *carry]
-    carried = sum(x.shape[0] for x in carry)
+    carried = payload[0] if carry else 0
     aliases = {}
     if everything is not None:
         aliases = {len(operands): 4}
@@ -440,7 +442,7 @@
     gather = gather_pieces(errors, spans, offsets, n_src, n_feat, codes_t)
     pieces, plan = next(gather)
     last = len(spans) - 1
-    join_near = last > 0 and spans[0] == spans[1]
+    join_near = last > 0 and spans[0] <= spans[1]
     owns, gots = [], []
     carry, everything = [], None
     send = lambda x, flip: lax.ppermute(x, "tgt", [(i, i ^ flip) for i in range(n_tgt)])

time: 158 us -> 155 us (0.981)
  waiting for transfers between devices: 42 us -> 39.5 us
    ppermute x9, waiting for transfers between devices: 13.8 us -> 10.8 us  [gather_pieces(): lax.ppermute(x, axes, [(i, i ^ flip) for i in range(n_src * n_feat)])]
where the time goes in v9:
time: 155 us
  Pallas kernels  93.1 us (60%)
  waiting for transfers between devices  39.5 us (25%)
  starting transfers between devices  21.1 us (14%)
    pallas_call x3, Pallas kernels, terms_call(): pl.pallas_call(functools.partial(terms_kernel, n_tgt, plan, offset, carri...  48.1 us
    ppermute x8, waiting for transfers between devices, body(): lax.ppermute(x, 'tgt', [(i, i ^ flip) for i in range(n_tgt)])  28.6 us
    pallas_call x2, Pallas kernels, grads_call(): pl.pallas_call(functools.partial(grads_kernel, t, tgt_count), grid=(layer...  20.1 us
    ppermute x9, starting transfers between devices, gather_pieces(): lax.ppermute(x, axes, [(i, i ^ flip) for i in range(n_src * n_feat)])  11.3 us
    pallas_call x3, Pallas kernels, finish_call(): pl.pallas_call(functools.partial(finish_kernel, len(gots), offset, stride...  10.9 us
    ppermute x9, waiting for transfers between devices, gather_pieces(): lax.ppermute(x, axes, [(i, i ^ flip) for i in range(n_src * n_feat)])  10.8 us
    ppermute x8, starting transfers between devices, body(): lax.ppermute(x, 'tgt', [(i, i ^ flip) for i in range(n_tgt)])  9.13 us
    pallas_call x4, Pallas kernels, cut_call(): pl.pallas_call(functools.partial(cut_kernel, len(join), offset), in_specs...  8.75 us
  transfers between devices with their start and end apart: 21, of which 8 were waited for; matrix products, arithmetic and copies ran while one was open for 0% of the time, Pallas kernels for 53%

profile of v9, /device:TPU:0, one launch (start us, length us, event | category | flops | bytes accessed | tf_op | source)
XLA Modules:
  0.0 154.8 jit_solution(6129972528580685843)
XLA Ops:
  0.6 0.5 collective-permute-start
  1.1 1.7 %cut.4 = bf16[2,64,1024]{2,1,0:T(8,128)(2,1)} custom-call(bf16[2,256,1024]{2,1,0:T(8,128)(2,1)} %refs_0_.5), custom_call_target="tpu_custom_call" | custom-call | bytes 262144 | tf_op jit(solution)/shard_map/cut/pallas_call | solution.py:101
  2.8 3.5 %collective-permute-start.3 = (bf16[2,64,1024]{2,1,0:T(8,128)(2,1)}, bf16[2,64,1024]{2,1,0:T(8,128)(2,1)S(1)}, u32[]{:S(2)}, u32[]{:S(2)}) collective-permute-start(bf16[2,64,1024]{2,1,0:T(8,128)(2,1)} %cut.4), channel_id=1, source_target_pairs={{0,18},{1,19},{2,16},{3,17},{16,2},{17,3},{18,0},{19,1},{4,22},{5,... | collective-permute-start | bytes 786440 | tf_op jit(solution)/shard_map/ppermute | solution.py:415
  6.3 0.5 collective-permute-start.2
  6.8 0.1 collective-permute-start.1
  7.0 5.3 %turn.1.refs_4_.codes_ref = bf16[4,512,1024]{2,1,0:T(8,128)(2,1)} custom-call(bf16[4,1024,512]{2,1,0:T(8,128)(2,1)} %codes_ref.1), custom_call_target="tpu_custom_call" | custom-call | flops 1048576 | bytes 4194304 | tf_op jit(solution)/shard_map/turn/pallas_call | solution.py:346
  12.3 1.5 collective-permute-done.3.refs_2_
  13.8 0.0 copy-start.3
  13.8 5.5 %collective-permute-done.2.refs_1_ = bf16[2,64,1024]{2,1,0:T(8,128)(2,1)} collective-permute-done((bf16[2,64,1024]{2,1,0:T(8,128)(2,1)}, bf16[2,64,1024]{2,1,0:T(8,128)(2,1)}, u32[]{:S(2)}, u32[]{:S(2)}) %collective-permute-start.2) | collective-permute-done | bytes 262176 | tf_op jit(solution)/shard_map/ppermute | solution.py:415
  19.2 0.3 collective-permute-done.1.refs_0_
  19.5 0.0 collective-permute-done.refs_3_.refs_1_
  19.5 0.0 copy-done.3
  19.5 2.3 %cut.5 = (bf16[3,2,64,1024]{3,2,1,0:T(8,128)(2,1)}, bf16[2,96,1024]{2,1,0:T(8,128)(2,1)}) custom-call(bf16[2,256,1024]{2,1,0:T(8,128)(2,1)} %refs_0_.5, bf16[2,64,1024]{2,1,0:T(8,128)(2,1)} %collective-permute-done.1.refs_0_, bf16[2,64,1024]{2,1,0:T(8,128)(2,1)} %collective-permute-done.2.refs_1_, bf16[2,64,1024]{2,1,0:T(8,128)(2,1)} %copy-done.3, ...), custom_call_target="tpu_custom_call" | custom-call | bytes 1179648 | tf_op jit(solution)/shard_map/cut/pallas_call | solution.py:101
  21.8 0.1 collective-permute-start.7
  21.9 1.6 %collective-permute-start.6 = (bf16[2,96,1024]{2,1,0:T(8,128)(2,1)}, bf16[2,96,1024]{2,1,0:T(8,128)(2,1)S(1)}, u32[]{:S(2)}, u32[]{:S(2)}) collective-permute-start(bf16[2,96,1024]{2,1,0:T(8,128)(2,1)} %get-tuple-element.21), channel_id=1, source_target_pairs={{0,18},{1,19},{2,16},{3,17},{16,2},{17,3},{18,0},{19,1},{4,22},{5,... | collective-permute-start | bytes 1179656 | tf_op jit(solution)/shard_map/ppermute | solution.py:415
  23.5 1.4 collective-permute-start.5
  24.9 0.5 collective-permute-start.4
  25.5 0.0 collective-permute-done.7.refs_3_
  25.5 14.0 %terms.3 = (f32[4,64,512]{2,1,0:T(8,128)}, s32[520,128]{1,0:T(8,128)}, s32[520,128]{1,0:T(8,128)}, s32[520,128]{1,0:T(8,128)}, bf16[1024,4096]{1,0:T(8,128)(2,1)}) custom-call(bf16[2,256,1024]{2,1,0:T(8,128)(2,1)} %refs_0_.5, bf16[2,256,1024]{2,1,0:T(8,128)(2,1)} %collective-permute-done.refs_3_.refs_1_, bf16[3,2,64,1024]{3,2,1,0:T(8,128)(2,1)} %get-tuple-element.22.refs_2_, ...), custom_call_target="tpu_custom_call" | custom-call | flops 2147483648 | bytes 8388608 | tf_op jit(solution)/shard_map/terms/pallas_call | solution.py:227
  39.5 0.0 collective-permute-done.6.refs_2_
  39.5 0.0 copy-start.2
  39.5 3.6 %collective-permute-done.5.refs_1_ = bf16[2,96,1024]{2,1,0:T(8,128)(2,1)} collective-permute-done((bf16[2,96,1024]{2,1,0:T(8,128)(2,1)}, bf16[2,96,1024]{2,1,0:T(8,128)(2,1)}, u32[]{:S(2)}, u32[]{:S(2)}) %collective-permute-start.5) | collective-permute-done | bytes 393248 | tf_op jit(solution)/shard_map/ppermute | solution.py:415
  43.1 0.0 collective-permute-done.4.refs_0_
  43.1 0.0 copy-done.2
  43.1 2.5 %cut.6 = (bf16[3,2,96,1024]{3,2,1,0:T(8,128)(2,1)}, bf16[2,96,1024]{2,1,0:T(8,128)(2,1)}) custom-call(bf16[2,256,1024]{2,1,0:T(8,128)(2,1)} %refs_0_.5, bf16[2,96,1024]{2,1,0:T(8,128)(2,1)} %collective-permute-done.4.refs_0_, bf16[2,96,1024]{2,1,0:T(8,128)(2,1)} %collective-permute-done.5.refs_1_, bf16[2,96,1024]{2,1,0:T(8,128)(2,1)} %copy-done.2, ...), custom_call_target="tpu_custom_call" | custom-call | bytes 1572864 | tf_op jit(solution)/shard_map/cut/pallas_call | solution.py:101
  45.6 0.1 collective-permute-start.11
  45.7 1.6 %collective-permute-start.10 = (bf16[2,96,1024]{2,1,0:T(8,128)(2,1)}, bf16[2,96,1024]{2,1,0:T(8,128)(2,1)}, u32[]{:S(2)}, u32[]{:S(2)}) collective-permute-start(bf16[2,96,1024]{2,1,0:T(8,128)(2,1)} %get-tuple-element.24), channel_id=1, source_target_pairs={{0,18},{1,19},{2,16},{3,17},{16,2},{17,3},{18,0},{19,1},{4,22},{5,... | collective-permute-start | bytes 1179656 | tf_op jit(solution)/shard_map/ppermute | solution.py:415
  47.3 1.4 collective-permute-start.9
  48.7 0.5 collective-permute-start.8
  49.3 3.6 %collective-permute-start.12 = (s32[520,128]{1,0:T(8,128)}, s32[520,128]{1,0:T(8,128)S(1)}, u32[]{:S(2)}, u32[]{:S(2)}) collective-permute-start(s32[520,128]{1,0:T(8,128)} %get-tuple-element.29), channel_id=1, source_target_pairs={{0,12},{4,8},{8,4},{12,0},{1,13},{5,9},{9,5},{13,1},{2,14},{6,10},... | collective-permute-start | bytes 798728 | tf_op jit(solution)/shard_map/ppermute | solution.py:448
  52.9 0.0 collective-permute-done.11.refs_3_
  52.9 0.0 collective-permute-start.13
  52.9 17.1 %terms.4 = (f32[4,96,512]{2,1,0:T(8,128)}, s32[1552,128]{1,0:T(8,128)}, s32[776,128]{1,0:T(8,128)}, s32[776,128]{1,0:T(8,128)}, bf16[1024,4096]{1,0:T(8,128)(2,1)}) custom-call(bf16[2,256,1024]{2,1,0:T(8,128)(2,1)} %refs_0_.5, bf16[2,256,1024]{2,1,0:T(8,128)(2,1)} %collective-permute-done.refs_3_.refs_1_, ...), custom_call_target="tpu_custom_call", output_to_operand_aliasing={{4}: (6, {})} | custom-call | flops 3221225472 | bytes 8388608 | tf_op jit(solution)/shard_map/terms/pallas_call | solution.py:227
  69.9 0.0 collective-permute-done.12.refs_4_.refs_0_
  69.9 0.0 copy-start.1
  70.0 5.7 %collective-permute-done.13.refs_5_.refs_1_ = s32[520,128]{1,0:T(8,128)} collective-permute-done((s32[520,128]{1,0:T(8,128)}, s32[520,128]{1,0:T(8,128)}, u32[]{:S(2)}, u32[]{:S(2)}) %collective-permute-start.13) | collective-permute-done | bytes 266272 | tf_op jit(solution)/shard_map/ppermute | solution.py:448
  75.6 0.0 collective-permute-done.10.refs_2_
  75.6 0.0 collective-permute-done.9.refs_1_
  75.6 0.0 collective-permute-done.8.refs_0_
  75.6 0.0 copy-done.1
  75.6 2.3 %cut.7.refs_2_ = bf16[3,2,96,1024]{3,2,1,0:T(8,128)(2,1)} custom-call(bf16[2,256,1024]{2,1,0:T(8,128)(2,1)} %refs_0_.5, bf16[2,96,1024]{2,1,0:T(8,128)(2,1)} %collective-permute-done.8.refs_0_, bf16[2,96,1024]{2,1,0:T(8,128)(2,1)} %collective-permute-done.9.refs_1_, bf16[2,96,1024]{2,1,0:T(8,128)(2,1)} %collective-permute-done.10.refs_2_, ...), custom_call_target="tpu_custom_call" | custom-call | bytes 1179648 | tf_op jit(solution)/shard_map/cut/pallas_call | solution.py:101
  77.9 0.1 collective-permute-start.14
  78.0 0.1 collective-permute-start.20
  78.1 2.5 %collective-permute-start.18 = (s32[776,128]{1,0:T(8,128)}, s32[776,128]{1,0:T(8,128)S(1)}, u32[]{:S(2)}, u32[]{:S(2)}) collective-permute-start(s32[776,128]{1,0:T(8,128)} %get-tuple-element.36), channel_id=1, source_target_pairs={{0,12},{4,8},{8,4},{12,0},{1,13},{5,9},{9,5},{13,1},{2,14},{6,10},... | collective-permute-start | bytes 1191944 | tf_op jit(solution)/shard_map/ppermute | solution.py:448
  80.6 0.9 collective-permute-start.19
  81.6 0.0 collective-permute-done.14.refs_3_
  81.6 17.0 %terms.5 = (f32[4,96,512]{2,1,0:T(8,128)}, s32[776,128]{1,0:T(8,128)}, s32[776,128]{1,0:T(8,128)}, s32[776,128]{1,0:T(8,128)}, bf16[1024,4096]{1,0:T(8,128)(2,1)}) custom-call(bf16[2,256,1024]{2,1,0:T(8,128)(2,1)} %refs_0_.5, bf16[2,256,1024]{2,1,0:T(8,128)(2,1)} %collective-permute-done.refs_3_.refs_1_, ...), custom_call_target="tpu_custom_call", output_to_operand_aliasing={{4}: (5, {})} | custom-call | flops 3221225472 | bytes 8388608 | tf_op jit(solution)/shard_map/terms/pallas_call | solution.py:227
  98.6 1.9 %collective-permute-start.15 = (s32[776,128]{1,0:T(8,128)}, s32[776,128]{1,0:T(8,128)}, u32[]{:S(2)}, u32[]{:S(2)}) collective-permute-start(s32[776,128]{1,0:T(8,128)} %get-tuple-element.33), channel_id=1, source_target_pairs={{0,12},{4,8},{8,4},{12,0},{1,13},{5,9},{9,5},{13,1},{2,14},{6,10},... | collective-permute-start | bytes 1191944 | tf_op jit(solution)/shard_map/ppermute | solution.py:448
  100.4 0.1 collective-permute-start.16
  100.5 9.4 %grads.2.refs_0_ = bf16[4,2,512,2048]{3,2,1,0:T(8,128)(2,1)} custom-call(bf16[4,512,1024]{2,1,0:T(8,128)(2,1)} %turn.1.refs_4_.codes_ref, bf16[1024,4096]{1,0:T(8,128)(2,1)} %get-tuple-element.39.err_ref), custom_call_target="tpu_custom_call" | custom-call | flops 4294967296 | bytes 8388608 | tf_op jit(solution)/shard_map/grads/pallas_call | solution.py:391
  110.0 5.1 %collective-permute-done.20.refs_1_.refs_2_ = s32[1552,128]{1,0:T(8,128)} collective-permute-done((s32[1552,128]{1,0:T(8,128)}, s32[1552,128]{1,0:T(8,128)}, u32[]{:S(2)}, u32[]{:S(2)}) %collective-permute-start.20) | collective-permute-done | bytes 794656 | tf_op jit(solution)/shard_map/ppermute | solution.py:448
  115.1 0.0 collective-permute-start.17
  115.1 10.7 %grads.3.refs_4_ = bf16[4,2,512,2048]{3,2,1,0:T(8,128)(2,1)} custom-call(bf16[4,512,1024]{2,1,0:T(8,128)(2,1)} %turn.1.refs_4_.codes_ref, bf16[1024,4096]{1,0:T(8,128)(2,1)} %get-tuple-element.39.err_ref, bf16[4,2,512,2048]{3,2,1,0:T(8,128)(2,1)} %grads.2.refs_0_, s32[1552,128]{1,0:T(8,128)} %collective-permute-done.20.refs_1_.refs_2_), custom_call_target="tpu_custom_call", output_to_operand_aliasing={{}: (2, {})} | custom-call | flops 4294967296 | bytes 8388608 | tf_op jit(solution)/shard_map/grads/pallas_call | solution.py:391
  125.8 0.0 collective-permute-done.18.refs_5_.refs_0_
  125.8 0.0 copy-start
  125.8 8.3 %collective-permute-done.19.refs_6_.refs_1_ = s32[776,128]{1,0:T(8,128)} collective-permute-done((s32[776,128]{1,0:T(8,128)}, s32[776,128]{1,0:T(8,128)}, u32[]{:S(2)}, u32[]{:S(2)}) %collective-permute-start.19) | collective-permute-done | bytes 397344 | tf_op jit(solution)/shard_map/ppermute | solution.py:448
  134.1 0.0 copy-done
  134.1 3.3 %finish.3.refs_4_ = bf16[4,256,512]{2,1,0:T(8,128)(2,1)} custom-call(f32[4,64,512]{2,1,0:T(8,128)} %get-tuple-element.23.refs_3_.own_ref, s32[520,128]{1,0:T(8,128)} %copy-done.1, s32[520,128]{1,0:T(8,128)} %collective-permute-done.13.refs_5_.refs_1_, s32[1552,128]{1,0:T(8,128)} %collective-permute-done.20.refs_1_.refs_2_, s32[4,256,512]{2,1,0:T(8,128)} %refs_3_.5, ...), custom_call_target="tpu_custom_call" | custom-call | flops 1310720 | bytes 1048576 | tf_op jit(solution)/shard_map/finish/pallas_call | solution.py:311
  137.5 3.8 %finish.4.refs_4_ = bf16[4,256,512]{2,1,0:T(8,128)(2,1)} custom-call(f32[4,96,512]{2,1,0:T(8,128)} %get-tuple-element.28.refs_3_.own_ref, s32[776,128]{1,0:T(8,128)} %copy-done, s32[776,128]{1,0:T(8,128)} %collective-permute-done.19.refs_6_.refs_1_, s32[1552,128]{1,0:T(8,128)} %collective-permute-done.20.refs_1_.refs_2_, ...), custom_call_target="tpu_custom_call", output_to_operand_aliasing={{}: (5, {})} | custom-call | flops 1966080 | bytes 1572864 | tf_op jit(solution)/shard_map/finish/pallas_call | solution.py:311
  141.2 0.0 collective-permute-done.15.refs_0_
  141.3 9.5 %collective-permute-done.16.refs_1_ = s32[776,128]{1,0:T(8,128)} collective-permute-done((s32[776,128]{1,0:T(8,128)}, s32[776,128]{1,0:T(8,128)}, u32[]{:S(2)}, u32[]{:S(2)}) %collective-permute-start.16) | collective-permute-done | bytes 397344 | tf_op jit(solution)/shard_map/ppermute | solution.py:448
  150.8 0.0 collective-permute-done.17.refs_2_
  150.8 3.8 %finish.5 = bf16[4,256,512]{2,1,0:T(8,128)(2,1)} custom-call(f32[4,96,512]{2,1,0:T(8,128)} %get-tuple-element.32.own_ref, s32[776,128]{1,0:T(8,128)} %collective-permute-done.15.refs_0_, s32[776,128]{1,0:T(8,128)} %collective-permute-done.16.refs_1_, s32[776,128]{1,0:T(8,128)} %collective-permute-done.17.refs_2_, ...), custom_call_target="tpu_custom_call", output_to_operand_aliasing={{}: (5, {})} | custom-call | flops 1966080 | bytes 1572864 | tf_op jit(solution)/shard_map/finish/pallas_call | solution.py:311
Async XLA Ops:
  0.6 18.9 %collective-permute-start = (bf16[2,256,1024]{2,1,0:T(8,128)(2,1)}, bf16[2,256,1024]{2,1,0:T(8,128)(2,1)}, u32[]{:S(2)}, u32[]{:S(2)}) collective-permute-start(bf16[2,256,1024]{2,1,0:T(8,128)(2,1)} %refs_0_.5), channel_id=1, source_target_pairs={{0,1},{1,0},{2,3},{3,2},{4,5},{5,4},{6,7},{7,6},{8,9},{9,8},{10,11... | collective-permute-start | bytes 3145736 | tf_op jit(solution)/shard_map/ppermute | solution.py:433
  2.8 10.9 %collective-permute-start.3 = (bf16[2,64,1024]{2,1,0:T(8,128)(2,1)}, bf16[2,64,1024]{2,1,0:T(8,128)(2,1)S(1)}, u32[]{:S(2)}, u32[]{:S(2)}) collective-permute-start(bf16[2,64,1024]{2,1,0:T(8,128)(2,1)} %cut.4), channel_id=1, source_target_pairs={{0,18},{1,19},{2,16},{3,17},{16,2},{17,3},{18,0},{19,1},{4,22},{5,... | collective-permute-start | bytes 786440 | tf_op jit(solution)/shard_map/ppermute | solution.py:415
  6.3 12.9 %collective-permute-start.2 = (bf16[2,64,1024]{2,1,0:T(8,128)(2,1)}, bf16[2,64,1024]{2,1,0:T(8,128)(2,1)}, u32[]{:S(2)}, u32[]{:S(2)}) collective-permute-start(bf16[2,64,1024]{2,1,0:T(8,128)(2,1)} %cut.4), channel_id=1, source_target_pairs={{0,2},{1,3},{2,0},{3,1},{16,18},{17,19},{18,16},{19,17},{4,6},{5,7... | collective-permute-start | bytes 786440 | tf_op jit(solution)/shard_map/ppermute | solution.py:415
  6.8 12.7 %collective-permute-start.1 = (bf16[2,64,1024]{2,1,0:T(8,128)(2,1)}, bf16[2,64,1024]{2,1,0:T(8,128)(2,1)}, u32[]{:S(2)}, u32[]{:S(2)}) collective-permute-start(bf16[2,64,1024]{2,1,0:T(8,128)(2,1)} %cut.4), channel_id=1, source_target_pairs={{0,16},{1,17},{2,18},{3,19},{16,0},{17,1},{18,2},{19,3},{4,20},{5,... | collective-permute-start | bytes 786440 | tf_op jit(solution)/shard_map/ppermute | solution.py:415
  13.8 5.8 %copy-start.3 = (bf16[2,64,1024]{2,1,0:T(8,128)(2,1)}, bf16[2,64,1024]{2,1,0:T(8,128)(2,1)S(1)}, u32[]{:S(2)}) copy-start(bf16[2,64,1024]{2,1,0:T(8,128)(2,1)S(1)} %collective-permute-done.3.refs_2_) | copy-start | bytes 786436
  21.8 3.6 %collective-permute-start.7 = (bf16[3,2,64,1024]{3,2,1,0:T(8,128)(2,1)}, bf16[3,2,64,1024]{3,2,1,0:T(8,128)(2,1)}, u32[]{:S(2)}, u32[]{:S(2)}) collective-permute-start(bf16[3,2,64,1024]{3,2,1,0:T(8,128)(2,1)} %get-tuple-element.22.refs_2_), channel_id=1, source_target_pairs={{0,1},{1,0},{2,3},{3,2},{4,5},{5,4},{6,7},{7,6},{8,9},{9,8},{10,11... | collective-permute-start | bytes 2359304 | tf_op jit(solution)/shard_map/ppermute | solution.py:433
  21.9 17.6 %collective-permute-start.6 = (bf16[2,96,1024]{2,1,0:T(8,128)(2,1)}, bf16[2,96,1024]{2,1,0:T(8,128)(2,1)S(1)}, u32[]{:S(2)}, u32[]{:S(2)}) collective-permute-start(bf16[2,96,1024]{2,1,0:T(8,128)(2,1)} %get-tuple-element.21), channel_id=1, source_target_pairs={{0,18},{1,19},{2,16},{3,17},{16,2},{17,3},{18,0},{19,1},{4,22},{5,... | collective-permute-start | bytes 1179656 | tf_op jit(solution)/shard_map/ppermute | solution.py:415
  23.5 19.6 %collective-permute-start.5 = (bf16[2,96,1024]{2,1,0:T(8,128)(2,1)}, bf16[2,96,1024]{2,1,0:T(8,128)(2,1)}, u32[]{:S(2)}, u32[]{:S(2)}) collective-permute-start(bf16[2,96,1024]{2,1,0:T(8,128)(2,1)} %get-tuple-element.21), channel_id=1, source_target_pairs={{0,2},{1,3},{2,0},{3,1},{16,18},{17,19},{18,16},{19,17},{4,6},{5,7... | collective-permute-start | bytes 1179656 | tf_op jit(solution)/shard_map/ppermute | solution.py:415
  24.9 18.2 %collective-permute-start.4 = (bf16[2,96,1024]{2,1,0:T(8,128)(2,1)}, bf16[2,96,1024]{2,1,0:T(8,128)(2,1)}, u32[]{:S(2)}, u32[]{:S(2)}) collective-permute-start(bf16[2,96,1024]{2,1,0:T(8,128)(2,1)} %get-tuple-element.21), channel_id=1, source_target_pairs={{0,16},{1,17},{2,18},{3,19},{16,0},{17,1},{18,2},{19,3},{4,20},{5,... | collective-permute-start | bytes 1179656 | tf_op jit(solution)/shard_map/ppermute | solution.py:415
  39.5 3.6 %copy-start.2 = (bf16[2,96,1024]{2,1,0:T(8,128)(2,1)}, bf16[2,96,1024]{2,1,0:T(8,128)(2,1)S(1)}, u32[]{:S(2)}) copy-start(bf16[2,96,1024]{2,1,0:T(8,128)(2,1)S(1)} %collective-permute-done.6.refs_2_) | copy-start | bytes 1179652
  45.6 7.2 %collective-permute-start.11 = (bf16[3,2,96,1024]{3,2,1,0:T(8,128)(2,1)}, bf16[3,2,96,1024]{3,2,1,0:T(8,128)(2,1)}, u32[]{:S(2)}, u32[]{:S(2)}) collective-permute-start(bf16[3,2,96,1024]{3,2,1,0:T(8,128)(2,1)} %get-tuple-element.25.refs_2_), channel_id=1, source_target_pairs={{0,1},{1,0},{2,3},{3,2},{4,5},{5,4},{6,7},{7,6},{8,9},{9,8},{10,11... | collective-permute-start | bytes 3538952 | tf_op jit(solution)/shard_map/ppermute | solution.py:433
  45.7 29.9 %collective-permute-start.10 = (bf16[2,96,1024]{2,1,0:T(8,128)(2,1)}, bf16[2,96,1024]{2,1,0:T(8,128)(2,1)}, u32[]{:S(2)}, u32[]{:S(2)}) collective-permute-start(bf16[2,96,1024]{2,1,0:T(8,128)(2,1)} %get-tuple-element.24), channel_id=1, source_target_pairs={{0,18},{1,19},{2,16},{3,17},{16,2},{17,3},{18,0},{19,1},{4,22},{5,... | collective-permute-start | bytes 1179656 | tf_op jit(solution)/shard_map/ppermute | solution.py:415
  47.3 28.3 %collective-permute-start.9 = (bf16[2,96,1024]{2,1,0:T(8,128)(2,1)}, bf16[2,96,1024]{2,1,0:T(8,128)(2,1)}, u32[]{:S(2)}, u32[]{:S(2)}) collective-permute-start(bf16[2,96,1024]{2,1,0:T(8,128)(2,1)} %get-tuple-element.24), channel_id=1, source_target_pairs={{0,2},{1,3},{2,0},{3,1},{16,18},{17,19},{18,16},{19,17},{4,6},{5,7... | collective-permute-start | bytes 1179656 | tf_op jit(solution)/shard_map/ppermute | solution.py:415
  48.7 26.9 %collective-permute-start.8 = (bf16[2,96,1024]{2,1,0:T(8,128)(2,1)}, bf16[2,96,1024]{2,1,0:T(8,128)(2,1)}, u32[]{:S(2)}, u32[]{:S(2)}) collective-permute-start(bf16[2,96,1024]{2,1,0:T(8,128)(2,1)} %get-tuple-element.24), channel_id=1, source_target_pairs={{0,16},{1,17},{2,18},{3,19},{16,0},{17,1},{18,2},{19,3},{4,20},{5,... | collective-permute-start | bytes 1179656 | tf_op jit(solution)/shard_map/ppermute | solution.py:415
  49.3 20.7 %collective-permute-start.12 = (s32[520,128]{1,0:T(8,128)}, s32[520,128]{1,0:T(8,128)S(1)}, u32[]{:S(2)}, u32[]{:S(2)}) collective-permute-start(s32[520,128]{1,0:T(8,128)} %get-tuple-element.29), channel_id=1, source_target_pairs={{0,12},{4,8},{8,4},{12,0},{1,13},{5,9},{9,5},{13,1},{2,14},{6,10},... | collective-permute-start | bytes 798728 | tf_op jit(solution)/shard_map/ppermute | solution.py:448
  52.9 22.7 %collective-permute-start.13 = (s32[520,128]{1,0:T(8,128)}, s32[520,128]{1,0:T(8,128)}, u32[]{:S(2)}, u32[]{:S(2)}) collective-permute-start(s32[520,128]{1,0:T(8,128)} %get-tuple-element.30), channel_id=1, source_target_pairs={{0,8},{4,12},{8,0},{12,4},{1,9},{5,13},{9,1},{13,5},{2,10},{6,14},... | collective-permute-start | bytes 798728 | tf_op jit(solution)/shard_map/ppermute | solution.py:448
  69.9 5.7 %copy-start.1 = (s32[520,128]{1,0:T(8,128)}, s32[520,128]{1,0:T(8,128)S(1)}, u32[]{:S(2)}) copy-start(s32[520,128]{1,0:T(8,128)S(1)} %collective-permute-done.12.refs_4_.refs_0_) | copy-start | bytes 798724
  77.9 3.6 %collective-permute-start.14 = (bf16[3,2,96,1024]{3,2,1,0:T(8,128)(2,1)}, bf16[3,2,96,1024]{3,2,1,0:T(8,128)(2,1)}, u32[]{:S(2)}, u32[]{:S(2)}) collective-permute-start(bf16[3,2,96,1024]{3,2,1,0:T(8,128)(2,1)} %cut.7.refs_2_), channel_id=1, source_target_pairs={{0,1},{1,0},{2,3},{3,2},{4,5},{5,4},{6,7},{7,6},{8,9},{9,8},{10,11... | collective-permute-start | bytes 3538952 | tf_op jit(solution)/shard_map/ppermute | solution.py:433
  78.0 37.1 %collective-permute-start.20 = (s32[1552,128]{1,0:T(8,128)}, s32[1552,128]{1,0:T(8,128)}, u32[]{:S(2)}, u32[]{:S(2)}) collective-permute-start(s32[1552,128]{1,0:T(8,128)} %get-tuple-element.38), channel_id=1, source_target_pairs={{0,4},{4,0},{8,12},{12,8},{1,5},{5,1},{9,13},{13,9},{2,6},{6,2},{1... | collective-permute-start | bytes 2383880 | tf_op jit(solution)/shard_map/ppermute | solution.py:448
  78.1 47.7 %collective-permute-start.18 = (s32[776,128]{1,0:T(8,128)}, s32[776,128]{1,0:T(8,128)S(1)}, u32[]{:S(2)}, u32[]{:S(2)}) collective-permute-start(s32[776,128]{1,0:T(8,128)} %get-tuple-element.36), channel_id=1, source_target_pairs={{0,12},{4,8},{8,4},{12,0},{1,13},{5,9},{9,5},{13,1},{2,14},{6,10},... | collective-permute-start | bytes 1191944 | tf_op jit(solution)/shard_map/ppermute | solution.py:448
  80.6 53.5 %collective-permute-start.19 = (s32[776,128]{1,0:T(8,128)}, s32[776,128]{1,0:T(8,128)}, u32[]{:S(2)}, u32[]{:S(2)}) collective-permute-start(s32[776,128]{1,0:T(8,128)} %get-tuple-element.37), channel_id=1, source_target_pairs={{0,8},{4,12},{8,0},{12,4},{1,9},{5,13},{9,1},{13,5},{2,10},{6,14},... | collective-permute-start | bytes 1191944 | tf_op jit(solution)/shard_map/ppermute | solution.py:448
  98.6 42.7 %collective-permute-start.15 = (s32[776,128]{1,0:T(8,128)}, s32[776,128]{1,0:T(8,128)}, u32[]{:S(2)}, u32[]{:S(2)}) collective-permute-start(s32[776,128]{1,0:T(8,128)} %get-tuple-element.33), channel_id=1, source_target_pairs={{0,12},{4,8},{8,4},{12,0},{1,13},{5,9},{9,5},{13,1},{2,14},{6,10},... | collective-permute-start | bytes 1191944 | tf_op jit(solution)/shard_map/ppermute | solution.py:448
  100.4 50.4 %collective-permute-start.16 = (s32[776,128]{1,0:T(8,128)}, s32[776,128]{1,0:T(8,128)}, u32[]{:S(2)}, u32[]{:S(2)}) collective-permute-start(s32[776,128]{1,0:T(8,128)} %get-tuple-element.34), channel_id=1, source_target_pairs={{0,8},{4,12},{8,0},{12,4},{1,9},{5,13},{9,1},{13,5},{2,10},{6,14},... | collective-permute-start | bytes 1191944 | tf_op jit(solution)/shard_map/ppermute | solution.py:448
  115.1 35.7 %collective-permute-start.17 = (s32[776,128]{1,0:T(8,128)}, s32[776,128]{1,0:T(8,128)}, u32[]{:S(2)}, u32[]{:S(2)}) collective-permute-start(s32[776,128]{1,0:T(8,128)} %get-tuple-element.35), channel_id=1, source_target_pairs={{0,4},{4,0},{8,12},{12,8},{1,5},{5,1},{9,13},{13,9},{2,6},{6,2},{1... | collective-permute-start | bytes 1191944 | tf_op jit(solution)/shard_map/ppermute | solution.py:448
  125.8 8.4 %copy-start = (s32[776,128]{1,0:T(8,128)}, s32[776,128]{1,0:T(8,128)S(1)}, u32[]{:S(2)}) copy-start(s32[776,128]{1,0:T(8,128)S(1)} %collective-permute-done.18.refs_5_.refs_0_) | copy-start | bytes 1191940

commit v10 on v9

--- a/solution.py
+++ b/solution.py
@@ -159,9 +159,6 @@
         copy.start()
     if carried:
         carry.start()
-    for layer in range(1, layers):
-        for t in range(tgt_count):
-            dec_copy(layer, t).start()
     for copy in copies:
         copy.wait()
     out_copy.start()
@@ -172,6 +169,9 @@
     tails = [jnp.zeros((SUBLANES, LANES), jnp.int32) for _ in flips]
 
     def multiply(layer):
+        if layer + 1 < layers:
+            for t in range(tgt_count):
+                dec_copy(layer + 1, t).start()
         for t in range(tgt_count):
             dec_copy(layer, t).wait()
             kept = tgt * tgt_count + t >= src * layers + layer

time: 155 us -> 155 us (level)
  Pallas kernels: 93.1 us -> 88.8 us
  waiting for transfers between devices: 39.5 us -> 43.7 us
    pallas_call x3, Pallas kernels: 48.1 us -> 43.7 us  [terms_call(): pl.pallas_call(functools.partial(terms_kernel, n_tgt, plan, offset, carri...]
    ppermute x8, waiting for transfers between devices: 28.6 us -> 31.5 us  [body(): lax.ppermute(x, 'tgt', [(i, i ^ flip) for i in range(n_tgt)])]
  transfers between devices with their start and end apart: 21 -> 21, of which waited for: 8 -> 8; matrix products, arithmetic and copies ran while one was open for 0% -> 0% of each run, Pallas kernels for 53% -> 50%
where the time goes in v10:
time: 155 us
  Pallas kernels  88.8 us (57%)
  waiting for transfers between devices  43.7 us (28%)
  starting transfers between devices  21.3 us (14%)
    pallas_call x3, Pallas kernels, terms_call(): pl.pallas_call(functools.partial(terms_kernel, n_tgt, plan, offset, carri...  43.7 us
    ppermute x8, waiting for transfers between devices, body(): lax.ppermute(x, 'tgt', [(i, i ^ flip) for i in range(n_tgt)])  31.5 us
    pallas_call x2, Pallas kernels, grads_call(): pl.pallas_call(functools.partial(grads_kernel, t, tgt_count), grid=(layer...  20.1 us
    ppermute x9, waiting for transfers between devices, gather_pieces(): lax.ppermute(x, axes, [(i, i ^ flip) for i in range(n_src * n_feat)])  12.2 us
    ppermute x9, starting transfers between devices, gather_pieces(): lax.ppermute(x, axes, [(i, i ^ flip) for i in range(n_src * n_feat)])  11.3 us
    pallas_call x3, Pallas kernels, finish_call(): pl.pallas_call(functools.partial(finish_kernel, len(gots), offset, stride...  10.9 us
    ppermute x8, starting transfers between devices, body(): lax.ppermute(x, 'tgt', [(i, i ^ flip) for i in range(n_tgt)])  9.26 us
    pallas_call x4, Pallas kernels, cut_call(): pl.pallas_call(functools.partial(cut_kernel, len(join), offset), in_specs...  8.75 us
  transfers between devices with their start and end apart: 21, of which 8 were waited for; matrix products, arithmetic and copies ran while one was open for 0% of the time, Pallas kernels for 50%

profile of v10, /device:TPU:0, one launch (start us, length us, event | category | flops | bytes accessed | tf_op | source)
XLA Modules:
  0.0 154.8 jit_solution(1560374227563414893)
XLA Ops:
  0.6 0.5 collective-permute-start
  1.1 1.7 %cut.4 = bf16[2,64,1024]{2,1,0:T(8,128)(2,1)} custom-call(bf16[2,256,1024]{2,1,0:T(8,128)(2,1)} %refs_0_.5), custom_call_target="tpu_custom_call" | custom-call | bytes 262144 | tf_op jit(solution)/shard_map/cut/pallas_call | solution.py:101
  2.8 3.5 %collective-permute-start.3 = (bf16[2,64,1024]{2,1,0:T(8,128)(2,1)}, bf16[2,64,1024]{2,1,0:T(8,128)(2,1)S(1)}, u32[]{:S(2)}, u32[]{:S(2)}) collective-permute-start(bf16[2,64,1024]{2,1,0:T(8,128)(2,1)} %cut.4), channel_id=1, source_target_pairs={{0,18},{1,19},{2,16},{3,17},{16,2},{17,3},{18,0},{19,1},{4,22},{5,... | collective-permute-start | bytes 786440 | tf_op jit(solution)/shard_map/ppermute | solution.py:415
  6.3 0.5 collective-permute-start.2
  6.8 0.1 collective-permute-start.1
  7.0 5.3 %turn.1.refs_4_.codes_ref = bf16[4,512,1024]{2,1,0:T(8,128)(2,1)} custom-call(bf16[4,1024,512]{2,1,0:T(8,128)(2,1)} %codes_ref.1), custom_call_target="tpu_custom_call" | custom-call | flops 1048576 | bytes 4194304 | tf_op jit(solution)/shard_map/turn/pallas_call | solution.py:346
  12.3 1.5 collective-permute-done.3.refs_2_
  13.8 0.0 copy-start.3
  13.8 5.5 %collective-permute-done.2.refs_1_ = bf16[2,64,1024]{2,1,0:T(8,128)(2,1)} collective-permute-done((bf16[2,64,1024]{2,1,0:T(8,128)(2,1)}, bf16[2,64,1024]{2,1,0:T(8,128)(2,1)}, u32[]{:S(2)}, u32[]{:S(2)}) %collective-permute-start.2) | collective-permute-done | bytes 262176 | tf_op jit(solution)/shard_map/ppermute | solution.py:415
  19.2 0.3 collective-permute-done.1.refs_0_
  19.5 0.0 collective-permute-done.refs_3_.refs_1_
  19.5 0.0 copy-done.3
  19.5 2.3 %cut.5 = (bf16[3,2,64,1024]{3,2,1,0:T(8,128)(2,1)}, bf16[2,96,1024]{2,1,0:T(8,128)(2,1)}) custom-call(bf16[2,256,1024]{2,1,0:T(8,128)(2,1)} %refs_0_.5, bf16[2,64,1024]{2,1,0:T(8,128)(2,1)} %collective-permute-done.1.refs_0_, bf16[2,64,1024]{2,1,0:T(8,128)(2,1)} %collective-permute-done.2.refs_1_, bf16[2,64,1024]{2,1,0:T(8,128)(2,1)} %copy-done.3, ...), custom_call_target="tpu_custom_call" | custom-call | bytes 1179648 | tf_op jit(solution)/shard_map/cut/pallas_call | solution.py:101
  21.8 0.1 collective-permute-start.7
  21.9 1.6 %collective-permute-start.6 = (bf16[2,96,1024]{2,1,0:T(8,128)(2,1)}, bf16[2,96,1024]{2,1,0:T(8,128)(2,1)S(1)}, u32[]{:S(2)}, u32[]{:S(2)}) collective-permute-start(bf16[2,96,1024]{2,1,0:T(8,128)(2,1)} %get-tuple-element.21), channel_id=1, source_target_pairs={{0,18},{1,19},{2,16},{3,17},{16,2},{17,3},{18,0},{19,1},{4,22},{5,... | collective-permute-start | bytes 1179656 | tf_op jit(solution)/shard_map/ppermute | solution.py:415
  23.5 1.4 collective-permute-start.5
  24.9 0.5 collective-permute-start.4
  25.5 0.0 collective-permute-done.7.refs_3_
  25.5 12.6 %terms.3 = (f32[4,64,512]{2,1,0:T(8,128)}, s32[520,128]{1,0:T(8,128)}, s32[520,128]{1,0:T(8,128)}, s32[520,128]{1,0:T(8,128)}, bf16[1024,4096]{1,0:T(8,128)(2,1)}) custom-call(bf16[2,256,1024]{2,1,0:T(8,128)(2,1)} %refs_0_.5, bf16[2,256,1024]{2,1,0:T(8,128)(2,1)} %collective-permute-done.refs_3_.refs_1_, bf16[3,2,64,1024]{3,2,1,0:T(8,128)(2,1)} %get-tuple-element.22.refs_2_, ...), custom_call_target="tpu_custom_call" | custom-call | flops 2147483648 | bytes 8388608 | tf_op jit(solution)/shard_map/terms/pallas_call | solution.py:227
  38.1 0.0 collective-permute-done.6.refs_2_
  38.1 0.0 copy-start.2
  38.1 4.9 %collective-permute-done.5.refs_1_ = bf16[2,96,1024]{2,1,0:T(8,128)(2,1)} collective-permute-done((bf16[2,96,1024]{2,1,0:T(8,128)(2,1)}, bf16[2,96,1024]{2,1,0:T(8,128)(2,1)}, u32[]{:S(2)}, u32[]{:S(2)}) %collective-permute-start.5) | collective-permute-done | bytes 393248 | tf_op jit(solution)/shard_map/ppermute | solution.py:415
  43.1 0.0 collective-permute-done.4.refs_0_
  43.1 0.0 copy-done.2
  43.1 2.5 %cut.6 = (bf16[3,2,96,1024]{3,2,1,0:T(8,128)(2,1)}, bf16[2,96,1024]{2,1,0:T(8,128)(2,1)}) custom-call(bf16[2,256,1024]{2,1,0:T(8,128)(2,1)} %refs_0_.5, bf16[2,96,1024]{2,1,0:T(8,128)(2,1)} %collective-permute-done.4.refs_0_, bf16[2,96,1024]{2,1,0:T(8,128)(2,1)} %collective-permute-done.5.refs_1_, bf16[2,96,1024]{2,1,0:T(8,128)(2,1)} %copy-done.2, ...), custom_call_target="tpu_custom_call" | custom-call | bytes 1572864 | tf_op jit(solution)/shard_map/cut/pallas_call | solution.py:101
  45.6 0.1 collective-permute-start.11
  45.7 1.6 %collective-permute-start.10 = (bf16[2,96,1024]{2,1,0:T(8,128)(2,1)}, bf16[2,96,1024]{2,1,0:T(8,128)(2,1)}, u32[]{:S(2)}, u32[]{:S(2)}) collective-permute-start(bf16[2,96,1024]{2,1,0:T(8,128)(2,1)} %get-tuple-element.24), channel_id=1, source_target_pairs={{0,18},{1,19},{2,16},{3,17},{16,2},{17,3},{18,0},{19,1},{4,22},{5,... | collective-permute-start | bytes 1179656 | tf_op jit(solution)/shard_map/ppermute | solution.py:415
  47.3 1.4 collective-permute-start.9
  48.7 0.5 collective-permute-start.8
  49.3 3.6 %collective-permute-start.12 = (s32[520,128]{1,0:T(8,128)}, s32[520,128]{1,0:T(8,128)S(1)}, u32[]{:S(2)}, u32[]{:S(2)}) collective-permute-start(s32[520,128]{1,0:T(8,128)} %get-tuple-element.29), channel_id=1, source_target_pairs={{0,12},{4,8},{8,4},{12,0},{1,13},{5,9},{9,5},{13,1},{2,14},{6,10},... | collective-permute-start | bytes 798728 | tf_op jit(solution)/shard_map/ppermute | solution.py:448
  52.9 0.0 collective-permute-done.11.refs_3_
  52.9 0.0 collective-permute-start.13
  52.9 15.6 %terms.4 = (f32[4,96,512]{2,1,0:T(8,128)}, s32[1552,128]{1,0:T(8,128)}, s32[776,128]{1,0:T(8,128)}, s32[776,128]{1,0:T(8,128)}, bf16[1024,4096]{1,0:T(8,128)(2,1)}) custom-call(bf16[2,256,1024]{2,1,0:T(8,128)(2,1)} %refs_0_.5, bf16[2,256,1024]{2,1,0:T(8,128)(2,1)} %collective-permute-done.refs_3_.refs_1_, ...), custom_call_target="tpu_custom_call", output_to_operand_aliasing={{4}: (6, {})} | custom-call | flops 3221225472 | bytes 8388608 | tf_op jit(solution)/shard_map/terms/pallas_call | solution.py:227
  68.5 0.0 collective-permute-done.12.refs_4_.refs_0_
  68.5 0.0 copy-start.1
  68.5 7.1 %collective-permute-done.13.refs_5_.refs_1_ = s32[520,128]{1,0:T(8,128)} collective-permute-done((s32[520,128]{1,0:T(8,128)}, s32[520,128]{1,0:T(8,128)}, u32[]{:S(2)}, u32[]{:S(2)}) %collective-permute-start.13) | collective-permute-done | bytes 266272 | tf_op jit(solution)/shard_map/ppermute | solution.py:448
  75.6 0.0 collective-permute-done.10.refs_2_
  75.6 0.0 collective-permute-done.9.refs_1_
  75.6 0.0 collective-permute-done.8.refs_0_
  75.6 0.0 copy-done.1
  75.6 2.3 %cut.7.refs_2_ = bf16[3,2,96,1024]{3,2,1,0:T(8,128)(2,1)} custom-call(bf16[2,256,1024]{2,1,0:T(8,128)(2,1)} %refs_0_.5, bf16[2,96,1024]{2,1,0:T(8,128)(2,1)} %collective-permute-done.8.refs_0_, bf16[2,96,1024]{2,1,0:T(8,128)(2,1)} %collective-permute-done.9.refs_1_, bf16[2,96,1024]{2,1,0:T(8,128)(2,1)} %collective-permute-done.10.refs_2_, ...), custom_call_target="tpu_custom_call" | custom-call | bytes 1179648 | tf_op jit(solution)/shard_map/cut/pallas_call | solution.py:101
  77.9 0.1 collective-permute-start.14
  78.0 0.1 collective-permute-start.20
  78.1 2.5 %collective-permute-start.18 = (s32[776,128]{1,0:T(8,128)}, s32[776,128]{1,0:T(8,128)S(1)}, u32[]{:S(2)}, u32[]{:S(2)}) collective-permute-start(s32[776,128]{1,0:T(8,128)} %get-tuple-element.36), channel_id=1, source_target_pairs={{0,12},{4,8},{8,4},{12,0},{1,13},{5,9},{9,5},{13,1},{2,14},{6,10},... | collective-permute-start | bytes 1191944 | tf_op jit(solution)/shard_map/ppermute | solution.py:448
  80.6 0.9 collective-permute-start.19
  81.6 0.0 collective-permute-done.14.refs_3_
  81.6 15.5 %terms.5 = (f32[4,96,512]{2,1,0:T(8,128)}, s32[776,128]{1,0:T(8,128)}, s32[776,128]{1,0:T(8,128)}, s32[776,128]{1,0:T(8,128)}, bf16[1024,4096]{1,0:T(8,128)(2,1)}) custom-call(bf16[2,256,1024]{2,1,0:T(8,128)(2,1)} %refs_0_.5, bf16[2,256,1024]{2,1,0:T(8,128)(2,1)} %collective-permute-done.refs_3_.refs_1_, ...), custom_call_target="tpu_custom_call", output_to_operand_aliasing={{4}: (5, {})} | custom-call | flops 3221225472 | bytes 8388608 | tf_op jit(solution)/shard_map/terms/pallas_call | solution.py:227
  97.1 2.0 %collective-permute-start.15 = (s32[776,128]{1,0:T(8,128)}, s32[776,128]{1,0:T(8,128)}, u32[]{:S(2)}, u32[]{:S(2)}) collective-permute-start(s32[776,128]{1,0:T(8,128)} %get-tuple-element.33), channel_id=1, source_target_pairs={{0,12},{4,8},{8,4},{12,0},{1,13},{5,9},{9,5},{13,1},{2,14},{6,10},... | collective-permute-start | bytes 1191944 | tf_op jit(solution)/shard_map/ppermute | solution.py:448
  99.1 0.1 collective-permute-start.16
  99.2 9.4 %grads.2.refs_0_ = bf16[4,2,512,2048]{3,2,1,0:T(8,128)(2,1)} custom-call(bf16[4,512,1024]{2,1,0:T(8,128)(2,1)} %turn.1.refs_4_.codes_ref, bf16[1024,4096]{1,0:T(8,128)(2,1)} %get-tuple-element.39.err_ref), custom_call_target="tpu_custom_call" | custom-call | flops 4294967296 | bytes 8388608 | tf_op jit(solution)/shard_map/grads/pallas_call | solution.py:391
  108.6 6.5 %collective-permute-done.20.refs_1_.refs_2_ = s32[1552,128]{1,0:T(8,128)} collective-permute-done((s32[1552,128]{1,0:T(8,128)}, s32[1552,128]{1,0:T(8,128)}, u32[]{:S(2)}, u32[]{:S(2)}) %collective-permute-start.20) | collective-permute-done | bytes 794656 | tf_op jit(solution)/shard_map/ppermute | solution.py:448
  115.1 0.0 collective-permute-start.17
  115.1 10.7 %grads.3.refs_4_ = bf16[4,2,512,2048]{3,2,1,0:T(8,128)(2,1)} custom-call(bf16[4,512,1024]{2,1,0:T(8,128)(2,1)} %turn.1.refs_4_.codes_ref, bf16[1024,4096]{1,0:T(8,128)(2,1)} %get-tuple-element.39.err_ref, bf16[4,2,512,2048]{3,2,1,0:T(8,128)(2,1)} %grads.2.refs_0_, s32[1552,128]{1,0:T(8,128)} %collective-permute-done.20.refs_1_.refs_2_), custom_call_target="tpu_custom_call", output_to_operand_aliasing={{}: (2, {})} | custom-call | flops 4294967296 | bytes 8388608 | tf_op jit(solution)/shard_map/grads/pallas_call | solution.py:391
  125.8 0.0 collective-permute-done.18.refs_5_.refs_0_
  125.8 0.0 copy-start
  125.8 8.3 %collective-permute-done.19.refs_6_.refs_1_ = s32[776,128]{1,0:T(8,128)} collective-permute-done((s32[776,128]{1,0:T(8,128)}, s32[776,128]{1,0:T(8,128)}, u32[]{:S(2)}, u32[]{:S(2)}) %collective-permute-start.19) | collective-permute-done | bytes 397344 | tf_op jit(solution)/shard_map/ppermute | solution.py:448
  134.1 0.0 copy-done
  134.1 3.3 %finish.3.refs_4_ = bf16[4,256,512]{2,1,0:T(8,128)(2,1)} custom-call(f32[4,64,512]{2,1,0:T(8,128)} %get-tuple-element.23.refs_3_.own_ref, s32[520,128]{1,0:T(8,128)} %copy-done.1, s32[520,128]{1,0:T(8,128)} %collective-permute-done.13.refs_5_.refs_1_, s32[1552,128]{1,0:T(8,128)} %collective-permute-done.20.refs_1_.refs_2_, s32[4,256,512]{2,1,0:T(8,128)} %refs_3_.5, ...), custom_call_target="tpu_custom_call" | custom-call | flops 1310720 | bytes 1048576 | tf_op jit(solution)/shard_map/finish/pallas_call | solution.py:311
  137.5 3.8 %finish.4.refs_4_ = bf16[4,256,512]{2,1,0:T(8,128)(2,1)} custom-call(f32[4,96,512]{2,1,0:T(8,128)} %get-tuple-element.28.refs_3_.own_ref, s32[776,128]{1,0:T(8,128)} %copy-done, s32[776,128]{1,0:T(8,128)} %collective-permute-done.19.refs_6_.refs_1_, s32[1552,128]{1,0:T(8,128)} %collective-permute-done.20.refs_1_.refs_2_, ...), custom_call_target="tpu_custom_call", output_to_operand_aliasing={{}: (5, {})} | custom-call | flops 1966080 | bytes 1572864 | tf_op jit(solution)/shard_map/finish/pallas_call | solution.py:311
  141.2 0.0 collective-permute-done.15.refs_0_
  141.3 9.5 %collective-permute-done.16.refs_1_ = s32[776,128]{1,0:T(8,128)} collective-permute-done((s32[776,128]{1,0:T(8,128)}, s32[776,128]{1,0:T(8,128)}, u32[]{:S(2)}, u32[]{:S(2)}) %collective-permute-start.16) | collective-permute-done | bytes 397344 | tf_op jit(solution)/shard_map/ppermute | solution.py:448
  150.8 0.0 collective-permute-done.17.refs_2_
  150.8 3.8 %finish.5 = bf16[4,256,512]{2,1,0:T(8,128)(2,1)} custom-call(f32[4,96,512]{2,1,0:T(8,128)} %get-tuple-element.32.own_ref, s32[776,128]{1,0:T(8,128)} %collective-permute-done.15.refs_0_, s32[776,128]{1,0:T(8,128)} %collective-permute-done.16.refs_1_, s32[776,128]{1,0:T(8,128)} %collective-permute-done.17.refs_2_, ...), custom_call_target="tpu_custom_call", output_to_operand_aliasing={{}: (5, {})} | custom-call | flops 1966080 | bytes 1572864 | tf_op jit(solution)/shard_map/finish/pallas_call | solution.py:311
Async XLA Ops:
  0.6 18.9 %collective-permute-start = (bf16[2,256,1024]{2,1,0:T(8,128)(2,1)}, bf16[2,256,1024]{2,1,0:T(8,128)(2,1)}, u32[]{:S(2)}, u32[]{:S(2)}) collective-permute-start(bf16[2,256,1024]{2,1,0:T(8,128)(2,1)} %refs_0_.5), channel_id=1, source_target_pairs={{0,1},{1,0},{2,3},{3,2},{4,5},{5,4},{6,7},{7,6},{8,9},{9,8},{10,11... | collective-permute-start | bytes 3145736 | tf_op jit(solution)/shard_map/ppermute | solution.py:433
  2.8 10.9 %collective-permute-start.3 = (bf16[2,64,1024]{2,1,0:T(8,128)(2,1)}, bf16[2,64,1024]{2,1,0:T(8,128)(2,1)S(1)}, u32[]{:S(2)}, u32[]{:S(2)}) collective-permute-start(bf16[2,64,1024]{2,1,0:T(8,128)(2,1)} %cut.4), channel_id=1, source_target_pairs={{0,18},{1,19},{2,16},{3,17},{16,2},{17,3},{18,0},{19,1},{4,22},{5,... | collective-permute-start | bytes 786440 | tf_op jit(solution)/shard_map/ppermute | solution.py:415
  6.3 12.9 %collective-permute-start.2 = (bf16[2,64,1024]{2,1,0:T(8,128)(2,1)}, bf16[2,64,1024]{2,1,0:T(8,128)(2,1)}, u32[]{:S(2)}, u32[]{:S(2)}) collective-permute-start(bf16[2,64,1024]{2,1,0:T(8,128)(2,1)} %cut.4), channel_id=1, source_target_pairs={{0,2},{1,3},{2,0},{3,1},{16,18},{17,19},{18,16},{19,17},{4,6},{5,7... | collective-permute-start | bytes 786440 | tf_op jit(solution)/shard_map/ppermute | solution.py:415
  6.8 12.7 %collective-permute-start.1 = (bf16[2,64,1024]{2,1,0:T(8,128)(2,1)}, bf16[2,64,1024]{2,1,0:T(8,128)(2,1)}, u32[]{:S(2)}, u32[]{:S(2)}) collective-permute-start(bf16[2,64,1024]{2,1,0:T(8,128)(2,1)} %cut.4), channel_id=1, source_target_pairs={{0,16},{1,17},{2,18},{3,19},{16,0},{17,1},{18,2},{19,3},{4,20},{5,... | collective-permute-start | bytes 786440 | tf_op jit(solution)/shard_map/ppermute | solution.py:415
  13.8 5.8 %copy-start.3 = (bf16[2,64,1024]{2,1,0:T(8,128)(2,1)}, bf16[2,64,1024]{2,1,0:T(8,128)(2,1)S(1)}, u32[]{:S(2)}) copy-start(bf16[2,64,1024]{2,1,0:T(8,128)(2,1)S(1)} %collective-permute-done.3.refs_2_) | copy-start | bytes 786436
  21.8 3.6 %collective-permute-start.7 = (bf16[3,2,64,1024]{3,2,1,0:T(8,128)(2,1)}, bf16[3,2,64,1024]{3,2,1,0:T(8,128)(2,1)}, u32[]{:S(2)}, u32[]{:S(2)}) collective-permute-start(bf16[3,2,64,1024]{3,2,1,0:T(8,128)(2,1)} %get-tuple-element.22.refs_2_), channel_id=1, source_target_pairs={{0,1},{1,0},{2,3},{3,2},{4,5},{5,4},{6,7},{7,6},{8,9},{9,8},{10,11... | collective-permute-start | bytes 2359304 | tf_op jit(solution)/shard_map/ppermute | solution.py:433
  21.9 16.2 %collective-permute-start.6 = (bf16[2,96,1024]{2,1,0:T(8,128)(2,1)}, bf16[2,96,1024]{2,1,0:T(8,128)(2,1)S(1)}, u32[]{:S(2)}, u32[]{:S(2)}) collective-permute-start(bf16[2,96,1024]{2,1,0:T(8,128)(2,1)} %get-tuple-element.21), channel_id=1, source_target_pairs={{0,18},{1,19},{2,16},{3,17},{16,2},{17,3},{18,0},{19,1},{4,22},{5,... | collective-permute-start | bytes 1179656 | tf_op jit(solution)/shard_map/ppermute | solution.py:415
  23.5 19.6 %collective-permute-start.5 = (bf16[2,96,1024]{2,1,0:T(8,128)(2,1)}, bf16[2,96,1024]{2,1,0:T(8,128)(2,1)}, u32[]{:S(2)}, u32[]{:S(2)}) collective-permute-start(bf16[2,96,1024]{2,1,0:T(8,128)(2,1)} %get-tuple-element.21), channel_id=1, source_target_pairs={{0,2},{1,3},{2,0},{3,1},{16,18},{17,19},{18,16},{19,17},{4,6},{5,7... | collective-permute-start | bytes 1179656 | tf_op jit(solution)/shard_map/ppermute | solution.py:415
  24.9 18.2 %collective-permute-start.4 = (bf16[2,96,1024]{2,1,0:T(8,128)(2,1)}, bf16[2,96,1024]{2,1,0:T(8,128)(2,1)}, u32[]{:S(2)}, u32[]{:S(2)}) collective-permute-start(bf16[2,96,1024]{2,1,0:T(8,128)(2,1)} %get-tuple-element.21), channel_id=1, source_target_pairs={{0,16},{1,17},{2,18},{3,19},{16,0},{17,1},{18,2},{19,3},{4,20},{5,... | collective-permute-start | bytes 1179656 | tf_op jit(solution)/shard_map/ppermute | solution.py:415
  38.1 5.0 %copy-start.2 = (bf16[2,96,1024]{2,1,0:T(8,128)(2,1)}, bf16[2,96,1024]{2,1,0:T(8,128)(2,1)S(1)}, u32[]{:S(2)}) copy-start(bf16[2,96,1024]{2,1,0:T(8,128)(2,1)S(1)} %collective-permute-done.6.refs_2_) | copy-start | bytes 1179652
  45.6 7.2 %collective-permute-start.11 = (bf16[3,2,96,1024]{3,2,1,0:T(8,128)(2,1)}, bf16[3,2,96,1024]{3,2,1,0:T(8,128)(2,1)}, u32[]{:S(2)}, u32[]{:S(2)}) collective-permute-start(bf16[3,2,96,1024]{3,2,1,0:T(8,128)(2,1)} %get-tuple-element.25.refs_2_), channel_id=1, source_target_pairs={{0,1},{1,0},{2,3},{3,2},{4,5},{5,4},{6,7},{7,6},{8,9},{9,8},{10,11... | collective-permute-start | bytes 3538952 | tf_op jit(solution)/shard_map/ppermute | solution.py:433
  45.7 29.9 %collective-permute-start.10 = (bf16[2,96,1024]{2,1,0:T(8,128)(2,1)}, bf16[2,96,1024]{2,1,0:T(8,128)(2,1)}, u32[]{:S(2)}, u32[]{:S(2)}) collective-permute-start(bf16[2,96,1024]{2,1,0:T(8,128)(2,1)} %get-tuple-element.24), channel_id=1, source_target_pairs={{0,18},{1,19},{2,16},{3,17},{16,2},{17,3},{18,0},{19,1},{4,22},{5,... | collective-permute-start | bytes 1179656 | tf_op jit(solution)/shard_map/ppermute | solution.py:415
  47.3 28.3 %collective-permute-start.9 = (bf16[2,96,1024]{2,1,0:T(8,128)(2,1)}, bf16[2,96,1024]{2,1,0:T(8,128)(2,1)}, u32[]{:S(2)}, u32[]{:S(2)}) collective-permute-start(bf16[2,96,1024]{2,1,0:T(8,128)(2,1)} %get-tuple-element.24), channel_id=1, source_target_pairs={{0,2},{1,3},{2,0},{3,1},{16,18},{17,19},{18,16},{19,17},{4,6},{5,7... | collective-permute-start | bytes 1179656 | tf_op jit(solution)/shard_map/ppermute | solution.py:415
  48.7 26.9 %collective-permute-start.8 = (bf16[2,96,1024]{2,1,0:T(8,128)(2,1)}, bf16[2,96,1024]{2,1,0:T(8,128)(2,1)}, u32[]{:S(2)}, u32[]{:S(2)}) collective-permute-start(bf16[2,96,1024]{2,1,0:T(8,128)(2,1)} %get-tuple-element.24), channel_id=1, source_target_pairs={{0,16},{1,17},{2,18},{3,19},{16,0},{17,1},{18,2},{19,3},{4,20},{5,... | collective-permute-start | bytes 1179656 | tf_op jit(solution)/shard_map/ppermute | solution.py:415
  49.3 19.2 %collective-permute-start.12 = (s32[520,128]{1,0:T(8,128)}, s32[520,128]{1,0:T(8,128)S(1)}, u32[]{:S(2)}, u32[]{:S(2)}) collective-permute-start(s32[520,128]{1,0:T(8,128)} %get-tuple-element.29), channel_id=1, source_target_pairs={{0,12},{4,8},{8,4},{12,0},{1,13},{5,9},{9,5},{13,1},{2,14},{6,10},... | collective-permute-start | bytes 798728 | tf_op jit(solution)/shard_map/ppermute | solution.py:448
  52.9 22.7 %collective-permute-start.13 = (s32[520,128]{1,0:T(8,128)}, s32[520,128]{1,0:T(8,128)}, u32[]{:S(2)}, u32[]{:S(2)}) collective-permute-start(s32[520,128]{1,0:T(8,128)} %get-tuple-element.30), channel_id=1, source_target_pairs={{0,8},{4,12},{8,0},{12,4},{1,9},{5,13},{9,1},{13,5},{2,10},{6,14},... | collective-permute-start | bytes 798728 | tf_op jit(solution)/shard_map/ppermute | solution.py:448
  68.5 7.2 %copy-start.1 = (s32[520,128]{1,0:T(8,128)}, s32[520,128]{1,0:T(8,128)S(1)}, u32[]{:S(2)}) copy-start(s32[520,128]{1,0:T(8,128)S(1)} %collective-permute-done.12.refs_4_.refs_0_) | copy-start | bytes 798724
  77.9 3.6 %collective-permute-start.14 = (bf16[3,2,96,1024]{3,2,1,0:T(8,128)(2,1)}, bf16[3,2,96,1024]{3,2,1,0:T(8,128)(2,1)}, u32[]{:S(2)}, u32[]{:S(2)}) collective-permute-start(bf16[3,2,96,1024]{3,2,1,0:T(8,128)(2,1)} %cut.7.refs_2_), channel_id=1, source_target_pairs={{0,1},{1,0},{2,3},{3,2},{4,5},{5,4},{6,7},{7,6},{8,9},{9,8},{10,11... | collective-permute-start | bytes 3538952 | tf_op jit(solution)/shard_map/ppermute | solution.py:433
  78.0 37.1 %collective-permute-start.20 = (s32[1552,128]{1,0:T(8,128)}, s32[1552,128]{1,0:T(8,128)}, u32[]{:S(2)}, u32[]{:S(2)}) collective-permute-start(s32[1552,128]{1,0:T(8,128)} %get-tuple-element.38), channel_id=1, source_target_pairs={{0,4},{4,0},{8,12},{12,8},{1,5},{5,1},{9,13},{13,9},{2,6},{6,2},{1... | collective-permute-start | bytes 2383880 | tf_op jit(solution)/shard_map/ppermute | solution.py:448
  78.1 47.7 %collective-permute-start.18 = (s32[776,128]{1,0:T(8,128)}, s32[776,128]{1,0:T(8,128)S(1)}, u32[]{:S(2)}, u32[]{:S(2)}) collective-permute-start(s32[776,128]{1,0:T(8,128)} %get-tuple-element.36), channel_id=1, source_target_pairs={{0,12},{4,8},{8,4},{12,0},{1,13},{5,9},{9,5},{13,1},{2,14},{6,10},... | collective-permute-start | bytes 1191944 | tf_op jit(solution)/shard_map/ppermute | solution.py:448
  80.6 53.5 %collective-permute-start.19 = (s32[776,128]{1,0:T(8,128)}, s32[776,128]{1,0:T(8,128)}, u32[]{:S(2)}, u32[]{:S(2)}) collective-permute-start(s32[776,128]{1,0:T(8,128)} %get-tuple-element.37), channel_id=1, source_target_pairs={{0,8},{4,12},{8,0},{12,4},{1,9},{5,13},{9,1},{13,5},{2,10},{6,14},... | collective-permute-start | bytes 1191944 | tf_op jit(solution)/shard_map/ppermute | solution.py:448
  97.1 44.2 %collective-permute-start.15 = (s32[776,128]{1,0:T(8,128)}, s32[776,128]{1,0:T(8,128)}, u32[]{:S(2)}, u32[]{:S(2)}) collective-permute-start(s32[776,128]{1,0:T(8,128)} %get-tuple-element.33), channel_id=1, source_target_pairs={{0,12},{4,8},{8,4},{12,0},{1,13},{5,9},{9,5},{13,1},{2,14},{6,10},... | collective-permute-start | bytes 1191944 | tf_op jit(solution)/shard_map/ppermute | solution.py:448
  99.1 51.7 %collective-permute-start.16 = (s32[776,128]{1,0:T(8,128)}, s32[776,128]{1,0:T(8,128)}, u32[]{:S(2)}, u32[]{:S(2)}) collective-permute-start(s32[776,128]{1,0:T(8,128)} %get-tuple-element.34), channel_id=1, source_target_pairs={{0,8},{4,12},{8,0},{12,4},{1,9},{5,13},{9,1},{13,5},{2,10},{6,14},... | collective-permute-start | bytes 1191944 | tf_op jit(solution)/shard_map/ppermute | solution.py:448
  115.1 35.7 %collective-permute-start.17 = (s32[776,128]{1,0:T(8,128)}, s32[776,128]{1,0:T(8,128)}, u32[]{:S(2)}, u32[]{:S(2)}) collective-permute-start(s32[776,128]{1,0:T(8,128)} %get-tuple-element.35), channel_id=1, source_target_pairs={{0,4},{4,0},{8,12},{12,8},{1,5},{5,1},{9,13},{13,9},{2,6},{6,2},{1... | collective-permute-start | bytes 1191944 | tf_op jit(solution)/shard_map/ppermute | solution.py:448
  125.8 8.4 %copy-start = (s32[776,128]{1,0:T(8,128)}, s32[776,128]{1,0:T(8,128)S(1)}, u32[]{:S(2)}) copy-start(s32[776,128]{1,0:T(8,128)S(1)} %collective-permute-done.18.refs_5_.refs_0_) | copy-start | bytes 1191940

commit v11 on v10

--- a/solution.py
+++ b/solution.py
@@ -12,7 +12,7 @@
 STEPS_PER_OCTAVE = 64
 TOP = 32760.0
 FLOOR = 1e-30
-EIGHTHS = (2, 3, 3)
+EIGHTHS = (3, 3, 2)
 VMEM = 127 << 19
 EASE = 2
 ANYWHERE = pl.BlockSpec(memory_space=pl.ANY)

time: 155 us -> 158 us (1.019)
  waiting for transfers between devices: 43.7 us -> 46.4 us
    ppermute x9, waiting for transfers between devices: 12.2 us -> 15.2 us  [gather_pieces(): lax.ppermute(x, axes, [(i, i ^ flip) for i in range(n_src * n_feat)])]
where the time goes in v11:
time: 158 us; the launch traced here: 157 us
  Pallas kernels  88.5 us (56%)
  waiting for transfers between devices  46.4 us (29%)
  starting transfers between devices  21.3 us (13%)
    pallas_call x3, Pallas kernels, terms_call(): pl.pallas_call(functools.partial(terms_kernel, n_tgt, plan, offset, carri...  43.6 us
    ppermute x8, waiting for transfers between devices, body(): lax.ppermute(x, 'tgt', [(i, i ^ flip) for i in range(n_tgt)])  31.2 us
    pallas_call x2, Pallas kernels, grads_call(): pl.pallas_call(functools.partial(grads_kernel, t, tgt_count), grid=(layer...  20.1 us
    ppermute x9, waiting for transfers between devices, gather_pieces(): lax.ppermute(x, axes, [(i, i ^ flip) for i in range(n_src * n_feat)])  15.2 us
    ppermute x9, starting transfers between devices, gather_pieces(): lax.ppermute(x, axes, [(i, i ^ flip) for i in range(n_src * n_feat)])  11.2 us
    pallas_call x3, Pallas kernels, finish_call(): pl.pallas_call(functools.partial(finish_kernel, len(gots), offset, stride...  10.9 us
    ppermute x8, starting transfers between devices, body(): lax.ppermute(x, 'tgt', [(i, i ^ flip) for i in range(n_tgt)])  9.31 us
    pallas_call x4, Pallas kernels, cut_call(): pl.pallas_call(functools.partial(cut_kernel, len(join), offset), in_specs...  8.74 us
  transfers between devices with their start and end apart: 21, of which 8 were waited for; matrix products, arithmetic and copies ran while one was open for 0% of the time, Pallas kernels for 50%

profile of v11, /device:TPU:0, one launch (start us, length us, event | category | flops | bytes accessed | tf_op | source)
XLA Modules:
  0.0 157.2 jit_solution(13595561005390935618)
XLA Ops:
  0.6 0.5 collective-permute-start
  1.1 1.7 %cut.4 = bf16[2,96,1024]{2,1,0:T(8,128)(2,1)} custom-call(bf16[2,256,1024]{2,1,0:T(8,128)(2,1)} %refs_0_.5), custom_call_target="tpu_custom_call" | custom-call | bytes 393216 | tf_op jit(solution)/shard_map/cut/pallas_call | solution.py:101
  2.9 3.5 %collective-permute-start.3 = (bf16[2,96,1024]{2,1,0:T(8,128)(2,1)}, bf16[2,96,1024]{2,1,0:T(8,128)(2,1)S(1)}, u32[]{:S(2)}, u32[]{:S(2)}) collective-permute-start(bf16[2,96,1024]{2,1,0:T(8,128)(2,1)} %cut.4), channel_id=1, source_target_pairs={{0,18},{1,19},{2,16},{3,17},{16,2},{17,3},{18,0},{19,1},{4,22},{5,... | collective-permute-start | bytes 1179656 | tf_op jit(solution)/shard_map/ppermute | solution.py:415
  6.4 0.5 collective-permute-start.2
  6.9 0.1 collective-permute-start.1
  7.1 5.2 %turn.1.refs_4_.codes_ref = bf16[4,512,1024]{2,1,0:T(8,128)(2,1)} custom-call(bf16[4,1024,512]{2,1,0:T(8,128)(2,1)} %codes_ref.1), custom_call_target="tpu_custom_call" | custom-call | flops 1048576 | bytes 4194304 | tf_op jit(solution)/shard_map/turn/pallas_call | solution.py:346
  12.3 4.3 %collective-permute-done.3.refs_2_ = bf16[2,96,1024]{2,1,0:T(8,128)(2,1)S(1)} collective-permute-done((bf16[2,96,1024]{2,1,0:T(8,128)(2,1)}, bf16[2,96,1024]{2,1,0:T(8,128)(2,1)S(1)}, u32[]{:S(2)}, u32[]{:S(2)}) %collective-permute-start.3) | collective-permute-done | bytes 393248 | tf_op jit(solution)/shard_map/ppermute | solution.py:415
  16.7 0.0 copy-start.2
  16.7 8.3 %collective-permute-done.2.refs_1_ = bf16[2,96,1024]{2,1,0:T(8,128)(2,1)} collective-permute-done((bf16[2,96,1024]{2,1,0:T(8,128)(2,1)}, bf16[2,96,1024]{2,1,0:T(8,128)(2,1)}, u32[]{:S(2)}, u32[]{:S(2)}) %collective-permute-start.2) | collective-permute-done | bytes 393248 | tf_op jit(solution)/shard_map/ppermute | solution.py:415
  24.9 0.3 collective-permute-done.1.refs_0_
  25.2 0.0 collective-permute-done.refs_3_.refs_1_
  25.2 0.0 copy-done.2
  25.2 2.5 %cut.5 = (bf16[3,2,96,1024]{3,2,1,0:T(8,128)(2,1)}, bf16[2,96,1024]{2,1,0:T(8,128)(2,1)}) custom-call(bf16[2,256,1024]{2,1,0:T(8,128)(2,1)} %refs_0_.5, bf16[2,96,1024]{2,1,0:T(8,128)(2,1)} %collective-permute-done.1.refs_0_, bf16[2,96,1024]{2,1,0:T(8,128)(2,1)} %collective-permute-done.2.refs_1_, bf16[2,96,1024]{2,1,0:T(8,128)(2,1)} %copy-done.2, ...), custom_call_target="tpu_custom_call" | custom-call | bytes 1572864 | tf_op jit(solution)/shard_map/cut/pallas_call | solution.py:101
  27.8 0.1 collective-permute-start.7
  27.8 1.6 %collective-permute-start.6 = (bf16[2,96,1024]{2,1,0:T(8,128)(2,1)}, bf16[2,96,1024]{2,1,0:T(8,128)(2,1)S(1)}, u32[]{:S(2)}, u32[]{:S(2)}) collective-permute-start(bf16[2,96,1024]{2,1,0:T(8,128)(2,1)} %get-tuple-element.21), channel_id=1, source_target_pairs={{0,18},{1,19},{2,16},{3,17},{16,2},{17,3},{18,0},{19,1},{4,22},{5,... | collective-permute-start | bytes 1179656 | tf_op jit(solution)/shard_map/ppermute | solution.py:415
  29.4 1.4 collective-permute-start.5
  30.9 0.5 collective-permute-start.4
  31.4 0.0 collective-permute-done.7.refs_3_
  31.4 15.3 %terms.3 = (f32[4,96,512]{2,1,0:T(8,128)}, s32[776,128]{1,0:T(8,128)}, s32[776,128]{1,0:T(8,128)}, s32[776,128]{1,0:T(8,128)}, bf16[1024,4096]{1,0:T(8,128)(2,1)}) custom-call(bf16[2,256,1024]{2,1,0:T(8,128)(2,1)} %refs_0_.5, bf16[2,256,1024]{2,1,0:T(8,128)(2,1)} %collective-permute-done.refs_3_.refs_1_, bf16[3,2,96,1024]{3,2,1,0:T(8,128)(2,1)} %get-tuple-element.22.refs_2_, ...), custom_call_target="tpu_custom_call" | custom-call | flops 3221225472 | bytes 8388608 | tf_op jit(solution)/shard_map/terms/pallas_call | solution.py:227
  46.7 0.0 collective-permute-done.6.refs_2_
  46.7 0.0 copy-start.3
  46.7 2.3 %collective-permute-done.5.refs_1_ = bf16[2,96,1024]{2,1,0:T(8,128)(2,1)} collective-permute-done((bf16[2,96,1024]{2,1,0:T(8,128)(2,1)}, bf16[2,96,1024]{2,1,0:T(8,128)(2,1)}, u32[]{:S(2)}, u32[]{:S(2)}) %collective-permute-start.5) | collective-permute-done | bytes 393248 | tf_op jit(solution)/shard_map/ppermute | solution.py:415
  49.0 0.0 collective-permute-done.4.refs_0_
  49.0 0.0 copy-done.3
  49.0 2.4 %cut.6 = (bf16[3,2,96,1024]{3,2,1,0:T(8,128)(2,1)}, bf16[2,64,1024]{2,1,0:T(8,128)(2,1)}) custom-call(bf16[2,256,1024]{2,1,0:T(8,128)(2,1)} %refs_0_.5, bf16[2,96,1024]{2,1,0:T(8,128)(2,1)} %collective-permute-done.4.refs_0_, bf16[2,96,1024]{2,1,0:T(8,128)(2,1)} %collective-permute-done.5.refs_1_, bf16[2,96,1024]{2,1,0:T(8,128)(2,1)} %copy-done.3, ...), custom_call_target="tpu_custom_call" | custom-call | bytes 1441792 | tf_op jit(solution)/shard_map/cut/pallas_call | solution.py:101
  51.5 0.1 collective-permute-start.11
  51.6 3.6 %collective-permute-start.12 = (s32[776,128]{1,0:T(8,128)}, s32[776,128]{1,0:T(8,128)S(1)}, u32[]{:S(2)}, u32[]{:S(2)}) collective-permute-start(s32[776,128]{1,0:T(8,128)} %get-tuple-element.29), channel_id=1, source_target_pairs={{0,12},{4,8},{8,4},{12,0},{1,13},{5,9},{9,5},{13,1},{2,14},{6,10},... | collective-permute-start | bytes 1191944 | tf_op jit(solution)/shard_map/ppermute | solution.py:448
  55.2 0.0 collective-permute-start.13
  55.2 1.6 %collective-permute-start.10 = (bf16[2,64,1024]{2,1,0:T(8,128)(2,1)}, bf16[2,64,1024]{2,1,0:T(8,128)(2,1)}, u32[]{:S(2)}, u32[]{:S(2)}) collective-permute-start(bf16[2,64,1024]{2,1,0:T(8,128)(2,1)} %get-tuple-element.24), channel_id=1, source_target_pairs={{0,18},{1,19},{2,16},{3,17},{16,2},{17,3},{18,0},{19,1},{4,22},{5,... | collective-permute-start | bytes 786440 | tf_op jit(solution)/shard_map/ppermute | solution.py:415
  56.9 1.3 collective-permute-start.9
  58.2 0.0 collective-permute-done.11.refs_3_
  58.2 0.5 collective-permute-start.8
  58.7 15.4 %terms.4 = (f32[4,96,512]{2,1,0:T(8,128)}, s32[1552,128]{1,0:T(8,128)}, s32[776,128]{1,0:T(8,128)}, s32[776,128]{1,0:T(8,128)}, bf16[1024,4096]{1,0:T(8,128)(2,1)}) custom-call(bf16[2,256,1024]{2,1,0:T(8,128)(2,1)} %refs_0_.5, bf16[2,256,1024]{2,1,0:T(8,128)(2,1)} %collective-permute-done.refs_3_.refs_1_, ...), custom_call_target="tpu_custom_call", output_to_operand_aliasing={{4}: (6, {})} | custom-call | flops 3221225472 | bytes 8388608 | tf_op jit(solution)/shard_map/terms/pallas_call | solution.py:227
  74.2 0.0 collective-permute-done.10.refs_2_
  74.2 0.0 collective-permute-done.9.refs_1_
  74.2 0.0 collective-permute-done.8.refs_0_
  74.2 0.0 collective-permute-done.12.refs_4_.refs_0_
  74.2 0.0 copy-start.1
  74.2 15.9 %collective-permute-done.13.refs_5_.refs_1_ = s32[776,128]{1,0:T(8,128)} collective-permute-done((s32[776,128]{1,0:T(8,128)}, s32[776,128]{1,0:T(8,128)}, u32[]{:S(2)}, u32[]{:S(2)}) %collective-permute-start.13) | collective-permute-done | bytes 397344 | tf_op jit(solution)/shard_map/ppermute | solution.py:448
  90.1 0.0 copy-done.1
  90.1 2.0 %cut.7.refs_2_ = bf16[3,2,64,1024]{3,2,1,0:T(8,128)(2,1)} custom-call(bf16[2,256,1024]{2,1,0:T(8,128)(2,1)} %refs_0_.5, bf16[2,64,1024]{2,1,0:T(8,128)(2,1)} %collective-permute-done.8.refs_0_, bf16[2,64,1024]{2,1,0:T(8,128)(2,1)} %collective-permute-done.9.refs_1_, bf16[2,64,1024]{2,1,0:T(8,128)(2,1)} %collective-permute-done.10.refs_2_, ...), custom_call_target="tpu_custom_call" | custom-call | bytes 786432 | tf_op jit(solution)/shard_map/cut/pallas_call | solution.py:101
  92.1 0.1 collective-permute-start.14
  92.2 0.1 collective-permute-start.20
  92.2 2.5 %collective-permute-start.18 = (s32[776,128]{1,0:T(8,128)}, s32[776,128]{1,0:T(8,128)S(1)}, u32[]{:S(2)}, u32[]{:S(2)}) collective-permute-start(s32[776,128]{1,0:T(8,128)} %get-tuple-element.36), channel_id=1, source_target_pairs={{0,12},{4,8},{8,4},{12,0},{1,13},{5,9},{9,5},{13,1},{2,14},{6,10},... | collective-permute-start | bytes 1191944 | tf_op jit(solution)/shard_map/ppermute | solution.py:448
  94.8 0.9 collective-permute-start.19
  95.7 0.0 collective-permute-done.14.refs_3_
  95.7 12.9 %terms.5 = (f32[4,64,512]{2,1,0:T(8,128)}, s32[520,128]{1,0:T(8,128)}, s32[520,128]{1,0:T(8,128)}, s32[520,128]{1,0:T(8,128)}, bf16[1024,4096]{1,0:T(8,128)(2,1)}) custom-call(bf16[2,256,1024]{2,1,0:T(8,128)(2,1)} %refs_0_.5, bf16[2,256,1024]{2,1,0:T(8,128)(2,1)} %collective-permute-done.refs_3_.refs_1_, ...), custom_call_target="tpu_custom_call", output_to_operand_aliasing={{4}: (5, {})} | custom-call | flops 2147483648 | bytes 8388608 | tf_op jit(solution)/shard_map/terms/pallas_call | solution.py:227
  108.6 2.0 %collective-permute-start.15 = (s32[520,128]{1,0:T(8,128)}, s32[520,128]{1,0:T(8,128)}, u32[]{:S(2)}, u32[]{:S(2)}) collective-permute-start(s32[520,128]{1,0:T(8,128)} %get-tuple-element.33), channel_id=1, source_target_pairs={{0,12},{4,8},{8,4},{12,0},{1,13},{5,9},{9,5},{13,1},{2,14},{6,10},... | collective-permute-start | bytes 798728 | tf_op jit(solution)/shard_map/ppermute | solution.py:448
  110.6 0.1 collective-permute-start.16
  110.7 9.4 %grads.2.refs_0_ = bf16[4,2,512,2048]{3,2,1,0:T(8,128)(2,1)} custom-call(bf16[4,512,1024]{2,1,0:T(8,128)(2,1)} %turn.1.refs_4_.codes_ref, bf16[1024,4096]{1,0:T(8,128)(2,1)} %get-tuple-element.39.err_ref), custom_call_target="tpu_custom_call" | custom-call | flops 4294967296 | bytes 8388608 | tf_op jit(solution)/shard_map/grads/pallas_call | solution.py:391
  120.1 8.9 %collective-permute-done.20.refs_1_.refs_2_ = s32[1552,128]{1,0:T(8,128)} collective-permute-done((s32[1552,128]{1,0:T(8,128)}, s32[1552,128]{1,0:T(8,128)}, u32[]{:S(2)}, u32[]{:S(2)}) %collective-permute-start.20) | collective-permute-done | bytes 794656 | tf_op jit(solution)/shard_map/ppermute | solution.py:448
  129.1 0.0 collective-permute-start.17
  129.1 10.7 %grads.3.refs_4_ = bf16[4,2,512,2048]{3,2,1,0:T(8,128)(2,1)} custom-call(bf16[4,512,1024]{2,1,0:T(8,128)(2,1)} %turn.1.refs_4_.codes_ref, bf16[1024,4096]{1,0:T(8,128)(2,1)} %get-tuple-element.39.err_ref, bf16[4,2,512,2048]{3,2,1,0:T(8,128)(2,1)} %grads.2.refs_0_, s32[1552,128]{1,0:T(8,128)} %collective-permute-done.20.refs_1_.refs_2_), custom_call_target="tpu_custom_call", output_to_operand_aliasing={{}: (2, {})} | custom-call | flops 4294967296 | bytes 8388608 | tf_op jit(solution)/shard_map/grads/pallas_call | solution.py:391
  139.8 0.0 collective-permute-done.18.refs_5_.refs_0_
  139.8 0.0 copy-start
  139.8 3.3 %collective-permute-done.19.refs_6_.refs_1_ = s32[776,128]{1,0:T(8,128)} collective-permute-done((s32[776,128]{1,0:T(8,128)}, s32[776,128]{1,0:T(8,128)}, u32[]{:S(2)}, u32[]{:S(2)}) %collective-permute-start.19) | collective-permute-done | bytes 397344 | tf_op jit(solution)/shard_map/ppermute | solution.py:448
  143.1 0.0 copy-done
  143.1 3.8 %finish.3.refs_4_ = bf16[4,256,512]{2,1,0:T(8,128)(2,1)} custom-call(f32[4,96,512]{2,1,0:T(8,128)} %get-tuple-element.23.refs_3_.own_ref, s32[776,128]{1,0:T(8,128)} %copy-done.1, s32[776,128]{1,0:T(8,128)} %collective-permute-done.13.refs_5_.refs_1_, s32[1552,128]{1,0:T(8,128)} %collective-permute-done.20.refs_1_.refs_2_, s32[4,256,512]{2,1,0:T(8,128)} %refs_3_.5, ...), custom_call_target="tpu_custom_call" | custom-call | flops 1966080 | bytes 1572864 | tf_op jit(solution)/shard_map/finish/pallas_call | solution.py:311
  146.9 3.8 %finish.4.refs_4_ = bf16[4,256,512]{2,1,0:T(8,128)(2,1)} custom-call(f32[4,96,512]{2,1,0:T(8,128)} %get-tuple-element.28.refs_3_.own_ref, s32[776,128]{1,0:T(8,128)} %copy-done, s32[776,128]{1,0:T(8,128)} %collective-permute-done.19.refs_6_.refs_1_, s32[1552,128]{1,0:T(8,128)} %collective-permute-done.20.refs_1_.refs_2_, ...), custom_call_target="tpu_custom_call", output_to_operand_aliasing={{}: (5, {})} | custom-call | flops 1966080 | bytes 1572864 | tf_op jit(solution)/shard_map/finish/pallas_call | solution.py:311
  150.7 0.0 collective-permute-done.15.refs_0_
  150.7 3.1 %collective-permute-done.16.refs_1_ = s32[520,128]{1,0:T(8,128)} collective-permute-done((s32[520,128]{1,0:T(8,128)}, s32[520,128]{1,0:T(8,128)}, u32[]{:S(2)}, u32[]{:S(2)}) %collective-permute-start.16) | collective-permute-done | bytes 266272 | tf_op jit(solution)/shard_map/ppermute | solution.py:448
  153.7 0.0 collective-permute-done.17.refs_2_
  153.7 3.3 %finish.5 = bf16[4,256,512]{2,1,0:T(8,128)(2,1)} custom-call(f32[4,64,512]{2,1,0:T(8,128)} %get-tuple-element.32.own_ref, s32[520,128]{1,0:T(8,128)} %collective-permute-done.15.refs_0_, s32[520,128]{1,0:T(8,128)} %collective-permute-done.16.refs_1_, s32[520,128]{1,0:T(8,128)} %collective-permute-done.17.refs_2_, ...), custom_call_target="tpu_custom_call", output_to_operand_aliasing={{}: (5, {})} | custom-call | flops 1310720 | bytes 1048576 | tf_op jit(solution)/shard_map/finish/pallas_call | solution.py:311
Async XLA Ops:
  0.6 24.6 %collective-permute-start = (bf16[2,256,1024]{2,1,0:T(8,128)(2,1)}, bf16[2,256,1024]{2,1,0:T(8,128)(2,1)}, u32[]{:S(2)}, u32[]{:S(2)}) collective-permute-start(bf16[2,256,1024]{2,1,0:T(8,128)(2,1)} %refs_0_.5), channel_id=1, source_target_pairs={{0,1},{1,0},{2,3},{3,2},{4,5},{5,4},{6,7},{7,6},{8,9},{9,8},{10,11... | collective-permute-start | bytes 3145736 | tf_op jit(solution)/shard_map/ppermute | solution.py:433
  2.9 13.7 %collective-permute-start.3 = (bf16[2,96,1024]{2,1,0:T(8,128)(2,1)}, bf16[2,96,1024]{2,1,0:T(8,128)(2,1)S(1)}, u32[]{:S(2)}, u32[]{:S(2)}) collective-permute-start(bf16[2,96,1024]{2,1,0:T(8,128)(2,1)} %cut.4), channel_id=1, source_target_pairs={{0,18},{1,19},{2,16},{3,17},{16,2},{17,3},{18,0},{19,1},{4,22},{5,... | collective-permute-start | bytes 1179656 | tf_op jit(solution)/shard_map/ppermute | solution.py:415
  6.4 18.5 %collective-permute-start.2 = (bf16[2,96,1024]{2,1,0:T(8,128)(2,1)}, bf16[2,96,1024]{2,1,0:T(8,128)(2,1)}, u32[]{:S(2)}, u32[]{:S(2)}) collective-permute-start(bf16[2,96,1024]{2,1,0:T(8,128)(2,1)} %cut.4), channel_id=1, source_target_pairs={{0,2},{1,3},{2,0},{3,1},{16,18},{17,19},{18,16},{19,17},{4,6},{5,7... | collective-permute-start | bytes 1179656 | tf_op jit(solution)/shard_map/ppermute | solution.py:415
  6.9 18.3 %collective-permute-start.1 = (bf16[2,96,1024]{2,1,0:T(8,128)(2,1)}, bf16[2,96,1024]{2,1,0:T(8,128)(2,1)}, u32[]{:S(2)}, u32[]{:S(2)}) collective-permute-start(bf16[2,96,1024]{2,1,0:T(8,128)(2,1)} %cut.4), channel_id=1, source_target_pairs={{0,16},{1,17},{2,18},{3,19},{16,0},{17,1},{18,2},{19,3},{4,20},{5,... | collective-permute-start | bytes 1179656 | tf_op jit(solution)/shard_map/ppermute | solution.py:415
  16.7 8.6 %copy-start.2 = (bf16[2,96,1024]{2,1,0:T(8,128)(2,1)}, bf16[2,96,1024]{2,1,0:T(8,128)(2,1)S(1)}, u32[]{:S(2)}) copy-start(bf16[2,96,1024]{2,1,0:T(8,128)(2,1)S(1)} %collective-permute-done.3.refs_2_) | copy-start | bytes 1179652
  27.8 3.6 %collective-permute-start.7 = (bf16[3,2,96,1024]{3,2,1,0:T(8,128)(2,1)}, bf16[3,2,96,1024]{3,2,1,0:T(8,128)(2,1)}, u32[]{:S(2)}, u32[]{:S(2)}) collective-permute-start(bf16[3,2,96,1024]{3,2,1,0:T(8,128)(2,1)} %get-tuple-element.22.refs_2_), channel_id=1, source_target_pairs={{0,1},{1,0},{2,3},{3,2},{4,5},{5,4},{6,7},{7,6},{8,9},{9,8},{10,11... | collective-permute-start | bytes 3538952 | tf_op jit(solution)/shard_map/ppermute | solution.py:433
  27.8 18.8 %collective-permute-start.6 = (bf16[2,96,1024]{2,1,0:T(8,128)(2,1)}, bf16[2,96,1024]{2,1,0:T(8,128)(2,1)S(1)}, u32[]{:S(2)}, u32[]{:S(2)}) collective-permute-start(bf16[2,96,1024]{2,1,0:T(8,128)(2,1)} %get-tuple-element.21), channel_id=1, source_target_pairs={{0,18},{1,19},{2,16},{3,17},{16,2},{17,3},{18,0},{19,1},{4,22},{5,... | collective-permute-start | bytes 1179656 | tf_op jit(solution)/shard_map/ppermute | solution.py:415
  29.4 19.6 %collective-permute-start.5 = (bf16[2,96,1024]{2,1,0:T(8,128)(2,1)}, bf16[2,96,1024]{2,1,0:T(8,128)(2,1)}, u32[]{:S(2)}, u32[]{:S(2)}) collective-permute-start(bf16[2,96,1024]{2,1,0:T(8,128)(2,1)} %get-tuple-element.21), channel_id=1, source_target_pairs={{0,2},{1,3},{2,0},{3,1},{16,18},{17,19},{18,16},{19,17},{4,6},{5,7... | collective-permute-start | bytes 1179656 | tf_op jit(solution)/shard_map/ppermute | solution.py:415
  30.9 18.2 %collective-permute-start.4 = (bf16[2,96,1024]{2,1,0:T(8,128)(2,1)}, bf16[2,96,1024]{2,1,0:T(8,128)(2,1)}, u32[]{:S(2)}, u32[]{:S(2)}) collective-permute-start(bf16[2,96,1024]{2,1,0:T(8,128)(2,1)} %get-tuple-element.21), channel_id=1, source_target_pairs={{0,16},{1,17},{2,18},{3,19},{16,0},{17,1},{18,2},{19,3},{4,20},{5,... | collective-permute-start | bytes 1179656 | tf_op jit(solution)/shard_map/ppermute | solution.py:415
  46.7 2.3 %copy-start.3 = (bf16[2,96,1024]{2,1,0:T(8,128)(2,1)}, bf16[2,96,1024]{2,1,0:T(8,128)(2,1)S(1)}, u32[]{:S(2)}) copy-start(bf16[2,96,1024]{2,1,0:T(8,128)(2,1)S(1)} %collective-permute-done.6.refs_2_) | copy-start | bytes 1179652
  51.5 6.7 %collective-permute-start.11 = (bf16[3,2,96,1024]{3,2,1,0:T(8,128)(2,1)}, bf16[3,2,96,1024]{3,2,1,0:T(8,128)(2,1)}, u32[]{:S(2)}, u32[]{:S(2)}) collective-permute-start(bf16[3,2,96,1024]{3,2,1,0:T(8,128)(2,1)} %get-tuple-element.25.refs_2_), channel_id=1, source_target_pairs={{0,1},{1,0},{2,3},{3,2},{4,5},{5,4},{6,7},{7,6},{8,9},{9,8},{10,11... | collective-permute-start | bytes 3538952 | tf_op jit(solution)/shard_map/ppermute | solution.py:433
  51.6 22.6 %collective-permute-start.12 = (s32[776,128]{1,0:T(8,128)}, s32[776,128]{1,0:T(8,128)S(1)}, u32[]{:S(2)}, u32[]{:S(2)}) collective-permute-start(s32[776,128]{1,0:T(8,128)} %get-tuple-element.29), channel_id=1, source_target_pairs={{0,12},{4,8},{8,4},{12,0},{1,13},{5,9},{9,5},{13,1},{2,14},{6,10},... | collective-permute-start | bytes 1191944 | tf_op jit(solution)/shard_map/ppermute | solution.py:448
  55.2 34.8 %collective-permute-start.13 = (s32[776,128]{1,0:T(8,128)}, s32[776,128]{1,0:T(8,128)}, u32[]{:S(2)}, u32[]{:S(2)}) collective-permute-start(s32[776,128]{1,0:T(8,128)} %get-tuple-element.30), channel_id=1, source_target_pairs={{0,8},{4,12},{8,0},{12,4},{1,9},{5,13},{9,1},{13,5},{2,10},{6,14},... | collective-permute-start | bytes 1191944 | tf_op jit(solution)/shard_map/ppermute | solution.py:448
  55.2 18.9 %collective-permute-start.10 = (bf16[2,64,1024]{2,1,0:T(8,128)(2,1)}, bf16[2,64,1024]{2,1,0:T(8,128)(2,1)}, u32[]{:S(2)}, u32[]{:S(2)}) collective-permute-start(bf16[2,64,1024]{2,1,0:T(8,128)(2,1)} %get-tuple-element.24), channel_id=1, source_target_pairs={{0,18},{1,19},{2,16},{3,17},{16,2},{17,3},{18,0},{19,1},{4,22},{5,... | collective-permute-start | bytes 786440 | tf_op jit(solution)/shard_map/ppermute | solution.py:415
  56.9 17.3 %collective-permute-start.9 = (bf16[2,64,1024]{2,1,0:T(8,128)(2,1)}, bf16[2,64,1024]{2,1,0:T(8,128)(2,1)}, u32[]{:S(2)}, u32[]{:S(2)}) collective-permute-start(bf16[2,64,1024]{2,1,0:T(8,128)(2,1)} %get-tuple-element.24), channel_id=1, source_target_pairs={{0,2},{1,3},{2,0},{3,1},{16,18},{17,19},{18,16},{19,17},{4,6},{5,7... | collective-permute-start | bytes 786440 | tf_op jit(solution)/shard_map/ppermute | solution.py:415
  58.2 16.0 %collective-permute-start.8 = (bf16[2,64,1024]{2,1,0:T(8,128)(2,1)}, bf16[2,64,1024]{2,1,0:T(8,128)(2,1)}, u32[]{:S(2)}, u32[]{:S(2)}) collective-permute-start(bf16[2,64,1024]{2,1,0:T(8,128)(2,1)} %get-tuple-element.24), channel_id=1, source_target_pairs={{0,16},{1,17},{2,18},{3,19},{16,0},{17,1},{18,2},{19,3},{4,20},{5,... | collective-permute-start | bytes 786440 | tf_op jit(solution)/shard_map/ppermute | solution.py:415
  74.2 15.9 %copy-start.1 = (s32[776,128]{1,0:T(8,128)}, s32[776,128]{1,0:T(8,128)S(1)}, u32[]{:S(2)}) copy-start(s32[776,128]{1,0:T(8,128)S(1)} %collective-permute-done.12.refs_4_.refs_0_) | copy-start | bytes 1191940
  92.1 3.6 %collective-permute-start.14 = (bf16[3,2,64,1024]{3,2,1,0:T(8,128)(2,1)}, bf16[3,2,64,1024]{3,2,1,0:T(8,128)(2,1)}, u32[]{:S(2)}, u32[]{:S(2)}) collective-permute-start(bf16[3,2,64,1024]{3,2,1,0:T(8,128)(2,1)} %cut.7.refs_2_), channel_id=1, source_target_pairs={{0,1},{1,0},{2,3},{3,2},{4,5},{5,4},{6,7},{7,6},{8,9},{9,8},{10,11... | collective-permute-start | bytes 2359304 | tf_op jit(solution)/shard_map/ppermute | solution.py:433
  92.2 36.9 %collective-permute-start.20 = (s32[1552,128]{1,0:T(8,128)}, s32[1552,128]{1,0:T(8,128)}, u32[]{:S(2)}, u32[]{:S(2)}) collective-permute-start(s32[1552,128]{1,0:T(8,128)} %get-tuple-element.38), channel_id=1, source_target_pairs={{0,4},{4,0},{8,12},{12,8},{1,5},{5,1},{9,13},{13,9},{2,6},{6,2},{1... | collective-permute-start | bytes 2383880 | tf_op jit(solution)/shard_map/ppermute | solution.py:448
  92.2 47.5 %collective-permute-start.18 = (s32[776,128]{1,0:T(8,128)}, s32[776,128]{1,0:T(8,128)S(1)}, u32[]{:S(2)}, u32[]{:S(2)}) collective-permute-start(s32[776,128]{1,0:T(8,128)} %get-tuple-element.36), channel_id=1, source_target_pairs={{0,12},{4,8},{8,4},{12,0},{1,13},{5,9},{9,5},{13,1},{2,14},{6,10},... | collective-permute-start | bytes 1191944 | tf_op jit(solution)/shard_map/ppermute | solution.py:448
  94.8 48.3 %collective-permute-start.19 = (s32[776,128]{1,0:T(8,128)}, s32[776,128]{1,0:T(8,128)}, u32[]{:S(2)}, u32[]{:S(2)}) collective-permute-start(s32[776,128]{1,0:T(8,128)} %get-tuple-element.37), channel_id=1, source_target_pairs={{0,8},{4,12},{8,0},{12,4},{1,9},{5,13},{9,1},{13,5},{2,10},{6,14},... | collective-permute-start | bytes 1191944 | tf_op jit(solution)/shard_map/ppermute | solution.py:448
  108.6 42.1 %collective-permute-start.15 = (s32[520,128]{1,0:T(8,128)}, s32[520,128]{1,0:T(8,128)}, u32[]{:S(2)}, u32[]{:S(2)}) collective-permute-start(s32[520,128]{1,0:T(8,128)} %get-tuple-element.33), channel_id=1, source_target_pairs={{0,12},{4,8},{8,4},{12,0},{1,13},{5,9},{9,5},{13,1},{2,14},{6,10},... | collective-permute-start | bytes 798728 | tf_op jit(solution)/shard_map/ppermute | solution.py:448
  110.6 43.1 %collective-permute-start.16 = (s32[520,128]{1,0:T(8,128)}, s32[520,128]{1,0:T(8,128)}, u32[]{:S(2)}, u32[]{:S(2)}) collective-permute-start(s32[520,128]{1,0:T(8,128)} %get-tuple-element.34), channel_id=1, source_target_pairs={{0,8},{4,12},{8,0},{12,4},{1,9},{5,13},{9,1},{13,5},{2,10},{6,14},... | collective-permute-start | bytes 798728 | tf_op jit(solution)/shard_map/ppermute | solution.py:448
  129.1 24.7 %collective-permute-start.17 = (s32[520,128]{1,0:T(8,128)}, s32[520,128]{1,0:T(8,128)}, u32[]{:S(2)}, u32[]{:S(2)}) collective-permute-start(s32[520,128]{1,0:T(8,128)} %get-tuple-element.35), channel_id=1, source_target_pairs={{0,4},{4,0},{8,12},{12,8},{1,5},{5,1},{9,13},{13,9},{2,6},{6,2},{1... | collective-permute-start | bytes 798728 | tf_op jit(solution)/shard_map/ppermute | solution.py:448
  139.8 3.3 %copy-start = (s32[776,128]{1,0:T(8,128)}, s32[776,128]{1,0:T(8,128)S(1)}, u32[]{:S(2)}) copy-start(s32[776,128]{1,0:T(8,128)S(1)} %collective-permute-done.18.refs_5_.refs_0_) | copy-start | bytes 1191940
